TPU v7x, 256 devices: a whole 4x4x8 slice. The times are simulated.
256 devices in a mesh: outer: 16 (over y_hi, x, core), inner: 16 (over z, y_lo).
Axes of the slice: x: 4, y: 4 (y_hi: 2, y_lo: 2; y = y_hi * 2 + y_lo), z: 8, core: 2. Of those that a mesh axis runs over, the one named last changes fastest.
Arguments:
- queries: bfloat16 [32768, 1024], P(('outer', 'inner')), may hold values from -4.5 to 4.5
- key_vectors: bfloat16 [32768, 128], P(('outer', 'inner')), may hold values from -4.5 to 4.5
- value_vectors: bfloat16 [32768, 128], P(('outer', 'inner')), may hold values from -4 to 4
- grad_output: bfloat16 [32768, 1024], P(('outer', 'inner')), may hold values from -4 to 4
- positions: int32 [32768], P(('outer', 'inner')), may hold values from 0 to 32767, as said below
Outputs:
- attended: bfloat16 [32768, 1024], P(('outer', 'inner'))
- grad_queries: bfloat16 [32768, 1024], P(('outer', 'inner'))
- grad_keys: bfloat16 [32768, 128], P(('outer', 'inner'))
- grad_values: bfloat16 [32768, 128], P(('outer', 'inner'))
Inputs may be any that keep to these rules, and one draw needn't show every extreme that they name: Each run of 2048 rows holds the positions of one segment, 2048 times the segment's number plus 0 to 2047, each once. The 128 rows of one device hold two blocks of 64 ascending consecutive positions: block b of its segment first, then block 31 - b, where b runs over a permutation of 0 to 15 drawn anew for each segment.
All inputs are finite; a program needn't handle non-finite values.
Results may differ from a plain program's by a relative error of at most 0.03.
Values may be sent and summed in bfloat16 or wider, within the bound.
No kernel may reach another device: no remote copies, remote signals or barrier semaphores. Data moves between devices by JAX's collectives and lax.ppermute only.
A program may use at most 64 MiB of HBM per device.

v0:
```python
import jax
import jax.numpy as jnp
from jax import lax
from jax.sharding import PartitionSpec as P

masked_score = -1e30


def from_behind(block, axis, distance):
    devices = range(lax.axis_size(axis))
    route = [(i - distance, i) for i in devices if i - distance in devices]
    return lax.ppermute(block, axis, route)


def block_scores(query_block, key_block, score_scale):
    return (
        jnp.einsum("thd,kd->thk", query_block, key_block, preferred_element_type=jnp.float32)
        * score_scale
    )


def body(queries, key_vectors, value_vectors, grad_output, positions):
    tok_rows, full_width = queries.shape
    head_dim = key_vectors.shape[1]
    head_count = full_width // head_dim
    score_scale = float(head_dim) ** (-0.5)
    key_value = jnp.concatenate([key_vectors, value_vectors], axis=1)
    group_kv, group_positions = (
        lax.all_gather(key_value, "inner", axis=0, tiled=True),
        lax.all_gather(positions, "inner", axis=0, tiled=True),
    )
    prev_kv = from_behind(group_kv, "outer", 1)
    own_keys = group_kv[:, :head_dim]
    own_values = group_kv[:, head_dim:]
    prev_keys = prev_kv[:, :head_dim]
    prev_values = prev_kv[:, head_dim:]
    has_prev = lax.axis_index("outer") > 0
    own_mask = group_positions[None, :] <= positions[:, None]
    head_block = head_count
    while head_block * tok_rows > 512 and head_block % 2 == 0:
        head_block = head_block // 2
    span_rows = group_kv.shape[0]
    own_terms = jnp.zeros((span_rows, 2 * head_dim), jnp.float32)
    prev_terms = jnp.zeros((span_rows, 2 * head_dim), jnp.float32)
    attn_parts = []
    query_parts = []
    for head_start in range(0, head_count, head_block):
        col_start = head_start * head_dim
        col_stop = (head_start + head_block) * head_dim
        query_block = queries[:, col_start:col_stop].reshape(tok_rows, head_block, head_dim)
        grad_block = grad_output[:, col_start:col_stop].reshape(tok_rows, head_block, head_dim)
        own_scores = jnp.where(
            own_mask[:, None, :], block_scores(query_block, own_keys, score_scale), masked_score
        )
        prev_scores = jnp.where(
            has_prev, block_scores(query_block, prev_keys, score_scale), masked_score
        )
        row_max = jnp.maximum(
            jnp.max(own_scores, axis=-1, keepdims=True),
            jnp.max(prev_scores, axis=-1, keepdims=True),
        )
        own_exp = jnp.exp(own_scores - row_max)
        prev_exp = jnp.exp(prev_scores - row_max)
        row_total = jnp.sum(own_exp, axis=-1, keepdims=True) + jnp.sum(
            prev_exp, axis=-1, keepdims=True
        )
        own_probs = own_exp / row_total
        prev_probs = prev_exp / row_total
        own_weights = own_probs.astype(jnp.bfloat16)
        prev_weights = prev_probs.astype(jnp.bfloat16)
        attn_sum = jnp.einsum(
            "thk,kd->thd", own_weights, own_values, preferred_element_type=jnp.float32
        )
        attn_sum = attn_sum + jnp.einsum(
            "thk,kd->thd", prev_weights, prev_values, preferred_element_type=jnp.float32
        )
        attn_out = attn_sum.astype(jnp.bfloat16)
        row_delta = jnp.sum(
            grad_block.astype(jnp.float32) * attn_out.astype(jnp.float32), axis=-1, keepdims=True
        )
        own_pgrad = jnp.einsum(
            "thd,kd->thk", grad_block, own_values, preferred_element_type=jnp.float32
        )
        prev_pgrad = jnp.einsum(
            "thd,kd->thk", grad_block, prev_values, preferred_element_type=jnp.float32
        )
        own_dscore = (own_probs * (own_pgrad - row_delta)).astype(jnp.bfloat16)
        prev_dscore = (prev_probs * (prev_pgrad - row_delta)).astype(jnp.bfloat16)
        query_grad = jnp.einsum(
            "thk,kd->thd", own_dscore, own_keys, preferred_element_type=jnp.float32
        )
        query_grad = query_grad + jnp.einsum(
            "thk,kd->thd", prev_dscore, prev_keys, preferred_element_type=jnp.float32
        )
        query_grad = (query_grad * score_scale).astype(jnp.bfloat16)
        own_terms = own_terms + jnp.concatenate(
            [
                jnp.einsum(
                    "thk,thd->kd", own_dscore, query_block, preferred_element_type=jnp.float32
                )
                * score_scale,
                jnp.einsum(
                    "thk,thd->kd", own_weights, grad_block, preferred_element_type=jnp.float32
                ),
            ],
            axis=1,
        )
        prev_terms = prev_terms + jnp.concatenate(
            [
                jnp.einsum(
                    "thk,thd->kd", prev_dscore, query_block, preferred_element_type=jnp.float32
                )
                * score_scale,
                jnp.einsum(
                    "thk,thd->kd", prev_weights, grad_block, preferred_element_type=jnp.float32
                ),
            ],
            axis=1,
        )
        attn_parts.append(attn_out.reshape(tok_rows, head_block * head_dim))
        query_parts.append(query_grad.reshape(tok_rows, head_block * head_dim))
    attended = jnp.concatenate(attn_parts, axis=1)
    grad_queries = jnp.concatenate(query_parts, axis=1)
    returned = from_behind(prev_terms.astype(jnp.bfloat16), "outer", -1).astype(prev_terms.dtype)
    key_grads = lax.psum_scatter(
        (own_terms + returned).astype(jnp.bfloat16), "inner", scatter_dimension=0, tiled=True
    ).astype(jnp.float32)
    grad_keys = key_grads[:, :head_dim].astype(jnp.bfloat16)
    grad_values = key_grads[:, head_dim:].astype(jnp.bfloat16)
    return (attended, grad_queries, grad_keys, grad_values)


def solution(mesh):
    return jax.shard_map(
        body,
        mesh=mesh,
        in_specs=(
            P(("outer", "inner"), None),
            P(("outer", "inner"), None),
            P(("outer", "inner"), None),
            P(("outer", "inner"), None),
            P(("outer", "inner")),
        ),
        out_specs=(
            P(("outer", "inner"), None),
            P(("outer", "inner"), None),
            P(("outer", "inner"), None),
            P(("outer", "inner"), None),
        ),
        check_vma=False,
    )
```

profile of v0, /device:TPU:16, one launch (start us, length us, event | category | flops | bytes accessed | tf_op | source)
XLA Modules:
  0.0 218.4 jit_solution(17593961631582976790)
XLA Ops:
  7.2 1.4 pad_maximum_fusion.2
  11.2 36.1 %all-gather = s32[16,1,128]{2,1,0:T(1,128)S(1)} all-gather(s32[1,1,128]{2,1,0:T(1,128)} %bitcast.188), channel_id=1, replica_groups=mesh['outer'=16,'inner'=16] {'inner'}, dimensions={0}, use_global_device_ids=true | all-gather | bytes 8704 | tf_op jit(solution)/shard_map/all_gather | solution.py:30
  47.3 34.4 %all-gather.3.cloned.1.call-done = bf16[2048,256]{1,0:T(8,128)(2,1)} async-done(((bf16[128,256]{1,0:T(8,128)(2,1)}), bf16[2048,256]{1,0:T(8,128)(2,1)}) %all-gather.3.cloned.1.call-update) | async-done | bytes 1048592 | tf_op jit(solution)/shard_map/all_gather | solution.py:29
  81.7 2.0 collective-permute-start
  84.7 1.7 fusion.46
  87.2 14.5 %collective-permute-done = bf16[2048,256]{1,0:T(8,128)(2,1)S(1)} collective-permute-done((bf16[2048,256]{1,0:T(8,128)(2,1)}, bf16[2048,256]{1,0:T(8,128)(2,1)S(1)}, u32[]{:S(2)}, u32[]{:S(2)}) %collective-permute-start) | collective-permute-done | bytes 1048608 | tf_op jit(solution)/shard_map/ppermute | solution.py:12
  103.2 3.0 %fusion.11 = (f32[128,4]{0,1:T(4,128)S(1)}, f32[128,4]{0,1:T(4,128)S(1)}, f32[128,4]{0,1:T(4,128)S(1)}, f32[128,4]{0,1:T(4,128)S(1)}) fusion(f32[2048,128,4]{1,0,2:T(8,128)S(1)} %get-tuple-element.33, f32[128,4]{0,1:T(4,128)S(1)} %max.16, pred[]{:T(512)S(6)} %gt.3, f32[128,4,2048]{0,2,1:T(8,128)S(1)} %get-tuple-element.31, ...), kind=kLoop, calls=%fused_computation.25 | loop fusion | flops 12580864 | bytes 16789504 | tf_op jit(solution)/shard_map/reduce_sum | solution.py:64
  106.9 1.2 convolution_bitcast_fusion
  108.8 1.2 convolution_bitcast_fusion.2
  111.3 1.2 multiply_reduce_fusion
  112.5 1.1 fusion.1
  114.3 1.3 fusion
  117.0 1.8 multiply_reduce_fusion.1
  118.8 1.3 fusion.2
  121.6 1.9 collective-permute-start.1
  124.3 1.0 fusion.3
  126.7 9.1 %collective-permute-done.1 = bf16[2048,256]{0,1:T(8,128)(2,1)S(1)} collective-permute-done((bf16[2048,256]{0,1:T(8,128)(2,1)S(1)}, bf16[2048,256]{0,1:T(8,128)(2,1)S(1)}, u32[]{:S(2)}, u32[]{:S(2)}) %collective-permute-start.1) | collective-permute-done | bytes 1048608 | tf_op jit(solution)/shard_map/ppermute | solution.py:12
  136.3 1.3 copy.173
  137.7 1.6 fusion.33
  139.4 2.2 %fusion.28 = bf16[128,4,128]{0,2,1:T(8,128)(2,1)S(1)} fusion(f32[128,4,128]{0,2,1:T(8,128)S(1)} %fusion.33, bf16[128,4,2048]{0,2,1:T(8,128)(2,1)} %copy-done, bf16[2048,256]{1,0:T(8,128)(2,1)S(1)} %copy-done.5), kind=kOutput, calls=%fused_computation.56 | convolution fusion | flops 268632064 | bytes 3014656 | tf_op jit(solution)/shard_map/thk,kd->thd/dot_general | solution.py:92
  142.8 2.2 fusion.34
  144.9 1.2 fusion.27
  148.6 61.6 %reduce-scatter.4.cloned.1.call-done = bf16[128,256]{1,0:T(8,128)(2,1)} async-done(((bf16[2048,256]{1,0:T(8,128)(2,1)}), bf16[128,256]{1,0:T(8,128)(2,1)}) %reduce-scatter.4.cloned.1.call-update) | async-done | bytes 65552
  210.2 1.4 fusion.45
  (50 shorter events, 18.2 us)
Async XLA Ops:
  7.2 74.5 %all-gather.3.cloned.1.call-start = ((), (), s32[]{:S(2)}) async-start(), calls=%async_computation.1 | async-start | bytes 1114112 | tf_op jit(solution)/shard_map/all_gather | solution.py:29
  8.7 201.5 %reduce-scatter.4.cloned.1.call-start = ((), (), s32[]{:S(2)}) async-start(), calls=%async_computation.2 | async-start | bytes 1114112
  81.7 4.8 %copy-start.6 = (bf16[2048,256]{1,0:T(8,128)(2,1)S(1)}, bf16[2048,256]{1,0:T(8,128)(2,1)}, u32[]{:S(2)}) copy-start(bf16[2048,256]{1,0:T(8,128)(2,1)} %all-gather.3.cloned.1.call-done) | copy-start | bytes 3145732
  81.7 20.1 %collective-permute-start = (bf16[2048,256]{1,0:T(8,128)(2,1)}, bf16[2048,256]{1,0:T(8,128)(2,1)S(1)}, u32[]{:S(2)}, u32[]{:S(2)}) collective-permute-start(bf16[2048,256]{1,0:T(8,128)(2,1)} %all-gather.3.cloned.1.call-done), channel_id=1, source_target_pairs={{0,16},{16,32},{32,48},{48,64},{64,80},{80,96},{96,112},{112,128},... | collective-permute-start | bytes 3145736 | tf_op jit(solution)/shard_map/ppermute | solution.py:12
  101.8 17.1 %copy-start.4 = (bf16[2048,256]{1,0:T(8,128)(2,1)}, bf16[2048,256]{1,0:T(8,128)(2,1)S(1)}, u32[]{:S(2)}) copy-start(bf16[2048,256]{1,0:T(8,128)(2,1)S(1)} %collective-permute-done) | copy-start | bytes 3145732
  115.7 3.1 %copy-start = (bf16[128,4,2048]{0,2,1:T(8,128)(2,1)}, bf16[128,4,2048]{0,2,1:T(8,128)(2,1)S(1)}, u32[]{:S(2)}) copy-start(bf16[128,4,2048]{0,2,1:T(8,128)(2,1)S(1)} %fusion) | copy-start | bytes 6291460
  120.2 1.4 copy-start.1
  121.6 14.2 %collective-permute-start.1 = (bf16[2048,256]{0,1:T(8,128)(2,1)S(1)}, bf16[2048,256]{0,1:T(8,128)(2,1)S(1)}, u32[]{:S(2)}, u32[]{:S(2)}) collective-permute-start(bf16[2048,256]{0,1:T(8,128)(2,1)S(1)} %fusion.20), channel_id=1, source_target_pairs={{16,0},{32,16},{48,32},{64,48},{80,64},{96,80},{112,96},{128,112},... | collective-permute-start | bytes 3145736 | tf_op jit(solution)/shard_map/ppermute | solution.py:12
  125.3 1.3 copy-start.3
  137.6 1.8 copy-start.5
  139.4 5.6 %copy-start.2 = (bf16[128,4,2048]{0,2,1:T(8,128)(2,1)S(1)}, bf16[128,4,2048]{0,2,1:T(8,128)(2,1)}, u32[]{:S(2)}) copy-start(bf16[128,4,2048]{0,2,1:T(8,128)(2,1)} %copy-done.1) | copy-start | bytes 6291460
Sparse Core Ops, SparseCore 0:
  10.4 71.2 all-gather.2
  137.7 72.3 reduce-scatter.3
where the time goes:
time: 219 us; the launch traced here: 218 us
  waiting for transfers between devices  120 us (55%)
  blocking collectives  36.1 us (16%)
  matrix products  27 us (12%)
  between operations  14.4 us (7%)
  other arithmetic  9.24 us (4%)
  local copies, waits for them, and re-layouts  7.95 us (4%)
  starting transfers between devices  4.04 us (2%)
    unnamed x3, waiting for transfers between devices  61.6 us
    all_gather x1, blocking collectives, body(): lax.all_gather(positions, 'inner', axis=0, tiled=True)  36.1 us
    all_gather x1, waiting for transfers between devices, body(): lax.all_gather(key_value, 'inner', axis=0, tiled=True)  34.4 us
    ppermute x2, waiting for transfers between devices, from_behind(): return lax.ppermute(block, axis, route)  23.7 us
  transfers between devices with their start and end apart: 4, of which 4 were waited for; matrix products, arithmetic and copies ran while one was open for 9% of the time, Pallas kernels for 0%

commit v1 on v0

--- a/solution.py
+++ b/solution.py
@@ -10,6 +10,20 @@
     devices = range(lax.axis_size(axis))
     route = [(i - distance, i) for i in devices if i - distance in devices]
     return lax.ppermute(block, axis, route)
+
+
+def gather_direct(block, axis):
+    count = lax.axis_size(axis)
+    copies = jnp.broadcast_to(block[None], (count,) + block.shape)
+    gathered = lax.all_to_all(copies, axis, 0, 0, tiled=True)
+    return gathered.reshape((count * block.shape[0],) + block.shape[1:])
+
+
+def sum_direct(terms, axis):
+    count = lax.axis_size(axis)
+    parts = terms.reshape((count, terms.shape[0] // count) + terms.shape[1:])
+    parts = lax.all_to_all(parts, axis, 0, 0, tiled=True)
+    return jnp.sum(parts.astype(jnp.float32), axis=0)
 
 
 def block_scores(query_block, key_block, score_scale):
@@ -26,8 +40,8 @@
     score_scale = float(head_dim) ** (-0.5)
     key_value = jnp.concatenate([key_vectors, value_vectors], axis=1)
     group_kv, group_positions = (
-        lax.all_gather(key_value, "inner", axis=0, tiled=True),
-        lax.all_gather(positions, "inner", axis=0, tiled=True),
+        gather_direct(key_value, "inner"),
+        gather_direct(positions, "inner"),
     )
     prev_kv = from_behind(group_kv, "outer", 1)
     own_keys = group_kv[:, :head_dim]
@@ -122,9 +136,7 @@
     attended = jnp.concatenate(attn_parts, axis=1)
     grad_queries = jnp.concatenate(query_parts, axis=1)
     returned = from_behind(prev_terms.astype(jnp.bfloat16), "outer", -1).astype(prev_terms.dtype)
-    key_grads = lax.psum_scatter(
-        (own_terms + returned).astype(jnp.bfloat16), "inner", scatter_dimension=0, tiled=True
-    ).astype(jnp.float32)
+    key_grads = sum_direct((own_terms + returned).astype(jnp.bfloat16), "inner")
     grad_keys = key_grads[:, :head_dim].astype(jnp.bfloat16)
     grad_values = key_grads[:, head_dim:].astype(jnp.bfloat16)
     return (attended, grad_queries, grad_keys, grad_values)

time: 219 us -> 140 us (0.64)
  waiting for transfers between devices: 120 us -> 66.8 us
  blocking collectives: 36.1 us -> 0 us
  starting transfers between devices: 4.04 us -> 24.6 us
  between operations: 14.4 us -> 1.04 us
  local copies, waits for them, and re-layouts: 7.95 us -> 10.4 us
    unnamed x3 -> x0, waiting for transfers between devices: 61.6 us -> none
    all_to_all x0 -> x3, waiting for transfers between devices: none -> 46.6 us  [the longest x2 32.6 us: gather_direct(): gathered = lax.all_to_all(copies, axis, 0, 0, tiled=True)]
    all_gather x1 -> x0, blocking collectives: 36.1 us -> none  [body(): lax.all_gather(positions, 'inner', axis=0, tiled=True)]
    all_gather x1 -> x0, waiting for transfers between devices: 34.4 us -> none  [body(): lax.all_gather(key_value, 'inner', axis=0, tiled=True)]
    all_to_all x0 -> x3, starting transfers between devices: none -> 20.8 us  [the longest x2 12.8 us: gather_direct(): gathered = lax.all_to_all(copies, axis, 0, 0, tiled=True)]
    ppermute x2, waiting for transfers between devices: 23.7 us -> 20.2 us  [from_behind(): return lax.ppermute(block, axis, route)]
    broadcast_in_dim x0 -> x2, local copies, waits for them, and re-layouts: none -> 2.35 us  [gather_direct(): copies = jnp.broadcast_to(block[None], (count,) + block.shape)]
  transfers between devices with their start and end apart: 4 -> 5, of which waited for: 4 -> 5; matrix products, arithmetic and copies ran while one was open for 9% -> 14% of each run, Pallas kernels for 0% -> 0%
where the time goes in v1:
time: 140 us; the launch traced here: 139 us
  waiting for transfers between devices  66.8 us (48%)
  matrix products  27 us (19%)
  starting transfers between devices  24.6 us (18%)
  local copies, waits for them, and re-layouts  10.4 us (7%)
  other arithmetic  8.96 us (6%)
    all_to_all x2, waiting for transfers between devices, gather_direct(): gathered = lax.all_to_all(copies, axis, 0, 0, tiled=True)  32.6 us
    ppermute x2, waiting for transfers between devices, from_behind(): return lax.ppermute(block, axis, route)  20.2 us
    all_to_all x1, waiting for transfers between devices, sum_direct(): parts = lax.all_to_all(parts, axis, 0, 0, tiled=True)  14 us
    all_to_all x2, starting transfers between devices, gather_direct(): gathered = lax.all_to_all(copies, axis, 0, 0, tiled=True)  12.8 us
    all_to_all x1, starting transfers between devices, sum_direct(): parts = lax.all_to_all(parts, axis, 0, 0, tiled=True)  8.04 us
    dot_general x2, matrix products, body(): jnp.einsum('thk,kd->thd', prev_dscore, prev_keys, preferred_element_type=...  4.51 us
    ppermute x2, starting transfers between devices, from_behind(): return lax.ppermute(block, axis, route)  3.84 us
    dot_general x2, matrix products, body(): jnp.einsum('thk,kd->thd', own_dscore, own_keys, preferred_element_type=jn...  3.7 us
  transfers between devices with their start and end apart: 5, of which 5 were waited for; matrix products, arithmetic and copies ran while one was open for 14% of the time, Pallas kernels for 0%

profile of v1, /device:TPU:16, one launch (start us, length us, event | category | flops | bytes accessed | tf_op | source)
XLA Modules:
  0.0 138.9 jit_solution(16201896005527296969)
XLA Ops:
  2.5 9.3 %all-to-all-start.1 = ((bf16[16,128,256]{2,1,0:T(8,128)(2,1)}), bf16[16,128,256]{2,1,0:T(8,128)(2,1)S(1)}, u32[]{:S(2)}, u32[]{:S(2)}) async-start(bf16[16,128,256]{2,1,0:T(8,128)(2,1)} %broadcast_in_dim.27), calls=%async_computation.1 | async-start | bytes 2097152 | tf_op jit(solution)/shard_map/all_to_all | solution.py:18
  12.8 27.7 %all-to-all-done.1 = bf16[16,128,256]{2,1,0:T(8,128)(2,1)S(1)} async-done(((bf16[16,128,256]{2,1,0:T(8,128)(2,1)}), bf16[16,128,256]{2,1,0:T(8,128)(2,1)S(1)}, u32[]{:S(2)}, u32[]{:S(2)}) %all-to-all-start.1) | async-done | bytes 1048608 | tf_op jit(solution)/shard_map/all_to_all | solution.py:18
  40.5 1.3 broadcast_in_dim.25
  41.8 3.5 %all-to-all-start = ((s32[16,1,128]{2,1,0:T(1,128)}), s32[16,1,128]{2,1,0:T(1,128)S(1)}, u32[]{:S(2)}, u32[]{:S(2)}) async-start(s32[16,1,128]{2,1,0:T(1,128)} %broadcast_in_dim.25), calls=%async_computation | async-start | bytes 16384 | tf_op jit(solution)/shard_map/all_to_all | solution.py:18
  46.7 1.9 %collective-permute-start = (bf16[2048,256]{1,0:T(8,128)(2,1)S(1)}, bf16[2048,256]{1,0:T(8,128)(2,1)S(1)}, u32[]{:S(2)}, u32[]{:S(2)}) collective-permute-start(bf16[2048,256]{1,0:T(8,128)(2,1)S(1)} %bitcast.179), channel_id=1, source_target_pairs={{0,16},{16,32},{32,48},{48,64},{64,80},{80,96},{96,112},{112,128},... | collective-permute-start | bytes 3145736 | tf_op jit(solution)/shard_map/ppermute | solution.py:12
  48.7 4.9 %all-to-all-done = s32[16,1,128]{2,1,0:T(1,128)S(1)} async-done(((s32[16,1,128]{2,1,0:T(1,128)}), s32[16,1,128]{2,1,0:T(1,128)S(1)}, u32[]{:S(2)}, u32[]{:S(2)}) %all-to-all-start) | async-done | bytes 8224 | tf_op jit(solution)/shard_map/all_to_all | solution.py:18
  55.4 11.1 %collective-permute-done = bf16[2048,256]{1,0:T(8,128)(2,1)S(1)} collective-permute-done((bf16[2048,256]{1,0:T(8,128)(2,1)S(1)}, bf16[2048,256]{1,0:T(8,128)(2,1)S(1)}, u32[]{:S(2)}, u32[]{:S(2)}) %collective-permute-start) | collective-permute-done | bytes 1048608 | tf_op jit(solution)/shard_map/ppermute | solution.py:12
  67.9 3.0 %fusion.11 = (f32[128,4]{0,1:T(4,128)S(1)}, f32[128,4]{0,1:T(4,128)S(1)}, f32[128,4]{0,1:T(4,128)S(1)}, f32[128,4]{0,1:T(4,128)S(1)}) fusion(f32[2048,128,4]{1,0,2:T(8,128)S(1)} %get-tuple-element.25, f32[128,4]{0,1:T(4,128)S(1)} %max.16, pred[]{:T(512)S(6)} %gt.3, f32[128,4,2048]{0,2,1:T(8,128)S(1)} %get-tuple-element.23, ...), kind=kLoop, calls=%fused_computation.25 | loop fusion | flops 12580864 | bytes 16789504 | tf_op jit(solution)/shard_map/reduce_sum | solution.py:78
  71.6 1.2 convolution_bitcast_fusion
  74.8 1.2 convolution_bitcast_fusion.2
  76.1 1.2 multiply_reduce_fusion
  79.2 1.4 fusion
  81.9 1.8 %multiply_reduce_fusion.1 = (f32[128,4]{0,1:T(4,128)S(1)}, bf16[128,4,128]{0,2,1:T(8,128)(2,1)}) fusion(bf16[128,512]{0,1:T(8,128)(2,1)S(1)} %copy.103, f32[128,4,128]{0,2,1:T(8,128)S(1)} %fusion.39, bf16[2048,256]{1,0:T(8,128)(2,1)S(1)} %copy-done.5, f32[128,4]{0,1:T(4,128)S(1)} %add.37, f32[128,4]{0,1:T(4,128)S(1)} %max.16, ...), kind=kOutput, calls=%fused_computation.71 | convolution fusion | flops 274071040 | bytes 5249025 | tf_op jit(solution)/shard_map/thk,kd->thd/dot_general | solution.py:88
  83.7 1.4 fusion.2
  85.0 1.3 copy-done.1
  87.7 1.9 %collective-permute-start.1 = (bf16[2048,256]{0,1:T(8,128)(2,1)S(1)}, bf16[2048,256]{0,1:T(8,128)(2,1)S(1)}, u32[]{:S(2)}, u32[]{:S(2)}) collective-permute-start(bf16[2048,256]{0,1:T(8,128)(2,1)S(1)} %fusion.20), channel_id=1, source_target_pairs={{16,0},{32,16},{48,32},{64,48},{80,64},{96,80},{112,96},{128,112},... | collective-permute-start | bytes 3145736 | tf_op jit(solution)/shard_map/ppermute | solution.py:12
  92.8 9.1 %collective-permute-done.1 = bf16[2048,256]{0,1:T(8,128)(2,1)S(1)} collective-permute-done((bf16[2048,256]{0,1:T(8,128)(2,1)S(1)}, bf16[2048,256]{0,1:T(8,128)(2,1)S(1)}, u32[]{:S(2)}, u32[]{:S(2)}) %collective-permute-start.1) | collective-permute-done | bytes 1048608 | tf_op jit(solution)/shard_map/ppermute | solution.py:12
  101.9 1.3 copy_bitcast_fusion
  103.3 8.0 %all-to-all-start.2 = ((bf16[16,128,256]{1,2,0:T(8,128)(2,1)}), bf16[16,128,256]{1,2,0:T(8,128)(2,1)S(1)}, u32[]{:S(2)}, u32[]{:S(2)}) async-start(bf16[16,128,256]{1,2,0:T(8,128)(2,1)} %copy_bitcast_fusion), calls=%async_computation.2 | async-start | bytes 2097152 | tf_op jit(solution)/shard_map/all_to_all | solution.py:25
  111.5 1.5 %fusion.34 = f32[128,4,128]{0,2,1:T(8,128)S(1)} fusion(bf16[128,4,2048]{0,2,1:T(8,128)(2,1)S(1)} %fusion.1, bf16[2048,256]{1,0:T(8,128)(2,1)} %bitcast.183), kind=kOutput, calls=%fused_computation.72 | convolution fusion | flops 268435456 | bytes 2883584 | tf_op jit(solution)/shard_map/thk,kd->thd/dot_general | solution.py:103
  113.0 2.3 %fusion.28 = bf16[128,4,128]{0,2,1:T(8,128)(2,1)S(1)} fusion(f32[128,4,128]{0,2,1:T(8,128)S(1)} %fusion.34, bf16[128,4,2048]{0,2,1:T(8,128)(2,1)} %copy-done, bf16[2048,256]{1,0:T(8,128)(2,1)} %copy-done.4), kind=kOutput, calls=%fused_computation.56 | convolution fusion | flops 268632064 | bytes 3014656 | tf_op jit(solution)/shard_map/thk,kd->thd/dot_general | solution.py:106
  116.5 2.2 %fusion.35 = f32[128,4,128]{0,2,1:T(8,128)S(1)} fusion(bf16[128,4,2048]{0,2,1:T(8,128)(2,1)} %copy-done.3, bf16[2048,256]{1,0:T(8,128)(2,1)} %bitcast.184), kind=kOutput, calls=%fused_computation.73 | convolution fusion | flops 268435456 | bytes 2883584 | tf_op jit(solution)/shard_map/thk,kd->thd/dot_general | solution.py:103
  118.6 2.2 %fusion.27 = bf16[128,4,128]{0,2,1:T(8,128)(2,1)} fusion(f32[128,4,128]{0,2,1:T(8,128)S(1)} %fusion.35, bf16[128,4,2048]{0,2,1:T(8,128)(2,1)S(1)} %copy-done.2, bf16[2048,256]{1,0:T(8,128)(2,1)} %copy-done.4), kind=kOutput, calls=%fused_computation.55 | convolution fusion | flops 268632064 | bytes 3014656 | tf_op jit(solution)/shard_map/thk,kd->thd/dot_general | solution.py:106
  123.3 14.0 %all-to-all-done.2 = bf16[16,128,256]{1,2,0:T(8,128)(2,1)S(1)} async-done(((bf16[16,128,256]{1,2,0:T(8,128)(2,1)}), bf16[16,128,256]{1,2,0:T(8,128)(2,1)S(1)}, u32[]{:S(2)}, u32[]{:S(2)}) %all-to-all-start.2) | async-done | bytes 1048608 | tf_op jit(solution)/shard_map/all_to_all | solution.py:25
  (57 shorter events, 23.3 us)
Async XLA Ops:
  0.6 53.0 %copy-start.8 = (s32[128]{0:T(128)S(1)}, s32[128]{0:T(128)}, u32[]{:S(2)}) copy-start(s32[128]{0:T(128)} %param.9) | copy-start | bytes 1540
  2.5 38.0 %all-to-all-start.1 = ((bf16[16,128,256]{2,1,0:T(8,128)(2,1)}), bf16[16,128,256]{2,1,0:T(8,128)(2,1)S(1)}, u32[]{:S(2)}, u32[]{:S(2)}) async-start(bf16[16,128,256]{2,1,0:T(8,128)(2,1)} %broadcast_in_dim.27), calls=%async_computation.1 | async-start | bytes 2097152 | tf_op jit(solution)/shard_map/all_to_all | solution.py:18
  40.5 32.3 %copy-start.6 = (bf16[16,128,256]{2,1,0:T(8,128)(2,1)}, bf16[16,128,256]{2,1,0:T(8,128)(2,1)S(1)}, u32[]{:S(2)}) copy-start(bf16[16,128,256]{2,1,0:T(8,128)(2,1)S(1)} %all-to-all-done.1) | copy-start | bytes 3145732
  41.8 11.8 %all-to-all-start = ((s32[16,1,128]{2,1,0:T(1,128)}), s32[16,1,128]{2,1,0:T(1,128)S(1)}, u32[]{:S(2)}, u32[]{:S(2)}) async-start(s32[16,1,128]{2,1,0:T(1,128)} %broadcast_in_dim.25), calls=%async_computation | async-start | bytes 16384 | tf_op jit(solution)/shard_map/all_to_all | solution.py:18
  46.7 19.7 %collective-permute-start = (bf16[2048,256]{1,0:T(8,128)(2,1)S(1)}, bf16[2048,256]{1,0:T(8,128)(2,1)S(1)}, u32[]{:S(2)}, u32[]{:S(2)}) collective-permute-start(bf16[2048,256]{1,0:T(8,128)(2,1)S(1)} %bitcast.179), channel_id=1, source_target_pairs={{0,16},{16,32},{32,48},{48,64},{64,80},{80,96},{96,112},{112,128},... | collective-permute-start | bytes 3145736 | tf_op jit(solution)/shard_map/ppermute | solution.py:12
  66.5 9.6 %copy-start.4 = (bf16[2048,256]{1,0:T(8,128)(2,1)}, bf16[2048,256]{1,0:T(8,128)(2,1)S(1)}, u32[]{:S(2)}) copy-start(bf16[2048,256]{1,0:T(8,128)(2,1)S(1)} %collective-permute-done) | copy-start | bytes 3145732
  76.0 1.2 copy-start.7
  77.3 1.9 %copy-start.5 = (bf16[2048,256]{1,0:T(8,128)(2,1)S(1)}, bf16[2048,256]{1,0:T(8,128)(2,1)}, u32[]{:S(2)}) copy-start(bf16[2048,256]{1,0:T(8,128)(2,1)} %copy-done.4) | copy-start | bytes 3145732
  80.5 3.1 %copy-start = (bf16[128,4,2048]{0,2,1:T(8,128)(2,1)}, bf16[128,4,2048]{0,2,1:T(8,128)(2,1)S(1)}, u32[]{:S(2)}) copy-start(bf16[128,4,2048]{0,2,1:T(8,128)(2,1)S(1)} %fusion) | copy-start | bytes 6291460
  85.0 1.4 copy-start.1
  87.7 14.2 %collective-permute-start.1 = (bf16[2048,256]{0,1:T(8,128)(2,1)S(1)}, bf16[2048,256]{0,1:T(8,128)(2,1)S(1)}, u32[]{:S(2)}, u32[]{:S(2)}) collective-permute-start(bf16[2048,256]{0,1:T(8,128)(2,1)S(1)} %fusion.20), channel_id=1, source_target_pairs={{16,0},{32,16},{48,32},{64,48},{80,64},{96,80},{112,96},{128,112},... | collective-permute-start | bytes 3145736 | tf_op jit(solution)/shard_map/ppermute | solution.py:12
  91.5 1.3 copy-start.3
  103.3 34.0 %all-to-all-start.2 = ((bf16[16,128,256]{1,2,0:T(8,128)(2,1)}), bf16[16,128,256]{1,2,0:T(8,128)(2,1)S(1)}, u32[]{:S(2)}, u32[]{:S(2)}) async-start(bf16[16,128,256]{1,2,0:T(8,128)(2,1)} %copy_bitcast_fusion), calls=%async_computation.2 | async-start | bytes 2097152 | tf_op jit(solution)/shard_map/all_to_all | solution.py:25
  113.0 5.6 %copy-start.2 = (bf16[128,4,2048]{0,2,1:T(8,128)(2,1)S(1)}, bf16[128,4,2048]{0,2,1:T(8,128)(2,1)}, u32[]{:S(2)}) copy-start(bf16[128,4,2048]{0,2,1:T(8,128)(2,1)} %copy-done.1) | copy-start | bytes 6291460

commit v2 on v1

v2 whole, which is shorter than its diff:
```python
import jax
import jax.numpy as jnp
from jax import lax
from jax.experimental import pallas as pl
from jax.experimental.pallas import tpu as pltpu
from jax.sharding import PartitionSpec as P

masked_score = -1e30
tile_keys = 256
log2_e = 1.4426950408889634
block_rows = 64
tag_rows = 16


def from_behind(block, axis, distance):
    devices = range(lax.axis_size(axis))
    route = [(i - distance, i) for i in devices if i - distance in devices]
    return lax.ppermute(block, axis, route)


def gather_direct(block, axis):
    count = lax.axis_size(axis)
    copies = jnp.broadcast_to(block[None], (count,) + block.shape)
    return lax.all_to_all(copies, axis, 0, 0, tiled=True)


def sum_direct(terms, axis):
    parts = lax.all_to_all(terms, axis, 0, 0, tiled=True)
    return jnp.sum(parts.astype(jnp.float32), axis=0)


def dot_nn(a, b):
    return lax.dot_general(a, b, (((1,), (0,)), ((), ())), preferred_element_type=jnp.float32)


def dot_nt(a, b):
    return lax.dot_general(a, b, (((1,), (1,)), ((), ())), preferred_element_type=jnp.float32)


def dot_tn(a, b):
    return lax.dot_general(a, b, (((0,), (0,)), ((), ())), preferred_element_type=jnp.float32)


def stack_heads(source, half, heads, head_dim):
    rows = slice(half * block_rows, (half + 1) * block_rows)
    return jnp.concatenate(
        [source[rows, h * head_dim : (h + 1) * head_dim] for h in range(heads)], axis=0
    )


def own_tile(step, low_tiles):
    half = jnp.where(step >= low_tiles, 1, 0)
    return half, pl.multiple_of((step - half * low_tiles) * tile_keys, tile_keys)


def low_tile_count(block_ref):
    per_tile = tile_keys // block_rows
    return (block_ref[0] + per_tile) // per_tile


def own_forward(
    block_ref, q_ref, k_ref, v_ref, qs_ref, ks_ref, vs_ref, slots_ref, p_ref, m_ref, l_ref, o_ref, s_ref
):
    group, span, head_dim = v_ref.shape
    heads = q_ref.shape[1] // head_dim
    steps, _, width = p_ref.shape
    blocks = 2 * group
    exponent_scale = log2_e * float(head_dim) ** (-0.5)
    for half in range(2):
        qs_ref[half] = stack_heads(q_ref, half, heads, head_dim)
    for g in range(group):
        slot = jnp.max(k_ref[g, span:, :].astype(jnp.float32)).astype(jnp.int32)
        slots_ref[g] = slot
        for half, place in ((0, slot), (1, blocks - 1 - slot)):
            target = pl.ds(pl.multiple_of(place * block_rows, block_rows), block_rows)
            rows = slice(half * block_rows, (half + 1) * block_rows)
            ks_ref[target, :] = k_ref[g, rows, :]
            vs_ref[target, :] = v_ref[g, rows, :]
    m_ref[...] = jnp.full(m_ref.shape, masked_score, jnp.float32)
    l_ref[...] = jnp.zeros(l_ref.shape, jnp.float32)
    o_ref[...] = jnp.zeros(o_ref.shape, jnp.float32)
    low_tiles = low_tile_count(block_ref)
    key_row = lax.broadcasted_iota(jnp.int32, (tile_keys, width), 0)
    query_row = lax.rem(lax.broadcasted_iota(jnp.int32, (1, width), 1), block_rows)
    for step in range(steps):
        half, start = own_tile(step, low_tiles)
        scores = dot_nt(ks_ref[pl.ds(start, tile_keys), :], qs_ref[half])
        block = jnp.where(half == 1, blocks - 1 - block_ref[0], block_ref[0])
        limit = block * block_rows + query_row - start
        scores = jnp.where(key_row <= limit, scores, masked_score)
        s_ref[step] = scores
        m_ref[half] = jnp.maximum(m_ref[half], jnp.max(scores, axis=0, keepdims=True))
    for step in range(steps):
        half, start = own_tile(step, low_tiles)
        raised = jnp.exp2((s_ref[step] - m_ref[half]) * exponent_scale)
        l_ref[half] += jnp.sum(raised, axis=0, keepdims=True)
        raised = raised.astype(jnp.bfloat16)
        p_ref[step] = raised
        o_ref[half] += dot_tn(vs_ref[pl.ds(start, tile_keys), :], raised)


def prev_both(
    has_ref, qs_ref, do_ref, k_ref, v_ref, m_own_ref, l_own_ref, o_own_ref,
    att_ref, terms_ref, dos_ref, shift_ref, dqt_ref, s_ref, p_ref,
):
    group, span, head_dim = v_ref.shape
    _, width, _ = qs_ref.shape
    heads = width // block_rows
    per_tile = tile_keys // span
    tiles = group // per_tile
    scale = float(head_dim) ** (-0.5)
    exponent_scale = log2_e * scale
    has_prev = has_ref[0] > 0

    def key_tile(ref, tile):
        return jnp.concatenate(
            [ref[tile * per_tile + j, :span, :] for j in range(per_tile)], axis=0
        )

    m_prev, shifts, scaled = [], [], []
    for half in range(2):
        peak = jnp.full((1, width), masked_score, jnp.float32)
        for tile in range(tiles):
            scores = dot_nt(key_tile(k_ref, tile), qs_ref[half])
            s_ref[half, tile] = scores
            peak = jnp.maximum(peak, jnp.max(scores, axis=0, keepdims=True))
        m_prev.append(jnp.where(has_prev, peak, masked_score))
    for half in range(2):
        peak = m_prev[half]
        total = jnp.zeros((1, width), jnp.float32)
        out = jnp.zeros((head_dim, width), jnp.float32)
        for tile in range(tiles):
            raised = jnp.exp2(
                jnp.where(has_prev, s_ref[half, tile] - peak, 0.0) * exponent_scale
            )
            total += jnp.sum(raised, axis=0, keepdims=True)
            raised = raised.astype(jnp.bfloat16)
            p_ref[half, tile] = raised
            out += dot_tn(key_tile(v_ref, tile), raised)
        top = jnp.maximum(peak, m_own_ref[half])
        own_factor = jnp.exp2((m_own_ref[half] - top) * exponent_scale)
        prev_factor = jnp.where(has_prev, jnp.exp2((peak - top) * exponent_scale), 0.0)
        full = own_factor * l_own_ref[half] + prev_factor * total
        inverse = 1.0 / full
        own_factor = own_factor * inverse
        prev_factor = prev_factor * inverse
        out = (own_factor * o_own_ref[half] + prev_factor * out).astype(jnp.bfloat16)
        out = out.astype(jnp.float32)
        grad = stack_heads(do_ref, half, heads, head_dim).astype(jnp.float32).T
        delta = jnp.sum(grad * out, axis=0, keepdims=True)
        dos_ref[half] = (grad * own_factor).astype(jnp.bfloat16)
        shift_ref[half] = delta * own_factor
        scaled.append((grad * prev_factor).astype(jnp.bfloat16))
        shifts.append(delta * prev_factor)
        out = out.T.astype(jnp.bfloat16)
        for h in range(heads):
            att_ref[half * block_rows : (half + 1) * block_rows, h * head_dim : (h + 1) * head_dim] = (
                out[h * block_rows : (h + 1) * block_rows]
            )
    dqt_ref[...] = jnp.zeros(dqt_ref.shape, jnp.float32)
    for tile in range(tiles):
        keys, values = key_tile(k_ref, tile), key_tile(v_ref, tile)
        key_grad = jnp.zeros((tile_keys, head_dim), jnp.float32)
        value_grad = jnp.zeros((tile_keys, head_dim), jnp.float32)
        for half in range(2):
            weights = p_ref[half, tile]
            value_grad += dot_nt(weights, scaled[half])
            change = dot_nn(values, scaled[half]) - shifts[half]
            change = (weights.astype(jnp.float32) * change).astype(jnp.bfloat16)
            key_grad += dot_nn(change, qs_ref[half])
            dqt_ref[half] += dot_tn(keys, change)
        key_grad = (key_grad * scale).astype(jnp.bfloat16)
        value_grad = value_grad.astype(jnp.bfloat16)
        for j in range(per_tile):
            rows = slice(j * span, (j + 1) * span)
            terms_ref[tile * per_tile + j, :, :head_dim] = key_grad[rows]
            terms_ref[tile * per_tile + j, :, head_dim:] = value_grad[rows]


def own_backward(
    block_ref, slots_ref, qs_ref, ks_ref, vs_ref, p_ref, dos_ref, shift_ref, dqt_ref,
    dq_ref, terms_ref, acc_ref, dqa_ref,
):
    steps, _, width = p_ref.shape
    group, span, _ = terms_ref.shape
    head_dim = ks_ref.shape[1]
    heads = width // block_rows
    blocks = 2 * group
    scale = float(head_dim) ** (-0.5)
    acc_ref[...] = jnp.zeros(acc_ref.shape, jnp.float32)
    dqa_ref[...] = dqt_ref[...]
    low_tiles = low_tile_count(block_ref)
    for step in range(steps):
        half, start = own_tile(step, low_tiles)
        window = pl.ds(start, tile_keys)
        weights = p_ref[step]
        grad = dos_ref[half]
        acc_ref[window, head_dim:] += dot_nt(weights, grad)
        change = dot_nn(vs_ref[window, :], grad) - shift_ref[half]
        change = (weights.astype(jnp.float32) * change).astype(jnp.bfloat16)
        acc_ref[window, :head_dim] += dot_nn(change, qs_ref[half]) * scale
        dqa_ref[half] += dot_tn(ks_ref[window, :], change)
    for g in range(group):
        slot = slots_ref[g]
        for half, place in ((0, slot), (1, blocks - 1 - slot)):
            source = pl.ds(pl.multiple_of(place * block_rows, block_rows), block_rows)
            terms_ref[g, half * block_rows : (half + 1) * block_rows, :] = acc_ref[
                source, :
            ].astype(jnp.bfloat16)
    for half in range(2):
        grad = (dqa_ref[half].T * scale).astype(jnp.bfloat16)
        for h in range(heads):
            dq_ref[half * block_rows : (half + 1) * block_rows, h * head_dim : (h + 1) * head_dim] = (
                grad[h * block_rows : (h + 1) * block_rows]
            )


def call(kernel, name, outs, in_smem, scratch, out_smem=(), flops=0):
    vmem = pl.BlockSpec(memory_space=pltpu.VMEM)
    smem = pl.BlockSpec(memory_space=pltpu.SMEM)

    def run(*operands):
        return pl.pallas_call(
            kernel,
            name=name,
            out_shape=[jax.ShapeDtypeStruct(shape, dtype) for shape, dtype in outs],
            in_specs=[smem if i in in_smem else vmem for i in range(len(operands))],
            out_specs=[smem if i in out_smem else vmem for i in range(len(outs))],
            scratch_shapes=[pltpu.VMEM(shape, dtype) for shape, dtype in scratch],
            compiler_params=pltpu.CompilerParams(vmem_limit_bytes=48 * 1024 * 1024),
            cost_estimate=pl.CostEstimate(flops=flops, bytes_accessed=4 << 20, transcendentals=0),
        )(*operands)

    return run


def body(queries, key_vectors, value_vectors, grad_output, positions):
    tok_rows, full_width = queries.shape
    head_dim = key_vectors.shape[1]
    heads = full_width // head_dim
    group = lax.axis_size("inner")
    span_rows = group * tok_rows
    width = heads * block_rows
    steps = span_rows // tile_keys + 1
    bf16, f32 = jnp.bfloat16, jnp.float32
    block = (positions[:1] % span_rows) // block_rows
    tag = jnp.broadcast_to(block.astype(bf16)[:, None], (tag_rows, head_dim))
    key_group = gather_direct(jnp.concatenate([key_vectors, tag], axis=0), "inner")
    value_group = gather_direct(value_vectors, "inner")
    prev_keys = from_behind(key_group, "outer", 1)
    prev_values = from_behind(value_group, "outer", 1)
    has_prev = (lax.axis_index("outer") > 0).astype(jnp.int32).reshape(1)

    unit = 2 * tile_keys * width * head_dim
    row_stat = ((2, 1, width), f32)
    by_query = ((2, head_dim, width), f32)
    qs, ks, vs, slots, p_own, m_own, l_own, o_own = call(
        own_forward,
        "own_forward",
        [
            ((2, width, head_dim), bf16),
            ((span_rows, head_dim), bf16),
            ((span_rows, head_dim), bf16),
            ((group,), jnp.int32),
            ((steps, tile_keys, width), bf16),
            row_stat,
            row_stat,
            by_query,
        ],
        (0,),
        [((steps, tile_keys, width), f32)],
        out_smem=(3,),
        flops=2 * steps * unit,
    )(block, queries, key_group, value_group)
    tiles = span_rows // tile_keys
    attended, prev_terms, dos, shift, dqt = call(
        prev_both,
        "prev_both",
        [
            ((tok_rows, full_width), bf16),
            ((group, tok_rows, 2 * head_dim), bf16),
            ((2, head_dim, width), bf16),
            row_stat,
            by_query,
        ],
        (0,),
        [((2, tiles, tile_keys, width), f32), ((2, tiles, tile_keys, width), bf16)],
        flops=6 * 2 * tiles * unit,
    )(has_prev, qs, grad_output, prev_keys, prev_values, m_own, l_own, o_own)
    returned = from_behind(prev_terms, "outer", -1)
    grad_queries, own_terms = call(
        own_backward,
        "own_backward",
        [((tok_rows, full_width), bf16), ((group, tok_rows, 2 * head_dim), bf16)],
        (0, 1),
        [((span_rows, 2 * head_dim), f32), by_query],
        flops=4 * steps * unit,
    )(block, slots, qs, ks, vs, p_own, dos, shift, dqt)
    terms = (own_terms.astype(f32) + returned.astype(f32)).astype(bf16)
    key_grads = sum_direct(terms, "inner")
    grad_keys = key_grads[:, :head_dim].astype(bf16)
    grad_values = key_grads[:, head_dim:].astype(bf16)
    return (attended, grad_queries, grad_keys, grad_values)


def solution(mesh):
    rows = P(("outer", "inner"), None)
    return jax.shard_map(
        body,
        mesh=mesh,
        in_specs=(rows, rows, rows, rows, P(("outer", "inner"))),
        out_specs=(rows, rows, rows, rows),
        check_vma=False,
    )
```

time: 140 us -> 123 us (0.88)
  blocking collectives: 0 us -> 57.8 us
  waiting for transfers between devices: 66.8 us -> 31.8 us
  matrix products: 27 us -> 0 us
  Pallas kernels: 0 us -> 16.8 us
  starting transfers between devices: 24.6 us -> 9.49 us
  other arithmetic: 8.96 us -> 0.48 us
  local copies, waits for them, and re-layouts: 10.4 us -> 3.19 us
  between operations: 1.04 us -> 2.73 us
    all_to_all x0 -> x2, blocking collectives: none -> 57.8 us  [the longest x1 29.2 us: sum_direct(): parts = lax.all_to_all(terms, axis, 0, 0, tiled=True)]
    all_to_all x3 -> x1, waiting for transfers between devices: 46.6 us -> 14.7 us  [gather_direct(): return lax.all_to_all(copies, axis, 0, 0, tiled=True)]
    dot_general x24 -> x0, matrix products: 27 us -> none  [the longest x2 4.51 us: body(): jnp.einsum('thk,kd->thd', prev_dscore, prev_keys, preferred_element_type=...]
    all_to_all x3 -> x1, starting transfers between devices: 20.8 us -> 3.57 us  [gather_direct(): return lax.all_to_all(copies, axis, 0, 0, tiled=True)]
    pallas_call x0 -> x3, Pallas kernels: none -> 16.8 us  [run(): pl.pallas_call(kernel, name=name, out_shape=[jax.ShapeDtypeStruct(shape,...]
    unnamed x22 -> x4, local copies, waits for them, and re-layouts: 3.63 us -> 0.01 us
    ppermute x2 -> x3, waiting for transfers between devices: 20.2 us -> 17.1 us  [from_behind(): return lax.ppermute(block, axis, route)]
    reduce_sum x1 -> x0, other arithmetic: 2.96 us -> none  [body(): jnp.sum(prev_exp, axis=-1, keepdims=True)]
  transfers between devices with their start and end apart: 5 -> 4, of which waited for: 5 -> 3; matrix products, arithmetic and copies ran while one was open for 14% -> 0% of each run, Pallas kernels for 0% -> 6%
where the time goes in v2:
time: 123 us; the launch traced here: 122 us
  blocking collectives  57.8 us (47%)
  waiting for transfers between devices  31.8 us (26%)
  Pallas kernels  16.8 us (14%)
  starting transfers between devices  9.49 us (8%)
  local copies, waits for them, and re-layouts  3.19 us (3%)
  between operations  2.73 us (2%)
    all_to_all x1, blocking collectives, sum_direct(): parts = lax.all_to_all(terms, axis, 0, 0, tiled=True)  29.2 us
    all_to_all x1, blocking collectives, gather_direct(): return lax.all_to_all(copies, axis, 0, 0, tiled=True)  28.7 us
    ppermute x3, waiting for transfers between devices, from_behind(): return lax.ppermute(block, axis, route)  17.1 us
    pallas_call x3, Pallas kernels, run(): pl.pallas_call(kernel, name=name, out_shape=[jax.ShapeDtypeStruct(shape,...  16.8 us
    all_to_all x1, waiting for transfers between devices, gather_direct(): return lax.all_to_all(copies, axis, 0, 0, tiled=True)  14.7 us
    ppermute x3, starting transfers between devices, from_behind(): return lax.ppermute(block, axis, route)  5.92 us
    all_to_all x1, starting transfers between devices, gather_direct(): return lax.all_to_all(copies, axis, 0, 0, tiled=True)  3.57 us
  transfers between devices with their start and end apart: 4, of which 3 were waited for; matrix products, arithmetic and copies ran while one was open for 0% of the time, Pallas kernels for 6%

profile of v2, /device:TPU:16, one launch (start us, length us, event | category | flops | bytes accessed | tf_op | source)
XLA Modules:
  0.0 122.3 jit_solution(16368212023742174593)
XLA Ops:
  0.6 0.0 copy-start
  2.7 0.8 concatenate.3
  3.4 0.1 broadcast_in_dim.7
  3.5 28.7 %all_to_all.15.k_ref = bf16[16,144,128]{2,1,0:T(8,128)(2,1)S(1)} all-to-all(bf16[16,144,128]{2,1,0:T(8,128)(2,1)S(1)} %broadcast_in_dim.7), channel_id=1, replica_groups=mesh['outer'=16,'inner'=16] {'inner'}, dimensions={0} | all-to-all | bytes 1179648 | tf_op jit(solution)/shard_map/all_to_all | solution.py:24
  32.2 0.0 copy-start.1
  32.2 1.7 %broadcast_in_dim.8 = bf16[16,128,128]{2,1,0:T(8,128)(2,1)} broadcast(bf16[128,128]{1,0:T(8,128)(2,1)} %param.7), dimensions={1,2} | broadcast | bytes 557056 | tf_op jit(solution)/shard_map/broadcast_in_dim | solution.py:23
  33.9 3.6 %all-to-all-start.1 = ((bf16[16,128,128]{2,1,0:T(8,128)(2,1)}), bf16[16,128,128]{2,1,0:T(8,128)(2,1)S(1)}, u32[]{:S(2)}, u32[]{:S(2)}) async-start(bf16[16,128,128]{2,1,0:T(8,128)(2,1)} %broadcast_in_dim.8), calls=%async_computation.1 | async-start | bytes 1048576 | tf_op jit(solution)/shard_map/all_to_all | solution.py:24
  37.4 1.9 %collective-permute-start = (bf16[16,144,128]{2,1,0:T(8,128)(2,1)S(1)}, bf16[16,144,128]{2,1,0:T(8,128)(2,1)S(1)}, u32[]{:S(2)}, u32[]{:S(2)}) collective-permute-start(bf16[16,144,128]{2,1,0:T(8,128)(2,1)S(1)} %all_to_all.15.k_ref), channel_id=1, source_target_pairs={{0,16},{16,32},{32,48},{48,64},{64,80},{80,96},{96,112},{112,128},... | collective-permute-start | bytes 1769480 | tf_op jit(solution)/shard_map/ppermute | solution.py:18
  39.4 14.7 %all-to-all-done.1.v_ref = bf16[16,128,128]{2,1,0:T(8,128)(2,1)S(1)} async-done(((bf16[16,128,128]{2,1,0:T(8,128)(2,1)}), bf16[16,128,128]{2,1,0:T(8,128)(2,1)S(1)}, u32[]{:S(2)}, u32[]{:S(2)}) %all-to-all-start.1) | async-done | bytes 524320 | tf_op jit(solution)/shard_map/all_to_all | solution.py:24
  54.0 1.9 %collective-permute-start.1 = (bf16[16,128,128]{2,1,0:T(8,128)(2,1)S(1)}, bf16[16,128,128]{2,1,0:T(8,128)(2,1)S(1)}, u32[]{:S(2)}, u32[]{:S(2)}) collective-permute-start(bf16[16,128,128]{2,1,0:T(8,128)(2,1)S(1)} %all-to-all-done.1.v_ref), channel_id=1, source_target_pairs={{0,16},{16,32},{32,48},{48,64},{64,80},{80,96},{96,112},{112,128},... | collective-permute-start | bytes 1572872 | tf_op jit(solution)/shard_map/ppermute | solution.py:18
  56.0 0.0 copy-done
  56.0 3.0 %own_forward.1 = (bf16[2,512,128]{2,1,0:T(8,128)(2,1)S(1)}, bf16[2048,128]{1,0:T(8,128)(2,1)S(1)}, bf16[2048,128]{1,0:T(8,128)(2,1)S(1)}, s32[16]{0:T(128)S(1)},...) custom-call(s32[1]{0:T(128)S(6)} %select_n.13.block_ref, ...), custom_call_target="tpu_custom_call" | custom-call | flops 603979776 | bytes 4194304 | tf_op jit(solution)/shard_map/own_forward/pallas_call | solution.py:223
  59.0 9.1 %collective-permute-done.1.v_ref = bf16[16,128,128]{2,1,0:T(8,128)(2,1)S(1)} collective-permute-done((bf16[16,128,128]{2,1,0:T(8,128)(2,1)S(1)}, bf16[16,128,128]{2,1,0:T(8,128)(2,1)S(1)}, u32[]{:S(2)}, u32[]{:S(2)}) %collective-permute-start.1) | collective-permute-done | bytes 524320 | tf_op jit(solution)/shard_map/ppermute | solution.py:18
  68.1 0.0 collective-permute-done.k_ref
  68.1 0.0 copy-done.1
  68.2 9.1 %prev_both.1 = (bf16[128,1024]{1,0:T(8,128)(2,1)}, bf16[16,128,256]{2,1,0:T(8,128)(2,1)S(1)}, bf16[2,128,512]{2,1,0:T(8,128)(2,1)S(1)}, f32[2,1,512]{2,1,0:T(1,128)S(1)}, f32[2,128,512]{2,1,0:T(8,128)S(1)}) custom-call(s32[1]{0:T(128)} %bitcast.has_ref, bf16[2,512,128]{2,1,0:T(8,128)(2,1)S(1)} %get-tuple-element.19.qs_ref, bf16[128,1024]{1,0:T(8,128)(2,1)S(1)} %copy-done.1, ...), custom_call_target="tpu_custom_call" | custom-call | flops 3221225472 | bytes 4194304 | tf_op jit(solution)/shard_map/prev_both/pallas_call | solution.py:223
  77.3 2.1 %collective-permute-start.2 = (bf16[16,128,256]{2,1,0:T(8,128)(2,1)S(1)}, bf16[16,128,256]{2,1,0:T(8,128)(2,1)S(1)}, u32[]{:S(2)}, u32[]{:S(2)}) collective-permute-start(bf16[16,128,256]{2,1,0:T(8,128)(2,1)S(1)} %get-tuple-element.33), channel_id=1, source_target_pairs={{16,0},{32,16},{48,32},{64,48},{80,64},{96,80},{112,96},{128,112},... | collective-permute-start | bytes 3145736 | tf_op jit(solution)/shard_map/ppermute | solution.py:18
  79.4 4.6 %own_backward.1 = (bf16[128,1024]{1,0:T(8,128)(2,1)}, bf16[16,128,256]{2,1,0:T(8,128)(2,1)S(1)}) custom-call(s32[1]{0:T(128)S(6)} %select_n.13.block_ref, s32[16]{0:T(128)S(1)} %get-tuple-element.24.slots_ref, bf16[2,512,128]{2,1,0:T(8,128)(2,1)S(1)} %get-tuple-element.19.qs_ref, bf16[2048,128]{1,0:T(8,128)(2,1)S(1)} %get-tuple-element.25.ks_ref, ...), custom_call_target="tpu_custom_call" | custom-call | flops 1207959552 | bytes 4194304 | tf_op jit(solution)/shard_map/own_backward/pallas_call | solution.py:223
  84.0 8.0 %collective-permute-done.2 = bf16[16,128,256]{2,1,0:T(8,128)(2,1)S(1)} collective-permute-done((bf16[16,128,256]{2,1,0:T(8,128)(2,1)S(1)}, bf16[16,128,256]{2,1,0:T(8,128)(2,1)S(1)}, u32[]{:S(2)}, u32[]{:S(2)}) %collective-permute-start.2) | collective-permute-done | bytes 1048608 | tf_op jit(solution)/shard_map/ppermute | solution.py:18
  92.0 0.3 add_convert_fusion
  92.3 29.2 %all_to_all.16 = bf16[16,128,256]{2,1,0:T(8,128)(2,1)S(1)} all-to-all(bf16[16,128,256]{2,1,0:T(8,128)(2,1)S(1)} %add_convert_fusion), channel_id=1, replica_groups=mesh['outer'=16,'inner'=16] {'inner'}, dimensions={0} | all-to-all | bytes 2097152 | tf_op jit(solution)/shard_map/all_to_all | solution.py:28
  121.5 0.1 reduce
  121.6 0.6 fusion
Async XLA Ops:
  0.6 55.3 %copy-start = (bf16[128,1024]{1,0:T(8,128)(2,1)S(1)}, bf16[128,1024]{1,0:T(8,128)(2,1)}, u32[]{:S(2)}) copy-start(bf16[128,1024]{1,0:T(8,128)(2,1)} %q_ref.1) | copy-start | bytes 786436
  32.2 36.0 %copy-start.1 = (bf16[128,1024]{1,0:T(8,128)(2,1)S(1)}, bf16[128,1024]{1,0:T(8,128)(2,1)}, u32[]{:S(2)}) copy-start(bf16[128,1024]{1,0:T(8,128)(2,1)} %do_ref.1) | copy-start | bytes 786436
  33.9 20.2 %all-to-all-start.1 = ((bf16[16,128,128]{2,1,0:T(8,128)(2,1)}), bf16[16,128,128]{2,1,0:T(8,128)(2,1)S(1)}, u32[]{:S(2)}, u32[]{:S(2)}) async-start(bf16[16,128,128]{2,1,0:T(8,128)(2,1)} %broadcast_in_dim.8), calls=%async_computation.1 | async-start | bytes 1048576 | tf_op jit(solution)/shard_map/all_to_all | solution.py:24
  37.4 30.7 %collective-permute-start = (bf16[16,144,128]{2,1,0:T(8,128)(2,1)S(1)}, bf16[16,144,128]{2,1,0:T(8,128)(2,1)S(1)}, u32[]{:S(2)}, u32[]{:S(2)}) collective-permute-start(bf16[16,144,128]{2,1,0:T(8,128)(2,1)S(1)} %all_to_all.15.k_ref), channel_id=1, source_target_pairs={{0,16},{16,32},{32,48},{48,64},{64,80},{80,96},{96,112},{112,128},... | collective-permute-start | bytes 1769480 | tf_op jit(solution)/shard_map/ppermute | solution.py:18
  54.0 14.1 %collective-permute-start.1 = (bf16[16,128,128]{2,1,0:T(8,128)(2,1)S(1)}, bf16[16,128,128]{2,1,0:T(8,128)(2,1)S(1)}, u32[]{:S(2)}, u32[]{:S(2)}) collective-permute-start(bf16[16,128,128]{2,1,0:T(8,128)(2,1)S(1)} %all-to-all-done.1.v_ref), channel_id=1, source_target_pairs={{0,16},{16,32},{32,48},{48,64},{64,80},{80,96},{96,112},{112,128},... | collective-permute-start | bytes 1572872 | tf_op jit(solution)/shard_map/ppermute | solution.py:18
  77.3 14.7 %collective-permute-start.2 = (bf16[16,128,256]{2,1,0:T(8,128)(2,1)S(1)}, bf16[16,128,256]{2,1,0:T(8,128)(2,1)S(1)}, u32[]{:S(2)}, u32[]{:S(2)}) collective-permute-start(bf16[16,128,256]{2,1,0:T(8,128)(2,1)S(1)} %get-tuple-element.33), channel_id=1, source_target_pairs={{16,0},{32,16},{48,32},{64,48},{80,64},{96,80},{112,96},{128,112},... | collective-permute-start | bytes 3145736 | tf_op jit(solution)/shard_map/ppermute | solution.py:18

commit v3 on v2

v3 whole, which is shorter than its diff:
```python
import jax
import jax.numpy as jnp
from jax import lax
from jax.experimental import pallas as pl
from jax.experimental.pallas import tpu as pltpu
from jax.sharding import PartitionSpec as P

masked_score = -1e30
tile_keys = 256
log2_e = 1.4426950408889634
block_rows = 64
tag_rows = 16


def from_behind(block, axis, distance):
    devices = range(lax.axis_size(axis))
    route = [(i - distance, i) for i in devices if i - distance in devices]
    return lax.ppermute(block, axis, route)


def to_partner(block, axis):
    return lax.ppermute(block, axis, [(i, i ^ 1) for i in range(lax.axis_size(axis))])


def exchange(parts, axis):
    count = lax.axis_size(axis)
    groups = [list(range(first, count, 2)) for first in range(2)]
    return lax.all_to_all(parts, axis, 0, 0, axis_index_groups=groups, tiled=True)


def dot_nn(a, b):
    return lax.dot_general(a, b, (((1,), (0,)), ((), ())), preferred_element_type=jnp.float32)


def dot_nt(a, b):
    return lax.dot_general(a, b, (((1,), (1,)), ((), ())), preferred_element_type=jnp.float32)


def dot_tn(a, b):
    return lax.dot_general(a, b, (((0,), (0,)), ((), ())), preferred_element_type=jnp.float32)


def stack_heads(source, half, heads, head_dim):
    rows = slice(half * block_rows, (half + 1) * block_rows)
    return jnp.concatenate(
        [source[rows, h * head_dim : (h + 1) * head_dim] for h in range(heads)], axis=0
    )


def own_tile(step, allowed_ref):
    low = 0 if step < 5 else 2
    local = step % 5
    per_tile = tile_keys // block_rows
    low_tiles = (allowed_ref[low] + per_tile - 1) // per_tile
    high = jnp.where(local >= low_tiles, 1, 0)
    tile = local - high * low_tiles
    return low + high, tile


def own_forward(
    block_ref, q_ref, q_partner_ref, kv_ref,
    qs_ref, ks_ref, vs_ref, slots_ref, allowed_ref, p_ref, m_ref, l_ref, o_ref, s_ref,
):
    group, _, both = kv_ref.shape
    head_dim = both // 2
    span = 2 * block_rows
    heads = q_ref.shape[1] // head_dim
    steps, _, width = p_ref.shape
    blocks = 2 * group
    tiles = blocks * block_rows // tile_keys
    exponent_scale = log2_e * float(head_dim) ** (-0.5)
    for j, source in enumerate((q_ref, q_partner_ref)):
        for half in range(2):
            qs_ref[2 * j + half] = stack_heads(source, half, heads, head_dim)
    tags = [jnp.max(kv_ref[g, span:, :].astype(jnp.float32)).astype(jnp.int32) for g in range(group)]

    def count(test):
        return sum(jnp.where(test(tag), 1, 0) for tag in tags)

    for j in range(2):
        mine = block_ref[j]
        allowed_ref[2 * j] = count(lambda tag: tag <= mine)
        allowed_ref[2 * j + 1] = blocks - count(lambda tag: tag < mine)
    for g in range(group):
        slot = count(lambda tag: tag < tags[g])
        slots_ref[g] = slot
        for half, place in ((0, slot), (1, blocks - 1 - slot)):
            target = pl.ds(pl.multiple_of(place * block_rows, block_rows), block_rows)
            rows = slice(half * block_rows, (half + 1) * block_rows)
            ks_ref[target, :] = kv_ref[g, rows, :head_dim]
            vs_ref[target, :] = kv_ref[g, rows, head_dim:]
    m_ref[...] = jnp.full(m_ref.shape, masked_score, jnp.float32)
    l_ref[...] = jnp.zeros(l_ref.shape, jnp.float32)
    o_ref[...] = jnp.zeros(o_ref.shape, jnp.float32)
    key_row = lax.broadcasted_iota(jnp.int32, (tile_keys, width), 0)
    query_row = lax.rem(lax.broadcasted_iota(jnp.int32, (1, width), 1), block_rows)
    for step in range(steps):
        at, tile = own_tile(step, allowed_ref)
        start = pl.multiple_of(jnp.minimum(tile, tiles - 1) * tile_keys, tile_keys)
        scores = dot_nt(ks_ref[pl.ds(start, tile_keys), :], qs_ref[at])
        last = query_row if step < 5 else block_rows - 1
        limit = (allowed_ref[at] - 1) * block_rows + last - tile * tile_keys
        scores = jnp.where(key_row <= limit, scores, masked_score)
        s_ref[step] = scores
        m_ref[at] = jnp.maximum(m_ref[at], jnp.max(scores, axis=0, keepdims=True))
    for step in range(steps):
        at, tile = own_tile(step, allowed_ref)
        start = pl.multiple_of(jnp.minimum(tile, tiles - 1) * tile_keys, tile_keys)
        raised = jnp.exp2((s_ref[step] - m_ref[at]) * exponent_scale)
        l_ref[at] += jnp.sum(raised, axis=0, keepdims=True)
        raised = raised.astype(jnp.bfloat16)
        p_ref[step] = raised
        o_ref[at] += dot_tn(vs_ref[pl.ds(start, tile_keys), :], raised)


def key_tile(ref, tile, columns):
    per_tile = tile_keys // (2 * block_rows)
    return jnp.concatenate(
        [ref[tile * per_tile + j, : 2 * block_rows, columns] for j in range(per_tile)], axis=0
    )


def prev_forward(
    has_ref, qs_ref, do_ref, do_partner_ref, kv_ref, m_own_ref, l_own_ref, o_own_ref,
    p_ref, m_prev_ref, stats_ref, dot_ref, out_ref, sent_ref, s_ref,
):
    sets, width, head_dim = qs_ref.shape
    heads = width // block_rows
    tiles = p_ref.shape[1]
    exponent_scale = log2_e * float(head_dim) ** (-0.5)
    has_prev = has_ref[0] > 0
    for at in range(sets):
        peak = jnp.full((1, width), masked_score, jnp.float32)
        for tile in range(tiles):
            scores = dot_nt(key_tile(kv_ref, tile, slice(0, head_dim)), qs_ref[at])
            s_ref[at, tile] = scores
            peak = jnp.maximum(peak, jnp.max(scores, axis=0, keepdims=True))
        m_prev_ref[at] = peak
    for at in range(sets):
        peak = m_prev_ref[at]
        total = jnp.zeros((1, width), jnp.float32)
        out = jnp.zeros((head_dim, width), jnp.float32)
        for tile in range(tiles):
            raised = jnp.exp2((s_ref[at, tile] - peak) * exponent_scale)
            total += jnp.sum(raised, axis=0, keepdims=True)
            raised = raised.astype(jnp.bfloat16)
            p_ref[at, tile] = raised
            out += dot_tn(key_tile(kv_ref, tile, slice(head_dim, 2 * head_dim)), raised)
        peak = jnp.where(has_prev, peak, masked_score)
        m_prev_ref[at] = peak
        top = jnp.maximum(peak, m_own_ref[at])
        own_factor = jnp.exp2((m_own_ref[at] - top) * exponent_scale)
        prev_factor = jnp.where(has_prev, jnp.exp2((peak - top) * exponent_scale), 0.0)
        total = own_factor * l_own_ref[at] + prev_factor * total
        out = own_factor * o_own_ref[at] + prev_factor * out
        grad = stack_heads((do_ref, do_partner_ref)[at // 2], at % 2, heads, head_dim)
        grad = grad.astype(jnp.float32).T
        dot_ref[at] = grad.astype(jnp.bfloat16)
        stats_ref[0, at] = top
        stats_ref[1, at] = total
        stats_ref[2, at] = jnp.sum(grad * out, axis=0, keepdims=True)
        if at < 2:
            out_ref[at] = out
        else:
            share = jnp.where(total > 0, 1.0 / total, 0.0)
            sent_ref[at - 2] = (out * share).astype(jnp.bfloat16)


def prev_backward(
    has_ref, qs_ref, dot_ref, kv_ref, p_ref, m_own_ref, m_prev_ref, stats_ref, other_ref,
    terms_ref, dos_ref, shift_ref, dqt_ref, factor_ref, scaled_ref, lower_ref,
):
    sets, width, head_dim = qs_ref.shape
    tiles = p_ref.shape[1]
    span = terms_ref.shape[1]
    per_tile = tile_keys // span
    scale = float(head_dim) ** (-0.5)
    exponent_scale = log2_e * scale
    has_prev = has_ref[0] > 0
    for at in range(sets):
        there = (at + 2) % 4
        top = jnp.maximum(stats_ref[0, at], other_ref[0, there])
        here = jnp.exp2((stats_ref[0, at] - top) * exponent_scale)
        away = jnp.exp2((other_ref[0, there] - top) * exponent_scale)
        inverse = 1.0 / (here * stats_ref[1, at] + away * other_ref[1, there])
        delta = (here * stats_ref[2, at] + away * other_ref[2, there]) * inverse
        if at < 2:
            factor_ref[0, at] = here * inverse
            factor_ref[1, at] = away * other_ref[1, there] * inverse
        own_factor = jnp.exp2((m_own_ref[at] - top) * exponent_scale) * inverse
        prev_factor = jnp.exp2((m_prev_ref[at] - top) * exponent_scale) * inverse
        prev_factor = jnp.where(has_prev, prev_factor, 0.0)
        grad = dot_ref[at].astype(jnp.float32)
        dos_ref[at] = (grad * own_factor).astype(jnp.bfloat16)
        shift_ref[at] = delta * own_factor
        scaled_ref[at] = (grad * prev_factor).astype(jnp.bfloat16)
        lower_ref[at] = delta * prev_factor
    dqt_ref[...] = jnp.zeros(dqt_ref.shape, jnp.float32)
    for tile in range(tiles):
        keys = key_tile(kv_ref, tile, slice(0, head_dim))
        values = key_tile(kv_ref, tile, slice(head_dim, 2 * head_dim))
        key_grad = jnp.zeros((tile_keys, head_dim), jnp.float32)
        value_grad = jnp.zeros((tile_keys, head_dim), jnp.float32)
        for at in range(sets):
            weights = p_ref[at, tile]
            value_grad += dot_nt(weights, scaled_ref[at])
            change = dot_nn(values, scaled_ref[at]) - lower_ref[at]
            change = (weights.astype(jnp.float32) * change).astype(jnp.bfloat16)
            key_grad += dot_nn(change, qs_ref[at])
            dqt_ref[at] += dot_tn(keys, change)
        key_grad = (key_grad * scale).astype(jnp.bfloat16)
        value_grad = value_grad.astype(jnp.bfloat16)
        for j in range(per_tile):
            rows = slice(j * span, (j + 1) * span)
            terms_ref[tile * per_tile + j, :, :head_dim] = key_grad[rows]
            terms_ref[tile * per_tile + j, :, head_dim:] = value_grad[rows]


def own_backward(
    allowed_ref, slots_ref, qs_ref, ks_ref, vs_ref, p_ref, dos_ref, shift_ref, dqt_ref,
    out_ref, got_ref, factor_ref,
    att_ref, dq_ref, dq_partner_ref, terms_ref, acc_ref, dqa_ref,
):
    steps, _, width = p_ref.shape
    group, span, _ = terms_ref.shape
    head_dim = ks_ref.shape[1]
    heads = width // block_rows
    blocks = 2 * group
    tiles = blocks * block_rows // tile_keys
    scale = float(head_dim) ** (-0.5)

    def store_heads(target_ref, half, block):
        rows = slice(half * block_rows, (half + 1) * block_rows)
        for h in range(heads):
            target_ref[rows, h * head_dim : (h + 1) * head_dim] = block[
                h * block_rows : (h + 1) * block_rows
            ].astype(target_ref.dtype)

    acc_ref[...] = jnp.zeros(acc_ref.shape, jnp.float32)
    dqa_ref[...] = dqt_ref[...]
    for step in range(steps):
        at, tile = own_tile(step, allowed_ref)
        start = pl.multiple_of(jnp.minimum(tile, tiles - 1) * tile_keys, tile_keys)
        window = pl.ds(start, tile_keys)
        weights = p_ref[step]
        grad = dos_ref[at]
        acc_ref[window, head_dim:] += dot_nt(weights, grad)
        change = dot_nn(vs_ref[window, :], grad) - shift_ref[at]
        change = (weights.astype(jnp.float32) * change).astype(jnp.bfloat16)
        acc_ref[window, :head_dim] += dot_nn(change, qs_ref[at]) * scale
        dqa_ref[at] += dot_tn(ks_ref[window, :], change)
    for g in range(group):
        slot = slots_ref[g]
        for half, place in ((0, slot), (1, blocks - 1 - slot)):
            source = pl.ds(pl.multiple_of(place * block_rows, block_rows), block_rows)
            terms_ref[g, half * block_rows : (half + 1) * block_rows, :] = acc_ref[
                source, :
            ].astype(jnp.bfloat16)
    for half in range(2):
        out = factor_ref[0, half] * out_ref[half] + factor_ref[1, half] * got_ref[half].astype(jnp.float32)
        store_heads(att_ref, half, out.T)
        store_heads(dq_ref, half, dqa_ref[half].T * scale)
        store_heads(dq_partner_ref, half, dqa_ref[2 + half].T * scale)


def call(kernel, name, outs, in_smem, scratch, out_smem=(), flops=0):
    vmem = pl.BlockSpec(memory_space=pltpu.VMEM)
    smem = pl.BlockSpec(memory_space=pltpu.SMEM)

    def run(*operands):
        return pl.pallas_call(
            kernel,
            name=name,
            out_shape=[jax.ShapeDtypeStruct(shape, dtype) for shape, dtype in outs],
            in_specs=[smem if i in in_smem else vmem for i in range(len(operands))],
            out_specs=[smem if i in out_smem else vmem for i in range(len(outs))],
            scratch_shapes=[pltpu.VMEM(shape, dtype) for shape, dtype in scratch],
            compiler_params=pltpu.CompilerParams(vmem_limit_bytes=32 * 1024 * 1024),
            cost_estimate=pl.CostEstimate(flops=flops, bytes_accessed=4 << 20, transcendentals=0),
        )(*operands)

    return run


def body(queries, key_vectors, value_vectors, grad_output, positions):
    tok_rows, full_width = queries.shape
    head_dim = key_vectors.shape[1]
    heads = full_width // head_dim
    group = lax.axis_size("inner") // 2
    segment = 2 * group * tok_rows
    span_rows = group * tok_rows
    width = heads * block_rows
    steps = 10
    bf16, f32 = jnp.bfloat16, jnp.float32
    block = (positions[:1] % segment) // block_rows
    query_partner = to_partner(queries, "inner")
    grad_partner = to_partner(grad_output, "inner")
    both_blocks = jnp.concatenate([block, (to_partner(positions, "inner")[:1] % segment) // block_rows])
    tag = jnp.broadcast_to(block.astype(bf16)[:, None], (tag_rows, 2 * head_dim))
    key_value = jnp.concatenate([jnp.concatenate([key_vectors, value_vectors], axis=1), tag], axis=0)
    group_kv = exchange(jnp.broadcast_to(key_value[None], (group,) + key_value.shape), "inner")
    prev_kv = from_behind(group_kv, "outer", 1)
    has_prev = (lax.axis_index("outer") > 0).astype(jnp.int32).reshape(1)

    unit = 2 * tile_keys * width * head_dim
    row_stat = ((4, 1, width), f32)
    by_query = ((4, head_dim, width), f32)
    by_query_16 = ((4, head_dim, width), bf16)
    tokens = ((tok_rows, full_width), bf16)
    terms_shape = ((group, tok_rows, 2 * head_dim), bf16)
    tiles = span_rows // tile_keys
    qs, ks, vs, slots, allowed, p_own, m_own, l_own, o_own = call(
        own_forward,
        "own_forward",
        [
            ((4, width, head_dim), bf16),
            ((span_rows, head_dim), bf16),
            ((span_rows, head_dim), bf16),
            ((group,), jnp.int32),
            ((4,), jnp.int32),
            ((steps, tile_keys, width), bf16),
            row_stat,
            row_stat,
            by_query,
        ],
        (0,),
        [((steps, tile_keys, width), f32)],
        out_smem=(3, 4),
        flops=2 * steps * unit,
    )(both_blocks, queries, query_partner, group_kv)
    p_prev, m_prev, stats, dot, out, sent = call(
        prev_forward,
        "prev_forward",
        [
            ((4, tiles, tile_keys, width), bf16),
            row_stat,
            ((3, 4, 1, width), f32),
            by_query_16,
            ((2, head_dim, width), f32),
            ((2, head_dim, width), bf16),
        ],
        (0,),
        [((4, tiles, tile_keys, width), f32)],
        flops=2 * 4 * tiles * unit,
    )(has_prev, qs, grad_output, grad_partner, prev_kv, m_own, l_own, o_own)
    other = to_partner(stats, "inner")
    got = to_partner(sent, "inner")
    prev_terms, dos, shift, dqt, factor = call(
        prev_backward,
        "prev_backward",
        [terms_shape, by_query_16, row_stat, by_query, ((2, 2, 1, width), f32)],
        (0,),
        [by_query_16, row_stat],
        flops=4 * 4 * tiles * unit,
    )(has_prev, qs, dot, prev_kv, p_prev, m_own, m_prev, stats, other)
    returned = from_behind(prev_terms, "outer", -1)
    attended, dq, dq_partner, own_terms = call(
        own_backward,
        "own_backward",
        [tokens, ((tok_rows, full_width), f32), tokens, terms_shape],
        (0, 1),
        [((span_rows, 2 * head_dim), f32), by_query],
        flops=4 * steps * unit,
    )(allowed, slots, qs, ks, vs, p_own, dos, shift, dqt, out, got, factor)
    dq_other = to_partner(dq_partner, "inner")
    terms = (own_terms.astype(f32) + returned.astype(f32)).astype(bf16)
    key_grads = jnp.sum(exchange(terms, "inner").astype(f32), axis=0)
    grad_queries = (dq + dq_other.astype(f32)).astype(bf16)
    grad_keys = key_grads[:, :head_dim].astype(bf16)
    grad_values = key_grads[:, head_dim:].astype(bf16)
    return (attended, grad_queries, grad_keys, grad_values)


def solution(mesh):
    rows = P(("outer", "inner"), None)
    return jax.shard_map(
        body,
        mesh=mesh,
        in_specs=(rows, rows, rows, rows, P(("outer", "inner"))),
        out_specs=(rows, rows, rows, rows),
        check_vma=False,
    )
```

time: 123 us -> 110 us (0.89)
  the two profiles are of different devices: /device:TPU:16 before, /device:TPU:1 now
where the time goes in v3:
time: 110 us
  waiting for transfers between devices  40.5 us (37%)
  blocking collectives  26.2 us (24%)
  starting transfers between devices  18.4 us (17%)
  Pallas kernels  17.8 us (16%)
  between operations  2.89 us (3%)
  other arithmetic  2.65 us (2%)
  local copies, waits for them, and re-layouts  1.63 us (1%)
    ppermute x6, waiting for transfers between devices, to_partner(): lax.ppermute(block, axis, [(i, i ^ 1) for i in range(lax.axis_size(axis))])  30.9 us
    all_to_all x1, blocking collectives, exchange(): lax.all_to_all(parts, axis, 0, 0, axis_index_groups=groups, tiled=True)  26.2 us
    pallas_call x4, Pallas kernels, run(): pl.pallas_call(kernel, name=name, out_shape=[jax.ShapeDtypeStruct(shape,...  17.8 us
    all_to_all x1, waiting for transfers between devices, exchange(): lax.all_to_all(parts, axis, 0, 0, axis_index_groups=groups, tiled=True)  9.58 us
    ppermute x2, starting transfers between devices, from_behind(): return lax.ppermute(block, axis, route)  7.71 us
    ppermute x6, starting transfers between devices, to_partner(): lax.ppermute(block, axis, [(i, i ^ 1) for i in range(lax.axis_size(axis))])  7.2 us
    all_to_all x1, starting transfers between devices, exchange(): lax.all_to_all(parts, axis, 0, 0, axis_index_groups=groups, tiled=True)  3.49 us
  transfers between devices with their start and end apart: 9, of which 5 were waited for; matrix products, arithmetic and copies ran while one was open for 1% of the time, Pallas kernels for 8%

profile of v3, /device:TPU:1, one launch (start us, length us, event | category | flops | bytes accessed | tf_op | source)
XLA Modules:
  0.0 110.1 jit_solution(2890519785533210280)
XLA Ops:
  2.7 0.8 fusion.2
  3.5 26.2 %all_to_all.10.kv_ref = bf16[8,144,256]{2,1,0:T(8,128)(2,1)S(1)} all-to-all(bf16[8,144,256]{2,1,0:T(8,128)(2,1)S(1)} %broadcast_in_dim.5), channel_id=1, replica_groups={{0,2,4,6,8,10,12,14},{1,3,5,7,9,11,13,15},{16,18,20,22,24,26,28,30},{17..., dimensions={0} | all-to-all | bytes 1179648 | tf_op jit(solution)/shard_map/all_to_all | solution.py:28
  29.7 5.4 %collective-permute-start.3 = (bf16[8,144,256]{2,1,0:T(8,128)(2,1)S(1)}, bf16[8,144,256]{2,1,0:T(8,128)(2,1)S(1)}, u32[]{:S(2)}, u32[]{:S(2)}) collective-permute-start(bf16[8,144,256]{2,1,0:T(8,128)(2,1)S(1)} %all_to_all.10.kv_ref), channel_id=1, source_target_pairs={{0,16},{16,32},{32,48},{48,64},{64,80},{80,96},{96,112},{112,128},... | collective-permute-start | bytes 1769480 | tf_op jit(solution)/shard_map/ppermute | solution.py:18
  35.2 1.4 %collective-permute-start.1 = (bf16[128,1024]{1,0:T(8,128)(2,1)}, bf16[128,1024]{1,0:T(8,128)(2,1)S(1)}, u32[]{:S(2)}, u32[]{:S(2)}) collective-permute-start(bf16[128,1024]{1,0:T(8,128)(2,1)} %q_ref.1), channel_id=1, source_target_pairs={{0,1},{1,0},{2,3},{3,2},{4,5},{5,4},{6,7},{7,6},{8,9},{9,8},{10,11... | collective-permute-start | bytes 786440 | tf_op jit(solution)/shard_map/ppermute | solution.py:22
  36.6 0.2 collective-permute-start.2
  36.7 1.3 %collective-permute-start = (s32[128]{0:T(128)}, s32[128]{0:T(128)S(1)}, u32[]{:S(2)}, u32[]{:S(2)}) collective-permute-start(s32[128]{0:T(128)} %param.9), channel_id=1, source_target_pairs={{0,1},{1,0},{2,3},{3,2},{4,5},{5,4},{6,7},{7,6},{8,9},{9,8},{10,11... | collective-permute-start | bytes 1544 | tf_op jit(solution)/shard_map/ppermute | solution.py:22
  38.0 16.3 %collective-permute-done = s32[128]{0:T(128)S(1)} collective-permute-done((s32[128]{0:T(128)}, s32[128]{0:T(128)S(1)}, u32[]{:S(2)}, u32[]{:S(2)}) %collective-permute-start) | collective-permute-done | bytes 544 | tf_op jit(solution)/shard_map/ppermute | solution.py:22
  54.5 0.9 copy-done
  55.5 4.0 %own_forward.1 = (bf16[4,512,128]{2,1,0:T(8,128)(2,1)S(1)}, bf16[1024,128]{1,0:T(8,128)(2,1)S(1)}, bf16[1024,128]{1,0:T(8,128)(2,1)S(1)}, s32[8]{0:T(128)S(1)}, ...) custom-call(s32[2]{0:T(128)S(1)} %pad_add_fusion.block_ref, ...), custom_call_target="tpu_custom_call" | custom-call | flops 671088640 | bytes 4194304 | tf_op jit(solution)/shard_map/own_forward/pallas_call | solution.py:271
  59.5 4.0 %prev_forward.1 = (bf16[4,4,256,512]{3,2,1,0:T(8,128)(2,1)S(1)}, f32[4,1,512]{2,1,0:T(1,128)S(1)}, f32[3,4,1,512]{3,2,1,0:T(1,128)S(1)}, bf16[4,128,512]{2,1,0:T...) custom-call(s32[1]{0:T(128)} %bitcast.1.has_ref, ...), custom_call_target="tpu_custom_call" | custom-call | flops 1073741824 | bytes 4194304 | tf_op jit(solution)/shard_map/prev_forward/pallas_call | solution.py:271
  63.5 1.6 %collective-permute-start.4 = (f32[3,4,1,512]{3,2,1,0:T(1,128)S(1)}, f32[3,4,1,512]{3,2,1,0:T(1,128)S(1)}, u32[]{:S(2)}, u32[]{:S(2)}) collective-permute-start(f32[3,4,1,512]{3,2,1,0:T(1,128)S(1)} %get-tuple-element.40.stats_ref), channel_id=1, source_target_pairs={{0,1},{1,0},{2,3},{3,2},{4,5},{5,4},{6,7},{7,6},{8,9},{9,8},{10,11... | collective-permute-start | bytes 73736 | tf_op jit(solution)/shard_map/ppermute | solution.py:22
  65.0 1.7 %collective-permute-done.4.other_ref = f32[3,4,1,512]{3,2,1,0:T(1,128)S(1)} collective-permute-done((f32[3,4,1,512]{3,2,1,0:T(1,128)S(1)}, f32[3,4,1,512]{3,2,1,0:T(1,128)S(1)}, u32[]{:S(2)}, u32[]{:S(2)}) %collective-permute-start.4) | collective-permute-done | bytes 24608 | tf_op jit(solution)/shard_map/ppermute | solution.py:22
  66.8 5.0 %prev_backward.1 = (bf16[8,128,256]{2,1,0:T(8,128)(2,1)S(1)}, bf16[4,128,512]{2,1,0:T(8,128)(2,1)S(1)}, f32[4,1,512]{2,1,0:T(1,128)S(1)}, f32[4,128,512]{2,1,0:T(8,128)S(1)}, f32[2,2,1,512]{3,2,1,0:T(1,128)S(1)}) custom-call(s32[1]{0:T(128)} %bitcast.1.has_ref, bf16[4,512,128]{2,1,0:T(8,128)(2,1)S(1)} %get-tuple-element.30.qs_ref, ...), custom_call_target="tpu_custom_call" | custom-call | flops 2147483648 | bytes 4194304 | tf_op jit(solution)/shard_map/prev_backward/pallas_call | solution.py:271
  71.8 2.3 %collective-permute-start.7 = (bf16[8,128,256]{2,1,0:T(8,128)(2,1)S(1)}, bf16[8,128,256]{2,1,0:T(8,128)(2,1)S(1)}, u32[]{:S(2)}, u32[]{:S(2)}) collective-permute-start(bf16[8,128,256]{2,1,0:T(8,128)(2,1)S(1)} %get-tuple-element.51), channel_id=1, source_target_pairs={{16,0},{32,16},{48,32},{64,48},{80,64},{96,80},{112,96},{128,112},... | collective-permute-start | bytes 1572872 | tf_op jit(solution)/shard_map/ppermute | solution.py:18
  74.1 1.4 %collective-permute-start.5 = (bf16[2,128,512]{2,1,0:T(8,128)(2,1)S(1)}, bf16[2,128,512]{2,1,0:T(8,128)(2,1)S(1)}, u32[]{:S(2)}, u32[]{:S(2)}) collective-permute-start(bf16[2,128,512]{2,1,0:T(8,128)(2,1)S(1)} %get-tuple-element.45), channel_id=1, source_target_pairs={{0,1},{1,0},{2,3},{3,2},{4,5},{5,4},{6,7},{7,6},{8,9},{9,8},{10,11... | collective-permute-start | bytes 786440 | tf_op jit(solution)/shard_map/ppermute | solution.py:22
  75.5 6.7 %collective-permute-done.5.got_ref = bf16[2,128,512]{2,1,0:T(8,128)(2,1)S(1)} collective-permute-done((bf16[2,128,512]{2,1,0:T(8,128)(2,1)S(1)}, bf16[2,128,512]{2,1,0:T(8,128)(2,1)S(1)}, u32[]{:S(2)}, u32[]{:S(2)}) %collective-permute-start.5) | collective-permute-done | bytes 262176 | tf_op jit(solution)/shard_map/ppermute | solution.py:22
  82.2 4.8 %own_backward.1 = (bf16[128,1024]{1,0:T(8,128)(2,1)}, f32[128,1024]{1,0:T(8,128)S(1)}, bf16[128,1024]{1,0:T(8,128)(2,1)S(1)}, bf16[8,128,256]{2,1,0:T(8,128)(2,1)S(1)}) custom-call(s32[4]{0:T(128)S(1)} %get-tuple-element.28.allowed_ref, s32[8]{0:T(128)S(1)} %get-tuple-element.29.slots_ref, bf16[4,512,128]{2,1,0:T(8,128)(2,1)S(1)} %get-tuple-element.30.qs_ref, ...), custom_call_target="tpu_custom_call" | custom-call | flops 1342177280 | bytes 4194304 | tf_op jit(solution)/shard_map/own_backward/pallas_call | solution.py:271
  87.0 0.9 add_convert_fusion
  87.9 3.5 %all-to-all-start.1 = ((bf16[8,128,256]{2,1,0:T(8,128)(2,1)}), bf16[8,128,256]{2,1,0:T(8,128)(2,1)S(1)}, u32[]{:S(2)}, u32[]{:S(2)}) async-start(bf16[8,128,256]{2,1,0:T(8,128)(2,1)} %add_convert_fusion), calls=%async_computation.1 | async-start | bytes 1048576 | tf_op jit(solution)/shard_map/all_to_all | solution.py:28
  91.4 1.4 %collective-permute-start.6 = (bf16[128,1024]{1,0:T(8,128)(2,1)S(1)}, bf16[128,1024]{1,0:T(8,128)(2,1)S(1)}, u32[]{:S(2)}, u32[]{:S(2)}) collective-permute-start(bf16[128,1024]{1,0:T(8,128)(2,1)S(1)} %get-tuple-element.49), channel_id=1, source_target_pairs={{0,1},{1,0},{2,3},{3,2},{4,5},{5,4},{6,7},{7,6},{8,9},{9,8},{10,11... | collective-permute-start | bytes 786440 | tf_op jit(solution)/shard_map/ppermute | solution.py:22
  92.8 6.2 %collective-permute-done.6 = bf16[128,1024]{1,0:T(8,128)(2,1)S(1)} collective-permute-done((bf16[128,1024]{1,0:T(8,128)(2,1)S(1)}, bf16[128,1024]{1,0:T(8,128)(2,1)S(1)}, u32[]{:S(2)}, u32[]{:S(2)}) %collective-permute-start.6) | collective-permute-done | bytes 262176 | tf_op jit(solution)/shard_map/ppermute | solution.py:22
  99.0 0.8 add_convert_fusion.1
  99.8 9.6 %all-to-all-done.1 = bf16[8,128,256]{2,1,0:T(8,128)(2,1)S(1)} async-done(((bf16[8,128,256]{2,1,0:T(8,128)(2,1)}), bf16[8,128,256]{2,1,0:T(8,128)(2,1)S(1)}, u32[]{:S(2)}, u32[]{:S(2)}) %all-to-all-start.1) | async-done | bytes 524320 | tf_op jit(solution)/shard_map/all_to_all | solution.py:28
  109.4 0.6 fusion.3
  (10 shorter events, 0.2 us)
Async XLA Ops:
  0.6 58.9 %copy-start.1 = (bf16[128,1024]{1,0:T(8,128)(2,1)S(1)}, bf16[128,1024]{1,0:T(8,128)(2,1)}, u32[]{:S(2)}) copy-start(bf16[128,1024]{1,0:T(8,128)(2,1)} %do_ref.1) | copy-start | bytes 786436
  29.7 29.7 %collective-permute-start.3 = (bf16[8,144,256]{2,1,0:T(8,128)(2,1)S(1)}, bf16[8,144,256]{2,1,0:T(8,128)(2,1)S(1)}, u32[]{:S(2)}, u32[]{:S(2)}) collective-permute-start(bf16[8,144,256]{2,1,0:T(8,128)(2,1)S(1)} %all_to_all.10.kv_ref), channel_id=1, source_target_pairs={{0,16},{16,32},{32,48},{48,64},{64,80},{80,96},{96,112},{112,128},... | collective-permute-start | bytes 1769480 | tf_op jit(solution)/shard_map/ppermute | solution.py:18
  35.2 19.3 %collective-permute-start.1 = (bf16[128,1024]{1,0:T(8,128)(2,1)}, bf16[128,1024]{1,0:T(8,128)(2,1)S(1)}, u32[]{:S(2)}, u32[]{:S(2)}) collective-permute-start(bf16[128,1024]{1,0:T(8,128)(2,1)} %q_ref.1), channel_id=1, source_target_pairs={{0,1},{1,0},{2,3},{3,2},{4,5},{5,4},{6,7},{7,6},{8,9},{9,8},{10,11... | collective-permute-start | bytes 786440 | tf_op jit(solution)/shard_map/ppermute | solution.py:22
  36.6 22.9 %collective-permute-start.2 = (bf16[128,1024]{1,0:T(8,128)(2,1)}, bf16[128,1024]{1,0:T(8,128)(2,1)S(1)}, u32[]{:S(2)}, u32[]{:S(2)}) collective-permute-start(bf16[128,1024]{1,0:T(8,128)(2,1)} %do_ref.1), channel_id=1, source_target_pairs={{0,1},{1,0},{2,3},{3,2},{4,5},{5,4},{6,7},{7,6},{8,9},{9,8},{10,11... | collective-permute-start | bytes 786440 | tf_op jit(solution)/shard_map/ppermute | solution.py:22
  36.7 17.6 %collective-permute-start = (s32[128]{0:T(128)}, s32[128]{0:T(128)S(1)}, u32[]{:S(2)}, u32[]{:S(2)}) collective-permute-start(s32[128]{0:T(128)} %param.9), channel_id=1, source_target_pairs={{0,1},{1,0},{2,3},{3,2},{4,5},{5,4},{6,7},{7,6},{8,9},{9,8},{10,11... | collective-permute-start | bytes 1544 | tf_op jit(solution)/shard_map/ppermute | solution.py:22
  54.5 1.0 copy-start
  63.5 3.3 %collective-permute-start.4 = (f32[3,4,1,512]{3,2,1,0:T(1,128)S(1)}, f32[3,4,1,512]{3,2,1,0:T(1,128)S(1)}, u32[]{:S(2)}, u32[]{:S(2)}) collective-permute-start(f32[3,4,1,512]{3,2,1,0:T(1,128)S(1)} %get-tuple-element.40.stats_ref), channel_id=1, source_target_pairs={{0,1},{1,0},{2,3},{3,2},{4,5},{5,4},{6,7},{7,6},{8,9},{9,8},{10,11... | collective-permute-start | bytes 73736 | tf_op jit(solution)/shard_map/ppermute | solution.py:22
  71.8 15.2 %collective-permute-start.7 = (bf16[8,128,256]{2,1,0:T(8,128)(2,1)S(1)}, bf16[8,128,256]{2,1,0:T(8,128)(2,1)S(1)}, u32[]{:S(2)}, u32[]{:S(2)}) collective-permute-start(bf16[8,128,256]{2,1,0:T(8,128)(2,1)S(1)} %get-tuple-element.51), channel_id=1, source_target_pairs={{16,0},{32,16},{48,32},{64,48},{80,64},{96,80},{112,96},{128,112},... | collective-permute-start | bytes 1572872 | tf_op jit(solution)/shard_map/ppermute | solution.py:18
  74.1 8.1 %collective-permute-start.5 = (bf16[2,128,512]{2,1,0:T(8,128)(2,1)S(1)}, bf16[2,128,512]{2,1,0:T(8,128)(2,1)S(1)}, u32[]{:S(2)}, u32[]{:S(2)}) collective-permute-start(bf16[2,128,512]{2,1,0:T(8,128)(2,1)S(1)} %get-tuple-element.45), channel_id=1, source_target_pairs={{0,1},{1,0},{2,3},{3,2},{4,5},{5,4},{6,7},{7,6},{8,9},{9,8},{10,11... | collective-permute-start | bytes 786440 | tf_op jit(solution)/shard_map/ppermute | solution.py:22
  87.9 21.4 %all-to-all-start.1 = ((bf16[8,128,256]{2,1,0:T(8,128)(2,1)}), bf16[8,128,256]{2,1,0:T(8,128)(2,1)S(1)}, u32[]{:S(2)}, u32[]{:S(2)}) async-start(bf16[8,128,256]{2,1,0:T(8,128)(2,1)} %add_convert_fusion), calls=%async_computation.1 | async-start | bytes 1048576 | tf_op jit(solution)/shard_map/all_to_all | solution.py:28
  91.4 7.6 %collective-permute-start.6 = (bf16[128,1024]{1,0:T(8,128)(2,1)S(1)}, bf16[128,1024]{1,0:T(8,128)(2,1)S(1)}, u32[]{:S(2)}, u32[]{:S(2)}) collective-permute-start(bf16[128,1024]{1,0:T(8,128)(2,1)S(1)} %get-tuple-element.49), channel_id=1, source_target_pairs={{0,1},{1,0},{2,3},{3,2},{4,5},{5,4},{6,7},{7,6},{8,9},{9,8},{10,11... | collective-permute-start | bytes 786440 | tf_op jit(solution)/shard_map/ppermute | solution.py:22

commit v4 on v3

--- a/solution.py
+++ b/solution.py
@@ -45,6 +45,44 @@
     return jnp.concatenate(
         [source[rows, h * head_dim : (h + 1) * head_dim] for h in range(heads)], axis=0
     )
+
+
+def store_heads(target_ref, half, block):
+    rows = slice(half * block_rows, (half + 1) * block_rows)
+    head_dim = block.shape[1]
+    for h in range(block.shape[0] // block_rows):
+        target_ref[rows, h * head_dim : (h + 1) * head_dim] = block[
+            h * block_rows : (h + 1) * block_rows
+        ].astype(target_ref.dtype)
+
+
+def pack(position_ref, key_ref, value_ref, packed_ref):
+    count, rows, both = packed_ref.shape
+    span = key_ref.shape[0]
+    segment = 2 * count * span
+    tag = (lax.rem(position_ref[0], segment) // block_rows).astype(jnp.float32)
+    tag = jnp.full((rows - span, both), tag, jnp.float32).astype(packed_ref.dtype)
+    for g in range(count):
+        packed_ref[g, :span, : both // 2] = key_ref[...]
+        packed_ref[g, :span, both // 2 :] = value_ref[...]
+        packed_ref[g, span:, :] = tag
+
+
+def stack_pair(q_ref, q_partner_ref, do_ref, do_partner_ref, qs_ref, dot_ref):
+    _, width, head_dim = qs_ref.shape
+    heads = width // block_rows
+    for j, (query, grad) in enumerate(((q_ref, do_ref), (q_partner_ref, do_partner_ref))):
+        for half in range(2):
+            qs_ref[2 * j + half] = stack_heads(query, half, heads, head_dim)
+            stacked = stack_heads(grad, half, heads, head_dim).astype(jnp.float32)
+            dot_ref[2 * j + half] = stacked.T.astype(jnp.bfloat16)
+
+
+def merge_attended(out_ref, got_ref, factor_ref, att_ref):
+    for half in range(2):
+        out = factor_ref[0, half] * out_ref[half]
+        out = out + factor_ref[1, half] * got_ref[half].astype(jnp.float32)
+        store_heads(att_ref, half, out.T)
 
 
 def own_tile(step, allowed_ref):
@@ -58,20 +96,16 @@
 
 
 def own_forward(
-    block_ref, q_ref, q_partner_ref, kv_ref,
-    qs_ref, ks_ref, vs_ref, slots_ref, allowed_ref, p_ref, m_ref, l_ref, o_ref, s_ref,
+    block_ref, qs_ref, kv_ref,
+    ks_ref, vs_ref, slots_ref, allowed_ref, p_ref, m_ref, l_ref, o_ref, s_ref,
 ):
     group, _, both = kv_ref.shape
     head_dim = both // 2
     span = 2 * block_rows
-    heads = q_ref.shape[1] // head_dim
     steps, _, width = p_ref.shape
     blocks = 2 * group
     tiles = blocks * block_rows // tile_keys
     exponent_scale = log2_e * float(head_dim) ** (-0.5)
-    for j, source in enumerate((q_ref, q_partner_ref)):
-        for half in range(2):
-            qs_ref[2 * j + half] = stack_heads(source, half, heads, head_dim)
     tags = [jnp.max(kv_ref[g, span:, :].astype(jnp.float32)).astype(jnp.int32) for g in range(group)]
 
     def count(test):
@@ -121,11 +155,10 @@
 
 
 def prev_forward(
-    has_ref, qs_ref, do_ref, do_partner_ref, kv_ref, m_own_ref, l_own_ref, o_own_ref,
-    p_ref, m_prev_ref, stats_ref, dot_ref, out_ref, sent_ref, s_ref,
+    has_ref, qs_ref, dot_ref, kv_ref, m_own_ref, l_own_ref, o_own_ref,
+    p_ref, m_prev_ref, stats_ref, out_ref, sent_ref, s_ref,
 ):
     sets, width, head_dim = qs_ref.shape
-    heads = width // block_rows
     tiles = p_ref.shape[1]
     exponent_scale = log2_e * float(head_dim) ** (-0.5)
     has_prev = has_ref[0] > 0
@@ -153,9 +186,7 @@
         prev_factor = jnp.where(has_prev, jnp.exp2((peak - top) * exponent_scale), 0.0)
         total = own_factor * l_own_ref[at] + prev_factor * total
         out = own_factor * o_own_ref[at] + prev_factor * out
-        grad = stack_heads((do_ref, do_partner_ref)[at // 2], at % 2, heads, head_dim)
-        grad = grad.astype(jnp.float32).T
-        dot_ref[at] = grad.astype(jnp.bfloat16)
+        grad = dot_ref[at].astype(jnp.float32)
         stats_ref[0, at] = top
         stats_ref[1, at] = total
         stats_ref[2, at] = jnp.sum(grad * out, axis=0, keepdims=True)
@@ -218,23 +249,14 @@
 
 def own_backward(
     allowed_ref, slots_ref, qs_ref, ks_ref, vs_ref, p_ref, dos_ref, shift_ref, dqt_ref,
-    out_ref, got_ref, factor_ref,
-    att_ref, dq_ref, dq_partner_ref, terms_ref, acc_ref, dqa_ref,
+    dq_ref, dq_partner_ref, terms_ref, acc_ref, dqa_ref,
 ):
     steps, _, width = p_ref.shape
     group, span, _ = terms_ref.shape
     head_dim = ks_ref.shape[1]
-    heads = width // block_rows
     blocks = 2 * group
     tiles = blocks * block_rows // tile_keys
     scale = float(head_dim) ** (-0.5)
-
-    def store_heads(target_ref, half, block):
-        rows = slice(half * block_rows, (half + 1) * block_rows)
-        for h in range(heads):
-            target_ref[rows, h * head_dim : (h + 1) * head_dim] = block[
-                h * block_rows : (h + 1) * block_rows
-            ].astype(target_ref.dtype)
 
     acc_ref[...] = jnp.zeros(acc_ref.shape, jnp.float32)
     dqa_ref[...] = dqt_ref[...]
@@ -257,8 +279,6 @@
                 source, :
             ].astype(jnp.bfloat16)
     for half in range(2):
-        out = factor_ref[0, half] * out_ref[half] + factor_ref[1, half] * got_ref[half].astype(jnp.float32)
-        store_heads(att_ref, half, out.T)
         store_heads(dq_ref, half, dqa_ref[half].T * scale)
         store_heads(dq_partner_ref, half, dqa_ref[2 + half].T * scale)
 
@@ -296,9 +316,14 @@
     query_partner = to_partner(queries, "inner")
     grad_partner = to_partner(grad_output, "inner")
     both_blocks = jnp.concatenate([block, (to_partner(positions, "inner")[:1] % segment) // block_rows])
-    tag = jnp.broadcast_to(block.astype(bf16)[:, None], (tag_rows, 2 * head_dim))
-    key_value = jnp.concatenate([jnp.concatenate([key_vectors, value_vectors], axis=1), tag], axis=0)
-    group_kv = exchange(jnp.broadcast_to(key_value[None], (group,) + key_value.shape), "inner")
+    (packed,) = call(
+        pack,
+        "pack",
+        [((group, tok_rows + tag_rows, 2 * head_dim), bf16)],
+        (0,),
+        [],
+    )(positions, key_vectors, value_vectors)
+    group_kv = exchange(packed, "inner")
     prev_kv = from_behind(group_kv, "outer", 1)
     has_prev = (lax.axis_index("outer") > 0).astype(jnp.int32).reshape(1)
 
@@ -309,11 +334,18 @@
     tokens = ((tok_rows, full_width), bf16)
     terms_shape = ((group, tok_rows, 2 * head_dim), bf16)
     tiles = span_rows // tile_keys
-    qs, ks, vs, slots, allowed, p_own, m_own, l_own, o_own = call(
+    qs, dot = call(
+        stack_pair,
+        "stack_pair",
+        [((4, width, head_dim), bf16), by_query_16],
+        (),
+        [],
+        flops=4 * 10**9,
+    )(queries, query_partner, grad_output, grad_partner)
+    ks, vs, slots, allowed, p_own, m_own, l_own, o_own = call(
         own_forward,
         "own_forward",
         [
-            ((4, width, head_dim), bf16),
             ((span_rows, head_dim), bf16),
             ((span_rows, head_dim), bf16),
             ((group,), jnp.int32),
@@ -325,24 +357,23 @@
         ],
         (0,),
         [((steps, tile_keys, width), f32)],
-        out_smem=(3, 4),
+        out_smem=(2, 3),
         flops=2 * steps * unit,
-    )(both_blocks, queries, query_partner, group_kv)
-    p_prev, m_prev, stats, dot, out, sent = call(
+    )(both_blocks, qs, group_kv)
+    p_prev, m_prev, stats, out, sent = call(
         prev_forward,
         "prev_forward",
         [
             ((4, tiles, tile_keys, width), bf16),
             row_stat,
             ((3, 4, 1, width), f32),
-            by_query_16,
             ((2, head_dim, width), f32),
             ((2, head_dim, width), bf16),
         ],
         (0,),
         [((4, tiles, tile_keys, width), f32)],
         flops=2 * 4 * tiles * unit,
-    )(has_prev, qs, grad_output, grad_partner, prev_kv, m_own, l_own, o_own)
+    )(has_prev, qs, dot, prev_kv, m_own, l_own, o_own)
     other = to_partner(stats, "inner")
     got = to_partner(sent, "inner")
     prev_terms, dos, shift, dqt, factor = call(
@@ -354,14 +385,15 @@
         flops=4 * 4 * tiles * unit,
     )(has_prev, qs, dot, prev_kv, p_prev, m_own, m_prev, stats, other)
     returned = from_behind(prev_terms, "outer", -1)
-    attended, dq, dq_partner, own_terms = call(
+    dq, dq_partner, own_terms = call(
         own_backward,
         "own_backward",
-        [tokens, ((tok_rows, full_width), f32), tokens, terms_shape],
+        [((tok_rows, full_width), f32), tokens, terms_shape],
         (0, 1),
         [((span_rows, 2 * head_dim), f32), by_query],
         flops=4 * steps * unit,
-    )(allowed, slots, qs, ks, vs, p_own, dos, shift, dqt, out, got, factor)
+    )(allowed, slots, qs, ks, vs, p_own, dos, shift, dqt)
+    (attended,) = call(merge_attended, "merge_attended", [tokens], (), [])(out, got, factor)
     dq_other = to_partner(dq_partner, "inner")
     terms = (own_terms.astype(f32) + returned.astype(f32)).astype(bf16)
     key_grads = jnp.sum(exchange(terms, "inner").astype(f32), axis=0)

time: 110 us -> 90.6 us (0.82)
  the two profiles are of different devices: /device:TPU:1 before, /device:TPU:16 now
where the time goes in v4:
time: 90.6 us; the launch traced here: 90.1 us
  waiting for transfers between devices  38.1 us (42%)
  starting transfers between devices  23.2 us (26%)
  Pallas kernels  19.4 us (21%)
  local copies, waits for them, and re-layouts  4.69 us (5%)
  between operations  2.87 us (3%)
  other arithmetic  1.83 us (2%)
    all_to_all x2, waiting for transfers between devices, exchange(): lax.all_to_all(parts, axis, 0, 0, axis_index_groups=groups, tiled=True)  20 us
    pallas_call x7, Pallas kernels, run(): pl.pallas_call(kernel, name=name, out_shape=[jax.ShapeDtypeStruct(shape,...  19.4 us
    ppermute x6, waiting for transfers between devices, to_partner(): lax.ppermute(block, axis, [(i, i ^ 1) for i in range(lax.axis_size(axis))])  12.6 us
    all_to_all x2, starting transfers between devices, exchange(): lax.all_to_all(parts, axis, 0, 0, axis_index_groups=groups, tiled=True)  12 us
    ppermute x6, starting transfers between devices, to_partner(): lax.ppermute(block, axis, [(i, i ^ 1) for i in range(lax.axis_size(axis))])  7.06 us
    ppermute x2, waiting for transfers between devices, from_behind(): return lax.ppermute(block, axis, route)  5.45 us
    ppermute x2, starting transfers between devices, from_behind(): return lax.ppermute(block, axis, route)  4.21 us
    unnamed x10, local copies, waits for them, and re-layouts  4.06 us
  transfers between devices with their start and end apart: 10, of which 8 were waited for; matrix products, arithmetic and copies ran while one was open for 1% of the time, Pallas kernels for 10%

profile of v4, /device:TPU:16, one launch (start us, length us, event | category | flops | bytes accessed | tf_op | source)
XLA Modules:
  0.0 90.1 jit_solution(1808380858697886551)
XLA Ops:
  2.8 1.4 %pack.1 = bf16[8,144,256]{2,1,0:T(8,128)(2,1)} custom-call(s32[128]{0:T(128)S(1)} %copy-done.2, bf16[128,128]{1,0:T(8,128)(2,1)S(1)} %copy-done, bf16[128,128]{1,0:T(8,128)(2,1)S(1)} %copy-done.1), custom_call_target="tpu_custom_call" | custom-call | bytes 4194304 | tf_op jit(solution)/shard_map/pack/pallas_call | solution.py:291
  4.2 8.5 %all-to-all-start = ((bf16[8,144,256]{2,1,0:T(8,128)(2,1)}), bf16[8,144,256]{2,1,0:T(8,128)(2,1)S(1)}, u32[]{:S(2)}, u32[]{:S(2)}) async-start(bf16[8,144,256]{2,1,0:T(8,128)(2,1)} %pack.1), calls=%async_computation | async-start | bytes 1179648 | tf_op jit(solution)/shard_map/all_to_all | solution.py:28
  12.7 1.3 %collective-permute-start = (bf16[128,1024]{1,0:T(8,128)(2,1)}, bf16[128,1024]{1,0:T(8,128)(2,1)S(1)}, u32[]{:S(2)}, u32[]{:S(2)}) collective-permute-start(bf16[128,1024]{1,0:T(8,128)(2,1)} %q_ref.1), channel_id=1, source_target_pairs={{0,1},{1,0},{2,3},{3,2},{4,5},{5,4},{6,7},{7,6},{8,9},{9,8},{10,11... | collective-permute-start | bytes 786440 | tf_op jit(solution)/shard_map/ppermute | solution.py:22
  14.7 16.9 %all-to-all-done.kv_ref = bf16[8,144,256]{2,1,0:T(8,128)(2,1)S(1)} async-done(((bf16[8,144,256]{2,1,0:T(8,128)(2,1)}), bf16[8,144,256]{2,1,0:T(8,128)(2,1)S(1)}, u32[]{:S(2)}, u32[]{:S(2)}) %all-to-all-start) | async-done | bytes 589856 | tf_op jit(solution)/shard_map/all_to_all | solution.py:28
  31.6 1.9 %collective-permute-start.2 = (bf16[8,144,256]{2,1,0:T(8,128)(2,1)S(1)}, bf16[8,144,256]{2,1,0:T(8,128)(2,1)S(1)}, u32[]{:S(2)}, u32[]{:S(2)}) collective-permute-start(bf16[8,144,256]{2,1,0:T(8,128)(2,1)S(1)} %all-to-all-done.kv_ref), channel_id=1, source_target_pairs={{0,16},{16,32},{32,48},{48,64},{64,80},{80,96},{96,112},{112,128},... | collective-permute-start | bytes 1769480 | tf_op jit(solution)/shard_map/ppermute | solution.py:18
  33.5 1.4 %collective-permute-start.3 = (s32[128]{0:T(128)}, s32[128]{0:T(128)S(1)}, u32[]{:S(2)}, u32[]{:S(2)}) collective-permute-start(s32[128]{0:T(128)} %position_ref.1), channel_id=1, source_target_pairs={{0,1},{1,0},{2,3},{3,2},{4,5},{5,4},{6,7},{7,6},{8,9},{9,8},{10,11... | collective-permute-start | bytes 1544 | tf_op jit(solution)/shard_map/ppermute | solution.py:22
  37.5 0.9 %copy-done.3 = bf16[128,1024]{1,0:T(8,128)(2,1)S(1)} copy-done((bf16[128,1024]{1,0:T(8,128)(2,1)S(1)}, bf16[128,1024]{1,0:T(8,128)(2,1)}, u32[]{:S(2)}) %copy-start.3) | copy-done | bytes 262168
  38.5 0.9 %copy-done.4 = bf16[128,1024]{1,0:T(8,128)(2,1)S(1)} copy-done((bf16[128,1024]{1,0:T(8,128)(2,1)S(1)}, bf16[128,1024]{1,0:T(8,128)(2,1)}, u32[]{:S(2)}) %copy-start.4) | copy-done | bytes 262168
  39.7 3.8 %own_forward.1 = (bf16[1024,128]{1,0:T(8,128)(2,1)S(1)}, bf16[1024,128]{1,0:T(8,128)(2,1)S(1)}, s32[8]{0:T(128)S(1)}, s32[4]{0:T(128)S(1)}, bf16[10,256,512]{2,1...) custom-call(s32[2]{0:T(128)S(1)} %pad_add_fusion.block_ref, ...), custom_call_target="tpu_custom_call" | custom-call | flops 671088640 | bytes 4194304 | tf_op jit(solution)/shard_map/own_forward/pallas_call | solution.py:291
  43.5 3.0 %collective-permute-done.2.kv_ref = bf16[8,144,256]{2,1,0:T(8,128)(2,1)S(1)} collective-permute-done((bf16[8,144,256]{2,1,0:T(8,128)(2,1)S(1)}, bf16[8,144,256]{2,1,0:T(8,128)(2,1)S(1)}, u32[]{:S(2)}, u32[]{:S(2)}) %collective-permute-start.2) | collective-permute-done | bytes 589856 | tf_op jit(solution)/shard_map/ppermute | solution.py:18
  46.4 3.9 %prev_forward.1 = (bf16[4,4,256,512]{3,2,1,0:T(8,128)(2,1)S(1)}, f32[4,1,512]{2,1,0:T(1,128)S(1)}, f32[3,4,1,512]{3,2,1,0:T(1,128)S(1)}, f32[2,128,512]{2,1,0:T(8,128)S(1)}, bf16[2,128,512]{2,1,0:T(8,128)(2,1)S(1)}) custom-call(s32[1]{0:T(128)} %bitcast.has_ref, bf16[4,512,128]{2,1,0:T(8,128)(2,1)S(1)} %get-tuple-element.27.qs_ref, ...), custom_call_target="tpu_custom_call" | custom-call | flops 1073741824 | bytes 4194304 | tf_op jit(solution)/shard_map/prev_forward/pallas_call | solution.py:291
  50.3 1.6 %collective-permute-start.5 = (f32[3,4,1,512]{3,2,1,0:T(1,128)S(1)}, f32[3,4,1,512]{3,2,1,0:T(1,128)S(1)}, u32[]{:S(2)}, u32[]{:S(2)}) collective-permute-start(f32[3,4,1,512]{3,2,1,0:T(1,128)S(1)} %get-tuple-element.36.stats_ref), channel_id=1, source_target_pairs={{0,1},{1,0},{2,3},{3,2},{4,5},{5,4},{6,7},{7,6},{8,9},{9,8},{10,11... | collective-permute-start | bytes 73736 | tf_op jit(solution)/shard_map/ppermute | solution.py:22
  51.8 2.5 %collective-permute-done.5.other_ref = f32[3,4,1,512]{3,2,1,0:T(1,128)S(1)} collective-permute-done((f32[3,4,1,512]{3,2,1,0:T(1,128)S(1)}, f32[3,4,1,512]{3,2,1,0:T(1,128)S(1)}, u32[]{:S(2)}, u32[]{:S(2)}) %collective-permute-start.5) | collective-permute-done | bytes 24608 | tf_op jit(solution)/shard_map/ppermute | solution.py:22
  54.4 5.0 %prev_backward.1 = (bf16[8,128,256]{2,1,0:T(8,128)(2,1)S(1)}, bf16[4,128,512]{2,1,0:T(8,128)(2,1)S(1)}, f32[4,1,512]{2,1,0:T(1,128)S(1)}, f32[4,128,512]{2,1,0:T(8,128)S(1)}, f32[2,2,1,512]{3,2,1,0:T(1,128)S(1)}) custom-call(s32[1]{0:T(128)} %bitcast.has_ref, bf16[4,512,128]{2,1,0:T(8,128)(2,1)S(1)} %get-tuple-element.27.qs_ref, ...), custom_call_target="tpu_custom_call" | custom-call | flops 2147483648 | bytes 4194304 | tf_op jit(solution)/shard_map/prev_backward/pallas_call | solution.py:291
  59.4 2.3 %collective-permute-start.7 = (bf16[8,128,256]{2,1,0:T(8,128)(2,1)S(1)}, bf16[8,128,256]{2,1,0:T(8,128)(2,1)S(1)}, u32[]{:S(2)}, u32[]{:S(2)}) collective-permute-start(bf16[8,128,256]{2,1,0:T(8,128)(2,1)S(1)} %get-tuple-element.49), channel_id=1, source_target_pairs={{16,0},{32,16},{48,32},{64,48},{80,64},{96,80},{112,96},{128,112},... | collective-permute-start | bytes 1572872 | tf_op jit(solution)/shard_map/ppermute | solution.py:18
  61.7 4.2 %own_backward.1 = (f32[128,1024]{1,0:T(8,128)S(1)}, bf16[128,1024]{1,0:T(8,128)(2,1)S(1)}, bf16[8,128,256]{2,1,0:T(8,128)(2,1)S(1)}) custom-call(s32[4]{0:T(128)S(1)} %get-tuple-element.38.allowed_ref, s32[8]{0:T(128)S(1)} %get-tuple-element.39.slots_ref, bf16[4,512,128]{2,1,0:T(8,128)(2,1)S(1)} %get-tuple-element.27.qs_ref, ...), custom_call_target="tpu_custom_call" | custom-call | flops 1342177280 | bytes 4194304 | tf_op jit(solution)/shard_map/own_backward/pallas_call | solution.py:291
  65.9 2.5 %collective-permute-done.7 = bf16[8,128,256]{2,1,0:T(8,128)(2,1)S(1)} collective-permute-done((bf16[8,128,256]{2,1,0:T(8,128)(2,1)S(1)}, bf16[8,128,256]{2,1,0:T(8,128)(2,1)S(1)}, u32[]{:S(2)}, u32[]{:S(2)}) %collective-permute-start.7) | collective-permute-done | bytes 524320 | tf_op jit(solution)/shard_map/ppermute | solution.py:18
  68.4 0.9 %add_convert_fusion = bf16[8,128,256]{2,1,0:T(8,128)(2,1)} fusion(bf16[8,128,256]{2,1,0:T(8,128)(2,1)S(1)} %collective-permute-done.7, bf16[8,128,256]{2,1,0:T(8,128)(2,1)S(1)} %get-tuple-element.48), kind=kLoop, calls=%fused_computation | loop fusion | flops 1048576 | bytes 1572864 | tf_op jit(solution)/shard_map/convert_element_type | solution.py:398
  69.3 3.5 %all-to-all-start.1 = ((bf16[8,128,256]{2,1,0:T(8,128)(2,1)}), bf16[8,128,256]{2,1,0:T(8,128)(2,1)S(1)}, u32[]{:S(2)}, u32[]{:S(2)}) async-start(bf16[8,128,256]{2,1,0:T(8,128)(2,1)} %add_convert_fusion), calls=%async_computation.1 | async-start | bytes 1048576 | tf_op jit(solution)/shard_map/all_to_all | solution.py:28
  72.8 1.7 %collective-permute-start.4 = (bf16[2,128,512]{2,1,0:T(8,128)(2,1)S(1)}, bf16[2,128,512]{2,1,0:T(8,128)(2,1)S(1)}, u32[]{:S(2)}, u32[]{:S(2)}) collective-permute-start(bf16[2,128,512]{2,1,0:T(8,128)(2,1)S(1)} %get-tuple-element.33), channel_id=1, source_target_pairs={{0,1},{1,0},{2,3},{3,2},{4,5},{5,4},{6,7},{7,6},{8,9},{9,8},{10,11... | collective-permute-start | bytes 786440 | tf_op jit(solution)/shard_map/ppermute | solution.py:22
  74.9 7.2 %collective-permute-done.4.got_ref = bf16[2,128,512]{2,1,0:T(8,128)(2,1)S(1)} collective-permute-done((bf16[2,128,512]{2,1,0:T(8,128)(2,1)S(1)}, bf16[2,128,512]{2,1,0:T(8,128)(2,1)S(1)}, u32[]{:S(2)}, u32[]{:S(2)}) %collective-permute-start.4) | collective-permute-done | bytes 262176 | tf_op jit(solution)/shard_map/ppermute | solution.py:22
  82.1 0.9 merge_attended.1
  83.0 2.4 %collective-permute-done.6 = bf16[128,1024]{1,0:T(8,128)(2,1)S(1)} collective-permute-done((bf16[128,1024]{1,0:T(8,128)(2,1)S(1)}, bf16[128,1024]{1,0:T(8,128)(2,1)S(1)}, u32[]{:S(2)}, u32[]{:S(2)}) %collective-permute-start.6) | collective-permute-done | bytes 262176 | tf_op jit(solution)/shard_map/ppermute | solution.py:22
  86.2 3.2 %all-to-all-done.1 = bf16[8,128,256]{2,1,0:T(8,128)(2,1)S(1)} async-done(((bf16[8,128,256]{2,1,0:T(8,128)(2,1)}), bf16[8,128,256]{2,1,0:T(8,128)(2,1)S(1)}, u32[]{:S(2)}, u32[]{:S(2)}) %all-to-all-start.1) | async-done | bytes 524320 | tf_op jit(solution)/shard_map/all_to_all | solution.py:28
  (18 shorter events, 5.5 us)
Async XLA Ops:
  0.6 0.8 copy-start
  1.4 0.8 copy-start.1
  2.1 0.7 copy-start.2
  4.2 27.4 %all-to-all-start = ((bf16[8,144,256]{2,1,0:T(8,128)(2,1)}), bf16[8,144,256]{2,1,0:T(8,128)(2,1)S(1)}, u32[]{:S(2)}, u32[]{:S(2)}) async-start(bf16[8,144,256]{2,1,0:T(8,128)(2,1)} %pack.1), calls=%async_computation | async-start | bytes 1179648 | tf_op jit(solution)/shard_map/all_to_all | solution.py:28
  12.7 24.8 %collective-permute-start = (bf16[128,1024]{1,0:T(8,128)(2,1)}, bf16[128,1024]{1,0:T(8,128)(2,1)S(1)}, u32[]{:S(2)}, u32[]{:S(2)}) collective-permute-start(bf16[128,1024]{1,0:T(8,128)(2,1)} %q_ref.1), channel_id=1, source_target_pairs={{0,1},{1,0},{2,3},{3,2},{4,5},{5,4},{6,7},{7,6},{8,9},{9,8},{10,11... | collective-permute-start | bytes 786440 | tf_op jit(solution)/shard_map/ppermute | solution.py:22
  14.0 23.5 %collective-permute-start.1 = (bf16[128,1024]{1,0:T(8,128)(2,1)}, bf16[128,1024]{1,0:T(8,128)(2,1)S(1)}, u32[]{:S(2)}, u32[]{:S(2)}) collective-permute-start(bf16[128,1024]{1,0:T(8,128)(2,1)} %do_ref.1), channel_id=1, source_target_pairs={{0,1},{1,0},{2,3},{3,2},{4,5},{5,4},{6,7},{7,6},{8,9},{9,8},{10,11... | collective-permute-start | bytes 786440 | tf_op jit(solution)/shard_map/ppermute | solution.py:22
  31.6 14.8 %collective-permute-start.2 = (bf16[8,144,256]{2,1,0:T(8,128)(2,1)S(1)}, bf16[8,144,256]{2,1,0:T(8,128)(2,1)S(1)}, u32[]{:S(2)}, u32[]{:S(2)}) collective-permute-start(bf16[8,144,256]{2,1,0:T(8,128)(2,1)S(1)} %all-to-all-done.kv_ref), channel_id=1, source_target_pairs={{0,16},{16,32},{32,48},{48,64},{64,80},{80,96},{96,112},{112,128},... | collective-permute-start | bytes 1769480 | tf_op jit(solution)/shard_map/ppermute | solution.py:18
  33.5 3.8 %collective-permute-start.3 = (s32[128]{0:T(128)}, s32[128]{0:T(128)S(1)}, u32[]{:S(2)}, u32[]{:S(2)}) collective-permute-start(s32[128]{0:T(128)} %position_ref.1), channel_id=1, source_target_pairs={{0,1},{1,0},{2,3},{3,2},{4,5},{5,4},{6,7},{7,6},{8,9},{9,8},{10,11... | collective-permute-start | bytes 1544 | tf_op jit(solution)/shard_map/ppermute | solution.py:22
  37.5 1.0 %copy-start.3 = (bf16[128,1024]{1,0:T(8,128)(2,1)S(1)}, bf16[128,1024]{1,0:T(8,128)(2,1)}, u32[]{:S(2)}) copy-start(bf16[128,1024]{1,0:T(8,128)(2,1)} %q_ref.1) | copy-start | bytes 786436
  38.5 0.9 %copy-start.4 = (bf16[128,1024]{1,0:T(8,128)(2,1)S(1)}, bf16[128,1024]{1,0:T(8,128)(2,1)}, u32[]{:S(2)}) copy-start(bf16[128,1024]{1,0:T(8,128)(2,1)} %do_ref.1) | copy-start | bytes 786436
  50.3 4.1 %collective-permute-start.5 = (f32[3,4,1,512]{3,2,1,0:T(1,128)S(1)}, f32[3,4,1,512]{3,2,1,0:T(1,128)S(1)}, u32[]{:S(2)}, u32[]{:S(2)}) collective-permute-start(f32[3,4,1,512]{3,2,1,0:T(1,128)S(1)} %get-tuple-element.36.stats_ref), channel_id=1, source_target_pairs={{0,1},{1,0},{2,3},{3,2},{4,5},{5,4},{6,7},{7,6},{8,9},{9,8},{10,11... | collective-permute-start | bytes 73736 | tf_op jit(solution)/shard_map/ppermute | solution.py:22
  59.4 9.0 %collective-permute-start.7 = (bf16[8,128,256]{2,1,0:T(8,128)(2,1)S(1)}, bf16[8,128,256]{2,1,0:T(8,128)(2,1)S(1)}, u32[]{:S(2)}, u32[]{:S(2)}) collective-permute-start(bf16[8,128,256]{2,1,0:T(8,128)(2,1)S(1)} %get-tuple-element.49), channel_id=1, source_target_pairs={{16,0},{32,16},{48,32},{64,48},{80,64},{96,80},{112,96},{128,112},... | collective-permute-start | bytes 1572872 | tf_op jit(solution)/shard_map/ppermute | solution.py:18
  69.3 20.0 %all-to-all-start.1 = ((bf16[8,128,256]{2,1,0:T(8,128)(2,1)}), bf16[8,128,256]{2,1,0:T(8,128)(2,1)S(1)}, u32[]{:S(2)}, u32[]{:S(2)}) async-start(bf16[8,128,256]{2,1,0:T(8,128)(2,1)} %add_convert_fusion), calls=%async_computation.1 | async-start | bytes 1048576 | tf_op jit(solution)/shard_map/all_to_all | solution.py:28
  72.8 9.3 %collective-permute-start.4 = (bf16[2,128,512]{2,1,0:T(8,128)(2,1)S(1)}, bf16[2,128,512]{2,1,0:T(8,128)(2,1)S(1)}, u32[]{:S(2)}, u32[]{:S(2)}) collective-permute-start(bf16[2,128,512]{2,1,0:T(8,128)(2,1)S(1)} %get-tuple-element.33), channel_id=1, source_target_pairs={{0,1},{1,0},{2,3},{3,2},{4,5},{5,4},{6,7},{7,6},{8,9},{9,8},{10,11... | collective-permute-start | bytes 786440 | tf_op jit(solution)/shard_map/ppermute | solution.py:22
  74.5 10.9 %collective-permute-start.6 = (bf16[128,1024]{1,0:T(8,128)(2,1)S(1)}, bf16[128,1024]{1,0:T(8,128)(2,1)S(1)}, u32[]{:S(2)}, u32[]{:S(2)}) collective-permute-start(bf16[128,1024]{1,0:T(8,128)(2,1)S(1)} %get-tuple-element.47), channel_id=1, source_target_pairs={{0,1},{1,0},{2,3},{3,2},{4,5},{5,4},{6,7},{7,6},{8,9},{9,8},{10,11... | collective-permute-start | bytes 786440 | tf_op jit(solution)/shard_map/ppermute | solution.py:22

commit v5 on v4

--- a/solution.py
+++ b/solution.py
@@ -1,3 +1,5 @@
+import functools
+
 import jax
 import jax.numpy as jnp
 from jax import lax
@@ -59,8 +61,7 @@
 def pack(position_ref, key_ref, value_ref, packed_ref):
     count, rows, both = packed_ref.shape
     span = key_ref.shape[0]
-    segment = 2 * count * span
-    tag = (lax.rem(position_ref[0], segment) // block_rows).astype(jnp.float32)
+    tag = (lax.rem(position_ref[0], 2 * count * span) // block_rows).astype(jnp.float32)
     tag = jnp.full((rows - span, both), tag, jnp.float32).astype(packed_ref.dtype)
     for g in range(count):
         packed_ref[g, :span, : both // 2] = key_ref[...]
@@ -68,9 +69,14 @@
         packed_ref[g, span:, :] = tag
 
 
-def stack_pair(q_ref, q_partner_ref, do_ref, do_partner_ref, qs_ref, dot_ref):
+def stack_pair(
+    segment, position_ref, position_partner_ref, q_ref, q_partner_ref, do_ref, do_partner_ref,
+    block_ref, qs_ref, dot_ref,
+):
     _, width, head_dim = qs_ref.shape
     heads = width // block_rows
+    block_ref[0] = lax.rem(position_ref[0], segment) // block_rows
+    block_ref[1] = lax.rem(position_partner_ref[0], segment) // block_rows
     for j, (query, grad) in enumerate(((q_ref, do_ref), (q_partner_ref, do_partner_ref))):
         for half in range(2):
             qs_ref[2 * j + half] = stack_heads(query, half, heads, head_dim)
@@ -155,17 +161,17 @@
 
 
 def prev_forward(
-    has_ref, qs_ref, dot_ref, kv_ref, m_own_ref, l_own_ref, o_own_ref,
-    p_ref, m_prev_ref, stats_ref, out_ref, sent_ref, s_ref,
+    first, has_ref, qs_ref, dot_ref, kv_ref, m_own_ref, l_own_ref, o_own_ref,
+    p_ref, m_prev_ref, stats_ref, out_ref, s_ref,
 ):
-    sets, width, head_dim = qs_ref.shape
-    tiles = p_ref.shape[1]
+    _, width, head_dim = qs_ref.shape
+    sets, tiles = p_ref.shape[:2]
     exponent_scale = log2_e * float(head_dim) ** (-0.5)
     has_prev = has_ref[0] > 0
     for at in range(sets):
         peak = jnp.full((1, width), masked_score, jnp.float32)
         for tile in range(tiles):
-            scores = dot_nt(key_tile(kv_ref, tile, slice(0, head_dim)), qs_ref[at])
+            scores = dot_nt(key_tile(kv_ref, tile, slice(0, head_dim)), qs_ref[first + at])
             s_ref[at, tile] = scores
             peak = jnp.maximum(peak, jnp.max(scores, axis=0, keepdims=True))
         m_prev_ref[at] = peak
@@ -181,52 +187,51 @@
             out += dot_tn(key_tile(kv_ref, tile, slice(head_dim, 2 * head_dim)), raised)
         peak = jnp.where(has_prev, peak, masked_score)
         m_prev_ref[at] = peak
-        top = jnp.maximum(peak, m_own_ref[at])
-        own_factor = jnp.exp2((m_own_ref[at] - top) * exponent_scale)
+        top = jnp.maximum(peak, m_own_ref[first + at])
+        own_factor = jnp.exp2((m_own_ref[first + at] - top) * exponent_scale)
         prev_factor = jnp.where(has_prev, jnp.exp2((peak - top) * exponent_scale), 0.0)
-        total = own_factor * l_own_ref[at] + prev_factor * total
-        out = own_factor * o_own_ref[at] + prev_factor * out
-        grad = dot_ref[at].astype(jnp.float32)
+        total = own_factor * l_own_ref[first + at] + prev_factor * total
+        out = own_factor * o_own_ref[first + at] + prev_factor * out
+        grad = dot_ref[first + at].astype(jnp.float32)
         stats_ref[0, at] = top
         stats_ref[1, at] = total
         stats_ref[2, at] = jnp.sum(grad * out, axis=0, keepdims=True)
-        if at < 2:
+        if first == 0:
             out_ref[at] = out
         else:
             share = jnp.where(total > 0, 1.0 / total, 0.0)
-            sent_ref[at - 2] = (out * share).astype(jnp.bfloat16)
-
-
-def prev_backward(
-    has_ref, qs_ref, dot_ref, kv_ref, p_ref, m_own_ref, m_prev_ref, stats_ref, other_ref,
-    terms_ref, dos_ref, shift_ref, dqt_ref, factor_ref, scaled_ref, lower_ref,
-):
-    sets, width, head_dim = qs_ref.shape
-    tiles = p_ref.shape[1]
-    span = terms_ref.shape[1]
+            out_ref[at] = (out * share).astype(jnp.bfloat16)
+
+
+def prev_backward(first, has_ref, qs_ref, dot_ref, kv_ref, p_ref, m_own_ref, m_prev_ref, stats_ref, other_ref, *rest):
+    if first == 0:
+        terms_ref, dos_ref, shift_ref, dqt_ref, factor_ref, scaled_ref, lower_ref = rest
+    else:
+        before_ref, terms_ref, dos_ref, shift_ref, dqt_ref, scaled_ref, lower_ref = rest
+    _, width, head_dim = qs_ref.shape
+    sets, tiles = p_ref.shape[:2]
+    span = 2 * block_rows
     per_tile = tile_keys // span
     scale = float(head_dim) ** (-0.5)
     exponent_scale = log2_e * scale
     has_prev = has_ref[0] > 0
     for at in range(sets):
-        there = (at + 2) % 4
-        top = jnp.maximum(stats_ref[0, at], other_ref[0, there])
+        top = jnp.maximum(stats_ref[0, at], other_ref[0, at])
         here = jnp.exp2((stats_ref[0, at] - top) * exponent_scale)
-        away = jnp.exp2((other_ref[0, there] - top) * exponent_scale)
-        inverse = 1.0 / (here * stats_ref[1, at] + away * other_ref[1, there])
-        delta = (here * stats_ref[2, at] + away * other_ref[2, there]) * inverse
-        if at < 2:
+        away = jnp.exp2((other_ref[0, at] - top) * exponent_scale)
+        inverse = 1.0 / (here * stats_ref[1, at] + away * other_ref[1, at])
+        delta = (here * stats_ref[2, at] + away * other_ref[2, at]) * inverse
+        if first == 0:
             factor_ref[0, at] = here * inverse
-            factor_ref[1, at] = away * other_ref[1, there] * inverse
-        own_factor = jnp.exp2((m_own_ref[at] - top) * exponent_scale) * inverse
+            factor_ref[1, at] = away * other_ref[1, at] * inverse
+        own_factor = jnp.exp2((m_own_ref[first + at] - top) * exponent_scale) * inverse
         prev_factor = jnp.exp2((m_prev_ref[at] - top) * exponent_scale) * inverse
         prev_factor = jnp.where(has_prev, prev_factor, 0.0)
-        grad = dot_ref[at].astype(jnp.float32)
+        grad = dot_ref[first + at].astype(jnp.float32)
         dos_ref[at] = (grad * own_factor).astype(jnp.bfloat16)
         shift_ref[at] = delta * own_factor
         scaled_ref[at] = (grad * prev_factor).astype(jnp.bfloat16)
         lower_ref[at] = delta * prev_factor
-    dqt_ref[...] = jnp.zeros(dqt_ref.shape, jnp.float32)
     for tile in range(tiles):
         keys = key_tile(kv_ref, tile, slice(0, head_dim))
         values = key_tile(kv_ref, tile, slice(head_dim, 2 * head_dim))
@@ -237,18 +242,27 @@
             value_grad += dot_nt(weights, scaled_ref[at])
             change = dot_nn(values, scaled_ref[at]) - lower_ref[at]
             change = (weights.astype(jnp.float32) * change).astype(jnp.bfloat16)
-            key_grad += dot_nn(change, qs_ref[at])
-            dqt_ref[at] += dot_tn(keys, change)
-        key_grad = (key_grad * scale).astype(jnp.bfloat16)
-        value_grad = value_grad.astype(jnp.bfloat16)
-        for j in range(per_tile):
-            rows = slice(j * span, (j + 1) * span)
-            terms_ref[tile * per_tile + j, :, :head_dim] = key_grad[rows]
-            terms_ref[tile * per_tile + j, :, head_dim:] = value_grad[rows]
+            key_grad += dot_nn(change, qs_ref[first + at])
+            dqt = dot_tn(keys, change)
+            dqt_ref[at] = dqt if tile == 0 else dqt_ref[at] + dqt
+        key_grad = key_grad * scale
+        if first == 0:
+            rows = slice(tile * tile_keys, (tile + 1) * tile_keys)
+            terms_ref[rows, :head_dim] = key_grad
+            terms_ref[rows, head_dim:] = value_grad
+        else:
+            rows = slice(tile * tile_keys, (tile + 1) * tile_keys)
+            key_grad = (key_grad + before_ref[rows, :head_dim]).astype(jnp.bfloat16)
+            value_grad = (value_grad + before_ref[rows, head_dim:]).astype(jnp.bfloat16)
+            for j in range(per_tile):
+                rows = slice(j * span, (j + 1) * span)
+                terms_ref[tile * per_tile + j, :, :head_dim] = key_grad[rows]
+                terms_ref[tile * per_tile + j, :, head_dim:] = value_grad[rows]
 
 
 def own_backward(
-    allowed_ref, slots_ref, qs_ref, ks_ref, vs_ref, p_ref, dos_ref, shift_ref, dqt_ref,
+    allowed_ref, slots_ref, qs_ref, ks_ref, vs_ref, p_ref,
+    dos_mine_ref, shift_mine_ref, dqt_mine_ref, dos_theirs_ref, shift_theirs_ref, dqt_theirs_ref,
     dq_ref, dq_partner_ref, terms_ref, acc_ref, dqa_ref,
 ):
     steps, _, width = p_ref.shape
@@ -259,15 +273,19 @@
     scale = float(head_dim) ** (-0.5)
 
     acc_ref[...] = jnp.zeros(acc_ref.shape, jnp.float32)
-    dqa_ref[...] = dqt_ref[...]
+    dqa_ref[:2] = dqt_mine_ref[...]
+    dqa_ref[2:] = dqt_theirs_ref[...]
     for step in range(steps):
         at, tile = own_tile(step, allowed_ref)
         start = pl.multiple_of(jnp.minimum(tile, tiles - 1) * tile_keys, tile_keys)
         window = pl.ds(start, tile_keys)
         weights = p_ref[step]
-        grad = dos_ref[at]
+        dos_ref, shift_ref, first = (
+            (dos_mine_ref, shift_mine_ref, 0) if step < 5 else (dos_theirs_ref, shift_theirs_ref, 2)
+        )
+        grad = dos_ref[at - first]
         acc_ref[window, head_dim:] += dot_nt(weights, grad)
-        change = dot_nn(vs_ref[window, :], grad) - shift_ref[at]
+        change = dot_nn(vs_ref[window, :], grad) - shift_ref[at - first]
         change = (weights.astype(jnp.float32) * change).astype(jnp.bfloat16)
         acc_ref[window, :head_dim] += dot_nn(change, qs_ref[at]) * scale
         dqa_ref[at] += dot_tn(ks_ref[window, :], change)
@@ -283,19 +301,27 @@
         store_heads(dq_partner_ref, half, dqa_ref[2 + half].T * scale)
 
 
-def call(kernel, name, outs, in_smem, scratch, out_smem=(), flops=0):
+def call(kernel, name, outs, in_smem, scratch, out_smem=(), flops=0, stream=()):
     vmem = pl.BlockSpec(memory_space=pltpu.VMEM)
     smem = pl.BlockSpec(memory_space=pltpu.SMEM)
+
+    def spec(at, operand):
+        if at in in_smem:
+            return smem
+        if at in stream:
+            return pl.BlockSpec(operand.shape, lambda step: (0,) * operand.ndim)
+        return vmem
 
     def run(*operands):
         return pl.pallas_call(
             kernel,
             name=name,
+            grid=(1,) if stream else (),
             out_shape=[jax.ShapeDtypeStruct(shape, dtype) for shape, dtype in outs],
-            in_specs=[smem if i in in_smem else vmem for i in range(len(operands))],
+            in_specs=[spec(i, operand) for i, operand in enumerate(operands)],
             out_specs=[smem if i in out_smem else vmem for i in range(len(outs))],
             scratch_shapes=[pltpu.VMEM(shape, dtype) for shape, dtype in scratch],
-            compiler_params=pltpu.CompilerParams(vmem_limit_bytes=32 * 1024 * 1024),
+            compiler_params=pltpu.CompilerParams(vmem_limit_bytes=16 * 1024 * 1024),
             cost_estimate=pl.CostEstimate(flops=flops, bytes_accessed=4 << 20, transcendentals=0),
         )(*operands)
 
@@ -312,16 +338,16 @@
     width = heads * block_rows
     steps = 10
     bf16, f32 = jnp.bfloat16, jnp.float32
-    block = (positions[:1] % segment) // block_rows
     query_partner = to_partner(queries, "inner")
     grad_partner = to_partner(grad_output, "inner")
-    both_blocks = jnp.concatenate([block, (to_partner(positions, "inner")[:1] % segment) // block_rows])
+    position_partner = to_partner(positions, "inner")
     (packed,) = call(
         pack,
         "pack",
         [((group, tok_rows + tag_rows, 2 * head_dim), bf16)],
         (0,),
         [],
+        stream=(1, 2),
     )(positions, key_vectors, value_vectors)
     group_kv = exchange(packed, "inner")
     prev_kv = from_behind(group_kv, "outer", 1)
@@ -334,14 +360,16 @@
     tokens = ((tok_rows, full_width), bf16)
     terms_shape = ((group, tok_rows, 2 * head_dim), bf16)
     tiles = span_rows // tile_keys
-    qs, dot = call(
-        stack_pair,
+    both_blocks, qs, dot = call(
+        functools.partial(stack_pair, segment),
         "stack_pair",
-        [((4, width, head_dim), bf16), by_query_16],
-        (),
+        [((2,), jnp.int32), ((4, width, head_dim), bf16), by_query_16],
+        (0, 1),
         [],
+        out_smem=(0,),
         flops=4 * 10**9,
-    )(queries, query_partner, grad_output, grad_partner)
+        stream=(2, 4),
+    )(positions, position_partner, queries, query_partner, grad_output, grad_partner)
     ks, vs, slots, allowed, p_own, m_own, l_own, o_own = call(
         own_forward,
         "own_forward",
@@ -360,30 +388,46 @@
         out_smem=(2, 3),
         flops=2 * steps * unit,
     )(both_blocks, qs, group_kv)
-    p_prev, m_prev, stats, out, sent = call(
-        prev_forward,
-        "prev_forward",
-        [
-            ((4, tiles, tile_keys, width), bf16),
-            row_stat,
-            ((3, 4, 1, width), f32),
-            ((2, head_dim, width), f32),
-            ((2, head_dim, width), bf16),
-        ],
+    half_stat = ((2, 1, width), f32)
+    half_query = ((2, head_dim, width), f32)
+    half_query_16 = ((2, head_dim, width), bf16)
+
+    def forward(first, name):
+        return call(
+            functools.partial(prev_forward, first),
+            name,
+            [
+                ((2, tiles, tile_keys, width), bf16),
+                half_stat,
+                ((3, 2, 1, width), f32),
+                half_query if first == 0 else half_query_16,
+            ],
+            (0,),
+            [((2, tiles, tile_keys, width), f32)],
+            flops=2 * 2 * tiles * unit,
+        )(has_prev, qs, dot, prev_kv, m_own, l_own, o_own)
+
+    p_theirs, m_theirs, stats_theirs, sent = forward(2, "prev_forward_theirs")
+    other_mine = to_partner(stats_theirs, "inner")
+    got = to_partner(sent, "inner")
+    p_mine, m_mine, stats_mine, out = forward(0, "prev_forward_mine")
+    other_theirs = to_partner(stats_mine, "inner")
+    first_terms, dos_mine, shift_mine, dqt_mine, factor = call(
+        functools.partial(prev_backward, 0),
+        "prev_backward_mine",
+        [((span_rows, 2 * head_dim), f32), half_query_16, half_stat, half_query, ((2, 2, 1, width), f32)],
         (0,),
-        [((4, tiles, tile_keys, width), f32)],
-        flops=2 * 4 * tiles * unit,
-    )(has_prev, qs, dot, prev_kv, m_own, l_own, o_own)
-    other = to_partner(stats, "inner")
-    got = to_partner(sent, "inner")
-    prev_terms, dos, shift, dqt, factor = call(
-        prev_backward,
-        "prev_backward",
-        [terms_shape, by_query_16, row_stat, by_query, ((2, 2, 1, width), f32)],
+        [half_query_16, half_stat],
+        flops=4 * 2 * tiles * unit,
+    )(has_prev, qs, dot, prev_kv, p_mine, m_own, m_mine, stats_mine, other_mine)
+    prev_terms, dos_theirs, shift_theirs, dqt_theirs = call(
+        functools.partial(prev_backward, 2),
+        "prev_backward_theirs",
+        [terms_shape, half_query_16, half_stat, half_query],
         (0,),
-        [by_query_16, row_stat],
-        flops=4 * 4 * tiles * unit,
-    )(has_prev, qs, dot, prev_kv, p_prev, m_own, m_prev, stats, other)
+        [half_query_16, half_stat],
+        flops=4 * 2 * tiles * unit,
+    )(has_prev, qs, dot, prev_kv, p_theirs, m_own, m_theirs, stats_theirs, other_theirs, first_terms)
     returned = from_behind(prev_terms, "outer", -1)
     dq, dq_partner, own_terms = call(
         own_backward,
@@ -392,7 +436,7 @@
         (0, 1),
         [((span_rows, 2 * head_dim), f32), by_query],
         flops=4 * steps * unit,
-    )(allowed, slots, qs, ks, vs, p_own, dos, shift, dqt)
+    )(allowed, slots, qs, ks, vs, p_own, dos_mine, shift_mine, dqt_mine, dos_theirs, shift_theirs, dqt_theirs)
     (attended,) = call(merge_attended, "merge_attended", [tokens], (), [])(out, got, factor)
     dq_other = to_partner(dq_partner, "inner")
     terms = (own_terms.astype(f32) + returned.astype(f32)).astype(bf16)

time: 90.6 us -> 91.1 us (level)
  starting transfers between devices: 23.2 us -> 25.9 us
  waiting for transfers between devices: 38.1 us -> 35.7 us
  between operations: 2.87 us -> 0.73 us
  Pallas kernels: 19.4 us -> 21.1 us
    ppermute x2, starting transfers between devices: 4.21 us -> 6.02 us  [from_behind(): return lax.ppermute(block, axis, route)]
    pallas_call x7 -> x9, Pallas kernels: 19.4 us -> 21.1 us  [run(): pl.pallas_call(kernel, name=name, grid=(1,) if stream else (), out_shape=...]
    ppermute x2, waiting for transfers between devices: 5.45 us -> 3.98 us  [from_behind(): return lax.ppermute(block, axis, route)]
    ppermute x6 -> x7, waiting for transfers between devices: 12.6 us -> 11.7 us  [to_partner(): lax.ppermute(block, axis, [(i, i ^ 1) for i in range(lax.axis_size(axis))])]
    ppermute x6 -> x7, starting transfers between devices: 7.06 us -> 7.89 us  [to_partner(): lax.ppermute(block, axis, [(i, i ^ 1) for i in range(lax.axis_size(axis))])]
    unnamed x10 -> x12, local copies, waits for them, and re-layouts: 4.06 us -> 4.72 us
  transfers between devices with their start and end apart: 10 -> 11, of which waited for: 8 -> 8; matrix products, arithmetic and copies ran while one was open for 1% -> 1% of each run, Pallas kernels for 10% -> 16%
where the time goes in v5:
time: 91.1 us; the launch traced here: 90.6 us
  waiting for transfers between devices  35.7 us (39%)
  starting transfers between devices  25.9 us (28%)
  Pallas kernels  21.1 us (23%)
  local copies, waits for them, and re-layouts  5.35 us (6%)
  other arithmetic  1.79 us (2%)
    pallas_call x9, Pallas kernels, run(): pl.pallas_call(kernel, name=name, grid=(1,) if stream else (), out_shape=...  21.1 us
    all_to_all x2, waiting for transfers between devices, exchange(): lax.all_to_all(parts, axis, 0, 0, axis_index_groups=groups, tiled=True)  20 us
    all_to_all x2, starting transfers between devices, exchange(): lax.all_to_all(parts, axis, 0, 0, axis_index_groups=groups, tiled=True)  12 us
    ppermute x7, waiting for transfers between devices, to_partner(): lax.ppermute(block, axis, [(i, i ^ 1) for i in range(lax.axis_size(axis))])  11.7 us
    ppermute x7, starting transfers between devices, to_partner(): lax.ppermute(block, axis, [(i, i ^ 1) for i in range(lax.axis_size(axis))])  7.89 us
    ppermute x2, starting transfers between devices, from_behind(): return lax.ppermute(block, axis, route)  6.02 us
    unnamed x12, local copies, waits for them, and re-layouts  4.72 us
    ppermute x2, waiting for transfers between devices, from_behind(): return lax.ppermute(block, axis, route)  3.98 us
  transfers between devices with their start and end apart: 11, of which 8 were waited for; matrix products, arithmetic and copies ran while one was open for 1% of the time, Pallas kernels for 16%

profile of v5, /device:TPU:16, one launch (start us, length us, event | category | flops | bytes accessed | tf_op | source)
XLA Modules:
  0.0 90.6 jit_solution(10093896805380357841)
XLA Ops:
  2.8 1.4 %pack.1 = bf16[8,144,256]{2,1,0:T(8,128)(2,1)} custom-call(s32[128]{0:T(128)S(1)} %copy-done.2, bf16[128,128]{1,0:T(8,128)(2,1)S(1)} %copy-done, bf16[128,128]{1,0:T(8,128)(2,1)S(1)} %copy-done.1), custom_call_target="tpu_custom_call" | custom-call | bytes 4194304 | tf_op jit(solution)/shard_map/pack/pallas_call | solution.py:316
  4.2 8.5 %all-to-all-start = ((bf16[8,144,256]{2,1,0:T(8,128)(2,1)}), bf16[8,144,256]{2,1,0:T(8,128)(2,1)S(1)}, u32[]{:S(2)}, u32[]{:S(2)}) async-start(bf16[8,144,256]{2,1,0:T(8,128)(2,1)} %pack.1), calls=%async_computation | async-start | bytes 1179648 | tf_op jit(solution)/shard_map/all_to_all | solution.py:30
  12.7 1.3 %collective-permute-start.1 = (bf16[128,1024]{1,0:T(8,128)(2,1)}, bf16[128,1024]{1,0:T(8,128)(2,1)S(1)}, u32[]{:S(2)}, u32[]{:S(2)}) collective-permute-start(bf16[128,1024]{1,0:T(8,128)(2,1)} %q_ref.1), channel_id=1, source_target_pairs={{0,1},{1,0},{2,3},{3,2},{4,5},{5,4},{6,7},{7,6},{8,9},{9,8},{10,11... | collective-permute-start | bytes 786440 | tf_op jit(solution)/shard_map/ppermute | solution.py:24
  14.7 16.9 %all-to-all-done.kv_ref = bf16[8,144,256]{2,1,0:T(8,128)(2,1)S(1)} async-done(((bf16[8,144,256]{2,1,0:T(8,128)(2,1)}), bf16[8,144,256]{2,1,0:T(8,128)(2,1)S(1)}, u32[]{:S(2)}, u32[]{:S(2)}) %all-to-all-start) | async-done | bytes 589856 | tf_op jit(solution)/shard_map/all_to_all | solution.py:30
  31.6 1.9 %collective-permute-start.3 = (bf16[8,144,256]{2,1,0:T(8,128)(2,1)S(1)}, bf16[8,144,256]{2,1,0:T(8,128)(2,1)S(1)}, u32[]{:S(2)}, u32[]{:S(2)}) collective-permute-start(bf16[8,144,256]{2,1,0:T(8,128)(2,1)S(1)} %all-to-all-done.kv_ref), channel_id=1, source_target_pairs={{0,16},{16,32},{32,48},{48,64},{64,80},{80,96},{96,112},{112,128},... | collective-permute-start | bytes 1769480 | tf_op jit(solution)/shard_map/ppermute | solution.py:20
  33.5 1.4 %collective-permute-start = (s32[128]{0:T(128)}, s32[128]{0:T(128)S(1)}, u32[]{:S(2)}, u32[]{:S(2)}) collective-permute-start(s32[128]{0:T(128)} %position_ref.3), channel_id=1, source_target_pairs={{0,1},{1,0},{2,3},{3,2},{4,5},{5,4},{6,7},{7,6},{8,9},{9,8},{10,11... | collective-permute-start | bytes 1544 | tf_op jit(solution)/shard_map/ppermute | solution.py:24
  34.9 2.4 %collective-permute-done.position_partner_ref = s32[128]{0:T(128)S(1)} collective-permute-done((s32[128]{0:T(128)}, s32[128]{0:T(128)S(1)}, u32[]{:S(2)}, u32[]{:S(2)}) %collective-permute-start) | collective-permute-done | bytes 544 | tf_op jit(solution)/shard_map/ppermute | solution.py:24
  39.9 1.2 %stack_pair.1 = (s32[2]{0:T(128)S(1)}, bf16[4,512,128]{2,1,0:T(8,128)(2,1)S(1)}, bf16[4,128,512]{2,1,0:T(8,128)(2,1)S(1)}) custom-call(s32[128]{0:T(128)S(1)} %copy-done.3, s32[128]{0:T(128)S(1)} %collective-permute-done.position_partner_ref, bf16[128,1024]{1,0:T(8,128)(2,1)S(1)} %copy-done.4, bf16[128,1024]{1,0:T(8,128)(2,1)S(1)} %collective-permute-done.1.q_partner_ref, ...), custom_call_target="tpu_custom_call" | custom-call | flops 4000000000 | bytes 4194304 | tf_op jit(solution)/shard_map/stack_pair/pallas_call | solution.py:316
  41.1 3.8 %own_forward.1 = (bf16[1024,128]{1,0:T(8,128)(2,1)S(1)}, bf16[1024,128]{1,0:T(8,128)(2,1)S(1)}, s32[8]{0:T(128)S(1)}, s32[4]{0:T(128)S(1)}, bf16[10,256,512]{2,1...) custom-call(s32[2]{0:T(128)S(1)} %get-tuple-element.37.block_ref, ...), custom_call_target="tpu_custom_call" | custom-call | flops 671088640 | bytes 4194304 | tf_op jit(solution)/shard_map/own_forward/pallas_call | solution.py:316
  44.9 1.5 %collective-permute-done.3.kv_ref = bf16[8,144,256]{2,1,0:T(8,128)(2,1)S(1)} collective-permute-done((bf16[8,144,256]{2,1,0:T(8,128)(2,1)S(1)}, bf16[8,144,256]{2,1,0:T(8,128)(2,1)S(1)}, u32[]{:S(2)}, u32[]{:S(2)}) %collective-permute-start.3) | collective-permute-done | bytes 589856 | tf_op jit(solution)/shard_map/ppermute | solution.py:20
  46.4 2.0 %prev_forward_theirs.1 = (bf16[2,4,256,512]{3,2,1,0:T(8,128)(2,1)S(1)}, f32[2,1,512]{2,1,0:T(1,128)S(1)}, f32[3,2,1,512]{3,2,1,0:T(1,128)S(1)}, bf16[2,128,512]{2,1,0:T(8,128)(2,1)S(1)}) custom-call(s32[1]{0:T(128)} %bitcast.has_ref, bf16[4,512,128]{2,1,0:T(8,128)(2,1)S(1)} %get-tuple-element.35.qs_ref, bf16[4,128,512]{2,1,0:T(8,128)(2,1)S(1)} %get-tuple-element.36.dot_ref, ...), custom_call_target="tpu_custom_call" | custom-call | flops 536870912 | bytes 4194304 | tf_op jit(solution)/shard_map/prev_forward_theirs/pallas_call | solution.py:316
  48.4 1.4 %collective-permute-start.5 = (f32[3,2,1,512]{3,2,1,0:T(1,128)S(1)}, f32[3,2,1,512]{3,2,1,0:T(1,128)S(1)}, u32[]{:S(2)}, u32[]{:S(2)}) collective-permute-start(f32[3,2,1,512]{3,2,1,0:T(1,128)S(1)} %get-tuple-element.46.stats_ref), channel_id=1, source_target_pairs={{0,1},{1,0},{2,3},{3,2},{4,5},{5,4},{6,7},{7,6},{8,9},{9,8},{10,11... | collective-permute-start | bytes 36872 | tf_op jit(solution)/shard_map/ppermute | solution.py:24
  49.7 1.9 %prev_forward_mine.1 = (bf16[2,4,256,512]{3,2,1,0:T(8,128)(2,1)S(1)}, f32[2,1,512]{2,1,0:T(1,128)S(1)}, f32[3,2,1,512]{3,2,1,0:T(1,128)S(1)}, f32[2,128,512]{2,1,0:T(8,128)S(1)}) custom-call(s32[1]{0:T(128)} %bitcast.has_ref, bf16[4,512,128]{2,1,0:T(8,128)(2,1)S(1)} %get-tuple-element.35.qs_ref, bf16[4,128,512]{2,1,0:T(8,128)(2,1)S(1)} %get-tuple-element.36.dot_ref, ...), custom_call_target="tpu_custom_call" | custom-call | flops 536870912 | bytes 4194304 | tf_op jit(solution)/shard_map/prev_forward_mine/pallas_call | solution.py:316
  51.7 1.0 %collective-permute-start.6 = (f32[3,2,1,512]{3,2,1,0:T(1,128)S(1)}, f32[3,2,1,512]{3,2,1,0:T(1,128)S(1)}, u32[]{:S(2)}, u32[]{:S(2)}) collective-permute-start(f32[3,2,1,512]{3,2,1,0:T(1,128)S(1)} %get-tuple-element.45.stats_ref), channel_id=1, source_target_pairs={{0,1},{1,0},{2,3},{3,2},{4,5},{5,4},{6,7},{7,6},{8,9},{9,8},{10,11... | collective-permute-start | bytes 36872 | tf_op jit(solution)/shard_map/ppermute | solution.py:24
  52.7 2.7 %prev_backward_mine.1 = (f32[1024,256]{1,0:T(8,128)S(1)}, bf16[2,128,512]{2,1,0:T(8,128)(2,1)S(1)}, f32[2,1,512]{2,1,0:T(1,128)S(1)}, f32[2,128,512]{2,1,0:T(8,128)S(1)}, f32[2,2,1,512]{3,2,1,0:T(1,128)S(1)}) custom-call(s32[1]{0:T(128)} %bitcast.has_ref, bf16[4,512,128]{2,1,0:T(8,128)(2,1)S(1)} %get-tuple-element.35.qs_ref, ...), custom_call_target="tpu_custom_call" | custom-call | flops 1073741824 | bytes 4194304 | tf_op jit(solution)/shard_map/prev_backward_mine/pallas_call | solution.py:316
  55.7 3.0 %prev_backward_theirs.1 = (bf16[8,128,256]{2,1,0:T(8,128)(2,1)S(1)}, bf16[2,128,512]{2,1,0:T(8,128)(2,1)S(1)}, f32[2,1,512]{2,1,0:T(1,128)S(1)}, f32[2,128,512]{2,1,0:T(8,128)S(1)}) custom-call(s32[1]{0:T(128)} %bitcast.has_ref, bf16[4,512,128]{2,1,0:T(8,128)(2,1)S(1)} %get-tuple-element.35.qs_ref, bf16[4,128,512]{2,1,0:T(8,128)(2,1)S(1)} %get-tuple-element.36.dot_ref, ...), custom_call_target="tpu_custom_call" | custom-call | flops 1073741824 | bytes 4194304 | tf_op jit(solution)/shard_map/prev_backward_theirs/pallas_call | solution.py:316
  58.7 4.1 %collective-permute-start.8 = (bf16[8,128,256]{2,1,0:T(8,128)(2,1)S(1)}, bf16[8,128,256]{2,1,0:T(8,128)(2,1)S(1)}, u32[]{:S(2)}, u32[]{:S(2)}) collective-permute-start(bf16[8,128,256]{2,1,0:T(8,128)(2,1)S(1)} %get-tuple-element.65), channel_id=1, source_target_pairs={{16,0},{32,16},{48,32},{64,48},{80,64},{96,80},{112,96},{128,112},... | collective-permute-start | bytes 1572872 | tf_op jit(solution)/shard_map/ppermute | solution.py:20
  62.8 4.2 %own_backward.1 = (f32[128,1024]{1,0:T(8,128)S(1)}, bf16[128,1024]{1,0:T(8,128)(2,1)S(1)}, bf16[8,128,256]{2,1,0:T(8,128)(2,1)S(1)}) custom-call(s32[4]{0:T(128)S(1)} %get-tuple-element.48.allowed_ref, s32[8]{0:T(128)S(1)} %get-tuple-element.49.slots_ref, bf16[4,512,128]{2,1,0:T(8,128)(2,1)S(1)} %get-tuple-element.35.qs_ref, ...), custom_call_target="tpu_custom_call" | custom-call | flops 1342177280 | bytes 4194304 | tf_op jit(solution)/shard_map/own_backward/pallas_call | solution.py:316
  67.0 2.5 %collective-permute-done.8 = bf16[8,128,256]{2,1,0:T(8,128)(2,1)S(1)} collective-permute-done((bf16[8,128,256]{2,1,0:T(8,128)(2,1)S(1)}, bf16[8,128,256]{2,1,0:T(8,128)(2,1)S(1)}, u32[]{:S(2)}, u32[]{:S(2)}) %collective-permute-start.8) | collective-permute-done | bytes 524320 | tf_op jit(solution)/shard_map/ppermute | solution.py:20
  70.4 3.5 %all-to-all-start.1 = ((bf16[8,128,256]{2,1,0:T(8,128)(2,1)}), bf16[8,128,256]{2,1,0:T(8,128)(2,1)S(1)}, u32[]{:S(2)}, u32[]{:S(2)}) async-start(bf16[8,128,256]{2,1,0:T(8,128)(2,1)} %add_convert_fusion), calls=%async_computation.1 | async-start | bytes 1048576 | tf_op jit(solution)/shard_map/all_to_all | solution.py:30
  73.9 1.4 %collective-permute-start.4 = (bf16[2,128,512]{2,1,0:T(8,128)(2,1)S(1)}, bf16[2,128,512]{2,1,0:T(8,128)(2,1)S(1)}, u32[]{:S(2)}, u32[]{:S(2)}) collective-permute-start(bf16[2,128,512]{2,1,0:T(8,128)(2,1)S(1)} %get-tuple-element.42), channel_id=1, source_target_pairs={{0,1},{1,0},{2,3},{3,2},{4,5},{5,4},{6,7},{7,6},{8,9},{9,8},{10,11... | collective-permute-start | bytes 786440 | tf_op jit(solution)/shard_map/ppermute | solution.py:24
  76.1 7.1 %collective-permute-done.4.got_ref = bf16[2,128,512]{2,1,0:T(8,128)(2,1)S(1)} collective-permute-done((bf16[2,128,512]{2,1,0:T(8,128)(2,1)S(1)}, bf16[2,128,512]{2,1,0:T(8,128)(2,1)S(1)}, u32[]{:S(2)}, u32[]{:S(2)}) %collective-permute-start.4) | collective-permute-done | bytes 262176 | tf_op jit(solution)/shard_map/ppermute | solution.py:24
  84.0 2.0 %collective-permute-done.7 = bf16[128,1024]{1,0:T(8,128)(2,1)S(1)} collective-permute-done((bf16[128,1024]{1,0:T(8,128)(2,1)S(1)}, bf16[128,1024]{1,0:T(8,128)(2,1)S(1)}, u32[]{:S(2)}, u32[]{:S(2)}) %collective-permute-start.7) | collective-permute-done | bytes 262176 | tf_op jit(solution)/shard_map/ppermute | solution.py:24
  86.7 3.2 %all-to-all-done.1 = bf16[8,128,256]{2,1,0:T(8,128)(2,1)S(1)} async-done(((bf16[8,128,256]{2,1,0:T(8,128)(2,1)}), bf16[8,128,256]{2,1,0:T(8,128)(2,1)S(1)}, u32[]{:S(2)}, u32[]{:S(2)}) %all-to-all-start.1) | async-done | bytes 524320 | tf_op jit(solution)/shard_map/all_to_all | solution.py:30
  (23 shorter events, 9.7 us)
Async XLA Ops:
  0.6 0.8 copy-start
  1.4 0.8 copy-start.1
  2.1 0.7 copy-start.2
  4.2 27.4 %all-to-all-start = ((bf16[8,144,256]{2,1,0:T(8,128)(2,1)}), bf16[8,144,256]{2,1,0:T(8,128)(2,1)S(1)}, u32[]{:S(2)}, u32[]{:S(2)}) async-start(bf16[8,144,256]{2,1,0:T(8,128)(2,1)} %pack.1), calls=%async_computation | async-start | bytes 1179648 | tf_op jit(solution)/shard_map/all_to_all | solution.py:30
  12.7 24.6 %collective-permute-start.1 = (bf16[128,1024]{1,0:T(8,128)(2,1)}, bf16[128,1024]{1,0:T(8,128)(2,1)S(1)}, u32[]{:S(2)}, u32[]{:S(2)}) collective-permute-start(bf16[128,1024]{1,0:T(8,128)(2,1)} %q_ref.1), channel_id=1, source_target_pairs={{0,1},{1,0},{2,3},{3,2},{4,5},{5,4},{6,7},{7,6},{8,9},{9,8},{10,11... | collective-permute-start | bytes 786440 | tf_op jit(solution)/shard_map/ppermute | solution.py:24
  14.0 23.3 %collective-permute-start.2 = (bf16[128,1024]{1,0:T(8,128)(2,1)}, bf16[128,1024]{1,0:T(8,128)(2,1)S(1)}, u32[]{:S(2)}, u32[]{:S(2)}) collective-permute-start(bf16[128,1024]{1,0:T(8,128)(2,1)} %do_ref.1), channel_id=1, source_target_pairs={{0,1},{1,0},{2,3},{3,2},{4,5},{5,4},{6,7},{7,6},{8,9},{9,8},{10,11... | collective-permute-start | bytes 786440 | tf_op jit(solution)/shard_map/ppermute | solution.py:24
  31.6 14.8 %collective-permute-start.3 = (bf16[8,144,256]{2,1,0:T(8,128)(2,1)S(1)}, bf16[8,144,256]{2,1,0:T(8,128)(2,1)S(1)}, u32[]{:S(2)}, u32[]{:S(2)}) collective-permute-start(bf16[8,144,256]{2,1,0:T(8,128)(2,1)S(1)} %all-to-all-done.kv_ref), channel_id=1, source_target_pairs={{0,16},{16,32},{32,48},{48,64},{64,80},{80,96},{96,112},{112,128},... | collective-permute-start | bytes 1769480 | tf_op jit(solution)/shard_map/ppermute | solution.py:20
  33.5 3.8 %collective-permute-start = (s32[128]{0:T(128)}, s32[128]{0:T(128)S(1)}, u32[]{:S(2)}, u32[]{:S(2)}) collective-permute-start(s32[128]{0:T(128)} %position_ref.3), channel_id=1, source_target_pairs={{0,1},{1,0},{2,3},{3,2},{4,5},{5,4},{6,7},{7,6},{8,9},{9,8},{10,11... | collective-permute-start | bytes 1544 | tf_op jit(solution)/shard_map/ppermute | solution.py:24
  37.3 0.7 copy-start.3
  38.0 0.9 %copy-start.4 = (bf16[128,1024]{1,0:T(8,128)(2,1)S(1)}, bf16[128,1024]{1,0:T(8,128)(2,1)}, u32[]{:S(2)}) copy-start(bf16[128,1024]{1,0:T(8,128)(2,1)} %q_ref.1) | copy-start | bytes 786436
  38.9 0.9 %copy-start.5 = (bf16[128,1024]{1,0:T(8,128)(2,1)S(1)}, bf16[128,1024]{1,0:T(8,128)(2,1)}, u32[]{:S(2)}) copy-start(bf16[128,1024]{1,0:T(8,128)(2,1)} %do_ref.1) | copy-start | bytes 786436
  48.4 4.3 %collective-permute-start.5 = (f32[3,2,1,512]{3,2,1,0:T(1,128)S(1)}, f32[3,2,1,512]{3,2,1,0:T(1,128)S(1)}, u32[]{:S(2)}, u32[]{:S(2)}) collective-permute-start(f32[3,2,1,512]{3,2,1,0:T(1,128)S(1)} %get-tuple-element.46.stats_ref), channel_id=1, source_target_pairs={{0,1},{1,0},{2,3},{3,2},{4,5},{5,4},{6,7},{7,6},{8,9},{9,8},{10,11... | collective-permute-start | bytes 36872 | tf_op jit(solution)/shard_map/ppermute | solution.py:24
  51.7 4.0 %collective-permute-start.6 = (f32[3,2,1,512]{3,2,1,0:T(1,128)S(1)}, f32[3,2,1,512]{3,2,1,0:T(1,128)S(1)}, u32[]{:S(2)}, u32[]{:S(2)}) collective-permute-start(f32[3,2,1,512]{3,2,1,0:T(1,128)S(1)} %get-tuple-element.45.stats_ref), channel_id=1, source_target_pairs={{0,1},{1,0},{2,3},{3,2},{4,5},{5,4},{6,7},{7,6},{8,9},{9,8},{10,11... | collective-permute-start | bytes 36872 | tf_op jit(solution)/shard_map/ppermute | solution.py:24
  58.7 10.8 %collective-permute-start.8 = (bf16[8,128,256]{2,1,0:T(8,128)(2,1)S(1)}, bf16[8,128,256]{2,1,0:T(8,128)(2,1)S(1)}, u32[]{:S(2)}, u32[]{:S(2)}) collective-permute-start(bf16[8,128,256]{2,1,0:T(8,128)(2,1)S(1)} %get-tuple-element.65), channel_id=1, source_target_pairs={{16,0},{32,16},{48,32},{64,48},{80,64},{96,80},{112,96},{128,112},... | collective-permute-start | bytes 1572872 | tf_op jit(solution)/shard_map/ppermute | solution.py:20
  70.4 19.4 %all-to-all-start.1 = ((bf16[8,128,256]{2,1,0:T(8,128)(2,1)}), bf16[8,128,256]{2,1,0:T(8,128)(2,1)S(1)}, u32[]{:S(2)}, u32[]{:S(2)}) async-start(bf16[8,128,256]{2,1,0:T(8,128)(2,1)} %add_convert_fusion), calls=%async_computation.1 | async-start | bytes 1048576 | tf_op jit(solution)/shard_map/all_to_all | solution.py:30
  73.9 9.2 %collective-permute-start.4 = (bf16[2,128,512]{2,1,0:T(8,128)(2,1)S(1)}, bf16[2,128,512]{2,1,0:T(8,128)(2,1)S(1)}, u32[]{:S(2)}, u32[]{:S(2)}) collective-permute-start(bf16[2,128,512]{2,1,0:T(8,128)(2,1)S(1)} %get-tuple-element.42), channel_id=1, source_target_pairs={{0,1},{1,0},{2,3},{3,2},{4,5},{5,4},{6,7},{7,6},{8,9},{9,8},{10,11... | collective-permute-start | bytes 786440 | tf_op jit(solution)/shard_map/ppermute | solution.py:24
  75.3 10.6 %collective-permute-start.7 = (bf16[128,1024]{1,0:T(8,128)(2,1)S(1)}, bf16[128,1024]{1,0:T(8,128)(2,1)S(1)}, u32[]{:S(2)}, u32[]{:S(2)}) collective-permute-start(bf16[128,1024]{1,0:T(8,128)(2,1)S(1)} %get-tuple-element.63), channel_id=1, source_target_pairs={{0,1},{1,0},{2,3},{3,2},{4,5},{5,4},{6,7},{7,6},{8,9},{9,8},{10,11... | collective-permute-start | bytes 786440 | tf_op jit(solution)/shard_map/ppermute | solution.py:24

commit v6 on v5

--- a/solution.py
+++ b/solution.py
@@ -58,15 +58,30 @@
         ].astype(target_ref.dtype)
 
 
-def pack(position_ref, key_ref, value_ref, packed_ref):
+def pack(position_ref, key_ref, value_ref, packed_ref, place_ref, block_ref, in_sems, out_sems):
     count, rows, both = packed_ref.shape
     span = key_ref.shape[0]
-    tag = (lax.rem(position_ref[0], 2 * count * span) // block_rows).astype(jnp.float32)
-    tag = jnp.full((rows - span, both), tag, jnp.float32).astype(packed_ref.dtype)
-    for g in range(count):
-        packed_ref[g, :span, : both // 2] = key_ref[...]
-        packed_ref[g, :span, both // 2 :] = value_ref[...]
-        packed_ref[g, span:, :] = tag
+    loads = [
+        pltpu.make_async_copy(position_ref, place_ref, in_sems.at[0]),
+        pltpu.make_async_copy(key_ref, block_ref.at[pl.ds(0, span), pl.ds(0, both // 2)], in_sems.at[1]),
+        pltpu.make_async_copy(
+            value_ref, block_ref.at[pl.ds(0, span), pl.ds(both // 2, both // 2)], in_sems.at[2]
+        ),
+    ]
+    for load in loads:
+        load.start()
+    loads[0].wait()
+    tag = (lax.rem(place_ref[0], 2 * count * span) // block_rows).astype(jnp.float32)
+    block_ref[span:, :] = jnp.full((rows - span, both), tag, jnp.float32).astype(packed_ref.dtype)
+    loads[1].wait()
+    loads[2].wait()
+    stores = [
+        pltpu.make_async_copy(block_ref, packed_ref.at[g], out_sems.at[g]) for g in range(count)
+    ]
+    for store in stores:
+        store.start()
+    for store in stores:
+        store.wait()
 
 
 def stack_pair(
@@ -341,16 +356,22 @@
     query_partner = to_partner(queries, "inner")
     grad_partner = to_partner(grad_output, "inner")
     position_partner = to_partner(positions, "inner")
-    (packed,) = call(
+    anywhere = pl.BlockSpec(memory_space=pl.ANY)
+    packed = pl.pallas_call(
         pack,
-        "pack",
-        [((group, tok_rows + tag_rows, 2 * head_dim), bf16)],
-        (0,),
-        [],
-        stream=(1, 2),
+        name="pack",
+        out_shape=jax.ShapeDtypeStruct((group, tok_rows + tag_rows, 2 * head_dim), bf16),
+        in_specs=[anywhere] * 3,
+        out_specs=anywhere,
+        scratch_shapes=[
+            pltpu.SMEM(positions.shape, jnp.int32),
+            pltpu.VMEM((tok_rows + tag_rows, 2 * head_dim), bf16),
+            pltpu.SemaphoreType.DMA((3,)),
+            pltpu.SemaphoreType.DMA((group,)),
+        ],
+        compiler_params=pltpu.CompilerParams(vmem_limit_bytes=60 * 1024 * 1024),
     )(positions, key_vectors, value_vectors)
     group_kv = exchange(packed, "inner")
-    prev_kv = from_behind(group_kv, "outer", 1)
     has_prev = (lax.axis_index("outer") > 0).astype(jnp.int32).reshape(1)
 
     unit = 2 * tile_keys * width * head_dim
@@ -370,6 +391,8 @@
         flops=4 * 10**9,
         stream=(2, 4),
     )(positions, position_partner, queries, query_partner, grad_output, grad_partner)
+    group_kv, qs, dot, both_blocks = lax.optimization_barrier((group_kv, qs, dot, both_blocks))
+    prev_kv = from_behind(group_kv, "outer", 1)
     ks, vs, slots, allowed, p_own, m_own, l_own, o_own = call(
         own_forward,
         "own_forward",
@@ -420,6 +443,7 @@
         [half_query_16, half_stat],
         flops=4 * 2 * tiles * unit,
     )(has_prev, qs, dot, prev_kv, p_mine, m_own, m_mine, stats_mine, other_mine)
+    first_terms, got = lax.optimization_barrier((first_terms, got))
     prev_terms, dos_theirs, shift_theirs, dqt_theirs = call(
         functools.partial(prev_backward, 2),
         "prev_backward_theirs",

time: 91.1 us -> 93.2 us (1.023); the launches traced: 90.6 us -> 91.7 us
  waiting for transfers between devices: 35.7 us -> 38.2 us
  local copies, waits for them, and re-layouts: 5.35 us -> 3.18 us
    all_to_all x2, waiting for transfers between devices: 20 us -> 10.2 us  [exchange(): lax.all_to_all(parts, axis, 0, 0, axis_index_groups=groups, tiled=True)]
    ppermute x2, waiting for transfers between devices: 3.98 us -> 11.6 us  [from_behind(): return lax.ppermute(block, axis, route)]
    ppermute x7, waiting for transfers between devices: 11.7 us -> 16.4 us  [to_partner(): lax.ppermute(block, axis, [(i, i ^ 1) for i in range(lax.axis_size(axis))])]
    unnamed x12 -> x6, local copies, waits for them, and re-layouts: 4.72 us -> 2.55 us
    all_to_all x2, starting transfers between devices: 12 us -> 14 us  [exchange(): lax.all_to_all(parts, axis, 0, 0, axis_index_groups=groups, tiled=True)]
    pallas_call x0 -> x1, Pallas kernels: none -> 1.7 us  [body(): pl.pallas_call(pack, name='pack', out_shape=jax.ShapeDtypeStruct((group,...]
    pallas_call x9 -> x8, Pallas kernels: 21.1 us -> 19.8 us  [run(): pl.pallas_call(kernel, name=name, grid=(1,) if stream else (), out_shape=...]
    ppermute x2, starting transfers between devices: 6.02 us -> 4.92 us  [from_behind(): return lax.ppermute(block, axis, route)]
  transfers between devices with their start and end apart: 11 -> 11, of which waited for: 8 -> 7; matrix products, arithmetic and copies ran while one was open for 1% -> 1% of each run, Pallas kernels for 16% -> 16%
where the time goes in v6:
time: 93.2 us; the launch traced here: 91.7 us
  waiting for transfers between devices  38.2 us (41%)
  starting transfers between devices  26.2 us (28%)
  Pallas kernels  21.5 us (23%)
  local copies, waits for them, and re-layouts  3.18 us (3%)
  other arithmetic  1.78 us (2%)
    pallas_call x8, Pallas kernels, run(): pl.pallas_call(kernel, name=name, grid=(1,) if stream else (), out_shape=...  19.8 us
    ppermute x7, waiting for transfers between devices, to_partner(): lax.ppermute(block, axis, [(i, i ^ 1) for i in range(lax.axis_size(axis))])  16.4 us
    all_to_all x2, starting transfers between devices, exchange(): lax.all_to_all(parts, axis, 0, 0, axis_index_groups=groups, tiled=True)  14 us
    ppermute x2, waiting for transfers between devices, from_behind(): return lax.ppermute(block, axis, route)  11.6 us
    all_to_all x2, waiting for transfers between devices, exchange(): lax.all_to_all(parts, axis, 0, 0, axis_index_groups=groups, tiled=True)  10.2 us
    ppermute x7, starting transfers between devices, to_partner(): lax.ppermute(block, axis, [(i, i ^ 1) for i in range(lax.axis_size(axis))])  7.34 us
    ppermute x2, starting transfers between devices, from_behind(): return lax.ppermute(block, axis, route)  4.92 us
    unnamed x6, local copies, waits for them, and re-layouts  2.55 us
  transfers between devices with their start and end apart: 11, of which 7 were waited for; matrix products, arithmetic and copies ran while one was open for 1% of the time, Pallas kernels for 16%

profile of v6, /device:TPU:16, one launch (start us, length us, event | category | flops | bytes accessed | tf_op | source)
XLA Modules:
  0.0 91.7 jit_solution(134527915640968616)
XLA Ops:
  0.6 1.7 %pack.1 = bf16[8,144,256]{2,1,0:T(8,128)(2,1)} custom-call(s32[128]{0:T(128)} %position_ref.3, bf16[128,128]{1,0:T(8,128)(2,1)} %key_ref.1, bf16[128,128]{1,0:T(8,128)(2,1)} %value_ref.1), custom_call_target="tpu_custom_call" | custom-call | tf_op jit(solution)/shard_map/pack/pallas_call | solution.py:360
  2.3 8.5 %all-to-all-start = ((bf16[8,144,256]{2,1,0:T(8,128)(2,1)}), bf16[8,144,256]{2,1,0:T(8,128)(2,1)S(1)}, u32[]{:S(2)}, u32[]{:S(2)}) async-start(bf16[8,144,256]{2,1,0:T(8,128)(2,1)} %pack.1), calls=%async_computation | async-start | bytes 1179648 | tf_op jit(solution)/shard_map/all_to_all | solution.py:30
  10.8 1.3 %collective-permute-start.1 = (bf16[128,1024]{1,0:T(8,128)(2,1)}, bf16[128,1024]{1,0:T(8,128)(2,1)S(1)}, u32[]{:S(2)}, u32[]{:S(2)}) collective-permute-start(bf16[128,1024]{1,0:T(8,128)(2,1)} %q_ref.1), channel_id=1, source_target_pairs={{0,1},{1,0},{2,3},{3,2},{4,5},{5,4},{6,7},{7,6},{8,9},{9,8},{10,11... | collective-permute-start | bytes 786440 | tf_op jit(solution)/shard_map/ppermute | solution.py:24
  12.8 1.3 %collective-permute-start = (s32[128]{0:T(128)}, s32[128]{0:T(128)S(1)}, u32[]{:S(2)}, u32[]{:S(2)}) collective-permute-start(s32[128]{0:T(128)} %position_ref.3), channel_id=1, source_target_pairs={{0,1},{1,0},{2,3},{3,2},{4,5},{5,4},{6,7},{7,6},{8,9},{9,8},{10,11... | collective-permute-start | bytes 1544 | tf_op jit(solution)/shard_map/ppermute | solution.py:24
  14.1 10.4 %collective-permute-done.position_partner_ref = s32[128]{0:T(128)S(1)} collective-permute-done((s32[128]{0:T(128)}, s32[128]{0:T(128)S(1)}, u32[]{:S(2)}, u32[]{:S(2)}) %collective-permute-start) | collective-permute-done | bytes 544 | tf_op jit(solution)/shard_map/ppermute | solution.py:24
  25.1 0.9 %copy-done.1 = bf16[128,1024]{1,0:T(8,128)(2,1)S(1)} copy-done((bf16[128,1024]{1,0:T(8,128)(2,1)S(1)}, bf16[128,1024]{1,0:T(8,128)(2,1)}, u32[]{:S(2)}) %copy-start.1) | copy-done | bytes 262168
  26.1 0.9 %copy-done.2 = bf16[128,1024]{1,0:T(8,128)(2,1)S(1)} copy-done((bf16[128,1024]{1,0:T(8,128)(2,1)S(1)}, bf16[128,1024]{1,0:T(8,128)(2,1)}, u32[]{:S(2)}) %copy-start.2) | copy-done | bytes 262168
  27.0 1.2 %stack_pair.1 = (s32[2]{0:T(128)S(1)}, bf16[4,512,128]{2,1,0:T(8,128)(2,1)S(1)}, bf16[4,128,512]{2,1,0:T(8,128)(2,1)S(1)}) custom-call(s32[128]{0:T(128)S(1)} %copy-done, s32[128]{0:T(128)S(1)} %collective-permute-done.position_partner_ref, bf16[128,1024]{1,0:T(8,128)(2,1)S(1)} %copy-done.1, bf16[128,1024]{1,0:T(8,128)(2,1)S(1)} %collective-permute-done.1.q_partner_ref, ...), custom_call_target="tpu_custom_call" | custom-call | flops 4000000000 | bytes 4194304 | tf_op jit(solution)/shard_map/stack_pair/pallas_call | solution.py:331
  28.2 1.5 %all-to-all-done.kv_ref = bf16[8,144,256]{2,1,0:T(8,128)(2,1)S(1)} async-done(((bf16[8,144,256]{2,1,0:T(8,128)(2,1)}), bf16[8,144,256]{2,1,0:T(8,128)(2,1)S(1)}, u32[]{:S(2)}, u32[]{:S(2)}) %all-to-all-start) | async-done | bytes 589856 | tf_op jit(solution)/shard_map/all_to_all | solution.py:30
  29.7 1.9 %collective-permute-start.3 = (bf16[8,144,256]{2,1,0:T(8,128)(2,1)S(1)}, bf16[8,144,256]{2,1,0:T(8,128)(2,1)S(1)}, u32[]{:S(2)}, u32[]{:S(2)}) collective-permute-start(bf16[8,144,256]{2,1,0:T(8,128)(2,1)S(1)} %all-to-all-done.kv_ref), channel_id=1, source_target_pairs={{0,16},{16,32},{32,48},{48,64},{64,80},{80,96},{96,112},{112,128},... | collective-permute-start | bytes 1769480 | tf_op jit(solution)/shard_map/ppermute | solution.py:20
  31.6 3.8 %own_forward.1 = (bf16[1024,128]{1,0:T(8,128)(2,1)S(1)}, bf16[1024,128]{1,0:T(8,128)(2,1)S(1)}, s32[8]{0:T(128)S(1)}, s32[4]{0:T(128)S(1)}, bf16[10,256,512]{2,1...) custom-call(s32[2]{0:T(128)S(1)} %get-tuple-element.47.block_ref, ...), custom_call_target="tpu_custom_call" | custom-call | flops 671088640 | bytes 4194304 | tf_op jit(solution)/shard_map/own_forward/pallas_call | solution.py:331
  35.5 9.1 %collective-permute-done.3.kv_ref = bf16[8,144,256]{2,1,0:T(8,128)(2,1)S(1)} collective-permute-done((bf16[8,144,256]{2,1,0:T(8,128)(2,1)S(1)}, bf16[8,144,256]{2,1,0:T(8,128)(2,1)S(1)}, u32[]{:S(2)}, u32[]{:S(2)}) %collective-permute-start.3) | collective-permute-done | bytes 589856 | tf_op jit(solution)/shard_map/ppermute | solution.py:20
  44.6 2.0 %prev_forward_theirs.1 = (bf16[2,4,256,512]{3,2,1,0:T(8,128)(2,1)S(1)}, f32[2,1,512]{2,1,0:T(1,128)S(1)}, f32[3,2,1,512]{3,2,1,0:T(1,128)S(1)}, bf16[2,128,512]{2,1,0:T(8,128)(2,1)S(1)}) custom-call(s32[1]{0:T(128)} %bitcast.has_ref, bf16[4,512,128]{2,1,0:T(8,128)(2,1)S(1)} %get-tuple-element.44.qs_ref, bf16[4,128,512]{2,1,0:T(8,128)(2,1)S(1)} %get-tuple-element.45.dot_ref, ...), custom_call_target="tpu_custom_call" | custom-call | flops 536870912 | bytes 4194304 | tf_op jit(solution)/shard_map/prev_forward_theirs/pallas_call | solution.py:331
  46.6 1.4 %collective-permute-start.5 = (bf16[2,128,512]{2,1,0:T(8,128)(2,1)S(1)}, bf16[2,128,512]{2,1,0:T(8,128)(2,1)S(1)}, u32[]{:S(2)}, u32[]{:S(2)}) collective-permute-start(bf16[2,128,512]{2,1,0:T(8,128)(2,1)S(1)} %get-tuple-element.57), channel_id=1, source_target_pairs={{0,1},{1,0},{2,3},{3,2},{4,5},{5,4},{6,7},{7,6},{8,9},{9,8},{10,11... | collective-permute-start | bytes 786440 | tf_op jit(solution)/shard_map/ppermute | solution.py:24
  48.8 2.0 %prev_forward_mine.1 = (bf16[2,4,256,512]{3,2,1,0:T(8,128)(2,1)S(1)}, f32[2,1,512]{2,1,0:T(1,128)S(1)}, f32[3,2,1,512]{3,2,1,0:T(1,128)S(1)}, f32[2,128,512]{2,1,0:T(8,128)S(1)}) custom-call(s32[1]{0:T(128)} %bitcast.has_ref, bf16[4,512,128]{2,1,0:T(8,128)(2,1)S(1)} %get-tuple-element.44.qs_ref, bf16[4,128,512]{2,1,0:T(8,128)(2,1)S(1)} %get-tuple-element.45.dot_ref, ...), custom_call_target="tpu_custom_call" | custom-call | flops 536870912 | bytes 4194304 | tf_op jit(solution)/shard_map/prev_forward_mine/pallas_call | solution.py:331
  50.8 1.6 %collective-permute-start.6 = (f32[3,2,1,512]{3,2,1,0:T(1,128)S(1)}, f32[3,2,1,512]{3,2,1,0:T(1,128)S(1)}, u32[]{:S(2)}, u32[]{:S(2)}) collective-permute-start(f32[3,2,1,512]{3,2,1,0:T(1,128)S(1)} %get-tuple-element.54.stats_ref), channel_id=1, source_target_pairs={{0,1},{1,0},{2,3},{3,2},{4,5},{5,4},{6,7},{7,6},{8,9},{9,8},{10,11... | collective-permute-start | bytes 36872 | tf_op jit(solution)/shard_map/ppermute | solution.py:24
  53.2 2.7 %prev_backward_mine.1 = (f32[1024,256]{1,0:T(8,128)S(1)}, bf16[2,128,512]{2,1,0:T(8,128)(2,1)S(1)}, f32[2,1,512]{2,1,0:T(1,128)S(1)}, f32[2,128,512]{2,1,0:T(8,128)S(1)}, f32[2,2,1,512]{3,2,1,0:T(1,128)S(1)}) custom-call(s32[1]{0:T(128)} %bitcast.has_ref, bf16[4,512,128]{2,1,0:T(8,128)(2,1)S(1)} %get-tuple-element.44.qs_ref, ...), custom_call_target="tpu_custom_call" | custom-call | flops 1073741824 | bytes 4194304 | tf_op jit(solution)/shard_map/prev_backward_mine/pallas_call | solution.py:331
  56.0 3.0 %prev_backward_theirs.1 = (bf16[8,128,256]{2,1,0:T(8,128)(2,1)S(1)}, bf16[2,128,512]{2,1,0:T(8,128)(2,1)S(1)}, f32[2,1,512]{2,1,0:T(1,128)S(1)}, f32[2,128,512]{2,1,0:T(8,128)S(1)}) custom-call(s32[1]{0:T(128)} %bitcast.has_ref, bf16[4,512,128]{2,1,0:T(8,128)(2,1)S(1)} %get-tuple-element.44.qs_ref, bf16[4,128,512]{2,1,0:T(8,128)(2,1)S(1)} %get-tuple-element.45.dot_ref, ...), custom_call_target="tpu_custom_call" | custom-call | flops 1073741824 | bytes 4194304 | tf_op jit(solution)/shard_map/prev_backward_theirs/pallas_call | solution.py:331
  59.0 3.0 %collective-permute-start.8 = (bf16[8,128,256]{2,1,0:T(8,128)(2,1)S(1)}, bf16[8,128,256]{2,1,0:T(8,128)(2,1)S(1)}, u32[]{:S(2)}, u32[]{:S(2)}) collective-permute-start(bf16[8,128,256]{2,1,0:T(8,128)(2,1)S(1)} %get-tuple-element.77), channel_id=1, source_target_pairs={{16,0},{32,16},{48,32},{64,48},{80,64},{96,80},{112,96},{128,112},... | collective-permute-start | bytes 1572872 | tf_op jit(solution)/shard_map/ppermute | solution.py:20
  62.0 4.2 %own_backward.1 = (f32[128,1024]{1,0:T(8,128)S(1)}, bf16[128,1024]{1,0:T(8,128)(2,1)S(1)}, bf16[8,128,256]{2,1,0:T(8,128)(2,1)S(1)}) custom-call(s32[4]{0:T(128)S(1)} %get-tuple-element.60.allowed_ref, s32[8]{0:T(128)S(1)} %get-tuple-element.61.slots_ref, bf16[4,512,128]{2,1,0:T(8,128)(2,1)S(1)} %get-tuple-element.44.qs_ref, ...), custom_call_target="tpu_custom_call" | custom-call | flops 1342177280 | bytes 4194304 | tf_op jit(solution)/shard_map/own_backward/pallas_call | solution.py:331
  66.2 2.5 %collective-permute-done.8 = bf16[8,128,256]{2,1,0:T(8,128)(2,1)S(1)} collective-permute-done((bf16[8,128,256]{2,1,0:T(8,128)(2,1)S(1)}, bf16[8,128,256]{2,1,0:T(8,128)(2,1)S(1)}, u32[]{:S(2)}, u32[]{:S(2)}) %collective-permute-start.8) | collective-permute-done | bytes 524320 | tf_op jit(solution)/shard_map/ppermute | solution.py:20
  69.6 5.5 %all-to-all-start.1 = ((bf16[8,128,256]{2,1,0:T(8,128)(2,1)}), bf16[8,128,256]{2,1,0:T(8,128)(2,1)S(1)}, u32[]{:S(2)}, u32[]{:S(2)}) async-start(bf16[8,128,256]{2,1,0:T(8,128)(2,1)} %add_convert_fusion), calls=%async_computation.1 | async-start | bytes 1048576 | tf_op jit(solution)/shard_map/all_to_all | solution.py:30
  76.3 5.1 %collective-permute-done.7 = bf16[128,1024]{1,0:T(8,128)(2,1)S(1)} collective-permute-done((bf16[128,1024]{1,0:T(8,128)(2,1)S(1)}, bf16[128,1024]{1,0:T(8,128)(2,1)S(1)}, u32[]{:S(2)}, u32[]{:S(2)}) %collective-permute-start.7) | collective-permute-done | bytes 262176 | tf_op jit(solution)/shard_map/ppermute | solution.py:24
  82.2 8.7 %all-to-all-done.1 = bf16[8,128,256]{2,1,0:T(8,128)(2,1)S(1)} async-done(((bf16[8,128,256]{2,1,0:T(8,128)(2,1)}), bf16[8,128,256]{2,1,0:T(8,128)(2,1)S(1)}, u32[]{:S(2)}, u32[]{:S(2)}) %all-to-all-start.1) | async-done | bytes 524320 | tf_op jit(solution)/shard_map/all_to_all | solution.py:30
  (17 shorter events, 6.7 us)
Async XLA Ops:
  2.3 27.4 %all-to-all-start = ((bf16[8,144,256]{2,1,0:T(8,128)(2,1)}), bf16[8,144,256]{2,1,0:T(8,128)(2,1)S(1)}, u32[]{:S(2)}, u32[]{:S(2)}) async-start(bf16[8,144,256]{2,1,0:T(8,128)(2,1)} %pack.1), calls=%async_computation | async-start | bytes 1179648 | tf_op jit(solution)/shard_map/all_to_all | solution.py:30
  10.8 13.7 %collective-permute-start.1 = (bf16[128,1024]{1,0:T(8,128)(2,1)}, bf16[128,1024]{1,0:T(8,128)(2,1)S(1)}, u32[]{:S(2)}, u32[]{:S(2)}) collective-permute-start(bf16[128,1024]{1,0:T(8,128)(2,1)} %q_ref.1), channel_id=1, source_target_pairs={{0,1},{1,0},{2,3},{3,2},{4,5},{5,4},{6,7},{7,6},{8,9},{9,8},{10,11... | collective-permute-start | bytes 786440 | tf_op jit(solution)/shard_map/ppermute | solution.py:24
  12.1 12.4 %collective-permute-start.2 = (bf16[128,1024]{1,0:T(8,128)(2,1)}, bf16[128,1024]{1,0:T(8,128)(2,1)S(1)}, u32[]{:S(2)}, u32[]{:S(2)}) collective-permute-start(bf16[128,1024]{1,0:T(8,128)(2,1)} %do_ref.1), channel_id=1, source_target_pairs={{0,1},{1,0},{2,3},{3,2},{4,5},{5,4},{6,7},{7,6},{8,9},{9,8},{10,11... | collective-permute-start | bytes 786440 | tf_op jit(solution)/shard_map/ppermute | solution.py:24
  12.8 11.6 %collective-permute-start = (s32[128]{0:T(128)}, s32[128]{0:T(128)S(1)}, u32[]{:S(2)}, u32[]{:S(2)}) collective-permute-start(s32[128]{0:T(128)} %position_ref.3), channel_id=1, source_target_pairs={{0,1},{1,0},{2,3},{3,2},{4,5},{5,4},{6,7},{7,6},{8,9},{9,8},{10,11... | collective-permute-start | bytes 1544 | tf_op jit(solution)/shard_map/ppermute | solution.py:24
  24.5 0.7 copy-start
  25.1 0.9 %copy-start.1 = (bf16[128,1024]{1,0:T(8,128)(2,1)S(1)}, bf16[128,1024]{1,0:T(8,128)(2,1)}, u32[]{:S(2)}) copy-start(bf16[128,1024]{1,0:T(8,128)(2,1)} %q_ref.1) | copy-start | bytes 786436
  26.1 0.9 %copy-start.2 = (bf16[128,1024]{1,0:T(8,128)(2,1)S(1)}, bf16[128,1024]{1,0:T(8,128)(2,1)}, u32[]{:S(2)}) copy-start(bf16[128,1024]{1,0:T(8,128)(2,1)} %do_ref.1) | copy-start | bytes 786436
  29.7 14.9 %collective-permute-start.3 = (bf16[8,144,256]{2,1,0:T(8,128)(2,1)S(1)}, bf16[8,144,256]{2,1,0:T(8,128)(2,1)S(1)}, u32[]{:S(2)}, u32[]{:S(2)}) collective-permute-start(bf16[8,144,256]{2,1,0:T(8,128)(2,1)S(1)} %all-to-all-done.kv_ref), channel_id=1, source_target_pairs={{0,16},{16,32},{32,48},{48,64},{64,80},{80,96},{96,112},{112,128},... | collective-permute-start | bytes 1769480 | tf_op jit(solution)/shard_map/ppermute | solution.py:20
  46.6 9.3 %collective-permute-start.5 = (bf16[2,128,512]{2,1,0:T(8,128)(2,1)S(1)}, bf16[2,128,512]{2,1,0:T(8,128)(2,1)S(1)}, u32[]{:S(2)}, u32[]{:S(2)}) collective-permute-start(bf16[2,128,512]{2,1,0:T(8,128)(2,1)S(1)} %get-tuple-element.57), channel_id=1, source_target_pairs={{0,1},{1,0},{2,3},{3,2},{4,5},{5,4},{6,7},{7,6},{8,9},{9,8},{10,11... | collective-permute-start | bytes 786440 | tf_op jit(solution)/shard_map/ppermute | solution.py:24
  48.0 5.2 %collective-permute-start.4 = (f32[3,2,1,512]{3,2,1,0:T(1,128)S(1)}, f32[3,2,1,512]{3,2,1,0:T(1,128)S(1)}, u32[]{:S(2)}, u32[]{:S(2)}) collective-permute-start(f32[3,2,1,512]{3,2,1,0:T(1,128)S(1)} %get-tuple-element.55.stats_ref), channel_id=1, source_target_pairs={{0,1},{1,0},{2,3},{3,2},{4,5},{5,4},{6,7},{7,6},{8,9},{9,8},{10,11... | collective-permute-start | bytes 36872 | tf_op jit(solution)/shard_map/ppermute | solution.py:24
  50.8 5.2 %collective-permute-start.6 = (f32[3,2,1,512]{3,2,1,0:T(1,128)S(1)}, f32[3,2,1,512]{3,2,1,0:T(1,128)S(1)}, u32[]{:S(2)}, u32[]{:S(2)}) collective-permute-start(f32[3,2,1,512]{3,2,1,0:T(1,128)S(1)} %get-tuple-element.54.stats_ref), channel_id=1, source_target_pairs={{0,1},{1,0},{2,3},{3,2},{4,5},{5,4},{6,7},{7,6},{8,9},{9,8},{10,11... | collective-permute-start | bytes 36872 | tf_op jit(solution)/shard_map/ppermute | solution.py:24
  59.0 9.7 %collective-permute-start.8 = (bf16[8,128,256]{2,1,0:T(8,128)(2,1)S(1)}, bf16[8,128,256]{2,1,0:T(8,128)(2,1)S(1)}, u32[]{:S(2)}, u32[]{:S(2)}) collective-permute-start(bf16[8,128,256]{2,1,0:T(8,128)(2,1)S(1)} %get-tuple-element.77), channel_id=1, source_target_pairs={{16,0},{32,16},{48,32},{64,48},{80,64},{96,80},{112,96},{128,112},... | collective-permute-start | bytes 1572872 | tf_op jit(solution)/shard_map/ppermute | solution.py:20
  69.6 21.3 %all-to-all-start.1 = ((bf16[8,128,256]{2,1,0:T(8,128)(2,1)}), bf16[8,128,256]{2,1,0:T(8,128)(2,1)S(1)}, u32[]{:S(2)}, u32[]{:S(2)}) async-start(bf16[8,128,256]{2,1,0:T(8,128)(2,1)} %add_convert_fusion), calls=%async_computation.1 | async-start | bytes 1048576 | tf_op jit(solution)/shard_map/all_to_all | solution.py:30
  75.1 6.4 %collective-permute-start.7 = (bf16[128,1024]{1,0:T(8,128)(2,1)S(1)}, bf16[128,1024]{1,0:T(8,128)(2,1)S(1)}, u32[]{:S(2)}, u32[]{:S(2)}) collective-permute-start(bf16[128,1024]{1,0:T(8,128)(2,1)S(1)} %get-tuple-element.75), channel_id=1, source_target_pairs={{0,1},{1,0},{2,3},{3,2},{4,5},{5,4},{6,7},{7,6},{8,9},{9,8},{10,11... | collective-permute-start | bytes 786440 | tf_op jit(solution)/shard_map/ppermute | solution.py:24

commit v7 on v6

--- a/solution.py
+++ b/solution.py
@@ -59,20 +59,19 @@
 
 
 def pack(position_ref, key_ref, value_ref, packed_ref, place_ref, block_ref, in_sems, out_sems):
-    count, rows, both = packed_ref.shape
+    count, rows, head_dim = packed_ref.shape
     span = key_ref.shape[0]
     loads = [
         pltpu.make_async_copy(position_ref, place_ref, in_sems.at[0]),
-        pltpu.make_async_copy(key_ref, block_ref.at[pl.ds(0, span), pl.ds(0, both // 2)], in_sems.at[1]),
-        pltpu.make_async_copy(
-            value_ref, block_ref.at[pl.ds(0, span), pl.ds(both // 2, both // 2)], in_sems.at[2]
-        ),
+        pltpu.make_async_copy(key_ref, block_ref.at[pl.ds(0, span)], in_sems.at[1]),
+        pltpu.make_async_copy(value_ref, block_ref.at[pl.ds(span, span)], in_sems.at[2]),
     ]
     for load in loads:
         load.start()
     loads[0].wait()
     tag = (lax.rem(place_ref[0], 2 * count * span) // block_rows).astype(jnp.float32)
-    block_ref[span:, :] = jnp.full((rows - span, both), tag, jnp.float32).astype(packed_ref.dtype)
+    tag = jnp.full((rows - 2 * span, head_dim), tag, jnp.float32)
+    block_ref[2 * span :, :] = tag.astype(packed_ref.dtype)
     loads[1].wait()
     loads[2].wait()
     stores = [
@@ -120,14 +119,13 @@
     block_ref, qs_ref, kv_ref,
     ks_ref, vs_ref, slots_ref, allowed_ref, p_ref, m_ref, l_ref, o_ref, s_ref,
 ):
-    group, _, both = kv_ref.shape
-    head_dim = both // 2
+    group, _, head_dim = kv_ref.shape
     span = 2 * block_rows
     steps, _, width = p_ref.shape
     blocks = 2 * group
     tiles = blocks * block_rows // tile_keys
     exponent_scale = log2_e * float(head_dim) ** (-0.5)
-    tags = [jnp.max(kv_ref[g, span:, :].astype(jnp.float32)).astype(jnp.int32) for g in range(group)]
+    tags = [jnp.max(kv_ref[g, 2 * span :, :].astype(jnp.float32)).astype(jnp.int32) for g in range(group)]
 
     def count(test):
         return sum(jnp.where(test(tag), 1, 0) for tag in tags)
@@ -142,8 +140,9 @@
         for half, place in ((0, slot), (1, blocks - 1 - slot)):
             target = pl.ds(pl.multiple_of(place * block_rows, block_rows), block_rows)
             rows = slice(half * block_rows, (half + 1) * block_rows)
-            ks_ref[target, :] = kv_ref[g, rows, :head_dim]
-            vs_ref[target, :] = kv_ref[g, rows, head_dim:]
+            ks_ref[target, :] = kv_ref[g, rows, :]
+            rows = slice(span + half * block_rows, span + (half + 1) * block_rows)
+            vs_ref[target, :] = kv_ref[g, rows, :]
     m_ref[...] = jnp.full(m_ref.shape, masked_score, jnp.float32)
     l_ref[...] = jnp.zeros(l_ref.shape, jnp.float32)
     o_ref[...] = jnp.zeros(o_ref.shape, jnp.float32)
@@ -168,10 +167,12 @@
         o_ref[at] += dot_tn(vs_ref[pl.ds(start, tile_keys), :], raised)
 
 
-def key_tile(ref, tile, columns):
-    per_tile = tile_keys // (2 * block_rows)
+def key_tile(ref, tile, part):
+    span = 2 * block_rows
+    per_tile = tile_keys // span
     return jnp.concatenate(
-        [ref[tile * per_tile + j, : 2 * block_rows, columns] for j in range(per_tile)], axis=0
+        [ref[tile * per_tile + j, part * span : (part + 1) * span, :] for j in range(per_tile)],
+        axis=0,
     )
 
 
@@ -186,7 +187,7 @@
     for at in range(sets):
         peak = jnp.full((1, width), masked_score, jnp.float32)
         for tile in range(tiles):
-            scores = dot_nt(key_tile(kv_ref, tile, slice(0, head_dim)), qs_ref[first + at])
+            scores = dot_nt(key_tile(kv_ref, tile, 0), qs_ref[first + at])
             s_ref[at, tile] = scores
             peak = jnp.maximum(peak, jnp.max(scores, axis=0, keepdims=True))
         m_prev_ref[at] = peak
@@ -199,7 +200,7 @@
             total += jnp.sum(raised, axis=0, keepdims=True)
             raised = raised.astype(jnp.bfloat16)
             p_ref[at, tile] = raised
-            out += dot_tn(key_tile(kv_ref, tile, slice(head_dim, 2 * head_dim)), raised)
+            out += dot_tn(key_tile(kv_ref, tile, 1), raised)
         peak = jnp.where(has_prev, peak, masked_score)
         m_prev_ref[at] = peak
         top = jnp.maximum(peak, m_own_ref[first + at])
@@ -220,9 +221,9 @@
 
 def prev_backward(first, has_ref, qs_ref, dot_ref, kv_ref, p_ref, m_own_ref, m_prev_ref, stats_ref, other_ref, *rest):
     if first == 0:
-        terms_ref, dos_ref, shift_ref, dqt_ref, factor_ref, scaled_ref, lower_ref = rest
+        terms_ref, dos_ref, shift_ref, ds_ref, factor_ref, scaled_ref, lower_ref = rest
     else:
-        before_ref, terms_ref, dos_ref, shift_ref, dqt_ref, scaled_ref, lower_ref = rest
+        before_ref, terms_ref, dos_ref, shift_ref, ds_ref, scaled_ref, lower_ref = rest
     _, width, head_dim = qs_ref.shape
     sets, tiles = p_ref.shape[:2]
     span = 2 * block_rows
@@ -248,8 +249,7 @@
         scaled_ref[at] = (grad * prev_factor).astype(jnp.bfloat16)
         lower_ref[at] = delta * prev_factor
     for tile in range(tiles):
-        keys = key_tile(kv_ref, tile, slice(0, head_dim))
-        values = key_tile(kv_ref, tile, slice(head_dim, 2 * head_dim))
+        values = key_tile(kv_ref, tile, 1)
         key_grad = jnp.zeros((tile_keys, head_dim), jnp.float32)
         value_grad = jnp.zeros((tile_keys, head_dim), jnp.float32)
         for at in range(sets):
@@ -258,8 +258,7 @@
             change = dot_nn(values, scaled_ref[at]) - lower_ref[at]
             change = (weights.astype(jnp.float32) * change).astype(jnp.bfloat16)
             key_grad += dot_nn(change, qs_ref[first + at])
-            dqt = dot_tn(keys, change)
-            dqt_ref[at] = dqt if tile == 0 else dqt_ref[at] + dqt
+            ds_ref[at, tile] = change
         key_grad = key_grad * scale
         if first == 0:
             rows = slice(tile * tile_keys, (tile + 1) * tile_keys)
@@ -277,7 +276,7 @@
 
 def own_backward(
     allowed_ref, slots_ref, qs_ref, ks_ref, vs_ref, p_ref,
-    dos_mine_ref, shift_mine_ref, dqt_mine_ref, dos_theirs_ref, shift_theirs_ref, dqt_theirs_ref,
+    dos_mine_ref, shift_mine_ref, ds_mine_ref, dos_theirs_ref, shift_theirs_ref, ds_theirs_ref, kv_ref,
     dq_ref, dq_partner_ref, terms_ref, acc_ref, dqa_ref,
 ):
     steps, _, width = p_ref.shape
@@ -288,8 +287,11 @@
     scale = float(head_dim) ** (-0.5)
 
     acc_ref[...] = jnp.zeros(acc_ref.shape, jnp.float32)
-    dqa_ref[:2] = dqt_mine_ref[...]
-    dqa_ref[2:] = dqt_theirs_ref[...]
+    for at in range(4):
+        changes = (ds_mine_ref, ds_theirs_ref)[at // 2]
+        dqa_ref[at] = sum(
+            dot_tn(key_tile(kv_ref, tile, 0), changes[at % 2, tile]) for tile in range(tiles)
+        )
     for step in range(steps):
         at, tile = own_tile(step, allowed_ref)
         start = pl.multiple_of(jnp.minimum(tile, tiles - 1) * tile_keys, tile_keys)
@@ -360,12 +362,12 @@
     packed = pl.pallas_call(
         pack,
         name="pack",
-        out_shape=jax.ShapeDtypeStruct((group, tok_rows + tag_rows, 2 * head_dim), bf16),
+        out_shape=jax.ShapeDtypeStruct((group, 2 * tok_rows + tag_rows, head_dim), bf16),
         in_specs=[anywhere] * 3,
         out_specs=anywhere,
         scratch_shapes=[
             pltpu.SMEM(positions.shape, jnp.int32),
-            pltpu.VMEM((tok_rows + tag_rows, 2 * head_dim), bf16),
+            pltpu.VMEM((2 * tok_rows + tag_rows, head_dim), bf16),
             pltpu.SemaphoreType.DMA((3,)),
             pltpu.SemaphoreType.DMA((group,)),
         ],
@@ -413,6 +415,7 @@
     )(both_blocks, qs, group_kv)
     half_stat = ((2, 1, width), f32)
     half_query = ((2, head_dim, width), f32)
+    changes = ((2, tiles, tile_keys, width), bf16)
     half_query_16 = ((2, head_dim, width), bf16)
 
     def forward(first, name):
@@ -435,19 +438,18 @@
     got = to_partner(sent, "inner")
     p_mine, m_mine, stats_mine, out = forward(0, "prev_forward_mine")
     other_theirs = to_partner(stats_mine, "inner")
-    first_terms, dos_mine, shift_mine, dqt_mine, factor = call(
+    first_terms, dos_mine, shift_mine, ds_mine, factor = call(
         functools.partial(prev_backward, 0),
         "prev_backward_mine",
-        [((span_rows, 2 * head_dim), f32), half_query_16, half_stat, half_query, ((2, 2, 1, width), f32)],
+        [((span_rows, 2 * head_dim), f32), half_query_16, half_stat, changes, ((2, 2, 1, width), f32)],
         (0,),
         [half_query_16, half_stat],
         flops=4 * 2 * tiles * unit,
     )(has_prev, qs, dot, prev_kv, p_mine, m_own, m_mine, stats_mine, other_mine)
-    first_terms, got = lax.optimization_barrier((first_terms, got))
-    prev_terms, dos_theirs, shift_theirs, dqt_theirs = call(
+    prev_terms, dos_theirs, shift_theirs, ds_theirs = call(
         functools.partial(prev_backward, 2),
         "prev_backward_theirs",
-        [terms_shape, half_query_16, half_stat, half_query],
+        [terms_shape, half_query_16, half_stat, changes],
         (0,),
         [half_query_16, half_stat],
         flops=4 * 2 * tiles * unit,
@@ -460,7 +462,7 @@
         (0, 1),
         [((span_rows, 2 * head_dim), f32), by_query],
         flops=4 * steps * unit,
-    )(allowed, slots, qs, ks, vs, p_own, dos_mine, shift_mine, dqt_mine, dos_theirs, shift_theirs, dqt_theirs)
+    )(allowed, slots, qs, ks, vs, p_own, dos_mine, shift_mine, ds_mine, dos_theirs, shift_theirs, ds_theirs, prev_kv)
     (attended,) = call(merge_attended, "merge_attended", [tokens], (), [])(out, got, factor)
     dq_other = to_partner(dq_partner, "inner")
     terms = (own_terms.astype(f32) + returned.astype(f32)).astype(bf16)

time: 93.2 us -> 88.2 us (0.946); the launches traced: 91.7 us -> 87.7 us
  waiting for transfers between devices: 38.2 us -> 35.4 us
  Pallas kernels: 21.5 us -> 20.4 us
    all_to_all x2, waiting for transfers between devices: 10.2 us -> 4.1 us  [exchange(): lax.all_to_all(parts, axis, 0, 0, axis_index_groups=groups, tiled=True)]
    ppermute x7, waiting for transfers between devices: 16.4 us -> 20.7 us  [to_partner(): lax.ppermute(block, axis, [(i, i ^ 1) for i in range(lax.axis_size(axis))])]
    pallas_call x8, Pallas kernels: 19.8 us -> 18.7 us  [run(): pl.pallas_call(kernel, name=name, grid=(1,) if stream else (), out_shape=...]
    ppermute x2, starting transfers between devices: 4.92 us -> 3.83 us  [from_behind(): return lax.ppermute(block, axis, route)]
    ppermute x2, waiting for transfers between devices: 11.6 us -> 10.7 us  [from_behind(): return lax.ppermute(block, axis, route)]
  transfers between devices with their start and end apart: 11 -> 11, of which waited for: 7 -> 8; matrix products, arithmetic and copies ran while one was open for 1% -> 1% of each run, Pallas kernels for 16% -> 17%
where the time goes in v7:
time: 88.2 us; the launch traced here: 87.7 us
  waiting for transfers between devices  35.4 us (40%)
  starting transfers between devices  26.2 us (30%)
  Pallas kernels  20.4 us (23%)
  local copies, waits for them, and re-layouts  3.18 us (4%)
  other arithmetic  1.8 us (2%)
    ppermute x7, waiting for transfers between devices, to_partner(): lax.ppermute(block, axis, [(i, i ^ 1) for i in range(lax.axis_size(axis))])  20.7 us
    pallas_call x8, Pallas kernels, run(): pl.pallas_call(kernel, name=name, grid=(1,) if stream else (), out_shape=...  18.7 us
    all_to_all x2, starting transfers between devices, exchange(): lax.all_to_all(parts, axis, 0, 0, axis_index_groups=groups, tiled=True)  14.7 us
    ppermute x2, waiting for transfers between devices, from_behind(): return lax.ppermute(block, axis, route)  10.7 us
    ppermute x7, starting transfers between devices, to_partner(): lax.ppermute(block, axis, [(i, i ^ 1) for i in range(lax.axis_size(axis))])  7.71 us
    all_to_all x2, waiting for transfers between devices, exchange(): lax.all_to_all(parts, axis, 0, 0, axis_index_groups=groups, tiled=True)  4.1 us
    ppermute x2, starting transfers between devices, from_behind(): return lax.ppermute(block, axis, route)  3.83 us
    unnamed x6, local copies, waits for them, and re-layouts  2.55 us
  transfers between devices with their start and end apart: 11, of which 8 were waited for; matrix products, arithmetic and copies ran while one was open for 1% of the time, Pallas kernels for 17%

profile of v7, /device:TPU:16, one launch (start us, length us, event | category | flops | bytes accessed | tf_op | source)
XLA Modules:
  0.0 87.7 jit_solution(10326788558032882738)
XLA Ops:
  0.6 1.7 %pack.1 = bf16[8,272,128]{2,1,0:T(8,128)(2,1)} custom-call(s32[128]{0:T(128)} %position_ref.3, bf16[128,128]{1,0:T(8,128)(2,1)} %key_ref.1, bf16[128,128]{1,0:T(8,128)(2,1)} %value_ref.1), custom_call_target="tpu_custom_call" | custom-call | tf_op jit(solution)/shard_map/pack/pallas_call | solution.py:362
  2.3 8.5 %all-to-all-start = ((bf16[8,272,128]{2,1,0:T(8,128)(2,1)}), bf16[8,272,128]{2,1,0:T(8,128)(2,1)S(1)}, u32[]{:S(2)}, u32[]{:S(2)}) async-start(bf16[8,272,128]{2,1,0:T(8,128)(2,1)} %pack.1), calls=%async_computation | async-start | bytes 1114112 | tf_op jit(solution)/shard_map/all_to_all | solution.py:30
  10.8 1.3 %collective-permute-start.1 = (bf16[128,1024]{1,0:T(8,128)(2,1)}, bf16[128,1024]{1,0:T(8,128)(2,1)S(1)}, u32[]{:S(2)}, u32[]{:S(2)}) collective-permute-start(bf16[128,1024]{1,0:T(8,128)(2,1)} %q_ref.1), channel_id=1, source_target_pairs={{0,1},{1,0},{2,3},{3,2},{4,5},{5,4},{6,7},{7,6},{8,9},{9,8},{10,11... | collective-permute-start | bytes 786440 | tf_op jit(solution)/shard_map/ppermute | solution.py:24
  12.8 1.3 %collective-permute-start = (s32[128]{0:T(128)}, s32[128]{0:T(128)S(1)}, u32[]{:S(2)}, u32[]{:S(2)}) collective-permute-start(s32[128]{0:T(128)} %position_ref.3), channel_id=1, source_target_pairs={{0,1},{1,0},{2,3},{3,2},{4,5},{5,4},{6,7},{7,6},{8,9},{9,8},{10,11... | collective-permute-start | bytes 1544 | tf_op jit(solution)/shard_map/ppermute | solution.py:24
  14.1 10.4 %collective-permute-done.position_partner_ref = s32[128]{0:T(128)S(1)} collective-permute-done((s32[128]{0:T(128)}, s32[128]{0:T(128)S(1)}, u32[]{:S(2)}, u32[]{:S(2)}) %collective-permute-start) | collective-permute-done | bytes 544 | tf_op jit(solution)/shard_map/ppermute | solution.py:24
  27.0 1.2 %stack_pair.1 = (s32[2]{0:T(128)S(1)}, bf16[4,512,128]{2,1,0:T(8,128)(2,1)S(1)}, bf16[4,128,512]{2,1,0:T(8,128)(2,1)S(1)}) custom-call(s32[128]{0:T(128)S(1)} %copy-done, s32[128]{0:T(128)S(1)} %collective-permute-done.position_partner_ref, bf16[128,1024]{1,0:T(8,128)(2,1)S(1)} %copy-done.1, bf16[128,1024]{1,0:T(8,128)(2,1)S(1)} %collective-permute-done.1.q_partner_ref, ...), custom_call_target="tpu_custom_call" | custom-call | flops 4000000000 | bytes 4194304 | tf_op jit(solution)/shard_map/stack_pair/pallas_call | solution.py:333
  29.0 1.9 %collective-permute-start.3 = (bf16[8,272,128]{2,1,0:T(8,128)(2,1)S(1)}, bf16[8,272,128]{2,1,0:T(8,128)(2,1)S(1)}, u32[]{:S(2)}, u32[]{:S(2)}) collective-permute-start(bf16[8,272,128]{2,1,0:T(8,128)(2,1)S(1)} %all-to-all-done.kv_ref), channel_id=1, source_target_pairs={{0,16},{16,32},{32,48},{48,64},{64,80},{80,96},{96,112},{112,128},... | collective-permute-start | bytes 1671176 | tf_op jit(solution)/shard_map/ppermute | solution.py:20
  30.9 3.9 %own_forward.1 = (bf16[1024,128]{1,0:T(8,128)(2,1)S(1)}, bf16[1024,128]{1,0:T(8,128)(2,1)S(1)}, s32[8]{0:T(128)S(1)}, s32[4]{0:T(128)S(1)}, bf16[10,256,512]{2,1...) custom-call(s32[2]{0:T(128)S(1)} %get-tuple-element.45.block_ref, ...), custom_call_target="tpu_custom_call" | custom-call | flops 671088640 | bytes 4194304 | tf_op jit(solution)/shard_map/own_forward/pallas_call | solution.py:333
  34.8 8.8 %collective-permute-done.3.kv_ref = bf16[8,272,128]{2,1,0:T(8,128)(2,1)S(1)} collective-permute-done((bf16[8,272,128]{2,1,0:T(8,128)(2,1)S(1)}, bf16[8,272,128]{2,1,0:T(8,128)(2,1)S(1)}, u32[]{:S(2)}, u32[]{:S(2)}) %collective-permute-start.3) | collective-permute-done | bytes 557088 | tf_op jit(solution)/shard_map/ppermute | solution.py:20
  43.6 2.0 %prev_forward_theirs.1 = (bf16[2,4,256,512]{3,2,1,0:T(8,128)(2,1)S(1)}, f32[2,1,512]{2,1,0:T(1,128)S(1)}, f32[3,2,1,512]{3,2,1,0:T(1,128)S(1)}, bf16[2,128,512]{2,1,0:T(8,128)(2,1)S(1)}) custom-call(s32[1]{0:T(128)} %bitcast.has_ref, bf16[4,512,128]{2,1,0:T(8,128)(2,1)S(1)} %get-tuple-element.42.qs_ref, bf16[4,128,512]{2,1,0:T(8,128)(2,1)S(1)} %get-tuple-element.43.dot_ref, ...), custom_call_target="tpu_custom_call" | custom-call | flops 536870912 | bytes 4194304 | tf_op jit(solution)/shard_map/prev_forward_theirs/pallas_call | solution.py:333
  45.5 1.4 %collective-permute-start.5 = (f32[3,2,1,512]{3,2,1,0:T(1,128)S(1)}, f32[3,2,1,512]{3,2,1,0:T(1,128)S(1)}, u32[]{:S(2)}, u32[]{:S(2)}) collective-permute-start(f32[3,2,1,512]{3,2,1,0:T(1,128)S(1)} %get-tuple-element.54.stats_ref), channel_id=1, source_target_pairs={{0,1},{1,0},{2,3},{3,2},{4,5},{5,4},{6,7},{7,6},{8,9},{9,8},{10,11... | collective-permute-start | bytes 36872 | tf_op jit(solution)/shard_map/ppermute | solution.py:24
  46.9 1.9 %prev_forward_mine.1 = (bf16[2,4,256,512]{3,2,1,0:T(8,128)(2,1)S(1)}, f32[2,1,512]{2,1,0:T(1,128)S(1)}, f32[3,2,1,512]{3,2,1,0:T(1,128)S(1)}, f32[2,128,512]{2,1,0:T(8,128)S(1)}) custom-call(s32[1]{0:T(128)} %bitcast.has_ref, bf16[4,512,128]{2,1,0:T(8,128)(2,1)S(1)} %get-tuple-element.42.qs_ref, bf16[4,128,512]{2,1,0:T(8,128)(2,1)S(1)} %get-tuple-element.43.dot_ref, ...), custom_call_target="tpu_custom_call" | custom-call | flops 536870912 | bytes 4194304 | tf_op jit(solution)/shard_map/prev_forward_mine/pallas_call | solution.py:333
  48.8 1.0 %collective-permute-start.6 = (f32[3,2,1,512]{3,2,1,0:T(1,128)S(1)}, f32[3,2,1,512]{3,2,1,0:T(1,128)S(1)}, u32[]{:S(2)}, u32[]{:S(2)}) collective-permute-start(f32[3,2,1,512]{3,2,1,0:T(1,128)S(1)} %get-tuple-element.53.stats_ref), channel_id=1, source_target_pairs={{0,1},{1,0},{2,3},{3,2},{4,5},{5,4},{6,7},{7,6},{8,9},{9,8},{10,11... | collective-permute-start | bytes 36872 | tf_op jit(solution)/shard_map/ppermute | solution.py:24
  49.8 1.9 %prev_backward_mine.1 = (f32[1024,256]{1,0:T(8,128)S(1)}, bf16[2,128,512]{2,1,0:T(8,128)(2,1)S(1)}, f32[2,1,512]{2,1,0:T(1,128)S(1)}, bf16[2,4,256,512]{3,2,1,0:T(8,128)(2,1)S(1)}, f32[2,2,1,512]{3,2,1,0:T(1,128)S(1)}) custom-call(s32[1]{0:T(128)} %bitcast.has_ref, bf16[4,512,128]{2,1,0:T(8,128)(2,1)S(1)} %get-tuple-element.42.qs_ref, ...), custom_call_target="tpu_custom_call" | custom-call | flops 1073741824 | bytes 4194304 | tf_op jit(solution)/shard_map/prev_backward_mine/pallas_call | solution.py:333
  51.8 1.0 %collective-permute-done.6.other_ref = f32[3,2,1,512]{3,2,1,0:T(1,128)S(1)} collective-permute-done((f32[3,2,1,512]{3,2,1,0:T(1,128)S(1)}, f32[3,2,1,512]{3,2,1,0:T(1,128)S(1)}, u32[]{:S(2)}, u32[]{:S(2)}) %collective-permute-start.6) | collective-permute-done | bytes 12320 | tf_op jit(solution)/shard_map/ppermute | solution.py:24
  52.8 2.2 %prev_backward_theirs.1 = (bf16[8,128,256]{2,1,0:T(8,128)(2,1)S(1)}, bf16[2,128,512]{2,1,0:T(8,128)(2,1)S(1)}, f32[2,1,512]{2,1,0:T(1,128)S(1)}, bf16[2,4,256,512]{3,2,1,0:T(8,128)(2,1)S(1)}) custom-call(s32[1]{0:T(128)} %bitcast.has_ref, bf16[4,512,128]{2,1,0:T(8,128)(2,1)S(1)} %get-tuple-element.42.qs_ref, ...), custom_call_target="tpu_custom_call" | custom-call | flops 1073741824 | bytes 4194304 | tf_op jit(solution)/shard_map/prev_backward_theirs/pallas_call | solution.py:333
  55.0 1.9 %collective-permute-start.8 = (bf16[8,128,256]{2,1,0:T(8,128)(2,1)S(1)}, bf16[8,128,256]{2,1,0:T(8,128)(2,1)S(1)}, u32[]{:S(2)}, u32[]{:S(2)}) collective-permute-start(bf16[8,128,256]{2,1,0:T(8,128)(2,1)S(1)} %get-tuple-element.73), channel_id=1, source_target_pairs={{16,0},{32,16},{48,32},{64,48},{80,64},{96,80},{112,96},{128,112},... | collective-permute-start | bytes 1572872 | tf_op jit(solution)/shard_map/ppermute | solution.py:20
  57.0 4.8 %own_backward.1 = (f32[128,1024]{1,0:T(8,128)S(1)}, bf16[128,1024]{1,0:T(8,128)(2,1)S(1)}, bf16[8,128,256]{2,1,0:T(8,128)(2,1)S(1)}) custom-call(s32[4]{0:T(128)S(1)} %get-tuple-element.56.allowed_ref, s32[8]{0:T(128)S(1)} %get-tuple-element.57.slots_ref, bf16[4,512,128]{2,1,0:T(8,128)(2,1)S(1)} %get-tuple-element.42.qs_ref, ...), custom_call_target="tpu_custom_call" | custom-call | flops 1342177280 | bytes 4194304 | tf_op jit(solution)/shard_map/own_backward/pallas_call | solution.py:333
  61.7 1.9 %collective-permute-done.8 = bf16[8,128,256]{2,1,0:T(8,128)(2,1)S(1)} collective-permute-done((bf16[8,128,256]{2,1,0:T(8,128)(2,1)S(1)}, bf16[8,128,256]{2,1,0:T(8,128)(2,1)S(1)}, u32[]{:S(2)}, u32[]{:S(2)}) %collective-permute-start.8) | collective-permute-done | bytes 524320 | tf_op jit(solution)/shard_map/ppermute | solution.py:20
  64.6 6.2 %all-to-all-start.1 = ((bf16[8,128,256]{2,1,0:T(8,128)(2,1)}), bf16[8,128,256]{2,1,0:T(8,128)(2,1)S(1)}, u32[]{:S(2)}, u32[]{:S(2)}) async-start(bf16[8,128,256]{2,1,0:T(8,128)(2,1)} %add_convert_fusion), calls=%async_computation.1 | async-start | bytes 1048576 | tf_op jit(solution)/shard_map/all_to_all | solution.py:30
  71.5 1.3 %collective-permute-start.7 = (bf16[128,1024]{1,0:T(8,128)(2,1)S(1)}, bf16[128,1024]{1,0:T(8,128)(2,1)S(1)}, u32[]{:S(2)}, u32[]{:S(2)}) collective-permute-start(bf16[128,1024]{1,0:T(8,128)(2,1)S(1)} %get-tuple-element.71), channel_id=1, source_target_pairs={{0,1},{1,0},{2,3},{3,2},{4,5},{5,4},{6,7},{7,6},{8,9},{9,8},{10,11... | collective-permute-start | bytes 786440 | tf_op jit(solution)/shard_map/ppermute | solution.py:24
  72.8 7.2 %collective-permute-done.4.got_ref = bf16[2,128,512]{2,1,0:T(8,128)(2,1)S(1)} collective-permute-done((bf16[2,128,512]{2,1,0:T(8,128)(2,1)S(1)}, bf16[2,128,512]{2,1,0:T(8,128)(2,1)S(1)}, u32[]{:S(2)}, u32[]{:S(2)}) %collective-permute-start.4) | collective-permute-done | bytes 262176 | tf_op jit(solution)/shard_map/ppermute | solution.py:24
  80.9 2.0 %collective-permute-done.7 = bf16[128,1024]{1,0:T(8,128)(2,1)S(1)} collective-permute-done((bf16[128,1024]{1,0:T(8,128)(2,1)S(1)}, bf16[128,1024]{1,0:T(8,128)(2,1)S(1)}, u32[]{:S(2)}, u32[]{:S(2)}) %collective-permute-start.7) | collective-permute-done | bytes 262176 | tf_op jit(solution)/shard_map/ppermute | solution.py:24
  83.7 3.3 %all-to-all-done.1 = bf16[8,128,256]{2,1,0:T(8,128)(2,1)S(1)} async-done(((bf16[8,128,256]{2,1,0:T(8,128)(2,1)}), bf16[8,128,256]{2,1,0:T(8,128)(2,1)S(1)}, u32[]{:S(2)}, u32[]{:S(2)}) %all-to-all-start.1) | async-done | bytes 524320 | tf_op jit(solution)/shard_map/all_to_all | solution.py:30
  (17 shorter events, 8.1 us)
Async XLA Ops:
  2.3 26.7 %all-to-all-start = ((bf16[8,272,128]{2,1,0:T(8,128)(2,1)}), bf16[8,272,128]{2,1,0:T(8,128)(2,1)S(1)}, u32[]{:S(2)}, u32[]{:S(2)}) async-start(bf16[8,272,128]{2,1,0:T(8,128)(2,1)} %pack.1), calls=%async_computation | async-start | bytes 1114112 | tf_op jit(solution)/shard_map/all_to_all | solution.py:30
  10.8 13.7 %collective-permute-start.1 = (bf16[128,1024]{1,0:T(8,128)(2,1)}, bf16[128,1024]{1,0:T(8,128)(2,1)S(1)}, u32[]{:S(2)}, u32[]{:S(2)}) collective-permute-start(bf16[128,1024]{1,0:T(8,128)(2,1)} %q_ref.1), channel_id=1, source_target_pairs={{0,1},{1,0},{2,3},{3,2},{4,5},{5,4},{6,7},{7,6},{8,9},{9,8},{10,11... | collective-permute-start | bytes 786440 | tf_op jit(solution)/shard_map/ppermute | solution.py:24
  12.1 12.4 %collective-permute-start.2 = (bf16[128,1024]{1,0:T(8,128)(2,1)}, bf16[128,1024]{1,0:T(8,128)(2,1)S(1)}, u32[]{:S(2)}, u32[]{:S(2)}) collective-permute-start(bf16[128,1024]{1,0:T(8,128)(2,1)} %do_ref.1), channel_id=1, source_target_pairs={{0,1},{1,0},{2,3},{3,2},{4,5},{5,4},{6,7},{7,6},{8,9},{9,8},{10,11... | collective-permute-start | bytes 786440 | tf_op jit(solution)/shard_map/ppermute | solution.py:24
  12.8 11.6 %collective-permute-start = (s32[128]{0:T(128)}, s32[128]{0:T(128)S(1)}, u32[]{:S(2)}, u32[]{:S(2)}) collective-permute-start(s32[128]{0:T(128)} %position_ref.3), channel_id=1, source_target_pairs={{0,1},{1,0},{2,3},{3,2},{4,5},{5,4},{6,7},{7,6},{8,9},{9,8},{10,11... | collective-permute-start | bytes 1544 | tf_op jit(solution)/shard_map/ppermute | solution.py:24
  24.5 0.7 copy-start
  25.1 0.9 %copy-start.1 = (bf16[128,1024]{1,0:T(8,128)(2,1)S(1)}, bf16[128,1024]{1,0:T(8,128)(2,1)}, u32[]{:S(2)}) copy-start(bf16[128,1024]{1,0:T(8,128)(2,1)} %q_ref.1) | copy-start | bytes 786436
  26.1 0.9 %copy-start.2 = (bf16[128,1024]{1,0:T(8,128)(2,1)S(1)}, bf16[128,1024]{1,0:T(8,128)(2,1)}, u32[]{:S(2)}) copy-start(bf16[128,1024]{1,0:T(8,128)(2,1)} %do_ref.1) | copy-start | bytes 786436
  29.0 14.6 %collective-permute-start.3 = (bf16[8,272,128]{2,1,0:T(8,128)(2,1)S(1)}, bf16[8,272,128]{2,1,0:T(8,128)(2,1)S(1)}, u32[]{:S(2)}, u32[]{:S(2)}) collective-permute-start(bf16[8,272,128]{2,1,0:T(8,128)(2,1)S(1)} %all-to-all-done.kv_ref), channel_id=1, source_target_pairs={{0,16},{16,32},{32,48},{48,64},{64,80},{80,96},{96,112},{112,128},... | collective-permute-start | bytes 1671176 | tf_op jit(solution)/shard_map/ppermute | solution.py:20
  45.5 4.3 %collective-permute-start.5 = (f32[3,2,1,512]{3,2,1,0:T(1,128)S(1)}, f32[3,2,1,512]{3,2,1,0:T(1,128)S(1)}, u32[]{:S(2)}, u32[]{:S(2)}) collective-permute-start(f32[3,2,1,512]{3,2,1,0:T(1,128)S(1)} %get-tuple-element.54.stats_ref), channel_id=1, source_target_pairs={{0,1},{1,0},{2,3},{3,2},{4,5},{5,4},{6,7},{7,6},{8,9},{9,8},{10,11... | collective-permute-start | bytes 36872 | tf_op jit(solution)/shard_map/ppermute | solution.py:24
  48.8 4.0 %collective-permute-start.6 = (f32[3,2,1,512]{3,2,1,0:T(1,128)S(1)}, f32[3,2,1,512]{3,2,1,0:T(1,128)S(1)}, u32[]{:S(2)}, u32[]{:S(2)}) collective-permute-start(f32[3,2,1,512]{3,2,1,0:T(1,128)S(1)} %get-tuple-element.53.stats_ref), channel_id=1, source_target_pairs={{0,1},{1,0},{2,3},{3,2},{4,5},{5,4},{6,7},{7,6},{8,9},{9,8},{10,11... | collective-permute-start | bytes 36872 | tf_op jit(solution)/shard_map/ppermute | solution.py:24
  55.0 8.6 %collective-permute-start.8 = (bf16[8,128,256]{2,1,0:T(8,128)(2,1)S(1)}, bf16[8,128,256]{2,1,0:T(8,128)(2,1)S(1)}, u32[]{:S(2)}, u32[]{:S(2)}) collective-permute-start(bf16[8,128,256]{2,1,0:T(8,128)(2,1)S(1)} %get-tuple-element.73), channel_id=1, source_target_pairs={{16,0},{32,16},{48,32},{64,48},{80,64},{96,80},{112,96},{128,112},... | collective-permute-start | bytes 1572872 | tf_op jit(solution)/shard_map/ppermute | solution.py:20
  64.6 22.4 %all-to-all-start.1 = ((bf16[8,128,256]{2,1,0:T(8,128)(2,1)}), bf16[8,128,256]{2,1,0:T(8,128)(2,1)S(1)}, u32[]{:S(2)}, u32[]{:S(2)}) async-start(bf16[8,128,256]{2,1,0:T(8,128)(2,1)} %add_convert_fusion), calls=%async_computation.1 | async-start | bytes 1048576 | tf_op jit(solution)/shard_map/all_to_all | solution.py:30
  70.8 9.2 %collective-permute-start.4 = (bf16[2,128,512]{2,1,0:T(8,128)(2,1)S(1)}, bf16[2,128,512]{2,1,0:T(8,128)(2,1)S(1)}, u32[]{:S(2)}, u32[]{:S(2)}) collective-permute-start(bf16[2,128,512]{2,1,0:T(8,128)(2,1)S(1)} %get-tuple-element.50), channel_id=1, source_target_pairs={{0,1},{1,0},{2,3},{3,2},{4,5},{5,4},{6,7},{7,6},{8,9},{9,8},{10,11... | collective-permute-start | bytes 786440 | tf_op jit(solution)/shard_map/ppermute | solution.py:24
  71.5 11.4 %collective-permute-start.7 = (bf16[128,1024]{1,0:T(8,128)(2,1)S(1)}, bf16[128,1024]{1,0:T(8,128)(2,1)S(1)}, u32[]{:S(2)}, u32[]{:S(2)}) collective-permute-start(bf16[128,1024]{1,0:T(8,128)(2,1)S(1)} %get-tuple-element.71), channel_id=1, source_target_pairs={{0,1},{1,0},{2,3},{3,2},{4,5},{5,4},{6,7},{7,6},{8,9},{9,8},{10,11... | collective-permute-start | bytes 786440 | tf_op jit(solution)/shard_map/ppermute | solution.py:24

commit v8 on v7

--- a/solution.py
+++ b/solution.py
@@ -463,9 +463,10 @@
         [((span_rows, 2 * head_dim), f32), by_query],
         flops=4 * steps * unit,
     )(allowed, slots, qs, ks, vs, p_own, dos_mine, shift_mine, ds_mine, dos_theirs, shift_theirs, ds_theirs, prev_kv)
+    own_terms, got, dq_partner = lax.optimization_barrier((own_terms, got, dq_partner))
+    terms = (own_terms.astype(f32) + returned.astype(f32)).astype(bf16)
     (attended,) = call(merge_attended, "merge_attended", [tokens], (), [])(out, got, factor)
     dq_other = to_partner(dq_partner, "inner")
-    terms = (own_terms.astype(f32) + returned.astype(f32)).astype(bf16)
     key_grads = jnp.sum(exchange(terms, "inner").astype(f32), axis=0)
     grad_queries = (dq + dq_other.astype(f32)).astype(bf16)
     grad_keys = key_grads[:, :head_dim].astype(bf16)

time: 88.2 us -> 93.5 us (1.060)
  the two profiles are of different devices: /device:TPU:16 before, /device:TPU:23 now
where the time goes in v8:
time: 93.5 us; the launch traced here: 93.1 us
  waiting for transfers between devices  36.9 us (39%)
  starting transfers between devices  30.2 us (32%)
  Pallas kernels  20.3 us (22%)
  local copies, waits for them, and re-layouts  3.18 us (3%)
  other arithmetic  1.77 us (2%)
    ppermute x7, waiting for transfers between devices, to_partner(): lax.ppermute(block, axis, [(i, i ^ 1) for i in range(lax.axis_size(axis))])  24.2 us
    pallas_call x8, Pallas kernels, run(): pl.pallas_call(kernel, name=name, grid=(1,) if stream else (), out_shape=...  18.6 us
    all_to_all x2, starting transfers between devices, exchange(): lax.all_to_all(parts, axis, 0, 0, axis_index_groups=groups, tiled=True)  14.1 us
    all_to_all x2, waiting for transfers between devices, exchange(): lax.all_to_all(parts, axis, 0, 0, axis_index_groups=groups, tiled=True)  12.6 us
    ppermute x2, starting transfers between devices, from_behind(): return lax.ppermute(block, axis, route)  10.8 us
    ppermute x7, starting transfers between devices, to_partner(): lax.ppermute(block, axis, [(i, i ^ 1) for i in range(lax.axis_size(axis))])  5.29 us
    unnamed x6, local copies, waits for them, and re-layouts  2.55 us
  transfers between devices with their start and end apart: 11, of which 6 were waited for; matrix products, arithmetic and copies ran while one was open for 1% of the time, Pallas kernels for 16%

profile of v8, /device:TPU:23, one launch (start us, length us, event | category | flops | bytes accessed | tf_op | source)
XLA Modules:
  0.0 93.1 jit_solution(8221095467345829006)
XLA Ops:
  0.6 1.7 %pack.1 = bf16[8,272,128]{2,1,0:T(8,128)(2,1)} custom-call(s32[128]{0:T(128)} %position_ref.3, bf16[128,128]{1,0:T(8,128)(2,1)} %key_ref.1, bf16[128,128]{1,0:T(8,128)(2,1)} %value_ref.1), custom_call_target="tpu_custom_call" | custom-call | tf_op jit(solution)/shard_map/pack/pallas_call | solution.py:362
  2.3 8.2 %all-to-all-start = ((bf16[8,272,128]{2,1,0:T(8,128)(2,1)}), bf16[8,272,128]{2,1,0:T(8,128)(2,1)S(1)}, u32[]{:S(2)}, u32[]{:S(2)}) async-start(bf16[8,272,128]{2,1,0:T(8,128)(2,1)} %pack.1), calls=%async_computation | async-start | bytes 1114112 | tf_op jit(solution)/shard_map/all_to_all | solution.py:30
  10.5 1.0 %collective-permute-start.1 = (bf16[128,1024]{1,0:T(8,128)(2,1)}, bf16[128,1024]{1,0:T(8,128)(2,1)S(1)}, u32[]{:S(2)}, u32[]{:S(2)}) collective-permute-start(bf16[128,1024]{1,0:T(8,128)(2,1)} %q_ref.1), channel_id=1, source_target_pairs={{0,1},{1,0},{2,3},{3,2},{4,5},{5,4},{6,7},{7,6},{8,9},{9,8},{10,11... | collective-permute-start | bytes 786440 | tf_op jit(solution)/shard_map/ppermute | solution.py:24
  12.0 1.0 %collective-permute-start = (s32[128]{0:T(128)}, s32[128]{0:T(128)S(1)}, u32[]{:S(2)}, u32[]{:S(2)}) collective-permute-start(s32[128]{0:T(128)} %position_ref.3), channel_id=1, source_target_pairs={{0,1},{1,0},{2,3},{3,2},{4,5},{5,4},{6,7},{7,6},{8,9},{9,8},{10,11... | collective-permute-start | bytes 1544 | tf_op jit(solution)/shard_map/ppermute | solution.py:24
  13.0 10.2 %collective-permute-done.position_partner_ref = s32[128]{0:T(128)S(1)} collective-permute-done((s32[128]{0:T(128)}, s32[128]{0:T(128)S(1)}, u32[]{:S(2)}, u32[]{:S(2)}) %collective-permute-start) | collective-permute-done | bytes 544 | tf_op jit(solution)/shard_map/ppermute | solution.py:24
  23.9 0.9 %copy-done.1 = bf16[128,1024]{1,0:T(8,128)(2,1)S(1)} copy-done((bf16[128,1024]{1,0:T(8,128)(2,1)S(1)}, bf16[128,1024]{1,0:T(8,128)(2,1)}, u32[]{:S(2)}) %copy-start.1) | copy-done | bytes 262168
  24.8 0.9 %copy-done.2 = bf16[128,1024]{1,0:T(8,128)(2,1)S(1)} copy-done((bf16[128,1024]{1,0:T(8,128)(2,1)S(1)}, bf16[128,1024]{1,0:T(8,128)(2,1)}, u32[]{:S(2)}) %copy-start.2) | copy-done | bytes 262168
  25.8 1.2 %stack_pair.1 = (s32[2]{0:T(128)S(1)}, bf16[4,512,128]{2,1,0:T(8,128)(2,1)S(1)}, bf16[4,128,512]{2,1,0:T(8,128)(2,1)S(1)}) custom-call(s32[128]{0:T(128)S(1)} %copy-done, s32[128]{0:T(128)S(1)} %collective-permute-done.position_partner_ref, bf16[128,1024]{1,0:T(8,128)(2,1)S(1)} %copy-done.1, bf16[128,1024]{1,0:T(8,128)(2,1)S(1)} %collective-permute-done.1.q_partner_ref, ...), custom_call_target="tpu_custom_call" | custom-call | flops 4000000000 | bytes 4194304 | tf_op jit(solution)/shard_map/stack_pair/pallas_call | solution.py:333
  27.0 2.2 %all-to-all-done.kv_ref = bf16[8,272,128]{2,1,0:T(8,128)(2,1)S(1)} async-done(((bf16[8,272,128]{2,1,0:T(8,128)(2,1)}), bf16[8,272,128]{2,1,0:T(8,128)(2,1)S(1)}, u32[]{:S(2)}, u32[]{:S(2)}) %all-to-all-start) | async-done | bytes 557088 | tf_op jit(solution)/shard_map/all_to_all | solution.py:30
  29.2 1.3 %collective-permute-start.3 = (bf16[8,272,128]{2,1,0:T(8,128)(2,1)S(1)}, bf16[8,272,128]{2,1,0:T(8,128)(2,1)S(1)}, u32[]{:S(2)}, u32[]{:S(2)}) collective-permute-start(bf16[8,272,128]{2,1,0:T(8,128)(2,1)S(1)} %all-to-all-done.kv_ref), channel_id=1, source_target_pairs={{0,16},{16,32},{32,48},{48,64},{64,80},{80,96},{96,112},{112,128},... | collective-permute-start | bytes 1671176 | tf_op jit(solution)/shard_map/ppermute | solution.py:20
  30.5 3.8 %own_forward.1 = (bf16[1024,128]{1,0:T(8,128)(2,1)S(1)}, bf16[1024,128]{1,0:T(8,128)(2,1)S(1)}, s32[8]{0:T(128)S(1)}, s32[4]{0:T(128)S(1)}, bf16[10,256,512]{2,1...) custom-call(s32[2]{0:T(128)S(1)} %get-tuple-element.48.block_ref, ...), custom_call_target="tpu_custom_call" | custom-call | flops 671088640 | bytes 4194304 | tf_op jit(solution)/shard_map/own_forward/pallas_call | solution.py:333
  34.3 1.9 %prev_forward_theirs.1 = (bf16[2,4,256,512]{3,2,1,0:T(8,128)(2,1)S(1)}, f32[2,1,512]{2,1,0:T(1,128)S(1)}, f32[3,2,1,512]{3,2,1,0:T(1,128)S(1)}, bf16[2,128,512]{2,1,0:T(8,128)(2,1)S(1)}) custom-call(s32[1]{0:T(128)} %bitcast.has_ref, bf16[4,512,128]{2,1,0:T(8,128)(2,1)S(1)} %get-tuple-element.45.qs_ref, bf16[4,128,512]{2,1,0:T(8,128)(2,1)S(1)} %get-tuple-element.46.dot_ref, ...), custom_call_target="tpu_custom_call" | custom-call | flops 536870912 | bytes 4194304 | tf_op jit(solution)/shard_map/prev_forward_theirs/pallas_call | solution.py:333
  36.3 1.1 %collective-permute-start.4 = (f32[3,2,1,512]{3,2,1,0:T(1,128)S(1)}, f32[3,2,1,512]{3,2,1,0:T(1,128)S(1)}, u32[]{:S(2)}, u32[]{:S(2)}) collective-permute-start(f32[3,2,1,512]{3,2,1,0:T(1,128)S(1)} %get-tuple-element.61.stats_ref), channel_id=1, source_target_pairs={{0,1},{1,0},{2,3},{3,2},{4,5},{5,4},{6,7},{7,6},{8,9},{9,8},{10,11... | collective-permute-start | bytes 36872 | tf_op jit(solution)/shard_map/ppermute | solution.py:24
  37.4 1.9 %prev_forward_mine.1 = (bf16[2,4,256,512]{3,2,1,0:T(8,128)(2,1)S(1)}, f32[2,1,512]{2,1,0:T(1,128)S(1)}, f32[3,2,1,512]{3,2,1,0:T(1,128)S(1)}, f32[2,128,512]{2,1,0:T(8,128)S(1)}) custom-call(s32[1]{0:T(128)} %bitcast.has_ref, bf16[4,512,128]{2,1,0:T(8,128)(2,1)S(1)} %get-tuple-element.45.qs_ref, bf16[4,128,512]{2,1,0:T(8,128)(2,1)S(1)} %get-tuple-element.46.dot_ref, ...), custom_call_target="tpu_custom_call" | custom-call | flops 536870912 | bytes 4194304 | tf_op jit(solution)/shard_map/prev_forward_mine/pallas_call | solution.py:333
  40.0 1.9 %prev_backward_mine.1 = (f32[1024,256]{1,0:T(8,128)S(1)}, bf16[2,128,512]{2,1,0:T(8,128)(2,1)S(1)}, f32[2,1,512]{2,1,0:T(1,128)S(1)}, bf16[2,4,256,512]{3,2,1,0:T(8,128)(2,1)S(1)}, f32[2,2,1,512]{3,2,1,0:T(1,128)S(1)}) custom-call(s32[1]{0:T(128)} %bitcast.has_ref, bf16[4,512,128]{2,1,0:T(8,128)(2,1)S(1)} %get-tuple-element.45.qs_ref, ...), custom_call_target="tpu_custom_call" | custom-call | flops 1073741824 | bytes 4194304 | tf_op jit(solution)/shard_map/prev_backward_mine/pallas_call | solution.py:333
  42.1 2.2 %prev_backward_theirs.1 = (bf16[8,128,256]{2,1,0:T(8,128)(2,1)S(1)}, bf16[2,128,512]{2,1,0:T(8,128)(2,1)S(1)}, f32[2,1,512]{2,1,0:T(1,128)S(1)}, bf16[2,4,256,512]{3,2,1,0:T(8,128)(2,1)S(1)}) custom-call(s32[1]{0:T(128)} %bitcast.has_ref, bf16[4,512,128]{2,1,0:T(8,128)(2,1)S(1)} %get-tuple-element.45.qs_ref, ...), custom_call_target="tpu_custom_call" | custom-call | flops 1073741824 | bytes 4194304 | tf_op jit(solution)/shard_map/prev_backward_theirs/pallas_call | solution.py:333
  44.4 9.5 %collective-permute-start.8 = (bf16[8,128,256]{2,1,0:T(8,128)(2,1)S(1)}, bf16[8,128,256]{2,1,0:T(8,128)(2,1)S(1)}, u32[]{:S(2)}, u32[]{:S(2)}) collective-permute-start(bf16[8,128,256]{2,1,0:T(8,128)(2,1)S(1)} %get-tuple-element.79), channel_id=1, source_target_pairs={{16,0},{32,16},{48,32},{64,48},{80,64},{96,80},{112,96},{128,112},... | collective-permute-start | bytes 1572872 | tf_op jit(solution)/shard_map/ppermute | solution.py:20
  54.5 4.8 %own_backward.1 = (f32[128,1024]{1,0:T(8,128)S(1)}, bf16[128,1024]{1,0:T(8,128)(2,1)S(1)}, bf16[8,128,256]{2,1,0:T(8,128)(2,1)S(1)}) custom-call(s32[4]{0:T(128)S(1)} %get-tuple-element.53.allowed_ref, s32[8]{0:T(128)S(1)} %get-tuple-element.54.slots_ref, bf16[4,512,128]{2,1,0:T(8,128)(2,1)S(1)} %get-tuple-element.45.qs_ref, ...), custom_call_target="tpu_custom_call" | custom-call | flops 1342177280 | bytes 4194304 | tf_op jit(solution)/shard_map/own_backward/pallas_call | solution.py:333
  59.2 8.4 %collective-permute-done.6.got_ref = bf16[2,128,512]{2,1,0:T(8,128)(2,1)S(1)} collective-permute-done((bf16[2,128,512]{2,1,0:T(8,128)(2,1)S(1)}, bf16[2,128,512]{2,1,0:T(8,128)(2,1)S(1)}, u32[]{:S(2)}, u32[]{:S(2)}) %collective-permute-start.6) | collective-permute-done | bytes 262176 | tf_op jit(solution)/shard_map/ppermute | solution.py:24
  67.6 0.9 %add_convert_fusion = bf16[8,128,256]{2,1,0:T(8,128)(2,1)} fusion(bf16[8,128,256]{2,1,0:T(8,128)(2,1)S(1)} %collective-permute-done.8, bf16[8,128,256]{2,1,0:T(8,128)(2,1)S(1)} %get-tuple-element.78), kind=kLoop, calls=%fused_computation | loop fusion | flops 1048576 | bytes 1572864 | tf_op jit(solution)/shard_map/convert_element_type | solution.py:467
  68.5 5.9 %all-to-all-start.1 = ((bf16[8,128,256]{2,1,0:T(8,128)(2,1)}), bf16[8,128,256]{2,1,0:T(8,128)(2,1)S(1)}, u32[]{:S(2)}, u32[]{:S(2)}) async-start(bf16[8,128,256]{2,1,0:T(8,128)(2,1)} %add_convert_fusion), calls=%async_computation.1 | async-start | bytes 1048576 | tf_op jit(solution)/shard_map/all_to_all | solution.py:30
  74.9 0.9 merge_attended.1
  75.8 5.4 %collective-permute-done.7 = bf16[128,1024]{1,0:T(8,128)(2,1)S(1)} collective-permute-done((bf16[128,1024]{1,0:T(8,128)(2,1)S(1)}, bf16[128,1024]{1,0:T(8,128)(2,1)S(1)}, u32[]{:S(2)}, u32[]{:S(2)}) %collective-permute-start.7) | collective-permute-done | bytes 262176 | tf_op jit(solution)/shard_map/ppermute | solution.py:24
  82.0 10.4 %all-to-all-done.1 = bf16[8,128,256]{2,1,0:T(8,128)(2,1)S(1)} async-done(((bf16[8,128,256]{2,1,0:T(8,128)(2,1)}), bf16[8,128,256]{2,1,0:T(8,128)(2,1)S(1)}, u32[]{:S(2)}, u32[]{:S(2)}) %all-to-all-start.1) | async-done | bytes 524320 | tf_op jit(solution)/shard_map/all_to_all | solution.py:30
  (17 shorter events, 4.5 us)
Async XLA Ops:
  2.3 26.9 %all-to-all-start = ((bf16[8,272,128]{2,1,0:T(8,128)(2,1)}), bf16[8,272,128]{2,1,0:T(8,128)(2,1)S(1)}, u32[]{:S(2)}, u32[]{:S(2)}) async-start(bf16[8,272,128]{2,1,0:T(8,128)(2,1)} %pack.1), calls=%async_computation | async-start | bytes 1114112 | tf_op jit(solution)/shard_map/all_to_all | solution.py:30
  10.5 12.7 %collective-permute-start.1 = (bf16[128,1024]{1,0:T(8,128)(2,1)}, bf16[128,1024]{1,0:T(8,128)(2,1)S(1)}, u32[]{:S(2)}, u32[]{:S(2)}) collective-permute-start(bf16[128,1024]{1,0:T(8,128)(2,1)} %q_ref.1), channel_id=1, source_target_pairs={{0,1},{1,0},{2,3},{3,2},{4,5},{5,4},{6,7},{7,6},{8,9},{9,8},{10,11... | collective-permute-start | bytes 786440 | tf_op jit(solution)/shard_map/ppermute | solution.py:24
  11.5 11.7 %collective-permute-start.2 = (bf16[128,1024]{1,0:T(8,128)(2,1)}, bf16[128,1024]{1,0:T(8,128)(2,1)S(1)}, u32[]{:S(2)}, u32[]{:S(2)}) collective-permute-start(bf16[128,1024]{1,0:T(8,128)(2,1)} %do_ref.1), channel_id=1, source_target_pairs={{0,1},{1,0},{2,3},{3,2},{4,5},{5,4},{6,7},{7,6},{8,9},{9,8},{10,11... | collective-permute-start | bytes 786440 | tf_op jit(solution)/shard_map/ppermute | solution.py:24
  12.0 11.2 %collective-permute-start = (s32[128]{0:T(128)}, s32[128]{0:T(128)S(1)}, u32[]{:S(2)}, u32[]{:S(2)}) collective-permute-start(s32[128]{0:T(128)} %position_ref.3), channel_id=1, source_target_pairs={{0,1},{1,0},{2,3},{3,2},{4,5},{5,4},{6,7},{7,6},{8,9},{9,8},{10,11... | collective-permute-start | bytes 1544 | tf_op jit(solution)/shard_map/ppermute | solution.py:24
  23.2 0.7 copy-start
  23.9 0.9 %copy-start.1 = (bf16[128,1024]{1,0:T(8,128)(2,1)S(1)}, bf16[128,1024]{1,0:T(8,128)(2,1)}, u32[]{:S(2)}) copy-start(bf16[128,1024]{1,0:T(8,128)(2,1)} %q_ref.1) | copy-start | bytes 786436
  24.8 0.9 %copy-start.2 = (bf16[128,1024]{1,0:T(8,128)(2,1)S(1)}, bf16[128,1024]{1,0:T(8,128)(2,1)}, u32[]{:S(2)}) copy-start(bf16[128,1024]{1,0:T(8,128)(2,1)} %do_ref.1) | copy-start | bytes 786436
  29.2 5.1 %collective-permute-start.3 = (bf16[8,272,128]{2,1,0:T(8,128)(2,1)S(1)}, bf16[8,272,128]{2,1,0:T(8,128)(2,1)S(1)}, u32[]{:S(2)}, u32[]{:S(2)}) collective-permute-start(bf16[8,272,128]{2,1,0:T(8,128)(2,1)S(1)} %all-to-all-done.kv_ref), channel_id=1, source_target_pairs={{0,16},{16,32},{32,48},{48,64},{64,80},{80,96},{96,112},{112,128},... | collective-permute-start | bytes 1671176 | tf_op jit(solution)/shard_map/ppermute | solution.py:20
  36.3 3.8 %collective-permute-start.4 = (f32[3,2,1,512]{3,2,1,0:T(1,128)S(1)}, f32[3,2,1,512]{3,2,1,0:T(1,128)S(1)}, u32[]{:S(2)}, u32[]{:S(2)}) collective-permute-start(f32[3,2,1,512]{3,2,1,0:T(1,128)S(1)} %get-tuple-element.61.stats_ref), channel_id=1, source_target_pairs={{0,1},{1,0},{2,3},{3,2},{4,5},{5,4},{6,7},{7,6},{8,9},{9,8},{10,11... | collective-permute-start | bytes 36872 | tf_op jit(solution)/shard_map/ppermute | solution.py:24
  39.3 2.8 %collective-permute-start.5 = (f32[3,2,1,512]{3,2,1,0:T(1,128)S(1)}, f32[3,2,1,512]{3,2,1,0:T(1,128)S(1)}, u32[]{:S(2)}, u32[]{:S(2)}) collective-permute-start(f32[3,2,1,512]{3,2,1,0:T(1,128)S(1)} %get-tuple-element.60.stats_ref), channel_id=1, source_target_pairs={{0,1},{1,0},{2,3},{3,2},{4,5},{5,4},{6,7},{7,6},{8,9},{9,8},{10,11... | collective-permute-start | bytes 36872 | tf_op jit(solution)/shard_map/ppermute | solution.py:24
  44.4 23.2 %collective-permute-start.8 = (bf16[8,128,256]{2,1,0:T(8,128)(2,1)S(1)}, bf16[8,128,256]{2,1,0:T(8,128)(2,1)S(1)}, u32[]{:S(2)}, u32[]{:S(2)}) collective-permute-start(bf16[8,128,256]{2,1,0:T(8,128)(2,1)S(1)} %get-tuple-element.79), channel_id=1, source_target_pairs={{16,0},{32,16},{48,32},{64,48},{80,64},{96,80},{112,96},{128,112},... | collective-permute-start | bytes 1572872 | tf_op jit(solution)/shard_map/ppermute | solution.py:20
  53.9 13.7 %collective-permute-start.6 = (bf16[2,128,512]{2,1,0:T(8,128)(2,1)S(1)}, bf16[2,128,512]{2,1,0:T(8,128)(2,1)S(1)}, u32[]{:S(2)}, u32[]{:S(2)}) collective-permute-start(bf16[2,128,512]{2,1,0:T(8,128)(2,1)S(1)} %get-tuple-element.72), channel_id=1, source_target_pairs={{0,1},{1,0},{2,3},{3,2},{4,5},{5,4},{6,7},{7,6},{8,9},{9,8},{10,11... | collective-permute-start | bytes 786440 | tf_op jit(solution)/shard_map/ppermute | solution.py:24
  68.5 23.9 %all-to-all-start.1 = ((bf16[8,128,256]{2,1,0:T(8,128)(2,1)}), bf16[8,128,256]{2,1,0:T(8,128)(2,1)S(1)}, u32[]{:S(2)}, u32[]{:S(2)}) async-start(bf16[8,128,256]{2,1,0:T(8,128)(2,1)} %add_convert_fusion), calls=%async_computation.1 | async-start | bytes 1048576 | tf_op jit(solution)/shard_map/all_to_all | solution.py:30
  74.4 6.8 %collective-permute-start.7 = (bf16[128,1024]{1,0:T(8,128)(2,1)S(1)}, bf16[128,1024]{1,0:T(8,128)(2,1)S(1)}, u32[]{:S(2)}, u32[]{:S(2)}) collective-permute-start(bf16[128,1024]{1,0:T(8,128)(2,1)S(1)} %get-tuple-element.77), channel_id=1, source_target_pairs={{0,1},{1,0},{2,3},{3,2},{4,5},{5,4},{6,7},{7,6},{8,9},{9,8},{10,11... | collective-permute-start | bytes 786440 | tf_op jit(solution)/shard_map/ppermute | solution.py:24

commit v9 on v7

--- a/solution.py
+++ b/solution.py
@@ -22,6 +22,11 @@
 
 def to_partner(block, axis):
     return lax.ppermute(block, axis, [(i, i ^ 1) for i in range(lax.axis_size(axis))])
+
+
+def turn(block, axis, distance):
+    count = lax.axis_size(axis)
+    return lax.ppermute(block, axis, [(i, (i + 2 * distance) % count) for i in range(count)])
 
 
 def exchange(parts, axis):
@@ -58,8 +63,8 @@
         ].astype(target_ref.dtype)
 
 
-def pack(position_ref, key_ref, value_ref, packed_ref, place_ref, block_ref, in_sems, out_sems):
-    count, rows, head_dim = packed_ref.shape
+def pack(segment, position_ref, key_ref, value_ref, packed_ref, place_ref, block_ref, in_sems, out_sem):
+    rows, head_dim = packed_ref.shape
     span = key_ref.shape[0]
     loads = [
         pltpu.make_async_copy(position_ref, place_ref, in_sems.at[0]),
@@ -69,18 +74,14 @@
     for load in loads:
         load.start()
     loads[0].wait()
-    tag = (lax.rem(place_ref[0], 2 * count * span) // block_rows).astype(jnp.float32)
+    tag = (lax.rem(place_ref[0], segment) // block_rows).astype(jnp.float32)
     tag = jnp.full((rows - 2 * span, head_dim), tag, jnp.float32)
     block_ref[2 * span :, :] = tag.astype(packed_ref.dtype)
     loads[1].wait()
     loads[2].wait()
-    stores = [
-        pltpu.make_async_copy(block_ref, packed_ref.at[g], out_sems.at[g]) for g in range(count)
-    ]
-    for store in stores:
-        store.start()
-    for store in stores:
-        store.wait()
+    store = pltpu.make_async_copy(block_ref, packed_ref, out_sem.at[0])
+    store.start()
+    store.wait()
 
 
 def stack_pair(
@@ -115,17 +116,16 @@
     return low + high, tile
 
 
-def own_forward(
-    block_ref, qs_ref, kv_ref,
-    ks_ref, vs_ref, slots_ref, allowed_ref, p_ref, m_ref, l_ref, o_ref, s_ref,
-):
-    group, _, head_dim = kv_ref.shape
+def own_forward(group, block_ref, qs_ref, *rest):
+    kv, rest = rest[:group], rest[group:]
+    ks_ref, vs_ref, slots_ref, allowed_ref, p_ref, m_ref, l_ref, o_ref, s_ref = rest
+    head_dim = kv[0].shape[1]
     span = 2 * block_rows
     steps, _, width = p_ref.shape
     blocks = 2 * group
     tiles = blocks * block_rows // tile_keys
     exponent_scale = log2_e * float(head_dim) ** (-0.5)
-    tags = [jnp.max(kv_ref[g, 2 * span :, :].astype(jnp.float32)).astype(jnp.int32) for g in range(group)]
+    tags = [jnp.max(kv[g][2 * span :, :].astype(jnp.float32)).astype(jnp.int32) for g in range(group)]
 
     def count(test):
         return sum(jnp.where(test(tag), 1, 0) for tag in tags)
@@ -140,9 +140,9 @@
         for half, place in ((0, slot), (1, blocks - 1 - slot)):
             target = pl.ds(pl.multiple_of(place * block_rows, block_rows), block_rows)
             rows = slice(half * block_rows, (half + 1) * block_rows)
-            ks_ref[target, :] = kv_ref[g, rows, :]
+            ks_ref[target, :] = kv[g][rows, :]
             rows = slice(span + half * block_rows, span + (half + 1) * block_rows)
-            vs_ref[target, :] = kv_ref[g, rows, :]
+            vs_ref[target, :] = kv[g][rows, :]
     m_ref[...] = jnp.full(m_ref.shape, masked_score, jnp.float32)
     l_ref[...] = jnp.zeros(l_ref.shape, jnp.float32)
     o_ref[...] = jnp.zeros(o_ref.shape, jnp.float32)
@@ -167,19 +167,18 @@
         o_ref[at] += dot_tn(vs_ref[pl.ds(start, tile_keys), :], raised)
 
 
-def key_tile(ref, tile, part):
+def key_tile(kv, tile, part):
     span = 2 * block_rows
     per_tile = tile_keys // span
     return jnp.concatenate(
-        [ref[tile * per_tile + j, part * span : (part + 1) * span, :] for j in range(per_tile)],
+        [kv[tile * per_tile + j][part * span : (part + 1) * span, :] for j in range(per_tile)],
         axis=0,
     )
 
 
-def prev_forward(
-    first, has_ref, qs_ref, dot_ref, kv_ref, m_own_ref, l_own_ref, o_own_ref,
-    p_ref, m_prev_ref, stats_ref, out_ref, s_ref,
-):
+def prev_forward(first, group, has_ref, qs_ref, dot_ref, m_own_ref, l_own_ref, o_own_ref, *rest):
+    kv, rest = rest[:group], rest[group:]
+    p_ref, m_prev_ref, stats_ref, out_ref, s_ref = rest
     _, width, head_dim = qs_ref.shape
     sets, tiles = p_ref.shape[:2]
     exponent_scale = log2_e * float(head_dim) ** (-0.5)
@@ -187,7 +186,7 @@
     for at in range(sets):
         peak = jnp.full((1, width), masked_score, jnp.float32)
         for tile in range(tiles):
-            scores = dot_nt(key_tile(kv_ref, tile, 0), qs_ref[first + at])
+            scores = dot_nt(key_tile(kv, tile, 0), qs_ref[first + at])
             s_ref[at, tile] = scores
             peak = jnp.maximum(peak, jnp.max(scores, axis=0, keepdims=True))
         m_prev_ref[at] = peak
@@ -200,7 +199,7 @@
             total += jnp.sum(raised, axis=0, keepdims=True)
             raised = raised.astype(jnp.bfloat16)
             p_ref[at, tile] = raised
-            out += dot_tn(key_tile(kv_ref, tile, 1), raised)
+            out += dot_tn(key_tile(kv, tile, 1), raised)
         peak = jnp.where(has_prev, peak, masked_score)
         m_prev_ref[at] = peak
         top = jnp.maximum(peak, m_own_ref[first + at])
@@ -219,7 +218,10 @@
             out_ref[at] = (out * share).astype(jnp.bfloat16)
 
 
-def prev_backward(first, has_ref, qs_ref, dot_ref, kv_ref, p_ref, m_own_ref, m_prev_ref, stats_ref, other_ref, *rest):
+def prev_backward(
+    first, group, has_ref, place_ref, qs_ref, dot_ref, p_ref, m_own_ref, m_prev_ref, stats_ref, other_ref, *rest
+):
+    kv, rest = rest[:group], rest[group:]
     if first == 0:
         terms_ref, dos_ref, shift_ref, ds_ref, factor_ref, scaled_ref, lower_ref = rest
     else:
@@ -249,7 +251,7 @@
         scaled_ref[at] = (grad * prev_factor).astype(jnp.bfloat16)
         lower_ref[at] = delta * prev_factor
     for tile in range(tiles):
-        values = key_tile(kv_ref, tile, 1)
+        values = key_tile(kv, tile, 1)
         key_grad = jnp.zeros((tile_keys, head_dim), jnp.float32)
         value_grad = jnp.zeros((tile_keys, head_dim), jnp.float32)
         for at in range(sets):
@@ -270,15 +272,17 @@
             value_grad = (value_grad + before_ref[rows, head_dim:]).astype(jnp.bfloat16)
             for j in range(per_tile):
                 rows = slice(j * span, (j + 1) * span)
-                terms_ref[tile * per_tile + j, :, :head_dim] = key_grad[rows]
-                terms_ref[tile * per_tile + j, :, head_dim:] = value_grad[rows]
+                place = place_ref[tile * per_tile + j]
+                terms_ref[place, :, :head_dim] = key_grad[rows]
+                terms_ref[place, :, head_dim:] = value_grad[rows]
 
 
 def own_backward(
-    allowed_ref, slots_ref, qs_ref, ks_ref, vs_ref, p_ref,
-    dos_mine_ref, shift_mine_ref, ds_mine_ref, dos_theirs_ref, shift_theirs_ref, ds_theirs_ref, kv_ref,
-    dq_ref, dq_partner_ref, terms_ref, acc_ref, dqa_ref,
+    allowed_ref, slots_ref, place_ref, qs_ref, ks_ref, vs_ref, p_ref,
+    dos_mine_ref, shift_mine_ref, ds_mine_ref, dos_theirs_ref, shift_theirs_ref, ds_theirs_ref, *rest
 ):
+    kv, rest = rest[: slots_ref.shape[0]], rest[slots_ref.shape[0] :]
+    dq_ref, dq_partner_ref, terms_ref, acc_ref, dqa_ref = rest
     steps, _, width = p_ref.shape
     group, span, _ = terms_ref.shape
     head_dim = ks_ref.shape[1]
@@ -290,7 +294,7 @@
     for at in range(4):
         changes = (ds_mine_ref, ds_theirs_ref)[at // 2]
         dqa_ref[at] = sum(
-            dot_tn(key_tile(kv_ref, tile, 0), changes[at % 2, tile]) for tile in range(tiles)
+            dot_tn(key_tile(kv, tile, 0), changes[at % 2, tile]) for tile in range(tiles)
         )
     for step in range(steps):
         at, tile = own_tile(step, allowed_ref)
@@ -310,7 +314,7 @@
         slot = slots_ref[g]
         for half, place in ((0, slot), (1, blocks - 1 - slot)):
             source = pl.ds(pl.multiple_of(place * block_rows, block_rows), block_rows)
-            terms_ref[g, half * block_rows : (half + 1) * block_rows, :] = acc_ref[
+            terms_ref[place_ref[g], half * block_rows : (half + 1) * block_rows, :] = acc_ref[
                 source, :
             ].astype(jnp.bfloat16)
     for half in range(2):
@@ -360,20 +364,26 @@
     position_partner = to_partner(positions, "inner")
     anywhere = pl.BlockSpec(memory_space=pl.ANY)
     packed = pl.pallas_call(
-        pack,
+        functools.partial(pack, segment),
         name="pack",
-        out_shape=jax.ShapeDtypeStruct((group, 2 * tok_rows + tag_rows, head_dim), bf16),
+        out_shape=jax.ShapeDtypeStruct((2 * tok_rows + tag_rows, head_dim), bf16),
         in_specs=[anywhere] * 3,
         out_specs=anywhere,
         scratch_shapes=[
             pltpu.SMEM(positions.shape, jnp.int32),
             pltpu.VMEM((2 * tok_rows + tag_rows, head_dim), bf16),
             pltpu.SemaphoreType.DMA((3,)),
-            pltpu.SemaphoreType.DMA((group,)),
+            pltpu.SemaphoreType.DMA((1,)),
         ],
         compiler_params=pltpu.CompilerParams(vmem_limit_bytes=60 * 1024 * 1024),
     )(positions, key_vectors, value_vectors)
-    group_kv = exchange(packed, "inner")
+    turns = [0] + [d if group // 2 >= d else d - group for d in range(1, group)]
+    turns.sort(key=abs, reverse=False)
+    turns.remove(0)
+    turns.insert(0, 0)
+    own_kv = [packed if d == 0 else turn(packed, "inner", d) for d in turns]
+    place = (lax.axis_index("inner") // 2 - jnp.array(turns, jnp.int32)) % group
+    prev_kv = [from_behind(block, "outer", 1) for block in own_kv]
     has_prev = (lax.axis_index("outer") > 0).astype(jnp.int32).reshape(1)
 
     unit = 2 * tile_keys * width * head_dim
@@ -393,10 +403,8 @@
         flops=4 * 10**9,
         stream=(2, 4),
     )(positions, position_partner, queries, query_partner, grad_output, grad_partner)
-    group_kv, qs, dot, both_blocks = lax.optimization_barrier((group_kv, qs, dot, both_blocks))
-    prev_kv = from_behind(group_kv, "outer", 1)
     ks, vs, slots, allowed, p_own, m_own, l_own, o_own = call(
-        own_forward,
+        functools.partial(own_forward, group),
         "own_forward",
         [
             ((span_rows, head_dim), bf16),
@@ -412,7 +420,7 @@
         [((steps, tile_keys, width), f32)],
         out_smem=(2, 3),
         flops=2 * steps * unit,
-    )(both_blocks, qs, group_kv)
+    )(both_blocks, qs, *own_kv)
     half_stat = ((2, 1, width), f32)
     half_query = ((2, head_dim, width), f32)
     changes = ((2, tiles, tile_keys, width), bf16)
@@ -420,7 +428,7 @@
 
     def forward(first, name):
         return call(
-            functools.partial(prev_forward, first),
+            functools.partial(prev_forward, first, group),
             name,
             [
                 ((2, tiles, tile_keys, width), bf16),
@@ -431,7 +439,7 @@
             (0,),
             [((2, tiles, tile_keys, width), f32)],
             flops=2 * 2 * tiles * unit,
-        )(has_prev, qs, dot, prev_kv, m_own, l_own, o_own)
+        )(has_prev, qs, dot, m_own, l_own, o_own, *prev_kv)
 
     p_theirs, m_theirs, stats_theirs, sent = forward(2, "prev_forward_theirs")
     other_mine = to_partner(stats_theirs, "inner")
@@ -439,30 +447,32 @@
     p_mine, m_mine, stats_mine, out = forward(0, "prev_forward_mine")
     other_theirs = to_partner(stats_mine, "inner")
     first_terms, dos_mine, shift_mine, ds_mine, factor = call(
-        functools.partial(prev_backward, 0),
+        functools.partial(prev_backward, 0, group),
         "prev_backward_mine",
         [((span_rows, 2 * head_dim), f32), half_query_16, half_stat, changes, ((2, 2, 1, width), f32)],
-        (0,),
+        (0, 1),
         [half_query_16, half_stat],
         flops=4 * 2 * tiles * unit,
-    )(has_prev, qs, dot, prev_kv, p_mine, m_own, m_mine, stats_mine, other_mine)
+    )(has_prev, place, qs, dot, p_mine, m_own, m_mine, stats_mine, other_mine, *prev_kv)
     prev_terms, dos_theirs, shift_theirs, ds_theirs = call(
-        functools.partial(prev_backward, 2),
+        functools.partial(prev_backward, 2, group),
         "prev_backward_theirs",
         [terms_shape, half_query_16, half_stat, changes],
-        (0,),
+        (0, 1),
         [half_query_16, half_stat],
         flops=4 * 2 * tiles * unit,
-    )(has_prev, qs, dot, prev_kv, p_theirs, m_own, m_theirs, stats_theirs, other_theirs, first_terms)
+    )(
+        has_prev, place, qs, dot, p_theirs, m_own, m_theirs, stats_theirs, other_theirs, *prev_kv, first_terms
+    )
     returned = from_behind(prev_terms, "outer", -1)
     dq, dq_partner, own_terms = call(
         own_backward,
         "own_backward",
         [((tok_rows, full_width), f32), tokens, terms_shape],
-        (0, 1),
+        (0, 1, 2),
         [((span_rows, 2 * head_dim), f32), by_query],
         flops=4 * steps * unit,
-    )(allowed, slots, qs, ks, vs, p_own, dos_mine, shift_mine, ds_mine, dos_theirs, shift_theirs, ds_theirs, prev_kv)
+    )(allowed, slots, place, qs, ks, vs, p_own, dos_mine, shift_mine, ds_mine, dos_theirs, shift_theirs, ds_theirs, *prev_kv)
     (attended,) = call(merge_attended, "merge_attended", [tokens], (), [])(out, got, factor)
     dq_other = to_partner(dq_partner, "inner")
     terms = (own_terms.astype(f32) + returned.astype(f32)).astype(bf16)

time: 88.2 us -> 104 us (1.18)
  the two profiles are of different devices: /device:TPU:16 before, /device:TPU:5 now
where the time goes in v9:
time: 104 us
  starting transfers between devices  56.6 us (54%)
  Pallas kernels  21.3 us (20%)
  waiting for transfers between devices  19.2 us (18%)
  local copies, waits for them, and re-layouts  3.18 us (3%)
  other arithmetic  2.46 us (2%)
    ppermute x9, starting transfers between devices, from_behind(): return lax.ppermute(block, axis, route)  29.8 us
    pallas_call x8, Pallas kernels, run(): pl.pallas_call(kernel, name=name, grid=(1,) if stream else (), out_shape=...  19.9 us
    ppermute x7, starting transfers between devices, turn(): lax.ppermute(block, axis, [(i, (i + 2 * distance) % count) for i in range...  15.3 us
    ppermute x7, waiting for transfers between devices, to_partner(): lax.ppermute(block, axis, [(i, i ^ 1) for i in range(lax.axis_size(axis))])  12.5 us
    ppermute x7, starting transfers between devices, to_partner(): lax.ppermute(block, axis, [(i, i ^ 1) for i in range(lax.axis_size(axis))])  5.87 us
    all_to_all x1, starting transfers between devices, exchange(): lax.all_to_all(parts, axis, 0, 0, axis_index_groups=groups, tiled=True)  5.69 us
    all_to_all x1, waiting for transfers between devices, exchange(): lax.all_to_all(parts, axis, 0, 0, axis_index_groups=groups, tiled=True)  3.6 us
    ppermute x9, waiting for transfers between devices, from_behind(): return lax.ppermute(block, axis, route)  3.09 us
  transfers between devices with their start and end apart: 24, of which 5 were waited for; matrix products, arithmetic and copies ran while one was open for 1% of the time, Pallas kernels for 15%

profile of v9, /device:TPU:5, one launch (start us, length us, event | category | flops | bytes accessed | tf_op | source)
XLA Modules:
  0.0 103.6 jit_solution(7396894029204270223)
XLA Ops:
  2.1 3.4 %collective-permute-start.10 = (bf16[272,128]{1,0:T(8,128)(2,1)}, bf16[272,128]{1,0:T(8,128)(2,1)S(1)}, u32[]{:S(2)}, u32[]{:S(2)}) collective-permute-start(bf16[272,128]{1,0:T(8,128)(2,1)} %pack.1.rest_0_), channel_id=1, source_target_pairs={{0,16},{16,32},{32,48},{48,64},{64,80},{80,96},{96,112},{112,128},... | collective-permute-start | bytes 208904 | tf_op jit(solution)/shard_map/ppermute | solution.py:20
  5.5 7.0 %collective-permute-start.9 = (bf16[272,128]{1,0:T(8,128)(2,1)}, bf16[272,128]{1,0:T(8,128)(2,1)S(1)}, u32[]{:S(2)}, u32[]{:S(2)}) collective-permute-start(bf16[272,128]{1,0:T(8,128)(2,1)} %pack.1.rest_0_), channel_id=1, source_target_pairs={{0,8},{1,9},{2,10},{3,11},{4,12},{5,13},{6,14},{7,15},{8,0},{9,1},... | collective-permute-start | bytes 208904 | tf_op jit(solution)/shard_map/ppermute | solution.py:29
  12.5 3.3 %collective-permute-start.7 = (bf16[272,128]{1,0:T(8,128)(2,1)}, bf16[272,128]{1,0:T(8,128)(2,1)S(1)}, u32[]{:S(2)}, u32[]{:S(2)}) collective-permute-start(bf16[272,128]{1,0:T(8,128)(2,1)} %pack.1.rest_0_), channel_id=1, source_target_pairs={{0,6},{1,7},{2,8},{3,9},{4,10},{5,11},{6,12},{7,13},{8,14},{9,15},... | collective-permute-start | bytes 208904 | tf_op jit(solution)/shard_map/ppermute | solution.py:29
  19.3 1.6 %collective-permute-start.5 = (bf16[272,128]{1,0:T(8,128)(2,1)}, bf16[272,128]{1,0:T(8,128)(2,1)S(1)}, u32[]{:S(2)}, u32[]{:S(2)}) collective-permute-start(bf16[272,128]{1,0:T(8,128)(2,1)} %pack.1.rest_0_), channel_id=1, source_target_pairs={{0,4},{1,5},{2,6},{3,7},{4,8},{5,9},{6,10},{7,11},{8,12},{9,13},{1... | collective-permute-start | bytes 208904 | tf_op jit(solution)/shard_map/ppermute | solution.py:29
  21.0 2.2 %collective-permute-start.4 = (bf16[272,128]{1,0:T(8,128)(2,1)}, bf16[272,128]{1,0:T(8,128)(2,1)S(1)}, u32[]{:S(2)}, u32[]{:S(2)}) collective-permute-start(bf16[272,128]{1,0:T(8,128)(2,1)} %pack.1.rest_0_), channel_id=1, source_target_pairs={{0,14},{1,15},{2,0},{3,1},{4,2},{5,3},{6,4},{7,5},{8,6},{9,7},{10,... | collective-permute-start | bytes 208904 | tf_op jit(solution)/shard_map/ppermute | solution.py:29
  25.0 5.5 %collective-permute-start.17 = (bf16[272,128]{1,0:T(8,128)(2,1)S(1)}, bf16[272,128]{1,0:T(8,128)(2,1)S(1)}, u32[]{:S(2)}, u32[]{:S(2)}) collective-permute-start(bf16[272,128]{1,0:T(8,128)(2,1)S(1)} %collective-permute-done.9.rest_7_), channel_id=1, source_target_pairs={{0,16},{16,32},{32,48},{48,64},{64,80},{80,96},{96,112},{112,128},... | collective-permute-start | bytes 208904 | tf_op jit(solution)/shard_map/ppermute | solution.py:20
  30.6 2.1 %collective-permute-start.16 = (bf16[272,128]{1,0:T(8,128)(2,1)S(1)}, bf16[272,128]{1,0:T(8,128)(2,1)S(1)}, u32[]{:S(2)}, u32[]{:S(2)}) collective-permute-start(bf16[272,128]{1,0:T(8,128)(2,1)S(1)} %collective-permute-done.8.rest_6_), channel_id=1, source_target_pairs={{0,16},{16,32},{32,48},{48,64},{64,80},{80,96},{96,112},{112,128},... | collective-permute-start | bytes 208904 | tf_op jit(solution)/shard_map/ppermute | solution.py:20
  33.4 5.0 %collective-permute-start.15 = (bf16[272,128]{1,0:T(8,128)(2,1)S(1)}, bf16[272,128]{1,0:T(8,128)(2,1)S(1)}, u32[]{:S(2)}, u32[]{:S(2)}) collective-permute-start(bf16[272,128]{1,0:T(8,128)(2,1)S(1)} %collective-permute-done.7.rest_5_), channel_id=1, source_target_pairs={{0,16},{16,32},{32,48},{48,64},{64,80},{80,96},{96,112},{112,128},... | collective-permute-start | bytes 208904 | tf_op jit(solution)/shard_map/ppermute | solution.py:20
  38.4 1.9 %collective-permute-start.14 = (bf16[272,128]{1,0:T(8,128)(2,1)S(1)}, bf16[272,128]{1,0:T(8,128)(2,1)S(1)}, u32[]{:S(2)}, u32[]{:S(2)}) collective-permute-start(bf16[272,128]{1,0:T(8,128)(2,1)S(1)} %collective-permute-done.6.rest_4_), channel_id=1, source_target_pairs={{0,16},{16,32},{32,48},{48,64},{64,80},{80,96},{96,112},{112,128},... | collective-permute-start | bytes 208904 | tf_op jit(solution)/shard_map/ppermute | solution.py:20
  40.4 3.5 %collective-permute-start.13 = (bf16[272,128]{1,0:T(8,128)(2,1)S(1)}, bf16[272,128]{1,0:T(8,128)(2,1)S(1)}, u32[]{:S(2)}, u32[]{:S(2)}) collective-permute-start(bf16[272,128]{1,0:T(8,128)(2,1)S(1)} %collective-permute-done.5.rest_3_), channel_id=1, source_target_pairs={{0,16},{16,32},{32,48},{48,64},{64,80},{80,96},{96,112},{112,128},... | collective-permute-start | bytes 208904 | tf_op jit(solution)/shard_map/ppermute | solution.py:20
  43.9 3.1 %collective-permute-start.12 = (bf16[272,128]{1,0:T(8,128)(2,1)S(1)}, bf16[272,128]{1,0:T(8,128)(2,1)S(1)}, u32[]{:S(2)}, u32[]{:S(2)}) collective-permute-start(bf16[272,128]{1,0:T(8,128)(2,1)S(1)} %collective-permute-done.4.rest_2_), channel_id=1, source_target_pairs={{0,16},{16,32},{32,48},{48,64},{64,80},{80,96},{96,112},{112,128},... | collective-permute-start | bytes 208904 | tf_op jit(solution)/shard_map/ppermute | solution.py:20
  47.0 2.7 %collective-permute-start.11 = (bf16[272,128]{1,0:T(8,128)(2,1)S(1)}, bf16[272,128]{1,0:T(8,128)(2,1)S(1)}, u32[]{:S(2)}, u32[]{:S(2)}) collective-permute-start(bf16[272,128]{1,0:T(8,128)(2,1)S(1)} %collective-permute-done.3.rest_1_), channel_id=1, source_target_pairs={{0,16},{16,32},{32,48},{48,64},{64,80},{80,96},{96,112},{112,128},... | collective-permute-start | bytes 208904 | tf_op jit(solution)/shard_map/ppermute | solution.py:20
  53.4 3.8 %own_forward.1 = (bf16[1024,128]{1,0:T(8,128)(2,1)S(1)}, bf16[1024,128]{1,0:T(8,128)(2,1)S(1)}, s32[8]{0:T(128)S(1)}, s32[4]{0:T(128)S(1)}, bf16[10,256,512]{2,1...) custom-call(s32[2]{0:T(128)S(1)} %get-tuple-element.37.block_ref, ...), custom_call_target="tpu_custom_call" | custom-call | flops 671088640 | bytes 4194304 | tf_op jit(solution)/shard_map/own_forward/pallas_call | solution.py:337
  57.3 2.0 %prev_forward_theirs.1 = (bf16[2,4,256,512]{3,2,1,0:T(8,128)(2,1)S(1)}, f32[2,1,512]{2,1,0:T(1,128)S(1)}, f32[3,2,1,512]{3,2,1,0:T(1,128)S(1)}, bf16[2,128,512]{2,1,0:T(8,128)(2,1)S(1)}) custom-call(s32[1]{0:T(128)} %bitcast.has_ref, bf16[4,512,128]{2,1,0:T(8,128)(2,1)S(1)} %get-tuple-element.35.qs_ref, bf16[4,128,512]{2,1,0:T(8,128)(2,1)S(1)} %get-tuple-element.36.dot_ref, ...), custom_call_target="tpu_custom_call" | custom-call | flops 536870912 | bytes 4194304 | tf_op jit(solution)/shard_map/prev_forward_theirs/pallas_call | solution.py:337
  59.8 2.0 %prev_forward_mine.1 = (bf16[2,4,256,512]{3,2,1,0:T(8,128)(2,1)S(1)}, f32[2,1,512]{2,1,0:T(1,128)S(1)}, f32[3,2,1,512]{3,2,1,0:T(1,128)S(1)}, f32[2,128,512]{2,1,0:T(8,128)S(1)}) custom-call(s32[1]{0:T(128)} %bitcast.has_ref, bf16[4,512,128]{2,1,0:T(8,128)(2,1)S(1)} %get-tuple-element.35.qs_ref, bf16[4,128,512]{2,1,0:T(8,128)(2,1)S(1)} %get-tuple-element.36.dot_ref, ...), custom_call_target="tpu_custom_call" | custom-call | flops 536870912 | bytes 4194304 | tf_op jit(solution)/shard_map/prev_forward_mine/pallas_call | solution.py:337
  62.9 2.4 %prev_backward_mine.1 = (f32[1024,256]{1,0:T(8,128)S(1)}, bf16[2,128,512]{2,1,0:T(8,128)(2,1)S(1)}, f32[2,1,512]{2,1,0:T(1,128)S(1)}, bf16[2,4,256,512]{3,2,1,0:T(8,128)(2,1)S(1)}, f32[2,2,1,512]{3,2,1,0:T(1,128)S(1)}) custom-call(s32[1]{0:T(128)} %bitcast.has_ref, s32[8]{0:T(128)S(1)} %and_select_fusion.place_ref, ...), custom_call_target="tpu_custom_call" | custom-call | flops 1073741824 | bytes 4194304 | tf_op jit(solution)/shard_map/prev_backward_mine/pallas_call | solution.py:337
  65.4 2.8 %prev_backward_theirs.1 = (bf16[8,128,256]{2,1,0:T(8,128)(2,1)S(1)}, bf16[2,128,512]{2,1,0:T(8,128)(2,1)S(1)}, f32[2,1,512]{2,1,0:T(1,128)S(1)}, bf16[2,4,256,512]{3,2,1,0:T(8,128)(2,1)S(1)}) custom-call(s32[1]{0:T(128)} %bitcast.has_ref, s32[8]{0:T(128)S(1)} %and_select_fusion.place_ref, bf16[4,512,128]{2,1,0:T(8,128)(2,1)S(1)} %get-tuple-element.35.qs_ref, ...), custom_call_target="tpu_custom_call" | custom-call | flops 1073741824 | bytes 4194304 | tf_op jit(solution)/shard_map/prev_backward_theirs/pallas_call | solution.py:337
  68.2 2.6 %collective-permute-start.22 = (bf16[8,128,256]{2,1,0:T(8,128)(2,1)S(1)}, bf16[8,128,256]{2,1,0:T(8,128)(2,1)S(1)}, u32[]{:S(2)}, u32[]{:S(2)}) collective-permute-start(bf16[8,128,256]{2,1,0:T(8,128)(2,1)S(1)} %get-tuple-element.65), channel_id=1, source_target_pairs={{16,0},{32,16},{48,32},{64,48},{80,64},{96,80},{112,96},{128,112},... | collective-permute-start | bytes 1572872 | tf_op jit(solution)/shard_map/ppermute | solution.py:20
  70.8 4.8 %own_backward.1 = (f32[128,1024]{1,0:T(8,128)S(1)}, bf16[128,1024]{1,0:T(8,128)(2,1)S(1)}, bf16[8,128,256]{2,1,0:T(8,128)(2,1)S(1)}) custom-call(s32[4]{0:T(128)S(1)} %get-tuple-element.48.allowed_ref, s32[8]{0:T(128)S(1)} %get-tuple-element.49.slots_ref, s32[8]{0:T(128)S(1)} %and_select_fusion.place_ref, bf16[4,512,128]{2,1,0:T(8,128)(2,1)S(1)} %get-tuple-element.35.qs_ref, ...), custom_call_target="tpu_custom_call" | custom-call | flops 1342177280 | bytes 4194304 | tf_op jit(solution)/shard_map/own_backward/pallas_call | solution.py:337
  75.6 3.1 %collective-permute-done.22 = bf16[8,128,256]{2,1,0:T(8,128)(2,1)S(1)} collective-permute-done((bf16[8,128,256]{2,1,0:T(8,128)(2,1)S(1)}, bf16[8,128,256]{2,1,0:T(8,128)(2,1)S(1)}, u32[]{:S(2)}, u32[]{:S(2)}) %collective-permute-start.22) | collective-permute-done | bytes 524320 | tf_op jit(solution)/shard_map/ppermute | solution.py:20
  79.6 5.7 %all-to-all-start = ((bf16[8,128,256]{2,1,0:T(8,128)(2,1)}), bf16[8,128,256]{2,1,0:T(8,128)(2,1)S(1)}, u32[]{:S(2)}, u32[]{:S(2)}) async-start(bf16[8,128,256]{2,1,0:T(8,128)(2,1)} %add_convert_fusion), calls=%async_computation | async-start | bytes 1048576 | tf_op jit(solution)/shard_map/all_to_all | solution.py:35
  86.8 6.8 %collective-permute-done.18.got_ref = bf16[2,128,512]{2,1,0:T(8,128)(2,1)S(1)} collective-permute-done((bf16[2,128,512]{2,1,0:T(8,128)(2,1)S(1)}, bf16[2,128,512]{2,1,0:T(8,128)(2,1)S(1)}, u32[]{:S(2)}, u32[]{:S(2)}) %collective-permute-start.18) | collective-permute-done | bytes 262176 | tf_op jit(solution)/shard_map/ppermute | solution.py:24
  94.4 4.2 %collective-permute-done.21 = bf16[128,1024]{1,0:T(8,128)(2,1)S(1)} collective-permute-done((bf16[128,1024]{1,0:T(8,128)(2,1)S(1)}, bf16[128,1024]{1,0:T(8,128)(2,1)S(1)}, u32[]{:S(2)}, u32[]{:S(2)}) %collective-permute-start.21) | collective-permute-done | bytes 262176 | tf_op jit(solution)/shard_map/ppermute | solution.py:24
  99.3 3.6 %all-to-all-done = bf16[8,128,256]{2,1,0:T(8,128)(2,1)S(1)} async-done(((bf16[8,128,256]{2,1,0:T(8,128)(2,1)}), bf16[8,128,256]{2,1,0:T(8,128)(2,1)S(1)}, u32[]{:S(2)}, u32[]{:S(2)}) %all-to-all-start) | async-done | bytes 524320 | tf_op jit(solution)/shard_map/all_to_all | solution.py:35
  (46 shorter events, 17.8 us)
Async XLA Ops:
  2.1 17.3 %collective-permute-start.10 = (bf16[272,128]{1,0:T(8,128)(2,1)}, bf16[272,128]{1,0:T(8,128)(2,1)S(1)}, u32[]{:S(2)}, u32[]{:S(2)}) collective-permute-start(bf16[272,128]{1,0:T(8,128)(2,1)} %pack.1.rest_0_), channel_id=1, source_target_pairs={{0,16},{16,32},{32,48},{48,64},{64,80},{80,96},{96,112},{112,128},... | collective-permute-start | bytes 208904 | tf_op jit(solution)/shard_map/ppermute | solution.py:20
  5.5 15.5 %collective-permute-start.9 = (bf16[272,128]{1,0:T(8,128)(2,1)}, bf16[272,128]{1,0:T(8,128)(2,1)S(1)}, u32[]{:S(2)}, u32[]{:S(2)}) collective-permute-start(bf16[272,128]{1,0:T(8,128)(2,1)} %pack.1.rest_0_), channel_id=1, source_target_pairs={{0,8},{1,9},{2,10},{3,11},{4,12},{5,13},{6,14},{7,15},{8,0},{9,1},... | collective-permute-start | bytes 208904 | tf_op jit(solution)/shard_map/ppermute | solution.py:29
  12.5 10.7 %collective-permute-start.8 = (bf16[272,128]{1,0:T(8,128)(2,1)}, bf16[272,128]{1,0:T(8,128)(2,1)S(1)}, u32[]{:S(2)}, u32[]{:S(2)}) collective-permute-start(bf16[272,128]{1,0:T(8,128)(2,1)} %pack.1.rest_0_), channel_id=1, source_target_pairs={{0,10},{1,11},{2,12},{3,13},{4,14},{5,15},{6,0},{7,1},{8,2},{9,3},... | collective-permute-start | bytes 208904 | tf_op jit(solution)/shard_map/ppermute | solution.py:29
  12.5 12.0 %collective-permute-start.7 = (bf16[272,128]{1,0:T(8,128)(2,1)}, bf16[272,128]{1,0:T(8,128)(2,1)S(1)}, u32[]{:S(2)}, u32[]{:S(2)}) collective-permute-start(bf16[272,128]{1,0:T(8,128)(2,1)} %pack.1.rest_0_), channel_id=1, source_target_pairs={{0,6},{1,7},{2,8},{3,9},{4,10},{5,11},{6,12},{7,13},{8,14},{9,15},... | collective-permute-start | bytes 208904 | tf_op jit(solution)/shard_map/ppermute | solution.py:29
  15.7 2.8 %collective-permute-start = (s32[128]{0:T(128)}, s32[128]{0:T(128)S(1)}, u32[]{:S(2)}, u32[]{:S(2)}) collective-permute-start(s32[128]{0:T(128)} %position_ref.3), channel_id=1, source_target_pairs={{0,1},{1,0},{2,3},{3,2},{4,5},{5,4},{6,7},{7,6},{8,9},{9,8},{10,11... | collective-permute-start | bytes 1544 | tf_op jit(solution)/shard_map/ppermute | solution.py:24
  18.6 6.1 %collective-permute-start.6 = (bf16[272,128]{1,0:T(8,128)(2,1)}, bf16[272,128]{1,0:T(8,128)(2,1)S(1)}, u32[]{:S(2)}, u32[]{:S(2)}) collective-permute-start(bf16[272,128]{1,0:T(8,128)(2,1)} %pack.1.rest_0_), channel_id=1, source_target_pairs={{0,12},{1,13},{2,14},{3,15},{4,0},{5,1},{6,2},{7,3},{8,4},{9,5},{1... | collective-permute-start | bytes 208904 | tf_op jit(solution)/shard_map/ppermute | solution.py:29
  19.3 5.7 %collective-permute-start.5 = (bf16[272,128]{1,0:T(8,128)(2,1)}, bf16[272,128]{1,0:T(8,128)(2,1)S(1)}, u32[]{:S(2)}, u32[]{:S(2)}) collective-permute-start(bf16[272,128]{1,0:T(8,128)(2,1)} %pack.1.rest_0_), channel_id=1, source_target_pairs={{0,4},{1,5},{2,6},{3,7},{4,8},{5,9},{6,10},{7,11},{8,12},{9,13},{1... | collective-permute-start | bytes 208904 | tf_op jit(solution)/shard_map/ppermute | solution.py:29
  21.0 9.6 %collective-permute-start.4 = (bf16[272,128]{1,0:T(8,128)(2,1)}, bf16[272,128]{1,0:T(8,128)(2,1)S(1)}, u32[]{:S(2)}, u32[]{:S(2)}) collective-permute-start(bf16[272,128]{1,0:T(8,128)(2,1)} %pack.1.rest_0_), channel_id=1, source_target_pairs={{0,14},{1,15},{2,0},{3,1},{4,2},{5,3},{6,4},{7,5},{8,6},{9,7},{10,... | collective-permute-start | bytes 208904 | tf_op jit(solution)/shard_map/ppermute | solution.py:29
  23.2 20.7 %collective-permute-start.1 = (bf16[128,1024]{1,0:T(8,128)(2,1)}, bf16[128,1024]{1,0:T(8,128)(2,1)S(1)}, u32[]{:S(2)}, u32[]{:S(2)}) collective-permute-start(bf16[128,1024]{1,0:T(8,128)(2,1)} %q_ref.1), channel_id=1, source_target_pairs={{0,1},{1,0},{2,3},{3,2},{4,5},{5,4},{6,7},{7,6},{8,9},{9,8},{10,11... | collective-permute-start | bytes 786440 | tf_op jit(solution)/shard_map/ppermute | solution.py:24
  24.5 22.5 %collective-permute-start.2 = (bf16[128,1024]{1,0:T(8,128)(2,1)}, bf16[128,1024]{1,0:T(8,128)(2,1)S(1)}, u32[]{:S(2)}, u32[]{:S(2)}) collective-permute-start(bf16[128,1024]{1,0:T(8,128)(2,1)} %do_ref.1), channel_id=1, source_target_pairs={{0,1},{1,0},{2,3},{3,2},{4,5},{5,4},{6,7},{7,6},{8,9},{9,8},{10,11... | collective-permute-start | bytes 786440 | tf_op jit(solution)/shard_map/ppermute | solution.py:24
  24.7 8.7 %collective-permute-start.3 = (bf16[272,128]{1,0:T(8,128)(2,1)}, bf16[272,128]{1,0:T(8,128)(2,1)S(1)}, u32[]{:S(2)}, u32[]{:S(2)}) collective-permute-start(bf16[272,128]{1,0:T(8,128)(2,1)} %pack.1.rest_0_), channel_id=1, source_target_pairs={{0,2},{1,3},{2,4},{3,5},{4,6},{5,7},{6,8},{7,9},{8,10},{9,11},{10,... | collective-permute-start | bytes 208904 | tf_op jit(solution)/shard_map/ppermute | solution.py:29
  25.0 13.4 %collective-permute-start.17 = (bf16[272,128]{1,0:T(8,128)(2,1)S(1)}, bf16[272,128]{1,0:T(8,128)(2,1)S(1)}, u32[]{:S(2)}, u32[]{:S(2)}) collective-permute-start(bf16[272,128]{1,0:T(8,128)(2,1)S(1)} %collective-permute-done.9.rest_7_), channel_id=1, source_target_pairs={{0,16},{16,32},{32,48},{48,64},{64,80},{80,96},{96,112},{112,128},... | collective-permute-start | bytes 208904 | tf_op jit(solution)/shard_map/ppermute | solution.py:20
  30.6 9.8 %collective-permute-start.16 = (bf16[272,128]{1,0:T(8,128)(2,1)S(1)}, bf16[272,128]{1,0:T(8,128)(2,1)S(1)}, u32[]{:S(2)}, u32[]{:S(2)}) collective-permute-start(bf16[272,128]{1,0:T(8,128)(2,1)S(1)} %collective-permute-done.8.rest_6_), channel_id=1, source_target_pairs={{0,16},{16,32},{32,48},{48,64},{64,80},{80,96},{96,112},{112,128},... | collective-permute-start | bytes 208904 | tf_op jit(solution)/shard_map/ppermute | solution.py:20
  33.4 23.9 %collective-permute-start.15 = (bf16[272,128]{1,0:T(8,128)(2,1)S(1)}, bf16[272,128]{1,0:T(8,128)(2,1)S(1)}, u32[]{:S(2)}, u32[]{:S(2)}) collective-permute-start(bf16[272,128]{1,0:T(8,128)(2,1)S(1)} %collective-permute-done.7.rest_5_), channel_id=1, source_target_pairs={{0,16},{16,32},{32,48},{48,64},{64,80},{80,96},{96,112},{112,128},... | collective-permute-start | bytes 208904 | tf_op jit(solution)/shard_map/ppermute | solution.py:20
  38.4 18.8 %collective-permute-start.14 = (bf16[272,128]{1,0:T(8,128)(2,1)S(1)}, bf16[272,128]{1,0:T(8,128)(2,1)S(1)}, u32[]{:S(2)}, u32[]{:S(2)}) collective-permute-start(bf16[272,128]{1,0:T(8,128)(2,1)S(1)} %collective-permute-done.6.rest_4_), channel_id=1, source_target_pairs={{0,16},{16,32},{32,48},{48,64},{64,80},{80,96},{96,112},{112,128},... | collective-permute-start | bytes 208904 | tf_op jit(solution)/shard_map/ppermute | solution.py:20
  40.4 16.9 %collective-permute-start.13 = (bf16[272,128]{1,0:T(8,128)(2,1)S(1)}, bf16[272,128]{1,0:T(8,128)(2,1)S(1)}, u32[]{:S(2)}, u32[]{:S(2)}) collective-permute-start(bf16[272,128]{1,0:T(8,128)(2,1)S(1)} %collective-permute-done.5.rest_3_), channel_id=1, source_target_pairs={{0,16},{16,32},{32,48},{48,64},{64,80},{80,96},{96,112},{112,128},... | collective-permute-start | bytes 208904 | tf_op jit(solution)/shard_map/ppermute | solution.py:20
  43.9 13.4 %collective-permute-start.12 = (bf16[272,128]{1,0:T(8,128)(2,1)S(1)}, bf16[272,128]{1,0:T(8,128)(2,1)S(1)}, u32[]{:S(2)}, u32[]{:S(2)}) collective-permute-start(bf16[272,128]{1,0:T(8,128)(2,1)S(1)} %collective-permute-done.4.rest_2_), channel_id=1, source_target_pairs={{0,16},{16,32},{32,48},{48,64},{64,80},{80,96},{96,112},{112,128},... | collective-permute-start | bytes 208904 | tf_op jit(solution)/shard_map/ppermute | solution.py:20
  47.0 10.3 %collective-permute-start.11 = (bf16[272,128]{1,0:T(8,128)(2,1)S(1)}, bf16[272,128]{1,0:T(8,128)(2,1)S(1)}, u32[]{:S(2)}, u32[]{:S(2)}) collective-permute-start(bf16[272,128]{1,0:T(8,128)(2,1)S(1)} %collective-permute-done.3.rest_1_), channel_id=1, source_target_pairs={{0,16},{16,32},{32,48},{48,64},{64,80},{80,96},{96,112},{112,128},... | collective-permute-start | bytes 208904 | tf_op jit(solution)/shard_map/ppermute | solution.py:20
  59.3 3.6 %collective-permute-start.19 = (f32[3,2,1,512]{3,2,1,0:T(1,128)S(1)}, f32[3,2,1,512]{3,2,1,0:T(1,128)S(1)}, u32[]{:S(2)}, u32[]{:S(2)}) collective-permute-start(f32[3,2,1,512]{3,2,1,0:T(1,128)S(1)} %get-tuple-element.46.stats_ref), channel_id=1, source_target_pairs={{0,1},{1,0},{2,3},{3,2},{4,5},{5,4},{6,7},{7,6},{8,9},{9,8},{10,11... | collective-permute-start | bytes 36872 | tf_op jit(solution)/shard_map/ppermute | solution.py:24
  61.8 3.6 %collective-permute-start.20 = (f32[3,2,1,512]{3,2,1,0:T(1,128)S(1)}, f32[3,2,1,512]{3,2,1,0:T(1,128)S(1)}, u32[]{:S(2)}, u32[]{:S(2)}) collective-permute-start(f32[3,2,1,512]{3,2,1,0:T(1,128)S(1)} %get-tuple-element.45.stats_ref), channel_id=1, source_target_pairs={{0,1},{1,0},{2,3},{3,2},{4,5},{5,4},{6,7},{7,6},{8,9},{9,8},{10,11... | collective-permute-start | bytes 36872 | tf_op jit(solution)/shard_map/ppermute | solution.py:24
  68.2 10.5 %collective-permute-start.22 = (bf16[8,128,256]{2,1,0:T(8,128)(2,1)S(1)}, bf16[8,128,256]{2,1,0:T(8,128)(2,1)S(1)}, u32[]{:S(2)}, u32[]{:S(2)}) collective-permute-start(bf16[8,128,256]{2,1,0:T(8,128)(2,1)S(1)} %get-tuple-element.65), channel_id=1, source_target_pairs={{16,0},{32,16},{48,32},{64,48},{80,64},{96,80},{112,96},{128,112},... | collective-permute-start | bytes 1572872 | tf_op jit(solution)/shard_map/ppermute | solution.py:20
  79.6 23.3 %all-to-all-start = ((bf16[8,128,256]{2,1,0:T(8,128)(2,1)}), bf16[8,128,256]{2,1,0:T(8,128)(2,1)S(1)}, u32[]{:S(2)}, u32[]{:S(2)}) async-start(bf16[8,128,256]{2,1,0:T(8,128)(2,1)} %add_convert_fusion), calls=%async_computation | async-start | bytes 1048576 | tf_op jit(solution)/shard_map/all_to_all | solution.py:35
  85.3 8.2 %collective-permute-start.18 = (bf16[2,128,512]{2,1,0:T(8,128)(2,1)S(1)}, bf16[2,128,512]{2,1,0:T(8,128)(2,1)S(1)}, u32[]{:S(2)}, u32[]{:S(2)}) collective-permute-start(bf16[2,128,512]{2,1,0:T(8,128)(2,1)S(1)} %get-tuple-element.42), channel_id=1, source_target_pairs={{0,1},{1,0},{2,3},{3,2},{4,5},{5,4},{6,7},{7,6},{8,9},{9,8},{10,11... | collective-permute-start | bytes 786440 | tf_op jit(solution)/shard_map/ppermute | solution.py:24
  85.7 12.9 %collective-permute-start.21 = (bf16[128,1024]{1,0:T(8,128)(2,1)S(1)}, bf16[128,1024]{1,0:T(8,128)(2,1)S(1)}, u32[]{:S(2)}, u32[]{:S(2)}) collective-permute-start(bf16[128,1024]{1,0:T(8,128)(2,1)S(1)} %get-tuple-element.63), channel_id=1, source_target_pairs={{0,1},{1,0},{2,3},{3,2},{4,5},{5,4},{6,7},{7,6},{8,9},{9,8},{10,11... | collective-permute-start | bytes 786440 | tf_op jit(solution)/shard_map/ppermute | solution.py:24
  (4 other events, 22.6 us)

commit v10 on v7

v10 whole, which is shorter than its diff:
```python
import functools

import jax
import jax.numpy as jnp
from jax import lax
from jax.experimental import pallas as pl
from jax.experimental.pallas import tpu as pltpu
from jax.sharding import PartitionSpec as P

masked_score = -1e30
tile_keys = 256
log2_e = 1.4426950408889634
block_rows = 64
tag_rows = 16


def from_behind(block, axis, distance):
    devices = range(lax.axis_size(axis))
    route = [(i - distance, i) for i in devices if i - distance in devices]
    return lax.ppermute(block, axis, route)


def to_partner(block, axis):
    return lax.ppermute(block, axis, [(i, i ^ 1) for i in range(lax.axis_size(axis))])


def to_corner(block, distance):
    outer, inner = lax.axis_size("outer"), lax.axis_size("inner")
    route = [
        (o * inner + i, (o + distance) * inner + (i ^ 1))
        for o in range(outer)
        for i in range(inner)
        if o + distance in range(outer)
    ]
    return lax.ppermute(block, ("outer", "inner"), route)


def exchange(parts, axis):
    count = lax.axis_size(axis)
    groups = [list(range(first, count, 2)) for first in range(2)]
    return lax.all_to_all(parts, axis, 0, 0, axis_index_groups=groups, tiled=True)


def dot_nn(a, b):
    return lax.dot_general(a, b, (((1,), (0,)), ((), ())), preferred_element_type=jnp.float32)


def dot_nt(a, b):
    return lax.dot_general(a, b, (((1,), (1,)), ((), ())), preferred_element_type=jnp.float32)


def dot_tn(a, b):
    return lax.dot_general(a, b, (((0,), (0,)), ((), ())), preferred_element_type=jnp.float32)


def stack_heads(source, start, heads, head_dim):
    rows = slice(start, start + block_rows)
    return jnp.concatenate(
        [source[rows, h * head_dim : (h + 1) * head_dim] for h in range(heads)], axis=0
    )


def store_heads(target_ref, half, block):
    rows = slice(half * block_rows, (half + 1) * block_rows)
    head_dim = block.shape[1]
    for h in range(block.shape[0] // block_rows):
        target_ref[rows, h * head_dim : (h + 1) * head_dim] = block[
            h * block_rows : (h + 1) * block_rows
        ].astype(target_ref.dtype)


def pack(position_ref, key_ref, value_ref, packed_ref, place_ref, block_ref, in_sems, out_sems):
    count, rows, head_dim = packed_ref.shape
    span = key_ref.shape[0]
    loads = [
        pltpu.make_async_copy(position_ref, place_ref, in_sems.at[0]),
        pltpu.make_async_copy(key_ref, block_ref.at[pl.ds(0, span)], in_sems.at[1]),
        pltpu.make_async_copy(value_ref, block_ref.at[pl.ds(span, span)], in_sems.at[2]),
    ]
    for load in loads:
        load.start()
    loads[0].wait()
    tag = (lax.rem(place_ref[0], 2 * count * span) // block_rows).astype(jnp.float32)
    tag = jnp.full((rows - 2 * span, head_dim), tag, jnp.float32)
    block_ref[2 * span :, :] = tag.astype(packed_ref.dtype)
    loads[1].wait()
    loads[2].wait()
    stores = [
        pltpu.make_async_copy(block_ref, packed_ref.at[g], out_sems.at[g]) for g in range(count)
    ]
    for store in stores:
        store.start()
    for store in stores:
        store.wait()


def stack_pair(both_ref, partner_ref, qs_ref, dot_ref):
    _, width, head_dim = qs_ref.shape
    heads = width // block_rows
    span = 2 * block_rows
    for j, source in enumerate((both_ref, partner_ref)):
        for half in range(2):
            start = half * block_rows
            qs_ref[2 * j + half] = stack_heads(source, start, heads, head_dim)
            stacked = stack_heads(source, span + start, heads, head_dim).astype(jnp.float32)
            dot_ref[2 * j + half] = stacked.T.astype(jnp.bfloat16)


def merge_attended(out_ref, got_pair_ref, got_next_ref, got_corner_ref, factor_ref, att_ref):
    for half in range(2):
        out = factor_ref[0, half] * out_ref[half]
        for k, got_ref in enumerate((got_pair_ref, got_next_ref, got_corner_ref)):
            out = out + factor_ref[1 + k, half] * got_ref[half].astype(jnp.float32)
        store_heads(att_ref, half, out.T)


def combine(stats, at, exponent_scale, valid=None):
    places = [at, (at + 2) % 4, at, (at + 2) % 4]
    peaks = [ref[0, place] for ref, place in zip(stats, places)]
    if valid is not None:
        peaks[2:] = [jnp.where(valid, peak, masked_score) for peak in peaks[2:]]
    top = functools.reduce(jnp.maximum, peaks)
    factors = [jnp.exp2((peak - top) * exponent_scale) for peak in peaks]
    totals = [factor * ref[1, place] for factor, ref, place in zip(factors, stats, places)]
    inverse = 1.0 / sum(totals)
    delta = sum(factor * ref[2, place] for factor, ref, place in zip(factors, stats, places)) * inverse
    return factors[0] * inverse, [total * inverse for total in totals], delta


def put_stats(stats_ref, at, peak, total, out, grad):
    stats_ref[0, at] = peak
    stats_ref[1, at] = total
    stats_ref[2, at] = jnp.sum(grad.astype(jnp.float32) * out, axis=0, keepdims=True)
    return (out * jnp.where(total > 0, 1.0 / total, 0.0)).astype(jnp.bfloat16)


def own_tile(step, allowed_ref):
    low = 0 if step < 5 else 2
    local = step % 5
    per_tile = tile_keys // block_rows
    low_tiles = (allowed_ref[low] + per_tile - 1) // per_tile
    high = jnp.where(local >= low_tiles, 1, 0)
    tile = local - high * low_tiles
    return low + high, tile


def own_forward(
    segment, position_ref, position_partner_ref, qs_ref, dot_ref, kv_ref,
    ks_ref, vs_ref, slots_ref, allowed_ref, p_ref, stats_ref, out_ref, sent_ref,
    s_ref, m_ref, l_ref, o_ref,
):
    group, _, head_dim = kv_ref.shape
    span = 2 * block_rows
    steps, _, width = p_ref.shape
    blocks = 2 * group
    tiles = blocks * block_rows // tile_keys
    exponent_scale = log2_e * float(head_dim) ** (-0.5)
    tags = [jnp.max(kv_ref[g, 2 * span :, :].astype(jnp.float32)).astype(jnp.int32) for g in range(group)]

    def count(test):
        return sum(jnp.where(test(tag), 1, 0) for tag in tags)

    for j in range(2):
        mine = lax.rem((position_ref, position_partner_ref)[j][0], segment) // block_rows
        allowed_ref[2 * j] = count(lambda tag: tag <= mine)
        allowed_ref[2 * j + 1] = blocks - count(lambda tag: tag < mine)
    for g in range(group):
        slot = count(lambda tag: tag < tags[g])
        slots_ref[g] = slot
        for half, place in ((0, slot), (1, blocks - 1 - slot)):
            target = pl.ds(pl.multiple_of(place * block_rows, block_rows), block_rows)
            rows = slice(half * block_rows, (half + 1) * block_rows)
            ks_ref[target, :] = kv_ref[g, rows, :]
            rows = slice(span + half * block_rows, span + (half + 1) * block_rows)
            vs_ref[target, :] = kv_ref[g, rows, :]
    m_ref[...] = jnp.full(m_ref.shape, masked_score, jnp.float32)
    l_ref[...] = jnp.zeros(l_ref.shape, jnp.float32)
    o_ref[...] = jnp.zeros(o_ref.shape, jnp.float32)
    key_row = lax.broadcasted_iota(jnp.int32, (tile_keys, width), 0)
    query_row = lax.rem(lax.broadcasted_iota(jnp.int32, (1, width), 1), block_rows)
    for step in range(steps):
        at, tile = own_tile(step, allowed_ref)
        start = pl.multiple_of(jnp.minimum(tile, tiles - 1) * tile_keys, tile_keys)
        scores = dot_nt(ks_ref[pl.ds(start, tile_keys), :], qs_ref[at])
        last = query_row if step < 5 else block_rows - 1
        limit = (allowed_ref[at] - 1) * block_rows + last - tile * tile_keys
        scores = jnp.where(key_row <= limit, scores, masked_score)
        s_ref[step] = scores
        m_ref[at] = jnp.maximum(m_ref[at], jnp.max(scores, axis=0, keepdims=True))
    for step in range(steps):
        at, tile = own_tile(step, allowed_ref)
        start = pl.multiple_of(jnp.minimum(tile, tiles - 1) * tile_keys, tile_keys)
        raised = jnp.exp2((s_ref[step] - m_ref[at]) * exponent_scale)
        l_ref[at] += jnp.sum(raised, axis=0, keepdims=True)
        raised = raised.astype(jnp.bfloat16)
        p_ref[step] = raised
        o_ref[at] += dot_tn(vs_ref[pl.ds(start, tile_keys), :], raised)


    for at in range(4):
        shared = put_stats(stats_ref, at, m_ref[at], l_ref[at], o_ref[at], dot_ref[at])
        if at < 2:
            out_ref[at] = o_ref[at]
        else:
            sent_ref[at - 2] = shared


def next_forward(
    qs_ref, dot_ref, ks_ref, vs_ref, p_ref, stats_ref, sent_ref, sent_corner_ref, s_ref
):
    sets, width, head_dim = qs_ref.shape
    tiles = p_ref.shape[1]
    exponent_scale = log2_e * float(head_dim) ** (-0.5)
    peaks = []
    for at in range(sets):
        peak = jnp.full((1, width), masked_score, jnp.float32)
        for tile in range(tiles):
            scores = dot_nt(ks_ref[tile * tile_keys : (tile + 1) * tile_keys, :], qs_ref[at])
            s_ref[at, tile] = scores
            peak = jnp.maximum(peak, jnp.max(scores, axis=0, keepdims=True))
        peaks.append(peak)
    for at in range(sets):
        total = jnp.zeros((1, width), jnp.float32)
        out = jnp.zeros((head_dim, width), jnp.float32)
        for tile in range(tiles):
            raised = jnp.exp2((s_ref[at, tile] - peaks[at]) * exponent_scale)
            total += jnp.sum(raised, axis=0, keepdims=True)
            raised = raised.astype(jnp.bfloat16)
            p_ref[at, tile] = raised
            out += dot_tn(vs_ref[tile * tile_keys : (tile + 1) * tile_keys, :], raised)
        shared = put_stats(stats_ref, at, peaks[at], total, out, dot_ref[at])
        (sent_ref, sent_corner_ref)[at // 2][at % 2] = shared


def next_backward(
    qs_ref, dot_ref, ks_ref, vs_ref, p_ref, stats_ref, other_ref, ahead_ref, corner_ref,
    terms_ref, dq_ref, dq_corner_ref, scaled_ref, lower_ref, dqa_ref,
):
    sets, width, head_dim = qs_ref.shape
    tiles = p_ref.shape[1]
    scale = float(head_dim) ** (-0.5)
    for at in range(sets):
        factor, _, delta = combine((stats_ref, other_ref, ahead_ref, corner_ref), at, log2_e * scale)
        scaled_ref[at] = (dot_ref[at].astype(jnp.float32) * factor).astype(jnp.bfloat16)
        lower_ref[at] = delta * factor
    for tile in range(tiles):
        rows = slice(tile * tile_keys, (tile + 1) * tile_keys)
        keys, values = ks_ref[rows, :], vs_ref[rows, :]
        key_grad = jnp.zeros((tile_keys, head_dim), jnp.float32)
        value_grad = jnp.zeros((tile_keys, head_dim), jnp.float32)
        for at in range(sets):
            weights = p_ref[at, tile]
            value_grad += dot_nt(weights, scaled_ref[at])
            change = dot_nn(values, scaled_ref[at]) - lower_ref[at]
            change = (weights.astype(jnp.float32) * change).astype(jnp.bfloat16)
            key_grad += dot_nn(change, qs_ref[at])
            query_grad = dot_tn(keys, change)
            dqa_ref[at] = query_grad if tile == 0 else dqa_ref[at] + query_grad
        terms_ref[rows, :head_dim] = key_grad * scale
        terms_ref[rows, head_dim:] = value_grad
    for half in range(2):
        store_heads(dq_ref, half, dqa_ref[half].T * scale)
        store_heads(dq_corner_ref, half, dqa_ref[2 + half].T * scale)


def own_backward(
    has_ref, allowed_ref, slots_ref, qs_ref, dot_ref, ks_ref, vs_ref, p_ref,
    stats_ref, other_ref, behind_ref, corner_ref, next_terms_ref,
    dq_ref, dq_partner_ref, terms_ref, factor_ref, acc_ref, dqa_ref, dos_ref, shift_ref,
):
    steps, _, width = p_ref.shape
    group, span, _ = terms_ref.shape
    head_dim = ks_ref.shape[1]
    blocks = 2 * group
    tiles = blocks * block_rows // tile_keys
    scale = float(head_dim) ** (-0.5)
    has_prev = has_ref[0] > 0
    for at in range(4):
        factor, shares, delta = combine(
            (stats_ref, other_ref, behind_ref, corner_ref), at, log2_e * scale, has_prev
        )
        dos_ref[at] = (dot_ref[at].astype(jnp.float32) * factor).astype(jnp.bfloat16)
        shift_ref[at] = delta * factor
        if at < 2:
            factor_ref[0, at] = factor
            for k in range(1, 4):
                factor_ref[k, at] = shares[k]
    acc_ref[...] = next_terms_ref[...]
    dqa_ref[...] = jnp.zeros(dqa_ref.shape, jnp.float32)
    for step in range(steps):
        at, tile = own_tile(step, allowed_ref)
        start = pl.multiple_of(jnp.minimum(tile, tiles - 1) * tile_keys, tile_keys)
        window = pl.ds(start, tile_keys)
        weights = p_ref[step]
        grad = dos_ref[at]
        acc_ref[window, head_dim:] += dot_nt(weights, grad)
        change = dot_nn(vs_ref[window, :], grad) - shift_ref[at]
        change = (weights.astype(jnp.float32) * change).astype(jnp.bfloat16)
        acc_ref[window, :head_dim] += dot_nn(change, qs_ref[at]) * scale
        dqa_ref[at] += dot_tn(ks_ref[window, :], change)
    for g in range(group):
        slot = slots_ref[g]
        for half, place in ((0, slot), (1, blocks - 1 - slot)):
            source = pl.ds(pl.multiple_of(place * block_rows, block_rows), block_rows)
            terms_ref[g, half * block_rows : (half + 1) * block_rows, :] = acc_ref[
                source, :
            ].astype(jnp.bfloat16)
    for half in range(2):
        store_heads(dq_ref, half, dqa_ref[half].T * scale)
        store_heads(dq_partner_ref, half, dqa_ref[2 + half].T * scale)


def call(kernel, name, outs, in_smem, scratch, out_smem=(), flops=0, stream=()):
    vmem = pl.BlockSpec(memory_space=pltpu.VMEM)
    smem = pl.BlockSpec(memory_space=pltpu.SMEM)

    def spec(at, operand):
        if at in in_smem:
            return smem
        if at in stream:
            return pl.BlockSpec(operand.shape, lambda step: (0,) * operand.ndim)
        return vmem

    def run(*operands):
        return pl.pallas_call(
            kernel,
            name=name,
            grid=(1,) if stream else (),
            out_shape=[jax.ShapeDtypeStruct(shape, dtype) for shape, dtype in outs],
            in_specs=[spec(i, operand) for i, operand in enumerate(operands)],
            out_specs=[smem if i in out_smem else vmem for i in range(len(outs))],
            scratch_shapes=[pltpu.VMEM(shape, dtype) for shape, dtype in scratch],
            compiler_params=pltpu.CompilerParams(vmem_limit_bytes=16 * 1024 * 1024),
            cost_estimate=pl.CostEstimate(flops=flops, bytes_accessed=4 << 20, transcendentals=0),
        )(*operands)

    return run


def body(queries, key_vectors, value_vectors, grad_output, positions):
    tok_rows, full_width = queries.shape
    head_dim = key_vectors.shape[1]
    heads = full_width // head_dim
    group = lax.axis_size("inner") // 2
    segment = 2 * group * tok_rows
    span_rows = group * tok_rows
    width = heads * block_rows
    steps = 10
    bf16, f32 = jnp.bfloat16, jnp.float32
    both = jnp.concatenate([queries, grad_output], axis=0)
    both_partner = to_partner(both, "inner")
    both_next = from_behind(both, "outer", -1)
    both_corner = to_partner(both_next, "inner")
    position_partner = to_partner(positions, "inner")
    anywhere = pl.BlockSpec(memory_space=pl.ANY)
    packed = pl.pallas_call(
        pack,
        name="pack",
        out_shape=jax.ShapeDtypeStruct((group, 2 * tok_rows + tag_rows, head_dim), bf16),
        in_specs=[anywhere] * 3,
        out_specs=anywhere,
        scratch_shapes=[
            pltpu.SMEM(positions.shape, jnp.int32),
            pltpu.VMEM((2 * tok_rows + tag_rows, head_dim), bf16),
            pltpu.SemaphoreType.DMA((3,)),
            pltpu.SemaphoreType.DMA((group,)),
        ],
        compiler_params=pltpu.CompilerParams(vmem_limit_bytes=60 * 1024 * 1024),
    )(positions, key_vectors, value_vectors)
    has_prev = (lax.axis_index("outer") > 0).astype(jnp.int32).reshape(1)
    packed, has_prev = lax.optimization_barrier((packed, has_prev))
    group_kv = exchange(packed, "inner")

    unit = 2 * tile_keys * width * head_dim
    tiles = span_rows // tile_keys
    stats_shape = ((3, 4, 1, width), f32)
    by_query = ((4, head_dim, width), f32)
    by_query_16 = ((4, head_dim, width), bf16)
    half_query = ((2, head_dim, width), f32)
    half_query_16 = ((2, head_dim, width), bf16)
    row_stat = ((4, 1, width), f32)
    stacked = ((4, width, head_dim), bf16)
    tokens = ((tok_rows, full_width), bf16)
    tokens_32 = ((tok_rows, full_width), f32)
    sorted_keys = ((span_rows, head_dim), bf16)
    terms_shape = ((group, tok_rows, 2 * head_dim), bf16)
    sum_shape = ((span_rows, 2 * head_dim), f32)

    qs, dot = call(stack_pair, "stack_pair", [stacked, by_query_16], (), [], flops=4 * 10**9)(
        both, both_partner
    )
    ks, vs, slots, allowed, p_own, stats_own, out, sent_pair = call(
        functools.partial(own_forward, segment),
        "own_forward",
        [
            sorted_keys,
            sorted_keys,
            ((group,), jnp.int32),
            ((4,), jnp.int32),
            ((steps, tile_keys, width), bf16),
            stats_shape,
            half_query,
            half_query_16,
        ],
        (0, 1),
        [((steps, tile_keys, width), f32), row_stat, row_stat, by_query],
        out_smem=(2, 3),
        flops=2 * steps * unit,
    )(positions, position_partner, qs, dot, group_kv)
    own_pair = to_partner(stats_own, "inner")
    own_ahead = from_behind(stats_own, "outer", -1)
    own_corner = to_corner(stats_own, -1)
    qs_next, dot_next = call(stack_pair, "stack_next", [stacked, by_query_16], (), [], flops=10**9)(
        both_next, both_corner
    )
    p_next, stats_next, sent_next, sent_corner = call(
        next_forward,
        "next_forward",
        [((4, tiles, tile_keys, width), bf16), stats_shape, half_query_16, half_query_16],
        (),
        [((4, tiles, tile_keys, width), f32)],
        flops=2 * 4 * tiles * unit,
    )(qs_next, dot_next, ks, vs)
    next_pair = to_partner(stats_next, "inner")
    next_behind = from_behind(stats_next, "outer", 1)
    next_corner = to_corner(stats_next, 1)
    next_terms, dq_next, dq_corner = call(
        next_backward,
        "next_backward",
        [sum_shape, tokens, tokens],
        (),
        [by_query_16, row_stat, by_query],
        flops=4 * 4 * tiles * unit,
    )(qs_next, dot_next, ks, vs, p_next, stats_next, next_pair, own_ahead, own_corner)
    dq, dq_partner, terms, factor = call(
        own_backward,
        "own_backward",
        [tokens_32, tokens, terms_shape, ((4, 2, 1, width), f32)],
        (0, 1, 2),
        [sum_shape, by_query, by_query_16, row_stat],
        flops=4 * steps * unit,
    )(has_prev, allowed, slots, qs, dot, ks, vs, p_own, stats_own, own_pair, next_behind, next_corner, next_terms)
    key_grads = jnp.sum(exchange(terms, "inner").astype(f32), axis=0)
    (attended,) = call(merge_attended, "merge_attended", [tokens], (), [])(
        out,
        to_partner(sent_pair, "inner"),
        from_behind(sent_next, "outer", 1),
        to_corner(sent_corner, 1),
        factor,
    )
    dq = dq + to_partner(dq_partner, "inner").astype(f32)
    dq = dq + from_behind(dq_next, "outer", 1).astype(f32)
    grad_queries = (dq + to_corner(dq_corner, 1).astype(f32)).astype(bf16)
    grad_keys = key_grads[:, :head_dim].astype(bf16)
    grad_values = key_grads[:, head_dim:].astype(bf16)
    return (attended, grad_queries, grad_keys, grad_values)


def solution(mesh):
    rows = P(("outer", "inner"), None)
    return jax.shard_map(
        body,
        mesh=mesh,
        in_specs=(rows, rows, rows, rows, P(("outer", "inner"))),
        out_specs=(rows, rows, rows, rows),
        check_vma=False,
    )
```

time: 88.2 us -> 111 us (1.26)
  the two profiles are of different devices: /device:TPU:16 before, /device:TPU:39 now
where the time goes in v10:
time: 111 us; the launch traced here: 110 us
  starting transfers between devices  50.5 us (45%)
  waiting for transfers between devices  33.1 us (30%)
  Pallas kernels  20.7 us (19%)
  local copies, waits for them, and re-layouts  3.27 us (3%)
  other arithmetic  1.96 us (2%)
    ppermute x5, starting transfers between devices, from_behind(): return lax.ppermute(block, axis, route)  22.3 us
    ppermute x7, waiting for transfers between devices, to_partner(): lax.ppermute(block, axis, [(i, i ^ 1) for i in range(lax.axis_size(axis))])  20.4 us
    pallas_call x7, Pallas kernels, run(): pl.pallas_call(kernel, name=name, grid=(1,) if stream else (), out_shape=...  19 us
    all_to_all x2, starting transfers between devices, exchange(): lax.all_to_all(parts, axis, 0, 0, axis_index_groups=groups, tiled=True)  14.7 us
    ppermute x4, waiting for transfers between devices, to_corner(): return lax.ppermute(block, ('outer', 'inner'), route)  12.2 us
    ppermute x4, starting transfers between devices, to_corner(): return lax.ppermute(block, ('outer', 'inner'), route)  9.04 us
    ppermute x7, starting transfers between devices, to_partner(): lax.ppermute(block, axis, [(i, i ^ 1) for i in range(lax.axis_size(axis))])  4.53 us
  transfers between devices with their start and end apart: 18, of which 5 were waited for; matrix products, arithmetic and copies ran while one was open for 1% of the time, Pallas kernels for 14%

profile of v10, /device:TPU:39, one launch (start us, length us, event | category | flops | bytes accessed | tf_op | source)
XLA Modules:
  0.0 110.4 jit_solution(13036559577515474289)
XLA Ops:
  2.6 2.6 %collective-permute-start.3 = (bf16[256,1024]{1,0:T(8,128)(2,1)S(1)}, bf16[256,1024]{1,0:T(8,128)(2,1)S(1)}, u32[]{:S(2)}, u32[]{:S(2)}) collective-permute-start(bf16[256,1024]{1,0:T(8,128)(2,1)S(1)} %constant_dynamic-update-slice_fusion.both_ref), channel_id=1, source_target_pairs={{16,0},{32,16},{48,32},{64,48},{80,64},{96,80},{112,96},{128,112},... | collective-permute-start | bytes 1572872 | tf_op jit(solution)/shard_map/ppermute | solution.py:20
  5.2 1.7 %pack.1 = bf16[8,272,128]{2,1,0:T(8,128)(2,1)} custom-call(s32[128]{0:T(128)} %position_ref.3, bf16[128,128]{1,0:T(8,128)(2,1)} %key_ref.1, bf16[128,128]{1,0:T(8,128)(2,1)} %value_ref.1), custom_call_target="tpu_custom_call" | custom-call | tf_op jit(solution)/shard_map/pack/pallas_call | solution.py:356
  6.9 8.0 %all-to-all-start = ((bf16[8,272,128]{2,1,0:T(8,128)(2,1)}), bf16[8,272,128]{2,1,0:T(8,128)(2,1)S(1)}, u32[]{:S(2)}, u32[]{:S(2)}) async-start(bf16[8,272,128]{2,1,0:T(8,128)(2,1)} %pack.1), calls=%async_computation | async-start | bytes 1114112 | tf_op jit(solution)/shard_map/all_to_all | solution.py:41
  14.9 1.3 %collective-permute-start.1 = (bf16[256,1024]{1,0:T(8,128)(2,1)S(1)}, bf16[256,1024]{1,0:T(8,128)(2,1)S(1)}, u32[]{:S(2)}, u32[]{:S(2)}) collective-permute-start(bf16[256,1024]{1,0:T(8,128)(2,1)S(1)} %constant_dynamic-update-slice_fusion.both_ref), channel_id=1, source_target_pairs={{0,1},{1,0},{2,3},{3,2},{4,5},{5,4},{6,7},{7,6},{8,9},{9,8},{10,11... | collective-permute-start | bytes 1572872 | tf_op jit(solution)/shard_map/ppermute | solution.py:24
  16.7 1.3 %collective-permute-start.4 = (bf16[256,1024]{1,0:T(8,128)(2,1)S(1)}, bf16[256,1024]{1,0:T(8,128)(2,1)S(1)}, u32[]{:S(2)}, u32[]{:S(2)}) collective-permute-start(bf16[256,1024]{1,0:T(8,128)(2,1)S(1)} %collective-permute-done.3.both_ref), channel_id=1, source_target_pairs={{0,1},{1,0},{2,3},{3,2},{4,5},{5,4},{6,7},{7,6},{8,9},{9,8},{10,11... | collective-permute-start | bytes 1572872 | tf_op jit(solution)/shard_map/ppermute | solution.py:24
  18.2 9.4 %collective-permute-done.1.partner_ref = bf16[256,1024]{1,0:T(8,128)(2,1)S(1)} collective-permute-done((bf16[256,1024]{1,0:T(8,128)(2,1)S(1)}, bf16[256,1024]{1,0:T(8,128)(2,1)S(1)}, u32[]{:S(2)}, u32[]{:S(2)}) %collective-permute-start.1) | collective-permute-done | bytes 524320 | tf_op jit(solution)/shard_map/ppermute | solution.py:24
  27.8 11.0 %collective-permute-done.position_partner_ref = s32[128]{0:T(128)S(1)} collective-permute-done((s32[128]{0:T(128)}, s32[128]{0:T(128)S(1)}, u32[]{:S(2)}, u32[]{:S(2)}) %collective-permute-start) | collective-permute-done | bytes 544 | tf_op jit(solution)/shard_map/ppermute | solution.py:24
  38.8 4.0 %own_forward.1 = (bf16[1024,128]{1,0:T(8,128)(2,1)S(1)}, bf16[1024,128]{1,0:T(8,128)(2,1)S(1)}, s32[8]{0:T(128)S(1)}, s32[4]{0:T(128)S(1)}, bf16[10,256,512]{2,1...) custom-call(s32[128]{0:T(128)S(1)} %copy-done, ...), custom_call_target="tpu_custom_call" | custom-call | flops 671088640 | bytes 4194304 | tf_op jit(solution)/shard_map/own_forward/pallas_call | solution.py:325
  42.8 3.7 %collective-permute-start.11 = (f32[3,4,1,512]{3,2,1,0:T(1,128)S(1)}, f32[3,4,1,512]{3,2,1,0:T(1,128)S(1)}, u32[]{:S(2)}, u32[]{:S(2)}) collective-permute-start(f32[3,4,1,512]{3,2,1,0:T(1,128)S(1)} %get-tuple-element.44.stats_ref), channel_id=1, source_target_pairs={{16,0},{32,16},{48,32},{64,48},{80,64},{96,80},{112,96},{128,112},... | collective-permute-start | bytes 73736 | tf_op jit(solution)/shard_map/ppermute | solution.py:20
  46.5 3.1 %collective-permute-start.12 = (f32[3,4,1,512]{3,2,1,0:T(1,128)S(1)}, f32[3,4,1,512]{3,2,1,0:T(1,128)S(1)}, u32[]{:S(2)}, u32[]{:S(2)}) collective-permute-start(f32[3,4,1,512]{3,2,1,0:T(1,128)S(1)} %get-tuple-element.44.stats_ref), channel_id=1, source_target_pairs={{16,1},{17,0},{18,3},{19,2},{20,5},{21,4},{22,7},{23,6},{24,9},{25... | collective-permute-start | bytes 73736 | tf_op jit(solution)/shard_map/ppermute | solution.py:35
  49.8 3.5 %next_forward.1 = (bf16[4,4,256,512]{3,2,1,0:T(8,128)(2,1)S(1)}, f32[3,4,1,512]{3,2,1,0:T(1,128)S(1)}, bf16[2,128,512]{2,1,0:T(8,128)(2,1)S(1)}, bf16[2,128,512]{2,1,0:T(8,128)(2,1)S(1)}) custom-call(bf16[4,512,128]{2,1,0:T(8,128)(2,1)S(1)} %get-tuple-element.34.qs_ref, bf16[4,128,512]{2,1,0:T(8,128)(2,1)S(1)} %get-tuple-element.35.dot_ref, ...), custom_call_target="tpu_custom_call" | custom-call | flops 1073741824 | bytes 4194304 | tf_op jit(solution)/shard_map/next_forward/pallas_call | solution.py:325
  53.6 1.3 %collective-permute-start.7 = (f32[3,4,1,512]{3,2,1,0:T(1,128)S(1)}, f32[3,4,1,512]{3,2,1,0:T(1,128)S(1)}, u32[]{:S(2)}, u32[]{:S(2)}) collective-permute-start(f32[3,4,1,512]{3,2,1,0:T(1,128)S(1)} %get-tuple-element.44.stats_ref), channel_id=1, source_target_pairs={{0,1},{1,0},{2,3},{3,2},{4,5},{5,4},{6,7},{7,6},{8,9},{9,8},{10,11... | collective-permute-start | bytes 73736 | tf_op jit(solution)/shard_map/ppermute | solution.py:24
  54.9 6.8 %collective-permute-start.8 = (f32[3,4,1,512]{3,2,1,0:T(1,128)S(1)}, f32[3,4,1,512]{3,2,1,0:T(1,128)S(1)}, u32[]{:S(2)}, u32[]{:S(2)}) collective-permute-start(f32[3,4,1,512]{3,2,1,0:T(1,128)S(1)} %get-tuple-element.45.stats_ref), channel_id=1, source_target_pairs={{0,16},{16,32},{32,48},{48,64},{64,80},{80,96},{96,112},{112,128},... | collective-permute-start | bytes 73736 | tf_op jit(solution)/shard_map/ppermute | solution.py:20
  61.7 2.1 %collective-permute-start.9 = (f32[3,4,1,512]{3,2,1,0:T(1,128)S(1)}, f32[3,4,1,512]{3,2,1,0:T(1,128)S(1)}, u32[]{:S(2)}, u32[]{:S(2)}) collective-permute-start(f32[3,4,1,512]{3,2,1,0:T(1,128)S(1)} %get-tuple-element.45.stats_ref), channel_id=1, source_target_pairs={{0,17},{1,16},{2,19},{3,18},{4,21},{5,20},{6,23},{7,22},{8,25},{9,... | collective-permute-start | bytes 73736 | tf_op jit(solution)/shard_map/ppermute | solution.py:35
  63.8 5.0 %next_backward.1 = (f32[1024,256]{1,0:T(8,128)S(1)}, bf16[128,1024]{1,0:T(8,128)(2,1)S(1)}, bf16[128,1024]{1,0:T(8,128)(2,1)S(1)}) custom-call(bf16[4,512,128]{2,1,0:T(8,128)(2,1)S(1)} %get-tuple-element.34.qs_ref, bf16[4,128,512]{2,1,0:T(8,128)(2,1)S(1)} %get-tuple-element.35.dot_ref, bf16[1024,128]{1,0:T(8,128)(2,1)S(1)} %get-tuple-element.36.ks_ref, ...), custom_call_target="tpu_custom_call" | custom-call | flops 2147483648 | bytes 4194304 | tf_op jit(solution)/shard_map/next_backward/pallas_call | solution.py:325
  68.9 5.0 %own_backward.1 = (f32[128,1024]{1,0:T(8,128)S(1)}, bf16[128,1024]{1,0:T(8,128)(2,1)S(1)}, bf16[8,128,256]{2,1,0:T(8,128)(2,1)}, f32[4,2,1,512]{3,2,1,0:T(1,128)S(1)}) custom-call(s32[1]{0:T(128)} %bitcast.has_ref, s32[4]{0:T(128)S(1)} %get-tuple-element.41.allowed_ref, s32[8]{0:T(128)S(1)} %get-tuple-element.42.slots_ref, ...), custom_call_target="tpu_custom_call" | custom-call | flops 1342177280 | bytes 4194304 | tf_op jit(solution)/shard_map/own_backward/pallas_call | solution.py:325
  74.6 6.7 %all-to-all-start.1 = ((bf16[8,128,256]{2,1,0:T(8,128)(2,1)}), bf16[8,128,256]{2,1,0:T(8,128)(2,1)}, u32[]{:S(2)}, u32[]{:S(2)}) async-start(bf16[8,128,256]{2,1,0:T(8,128)(2,1)} %get-tuple-element.53), calls=%async_computation.1 | async-start | bytes 1048576 | tf_op jit(solution)/shard_map/all_to_all | solution.py:41
  81.4 5.1 %collective-permute-start.5 = (bf16[2,128,512]{2,1,0:T(8,128)(2,1)S(1)}, bf16[2,128,512]{2,1,0:T(8,128)(2,1)S(1)}, u32[]{:S(2)}, u32[]{:S(2)}) collective-permute-start(bf16[2,128,512]{2,1,0:T(8,128)(2,1)S(1)} %get-tuple-element.38), channel_id=1, source_target_pairs={{0,16},{16,32},{32,48},{48,64},{64,80},{80,96},{96,112},{112,128},... | collective-permute-start | bytes 786440 | tf_op jit(solution)/shard_map/ppermute | solution.py:20
  86.5 1.9 %collective-permute-start.6 = (bf16[2,128,512]{2,1,0:T(8,128)(2,1)S(1)}, bf16[2,128,512]{2,1,0:T(8,128)(2,1)S(1)}, u32[]{:S(2)}, u32[]{:S(2)}) collective-permute-start(bf16[2,128,512]{2,1,0:T(8,128)(2,1)S(1)} %get-tuple-element.39), channel_id=1, source_target_pairs={{0,17},{1,16},{2,19},{3,18},{4,21},{5,20},{6,23},{7,22},{8,25},{9,... | collective-permute-start | bytes 786440 | tf_op jit(solution)/shard_map/ppermute | solution.py:35
  88.5 4.2 %collective-permute-start.14 = (bf16[128,1024]{1,0:T(8,128)(2,1)}, bf16[128,1024]{1,0:T(8,128)(2,1)S(1)}, u32[]{:S(2)}, u32[]{:S(2)}) collective-permute-start(bf16[128,1024]{1,0:T(8,128)(2,1)} %copy-done.1), channel_id=1, source_target_pairs={{0,16},{16,32},{32,48},{48,64},{64,80},{80,96},{96,112},{112,128},... | collective-permute-start | bytes 786440 | tf_op jit(solution)/shard_map/ppermute | solution.py:20
  92.7 1.9 %collective-permute-start.15 = (bf16[128,1024]{1,0:T(8,128)(2,1)S(1)}, bf16[128,1024]{1,0:T(8,128)(2,1)S(1)}, u32[]{:S(2)}, u32[]{:S(2)}) collective-permute-start(bf16[128,1024]{1,0:T(8,128)(2,1)S(1)} %get-tuple-element.52), channel_id=1, source_target_pairs={{0,17},{1,16},{2,19},{3,18},{4,21},{5,20},{6,23},{7,22},{8,25},{9,... | collective-permute-start | bytes 786440 | tf_op jit(solution)/shard_map/ppermute | solution.py:35
  94.6 7.6 %collective-permute-done.6.got_corner_ref = bf16[2,128,512]{2,1,0:T(8,128)(2,1)S(1)} collective-permute-done((bf16[2,128,512]{2,1,0:T(8,128)(2,1)S(1)}, bf16[2,128,512]{2,1,0:T(8,128)(2,1)S(1)}, u32[]{:S(2)}, u32[]{:S(2)}) %collective-permute-start.6) | collective-permute-done | bytes 262176 | tf_op jit(solution)/shard_map/ppermute | solution.py:35
  103.2 4.7 %collective-permute-done.15 = bf16[128,1024]{1,0:T(8,128)(2,1)S(1)} collective-permute-done((bf16[128,1024]{1,0:T(8,128)(2,1)S(1)}, bf16[128,1024]{1,0:T(8,128)(2,1)S(1)}, u32[]{:S(2)}, u32[]{:S(2)}) %collective-permute-start.15) | collective-permute-done | bytes 262176 | tf_op jit(solution)/shard_map/ppermute | solution.py:35
  108.7 1.1 %reduce = bf16[128,256]{1,0:T(8,128)(2,1)S(1)} reduce(bf16[8,128,256]{2,1,0:T(8,128)(2,1)} %all-to-all-done.1, bf16[]{:T(256)} %constant.14), dimensions={0}, to_apply=%region_0.0.clone | reduce | flops 229376 | bytes 589826 | tf_op jit(solution)/shard_map/reduce_sum | solution.py:443
  (31 shorter events, 6.7 us)
Async XLA Ops:
  2.6 14.1 %collective-permute-start.3 = (bf16[256,1024]{1,0:T(8,128)(2,1)S(1)}, bf16[256,1024]{1,0:T(8,128)(2,1)S(1)}, u32[]{:S(2)}, u32[]{:S(2)}) collective-permute-start(bf16[256,1024]{1,0:T(8,128)(2,1)S(1)} %constant_dynamic-update-slice_fusion.both_ref), channel_id=1, source_target_pairs={{16,0},{32,16},{48,32},{64,48},{80,64},{96,80},{112,96},{128,112},... | collective-permute-start | bytes 1572872 | tf_op jit(solution)/shard_map/ppermute | solution.py:20
  6.9 31.9 %all-to-all-start = ((bf16[8,272,128]{2,1,0:T(8,128)(2,1)}), bf16[8,272,128]{2,1,0:T(8,128)(2,1)S(1)}, u32[]{:S(2)}, u32[]{:S(2)}) async-start(bf16[8,272,128]{2,1,0:T(8,128)(2,1)} %pack.1), calls=%async_computation | async-start | bytes 1114112 | tf_op jit(solution)/shard_map/all_to_all | solution.py:41
  14.9 23.9 %copy-start = (s32[128]{0:T(128)S(1)}, s32[128]{0:T(128)}, u32[]{:S(2)}) copy-start(s32[128]{0:T(128)} %position_ref.3) | copy-start | bytes 1540
  14.9 12.6 %collective-permute-start.1 = (bf16[256,1024]{1,0:T(8,128)(2,1)S(1)}, bf16[256,1024]{1,0:T(8,128)(2,1)S(1)}, u32[]{:S(2)}, u32[]{:S(2)}) collective-permute-start(bf16[256,1024]{1,0:T(8,128)(2,1)S(1)} %constant_dynamic-update-slice_fusion.both_ref), channel_id=1, source_target_pairs={{0,1},{1,0},{2,3},{3,2},{4,5},{5,4},{6,7},{7,6},{8,9},{9,8},{10,11... | collective-permute-start | bytes 1572872 | tf_op jit(solution)/shard_map/ppermute | solution.py:24
  16.7 32.9 %collective-permute-start.4 = (bf16[256,1024]{1,0:T(8,128)(2,1)S(1)}, bf16[256,1024]{1,0:T(8,128)(2,1)S(1)}, u32[]{:S(2)}, u32[]{:S(2)}) collective-permute-start(bf16[256,1024]{1,0:T(8,128)(2,1)S(1)} %collective-permute-done.3.both_ref), channel_id=1, source_target_pairs={{0,1},{1,0},{2,3},{3,2},{4,5},{5,4},{6,7},{7,6},{8,9},{9,8},{10,11... | collective-permute-start | bytes 1572872 | tf_op jit(solution)/shard_map/ppermute | solution.py:24
  18.0 20.8 %collective-permute-start = (s32[128]{0:T(128)}, s32[128]{0:T(128)S(1)}, u32[]{:S(2)}, u32[]{:S(2)}) collective-permute-start(s32[128]{0:T(128)} %position_ref.3), channel_id=1, source_target_pairs={{0,1},{1,0},{2,3},{3,2},{4,5},{5,4},{6,7},{7,6},{8,9},{9,8},{10,11... | collective-permute-start | bytes 1544 | tf_op jit(solution)/shard_map/ppermute | solution.py:24
  42.8 18.9 %collective-permute-start.11 = (f32[3,4,1,512]{3,2,1,0:T(1,128)S(1)}, f32[3,4,1,512]{3,2,1,0:T(1,128)S(1)}, u32[]{:S(2)}, u32[]{:S(2)}) collective-permute-start(f32[3,4,1,512]{3,2,1,0:T(1,128)S(1)} %get-tuple-element.44.stats_ref), channel_id=1, source_target_pairs={{16,0},{32,16},{48,32},{64,48},{80,64},{96,80},{112,96},{128,112},... | collective-permute-start | bytes 73736 | tf_op jit(solution)/shard_map/ppermute | solution.py:20
  46.5 17.3 %collective-permute-start.12 = (f32[3,4,1,512]{3,2,1,0:T(1,128)S(1)}, f32[3,4,1,512]{3,2,1,0:T(1,128)S(1)}, u32[]{:S(2)}, u32[]{:S(2)}) collective-permute-start(f32[3,4,1,512]{3,2,1,0:T(1,128)S(1)} %get-tuple-element.44.stats_ref), channel_id=1, source_target_pairs={{16,1},{17,0},{18,3},{19,2},{20,5},{21,4},{22,7},{23,6},{24,9},{25... | collective-permute-start | bytes 73736 | tf_op jit(solution)/shard_map/ppermute | solution.py:35
  53.4 10.4 %collective-permute-start.10 = (f32[3,4,1,512]{3,2,1,0:T(1,128)S(1)}, f32[3,4,1,512]{3,2,1,0:T(1,128)S(1)}, u32[]{:S(2)}, u32[]{:S(2)}) collective-permute-start(f32[3,4,1,512]{3,2,1,0:T(1,128)S(1)} %get-tuple-element.45.stats_ref), channel_id=1, source_target_pairs={{0,1},{1,0},{2,3},{3,2},{4,5},{5,4},{6,7},{7,6},{8,9},{9,8},{10,11... | collective-permute-start | bytes 73736 | tf_op jit(solution)/shard_map/ppermute | solution.py:24
  53.6 15.2 %collective-permute-start.7 = (f32[3,4,1,512]{3,2,1,0:T(1,128)S(1)}, f32[3,4,1,512]{3,2,1,0:T(1,128)S(1)}, u32[]{:S(2)}, u32[]{:S(2)}) collective-permute-start(f32[3,4,1,512]{3,2,1,0:T(1,128)S(1)} %get-tuple-element.44.stats_ref), channel_id=1, source_target_pairs={{0,1},{1,0},{2,3},{3,2},{4,5},{5,4},{6,7},{7,6},{8,9},{9,8},{10,11... | collective-permute-start | bytes 73736 | tf_op jit(solution)/shard_map/ppermute | solution.py:24
  54.9 14.0 %collective-permute-start.8 = (f32[3,4,1,512]{3,2,1,0:T(1,128)S(1)}, f32[3,4,1,512]{3,2,1,0:T(1,128)S(1)}, u32[]{:S(2)}, u32[]{:S(2)}) collective-permute-start(f32[3,4,1,512]{3,2,1,0:T(1,128)S(1)} %get-tuple-element.45.stats_ref), channel_id=1, source_target_pairs={{0,16},{16,32},{32,48},{48,64},{64,80},{80,96},{96,112},{112,128},... | collective-permute-start | bytes 73736 | tf_op jit(solution)/shard_map/ppermute | solution.py:20
  61.7 7.2 %collective-permute-start.9 = (f32[3,4,1,512]{3,2,1,0:T(1,128)S(1)}, f32[3,4,1,512]{3,2,1,0:T(1,128)S(1)}, u32[]{:S(2)}, u32[]{:S(2)}) collective-permute-start(f32[3,4,1,512]{3,2,1,0:T(1,128)S(1)} %get-tuple-element.45.stats_ref), channel_id=1, source_target_pairs={{0,17},{1,16},{2,19},{3,18},{4,21},{5,20},{6,23},{7,22},{8,25},{9,... | collective-permute-start | bytes 73736 | tf_op jit(solution)/shard_map/ppermute | solution.py:35
  68.8 5.1 %copy-start.1 = (bf16[128,1024]{1,0:T(8,128)(2,1)}, bf16[128,1024]{1,0:T(8,128)(2,1)S(1)}, u32[]{:S(2)}) copy-start(bf16[128,1024]{1,0:T(8,128)(2,1)S(1)} %get-tuple-element.51) | copy-start | bytes 786436
  73.9 0.7 copy-start.2
  74.6 34.1 %all-to-all-start.1 = ((bf16[8,128,256]{2,1,0:T(8,128)(2,1)}), bf16[8,128,256]{2,1,0:T(8,128)(2,1)}, u32[]{:S(2)}, u32[]{:S(2)}) async-start(bf16[8,128,256]{2,1,0:T(8,128)(2,1)} %get-tuple-element.53), calls=%async_computation.1 | async-start | bytes 1048576 | tf_op jit(solution)/shard_map/all_to_all | solution.py:41
  81.3 11.4 %collective-permute-start.2 = (bf16[2,128,512]{2,1,0:T(8,128)(2,1)S(1)}, bf16[2,128,512]{2,1,0:T(8,128)(2,1)S(1)}, u32[]{:S(2)}, u32[]{:S(2)}) collective-permute-start(bf16[2,128,512]{2,1,0:T(8,128)(2,1)S(1)} %get-tuple-element.33), channel_id=1, source_target_pairs={{0,1},{1,0},{2,3},{3,2},{4,5},{5,4},{6,7},{7,6},{8,9},{9,8},{10,11... | collective-permute-start | bytes 786440 | tf_op jit(solution)/shard_map/ppermute | solution.py:24
  81.4 13.2 %collective-permute-start.5 = (bf16[2,128,512]{2,1,0:T(8,128)(2,1)S(1)}, bf16[2,128,512]{2,1,0:T(8,128)(2,1)S(1)}, u32[]{:S(2)}, u32[]{:S(2)}) collective-permute-start(bf16[2,128,512]{2,1,0:T(8,128)(2,1)S(1)} %get-tuple-element.38), channel_id=1, source_target_pairs={{0,16},{16,32},{32,48},{48,64},{64,80},{80,96},{96,112},{112,128},... | collective-permute-start | bytes 786440 | tf_op jit(solution)/shard_map/ppermute | solution.py:20
  86.5 15.7 %collective-permute-start.6 = (bf16[2,128,512]{2,1,0:T(8,128)(2,1)S(1)}, bf16[2,128,512]{2,1,0:T(8,128)(2,1)S(1)}, u32[]{:S(2)}, u32[]{:S(2)}) collective-permute-start(bf16[2,128,512]{2,1,0:T(8,128)(2,1)S(1)} %get-tuple-element.39), channel_id=1, source_target_pairs={{0,17},{1,16},{2,19},{3,18},{4,21},{5,20},{6,23},{7,22},{8,25},{9,... | collective-permute-start | bytes 786440 | tf_op jit(solution)/shard_map/ppermute | solution.py:35
  88.4 14.8 %collective-permute-start.13 = (bf16[128,1024]{1,0:T(8,128)(2,1)}, bf16[128,1024]{1,0:T(8,128)(2,1)S(1)}, u32[]{:S(2)}, u32[]{:S(2)}) collective-permute-start(bf16[128,1024]{1,0:T(8,128)(2,1)} %copy-done.2), channel_id=1, source_target_pairs={{0,1},{1,0},{2,3},{3,2},{4,5},{5,4},{6,7},{7,6},{8,9},{9,8},{10,11... | collective-permute-start | bytes 786440 | tf_op jit(solution)/shard_map/ppermute | solution.py:24
  88.5 14.7 %collective-permute-start.14 = (bf16[128,1024]{1,0:T(8,128)(2,1)}, bf16[128,1024]{1,0:T(8,128)(2,1)S(1)}, u32[]{:S(2)}, u32[]{:S(2)}) collective-permute-start(bf16[128,1024]{1,0:T(8,128)(2,1)} %copy-done.1), channel_id=1, source_target_pairs={{0,16},{16,32},{32,48},{48,64},{64,80},{80,96},{96,112},{112,128},... | collective-permute-start | bytes 786440 | tf_op jit(solution)/shard_map/ppermute | solution.py:20
  92.7 15.1 %collective-permute-start.15 = (bf16[128,1024]{1,0:T(8,128)(2,1)S(1)}, bf16[128,1024]{1,0:T(8,128)(2,1)S(1)}, u32[]{:S(2)}, u32[]{:S(2)}) collective-permute-start(bf16[128,1024]{1,0:T(8,128)(2,1)S(1)} %get-tuple-element.52), channel_id=1, source_target_pairs={{0,17},{1,16},{2,19},{3,18},{4,21},{5,20},{6,23},{7,22},{8,25},{9,... | collective-permute-start | bytes 786440 | tf_op jit(solution)/shard_map/ppermute | solution.py:35

commit v11 on v7

--- a/solution.py
+++ b/solution.py
@@ -167,19 +167,23 @@
         o_ref[at] += dot_tn(vs_ref[pl.ds(start, tile_keys), :], raised)
 
 
-def key_tile(ref, tile, part):
-    span = 2 * block_rows
-    per_tile = tile_keys // span
-    return jnp.concatenate(
-        [ref[tile * per_tile + j, part * span : (part + 1) * span, :] for j in range(per_tile)],
-        axis=0,
-    )
+def key_tile(ref, tile):
+    return ref[tile * tile_keys : (tile + 1) * tile_keys, :]
 
 
 def prev_forward(
-    first, has_ref, qs_ref, dot_ref, kv_ref, m_own_ref, l_own_ref, o_own_ref,
-    p_ref, m_prev_ref, stats_ref, out_ref, s_ref,
+    first, has_ref, qs_ref, dot_ref, *rest
 ):
+    if first == 0:
+        ks_ref, vs_ref, m_own_ref, l_own_ref, o_own_ref, *rest = rest
+        p_ref, m_prev_ref, stats_ref, out_ref, s_ref = rest
+    else:
+        kv_ref, m_own_ref, l_own_ref, o_own_ref, *rest = rest
+        p_ref, m_prev_ref, stats_ref, out_ref, ks_ref, vs_ref, s_ref = rest
+        span = 2 * block_rows
+        for g in range(kv_ref.shape[0]):
+            ks_ref[g * span : (g + 1) * span, :] = kv_ref[g, :span, :]
+            vs_ref[g * span : (g + 1) * span, :] = kv_ref[g, span : 2 * span, :]
     _, width, head_dim = qs_ref.shape
     sets, tiles = p_ref.shape[:2]
     exponent_scale = log2_e * float(head_dim) ** (-0.5)
@@ -187,7 +191,7 @@
     for at in range(sets):
         peak = jnp.full((1, width), masked_score, jnp.float32)
         for tile in range(tiles):
-            scores = dot_nt(key_tile(kv_ref, tile, 0), qs_ref[first + at])
+            scores = dot_nt(key_tile(ks_ref, tile), qs_ref[first + at])
             s_ref[at, tile] = scores
             peak = jnp.maximum(peak, jnp.max(scores, axis=0, keepdims=True))
         m_prev_ref[at] = peak
@@ -200,7 +204,7 @@
             total += jnp.sum(raised, axis=0, keepdims=True)
             raised = raised.astype(jnp.bfloat16)
             p_ref[at, tile] = raised
-            out += dot_tn(key_tile(kv_ref, tile, 1), raised)
+            out += dot_tn(key_tile(vs_ref, tile), raised)
         peak = jnp.where(has_prev, peak, masked_score)
         m_prev_ref[at] = peak
         top = jnp.maximum(peak, m_own_ref[first + at])
@@ -219,11 +223,12 @@
             out_ref[at] = (out * share).astype(jnp.bfloat16)
 
 
-def prev_backward(first, has_ref, qs_ref, dot_ref, kv_ref, p_ref, m_own_ref, m_prev_ref, stats_ref, other_ref, *rest):
+def prev_backward(first, has_ref, qs_ref, dot_ref, ks_ref, vs_ref, p_ref, m_own_ref, m_prev_ref, stats_ref, other_ref, *rest):
     if first == 0:
-        terms_ref, dos_ref, shift_ref, ds_ref, factor_ref, scaled_ref, lower_ref = rest
+        key_terms_ref, value_terms_ref, dos_ref, shift_ref, ds_ref, factor_ref, scaled_ref, lower_ref = rest
     else:
-        before_ref, terms_ref, dos_ref, shift_ref, ds_ref, scaled_ref, lower_ref = rest
+        key_before_ref, value_before_ref, key_terms_ref, value_terms_ref = rest[:4]
+        dos_ref, shift_ref, ds_ref, scaled_ref, lower_ref = rest[4:]
     _, width, head_dim = qs_ref.shape
     sets, tiles = p_ref.shape[:2]
     span = 2 * block_rows
@@ -249,7 +254,7 @@
         scaled_ref[at] = (grad * prev_factor).astype(jnp.bfloat16)
         lower_ref[at] = delta * prev_factor
     for tile in range(tiles):
-        values = key_tile(kv_ref, tile, 1)
+        values = key_tile(vs_ref, tile)
         key_grad = jnp.zeros((tile_keys, head_dim), jnp.float32)
         value_grad = jnp.zeros((tile_keys, head_dim), jnp.float32)
         for at in range(sets):
@@ -262,21 +267,21 @@
         key_grad = key_grad * scale
         if first == 0:
             rows = slice(tile * tile_keys, (tile + 1) * tile_keys)
-            terms_ref[rows, :head_dim] = key_grad
-            terms_ref[rows, head_dim:] = value_grad
+            key_terms_ref[rows, :] = key_grad
+            value_terms_ref[rows, :] = value_grad
         else:
             rows = slice(tile * tile_keys, (tile + 1) * tile_keys)
-            key_grad = (key_grad + before_ref[rows, :head_dim]).astype(jnp.bfloat16)
-            value_grad = (value_grad + before_ref[rows, head_dim:]).astype(jnp.bfloat16)
+            key_grad = (key_grad + key_before_ref[rows, :]).astype(jnp.bfloat16)
+            value_grad = (value_grad + value_before_ref[rows, :]).astype(jnp.bfloat16)
             for j in range(per_tile):
                 rows = slice(j * span, (j + 1) * span)
-                terms_ref[tile * per_tile + j, :, :head_dim] = key_grad[rows]
-                terms_ref[tile * per_tile + j, :, head_dim:] = value_grad[rows]
+                key_terms_ref[tile * per_tile + j] = key_grad[rows]
+                value_terms_ref[tile * per_tile + j] = value_grad[rows]
 
 
 def own_backward(
     allowed_ref, slots_ref, qs_ref, ks_ref, vs_ref, p_ref,
-    dos_mine_ref, shift_mine_ref, ds_mine_ref, dos_theirs_ref, shift_theirs_ref, ds_theirs_ref, kv_ref,
+    dos_mine_ref, shift_mine_ref, ds_mine_ref, dos_theirs_ref, shift_theirs_ref, ds_theirs_ref, prev_ks_ref,
     dq_ref, dq_partner_ref, terms_ref, acc_ref, dqa_ref,
 ):
     steps, _, width = p_ref.shape
@@ -290,7 +295,7 @@
     for at in range(4):
         changes = (ds_mine_ref, ds_theirs_ref)[at // 2]
         dqa_ref[at] = sum(
-            dot_tn(key_tile(kv_ref, tile, 0), changes[at % 2, tile]) for tile in range(tiles)
+            dot_tn(key_tile(prev_ks_ref, tile), changes[at % 2, tile]) for tile in range(tiles)
         )
     for step in range(steps):
         at, tile = own_tile(step, allowed_ref)
@@ -415,10 +420,12 @@
     )(both_blocks, qs, group_kv)
     half_stat = ((2, 1, width), f32)
     half_query = ((2, head_dim, width), f32)
+    half_terms = ((group, tok_rows, head_dim), bf16)
     changes = ((2, tiles, tile_keys, width), bf16)
     half_query_16 = ((2, head_dim, width), bf16)
 
-    def forward(first, name):
+    def forward(first, name, *keys_and_values):
+        sorted_out = [((span_rows, head_dim), bf16)] * 2
         return call(
             functools.partial(prev_forward, first),
             name,
@@ -427,34 +434,43 @@
                 half_stat,
                 ((3, 2, 1, width), f32),
                 half_query if first == 0 else half_query_16,
-            ],
+            ]
+            + (sorted_out if first else []),
             (0,),
             [((2, tiles, tile_keys, width), f32)],
             flops=2 * 2 * tiles * unit,
-        )(has_prev, qs, dot, prev_kv, m_own, l_own, o_own)
-
-    p_theirs, m_theirs, stats_theirs, sent = forward(2, "prev_forward_theirs")
+        )(has_prev, qs, dot, *keys_and_values, m_own, l_own, o_own)
+
+    p_theirs, m_theirs, stats_theirs, sent, prev_ks, prev_vs = forward(2, "prev_forward_theirs", prev_kv)
     other_mine = to_partner(stats_theirs, "inner")
     got = to_partner(sent, "inner")
-    p_mine, m_mine, stats_mine, out = forward(0, "prev_forward_mine")
+    p_mine, m_mine, stats_mine, out = forward(0, "prev_forward_mine", prev_ks, prev_vs)
     other_theirs = to_partner(stats_mine, "inner")
-    first_terms, dos_mine, shift_mine, ds_mine, factor = call(
+    key_first, value_first, dos_mine, shift_mine, ds_mine, factor = call(
         functools.partial(prev_backward, 0),
         "prev_backward_mine",
-        [((span_rows, 2 * head_dim), f32), half_query_16, half_stat, changes, ((2, 2, 1, width), f32)],
+        [
+            ((span_rows, head_dim), f32),
+            ((span_rows, head_dim), f32),
+            half_query_16,
+            half_stat,
+            changes,
+            ((2, 2, 1, width), f32),
+        ],
         (0,),
         [half_query_16, half_stat],
         flops=4 * 2 * tiles * unit,
-    )(has_prev, qs, dot, prev_kv, p_mine, m_own, m_mine, stats_mine, other_mine)
-    prev_terms, dos_theirs, shift_theirs, ds_theirs = call(
+    )(has_prev, qs, dot, prev_ks, prev_vs, p_mine, m_own, m_mine, stats_mine, other_mine)
+    key_terms, value_terms, dos_theirs, shift_theirs, ds_theirs = call(
         functools.partial(prev_backward, 2),
         "prev_backward_theirs",
-        [terms_shape, half_query_16, half_stat, changes],
+        [half_terms, half_terms, half_query_16, half_stat, changes],
         (0,),
         [half_query_16, half_stat],
         flops=4 * 2 * tiles * unit,
-    )(has_prev, qs, dot, prev_kv, p_theirs, m_own, m_theirs, stats_theirs, other_theirs, first_terms)
-    returned = from_behind(prev_terms, "outer", -1)
+    )(has_prev, qs, dot, prev_ks, prev_vs, p_theirs, m_own, m_theirs, stats_theirs, other_theirs, key_first, value_first)
+    key_returned = from_behind(key_terms, "outer", -1)
+    value_returned = from_behind(value_terms, "outer", -1)
     dq, dq_partner, own_terms = call(
         own_backward,
         "own_backward",
@@ -462,9 +478,10 @@
         (0, 1),
         [((span_rows, 2 * head_dim), f32), by_query],
         flops=4 * steps * unit,
-    )(allowed, slots, qs, ks, vs, p_own, dos_mine, shift_mine, ds_mine, dos_theirs, shift_theirs, ds_theirs, prev_kv)
+    )(allowed, slots, qs, ks, vs, p_own, dos_mine, shift_mine, ds_mine, dos_theirs, shift_theirs, ds_theirs, prev_ks)
     (attended,) = call(merge_attended, "merge_attended", [tokens], (), [])(out, got, factor)
     dq_other = to_partner(dq_partner, "inner")
+    returned = jnp.concatenate([key_returned, value_returned], axis=2)
     terms = (own_terms.astype(f32) + returned.astype(f32)).astype(bf16)
     key_grads = jnp.sum(exchange(terms, "inner").astype(f32), axis=0)
     grad_queries = (dq + dq_other.astype(f32)).astype(bf16)

time: 88.2 us -> 91.4 us (1.036)
  starting transfers between devices: 26.2 us -> 28.1 us
    ppermute x7, waiting for transfers between devices: 20.7 us -> 23.1 us  [to_partner(): lax.ppermute(block, axis, [(i, i ^ 1) for i in range(lax.axis_size(axis))])]
    ppermute x2 -> x3, starting transfers between devices: 3.83 us -> 5.75 us  [from_behind(): return lax.ppermute(block, axis, route)]
    ppermute x2 -> x3, waiting for transfers between devices: 10.7 us -> 8.78 us  [from_behind(): return lax.ppermute(block, axis, route)]
  transfers between devices with their start and end apart: 11 -> 12, of which waited for: 8 -> 7; matrix products, arithmetic and copies ran while one was open for 1% -> 1% of each run, Pallas kernels for 17% -> 16%
where the time goes in v11:
time: 91.4 us; the launch traced here: 90.6 us
  waiting for transfers between devices  36.2 us (40%)
  starting transfers between devices  28.1 us (31%)
  Pallas kernels  20.5 us (22%)
  local copies, waits for them, and re-layouts  3.18 us (3%)
  other arithmetic  1.81 us (2%)
    ppermute x7, waiting for transfers between devices, to_partner(): lax.ppermute(block, axis, [(i, i ^ 1) for i in range(lax.axis_size(axis))])  23.1 us
    pallas_call x8, Pallas kernels, run(): pl.pallas_call(kernel, name=name, grid=(1,) if stream else (), out_shape=...  18.8 us
    all_to_all x2, starting transfers between devices, exchange(): lax.all_to_all(parts, axis, 0, 0, axis_index_groups=groups, tiled=True)  14.7 us
    ppermute x3, waiting for transfers between devices, from_behind(): return lax.ppermute(block, axis, route)  8.78 us
    ppermute x7, starting transfers between devices, to_partner(): lax.ppermute(block, axis, [(i, i ^ 1) for i in range(lax.axis_size(axis))])  7.71 us
    ppermute x3, starting transfers between devices, from_behind(): return lax.ppermute(block, axis, route)  5.75 us
    all_to_all x2, waiting for transfers between devices, exchange(): lax.all_to_all(parts, axis, 0, 0, axis_index_groups=groups, tiled=True)  4.35 us
    unnamed x6, local copies, waits for them, and re-layouts  2.55 us
  transfers between devices with their start and end apart: 12, of which 7 were waited for; matrix products, arithmetic and copies ran while one was open for 1% of the time, Pallas kernels for 16%

profile of v11, /device:TPU:16, one launch (start us, length us, event | category | flops | bytes accessed | tf_op | source)
XLA Modules:
  0.0 90.6 jit_solution(13239217996279574486)
XLA Ops:
  0.6 1.7 %pack.1 = bf16[8,272,128]{2,1,0:T(8,128)(2,1)} custom-call(s32[128]{0:T(128)} %position_ref.3, bf16[128,128]{1,0:T(8,128)(2,1)} %key_ref.1, bf16[128,128]{1,0:T(8,128)(2,1)} %value_ref.1), custom_call_target="tpu_custom_call" | custom-call | tf_op jit(solution)/shard_map/pack/pallas_call | solution.py:367
  2.3 8.5 %all-to-all-start = ((bf16[8,272,128]{2,1,0:T(8,128)(2,1)}), bf16[8,272,128]{2,1,0:T(8,128)(2,1)S(1)}, u32[]{:S(2)}, u32[]{:S(2)}) async-start(bf16[8,272,128]{2,1,0:T(8,128)(2,1)} %pack.1), calls=%async_computation | async-start | bytes 1114112 | tf_op jit(solution)/shard_map/all_to_all | solution.py:30
  10.8 1.3 %collective-permute-start.1 = (bf16[128,1024]{1,0:T(8,128)(2,1)}, bf16[128,1024]{1,0:T(8,128)(2,1)S(1)}, u32[]{:S(2)}, u32[]{:S(2)}) collective-permute-start(bf16[128,1024]{1,0:T(8,128)(2,1)} %q_ref.1), channel_id=1, source_target_pairs={{0,1},{1,0},{2,3},{3,2},{4,5},{5,4},{6,7},{7,6},{8,9},{9,8},{10,11... | collective-permute-start | bytes 786440 | tf_op jit(solution)/shard_map/ppermute | solution.py:24
  12.8 1.3 %collective-permute-start = (s32[128]{0:T(128)}, s32[128]{0:T(128)S(1)}, u32[]{:S(2)}, u32[]{:S(2)}) collective-permute-start(s32[128]{0:T(128)} %position_ref.3), channel_id=1, source_target_pairs={{0,1},{1,0},{2,3},{3,2},{4,5},{5,4},{6,7},{7,6},{8,9},{9,8},{10,11... | collective-permute-start | bytes 1544 | tf_op jit(solution)/shard_map/ppermute | solution.py:24
  14.1 10.4 %collective-permute-done.position_partner_ref = s32[128]{0:T(128)S(1)} collective-permute-done((s32[128]{0:T(128)}, s32[128]{0:T(128)S(1)}, u32[]{:S(2)}, u32[]{:S(2)}) %collective-permute-start) | collective-permute-done | bytes 544 | tf_op jit(solution)/shard_map/ppermute | solution.py:24
  27.0 1.2 %stack_pair.1 = (s32[2]{0:T(128)S(1)}, bf16[4,512,128]{2,1,0:T(8,128)(2,1)S(1)}, bf16[4,128,512]{2,1,0:T(8,128)(2,1)S(1)}) custom-call(s32[128]{0:T(128)S(1)} %copy-done, s32[128]{0:T(128)S(1)} %collective-permute-done.position_partner_ref, bf16[128,1024]{1,0:T(8,128)(2,1)S(1)} %copy-done.1, bf16[128,1024]{1,0:T(8,128)(2,1)S(1)} %collective-permute-done.1.q_partner_ref, ...), custom_call_target="tpu_custom_call" | custom-call | flops 4000000000 | bytes 4194304 | tf_op jit(solution)/shard_map/stack_pair/pallas_call | solution.py:338
  29.0 1.9 %collective-permute-start.3 = (bf16[8,272,128]{2,1,0:T(8,128)(2,1)S(1)}, bf16[8,272,128]{2,1,0:T(8,128)(2,1)S(1)}, u32[]{:S(2)}, u32[]{:S(2)}) collective-permute-start(bf16[8,272,128]{2,1,0:T(8,128)(2,1)S(1)} %all-to-all-done.kv_ref), channel_id=1, source_target_pairs={{0,16},{16,32},{32,48},{48,64},{64,80},{80,96},{96,112},{112,128},... | collective-permute-start | bytes 1671176 | tf_op jit(solution)/shard_map/ppermute | solution.py:20
  30.9 3.8 %own_forward.1 = (bf16[1024,128]{1,0:T(8,128)(2,1)S(1)}, bf16[1024,128]{1,0:T(8,128)(2,1)S(1)}, s32[8]{0:T(128)S(1)}, s32[4]{0:T(128)S(1)}, bf16[10,256,512]{2,1...) custom-call(s32[2]{0:T(128)S(1)} %get-tuple-element.49.block_ref, ...), custom_call_target="tpu_custom_call" | custom-call | flops 671088640 | bytes 4194304 | tf_op jit(solution)/shard_map/own_forward/pallas_call | solution.py:338
  34.8 8.8 %collective-permute-done.3.rest_0_ = bf16[8,272,128]{2,1,0:T(8,128)(2,1)S(1)} collective-permute-done((bf16[8,272,128]{2,1,0:T(8,128)(2,1)S(1)}, bf16[8,272,128]{2,1,0:T(8,128)(2,1)S(1)}, u32[]{:S(2)}, u32[]{:S(2)}) %collective-permute-start.3) | collective-permute-done | bytes 557088 | tf_op jit(solution)/shard_map/ppermute | solution.py:20
  43.6 2.0 %prev_forward_theirs.1 = (bf16[2,4,256,512]{3,2,1,0:T(8,128)(2,1)S(1)}, f32[2,1,512]{2,1,0:T(1,128)S(1)}, f32[3,2,1,512]{3,2,1,0:T(1,128)S(1)}, bf16[2,128,512]{...) custom-call(s32[1]{0:T(128)} %bitcast.has_ref, ...), custom_call_target="tpu_custom_call" | custom-call | flops 536870912 | bytes 4194304 | tf_op jit(solution)/shard_map/prev_forward_theirs/pallas_call | solution.py:338
  45.6 1.4 %collective-permute-start.5 = (f32[3,2,1,512]{3,2,1,0:T(1,128)S(1)}, f32[3,2,1,512]{3,2,1,0:T(1,128)S(1)}, u32[]{:S(2)}, u32[]{:S(2)}) collective-permute-start(f32[3,2,1,512]{3,2,1,0:T(1,128)S(1)} %get-tuple-element.60.stats_ref), channel_id=1, source_target_pairs={{0,1},{1,0},{2,3},{3,2},{4,5},{5,4},{6,7},{7,6},{8,9},{9,8},{10,11... | collective-permute-start | bytes 36872 | tf_op jit(solution)/shard_map/ppermute | solution.py:24
  47.0 2.0 %prev_forward_mine.1 = (bf16[2,4,256,512]{3,2,1,0:T(8,128)(2,1)S(1)}, f32[2,1,512]{2,1,0:T(1,128)S(1)}, f32[3,2,1,512]{3,2,1,0:T(1,128)S(1)}, f32[2,128,512]{2,1,0:T(8,128)S(1)}) custom-call(s32[1]{0:T(128)} %bitcast.has_ref, bf16[4,512,128]{2,1,0:T(8,128)(2,1)S(1)} %get-tuple-element.46.qs_ref, bf16[4,128,512]{2,1,0:T(8,128)(2,1)S(1)} %get-tuple-element.47.dot_ref, ...), custom_call_target="tpu_custom_call" | custom-call | flops 536870912 | bytes 4194304 | tf_op jit(solution)/shard_map/prev_forward_mine/pallas_call | solution.py:338
  49.0 1.0 %collective-permute-start.6 = (f32[3,2,1,512]{3,2,1,0:T(1,128)S(1)}, f32[3,2,1,512]{3,2,1,0:T(1,128)S(1)}, u32[]{:S(2)}, u32[]{:S(2)}) collective-permute-start(f32[3,2,1,512]{3,2,1,0:T(1,128)S(1)} %get-tuple-element.59.stats_ref), channel_id=1, source_target_pairs={{0,1},{1,0},{2,3},{3,2},{4,5},{5,4},{6,7},{7,6},{8,9},{9,8},{10,11... | collective-permute-start | bytes 36872 | tf_op jit(solution)/shard_map/ppermute | solution.py:24
  50.0 1.9 %prev_backward_mine.1 = (f32[1024,128]{1,0:T(8,128)S(1)}, f32[1024,128]{1,0:T(8,128)S(1)}, bf16[2,128,512]{2,1,0:T(8,128)(2,1)S(1)}, f32[2,1,512]{2,1,0:T(1,128)...) custom-call(s32[1]{0:T(128)} %bitcast.has_ref, ...), custom_call_target="tpu_custom_call" | custom-call | flops 1073741824 | bytes 4194304 | tf_op jit(solution)/shard_map/prev_backward_mine/pallas_call | solution.py:338
  51.9 1.1 %collective-permute-done.6.other_ref = f32[3,2,1,512]{3,2,1,0:T(1,128)S(1)} collective-permute-done((f32[3,2,1,512]{3,2,1,0:T(1,128)S(1)}, f32[3,2,1,512]{3,2,1,0:T(1,128)S(1)}, u32[]{:S(2)}, u32[]{:S(2)}) %collective-permute-start.6) | collective-permute-done | bytes 12320 | tf_op jit(solution)/shard_map/ppermute | solution.py:24
  52.9 2.3 %prev_backward_theirs.1 = (bf16[8,128,128]{2,1,0:T(8,128)(2,1)S(1)}, bf16[8,128,128]{2,1,0:T(8,128)(2,1)S(1)}, bf16[2,128,512]{2,1,0:T(8,128)(2,1)S(1)}, f32[2,1...) custom-call(s32[1]{0:T(128)} %bitcast.has_ref, bf16[4,512,128]{2,1,0:T(8,128)(2,1)S(1)} %get-tuple-element.46.qs_ref, ...), custom_call_target="tpu_custom_call" | custom-call | flops 1073741824 | bytes 4194304 | tf_op jit(solution)/shard_map/prev_backward_theirs/pallas_call | solution.py:338
  55.2 1.9 %collective-permute-start.9 = (bf16[8,128,128]{2,1,0:T(8,128)(2,1)S(1)}, bf16[8,128,128]{2,1,0:T(8,128)(2,1)S(1)}, u32[]{:S(2)}, u32[]{:S(2)}) collective-permute-start(bf16[8,128,128]{2,1,0:T(8,128)(2,1)S(1)} %get-tuple-element.81), channel_id=1, source_target_pairs={{16,0},{32,16},{48,32},{64,48},{80,64},{96,80},{112,96},{128,112},... | collective-permute-start | bytes 786440 | tf_op jit(solution)/shard_map/ppermute | solution.py:20
  57.1 1.9 %collective-permute-start.8 = (bf16[8,128,128]{2,1,0:T(8,128)(2,1)S(1)}, bf16[8,128,128]{2,1,0:T(8,128)(2,1)S(1)}, u32[]{:S(2)}, u32[]{:S(2)}) collective-permute-start(bf16[8,128,128]{2,1,0:T(8,128)(2,1)S(1)} %get-tuple-element.80), channel_id=1, source_target_pairs={{16,0},{32,16},{48,32},{64,48},{80,64},{96,80},{112,96},{128,112},... | collective-permute-start | bytes 786440 | tf_op jit(solution)/shard_map/ppermute | solution.py:20
  59.1 4.8 %own_backward.1 = (f32[128,1024]{1,0:T(8,128)S(1)}, bf16[128,1024]{1,0:T(8,128)(2,1)S(1)}, bf16[8,128,256]{2,1,0:T(8,128)(2,1)S(1)}) custom-call(s32[4]{0:T(128)S(1)} %get-tuple-element.62.allowed_ref, s32[8]{0:T(128)S(1)} %get-tuple-element.63.slots_ref, bf16[4,512,128]{2,1,0:T(8,128)(2,1)S(1)} %get-tuple-element.46.qs_ref, ...), custom_call_target="tpu_custom_call" | custom-call | flops 1342177280 | bytes 4194304 | tf_op jit(solution)/shard_map/own_backward/pallas_call | solution.py:338
  64.8 6.2 %all-to-all-start.1 = ((bf16[8,128,256]{2,1,0:T(8,128)(2,1)}), bf16[8,128,256]{2,1,0:T(8,128)(2,1)S(1)}, u32[]{:S(2)}, u32[]{:S(2)}) async-start(bf16[8,128,256]{2,1,0:T(8,128)(2,1)} %add_convert_fusion), calls=%async_computation.1 | async-start | bytes 1048576 | tf_op jit(solution)/shard_map/all_to_all | solution.py:30
  71.7 1.3 %collective-permute-start.7 = (bf16[128,1024]{1,0:T(8,128)(2,1)S(1)}, bf16[128,1024]{1,0:T(8,128)(2,1)S(1)}, u32[]{:S(2)}, u32[]{:S(2)}) collective-permute-start(bf16[128,1024]{1,0:T(8,128)(2,1)S(1)} %get-tuple-element.78), channel_id=1, source_target_pairs={{0,1},{1,0},{2,3},{3,2},{4,5},{5,4},{6,7},{7,6},{8,9},{9,8},{10,11... | collective-permute-start | bytes 786440 | tf_op jit(solution)/shard_map/ppermute | solution.py:24
  73.0 6.9 %collective-permute-done.4.got_ref = bf16[2,128,512]{2,1,0:T(8,128)(2,1)S(1)} collective-permute-done((bf16[2,128,512]{2,1,0:T(8,128)(2,1)S(1)}, bf16[2,128,512]{2,1,0:T(8,128)(2,1)S(1)}, u32[]{:S(2)}, u32[]{:S(2)}) %collective-permute-start.4) | collective-permute-done | bytes 262176 | tf_op jit(solution)/shard_map/ppermute | solution.py:24
  80.8 4.8 %collective-permute-done.7 = bf16[128,1024]{1,0:T(8,128)(2,1)S(1)} collective-permute-done((bf16[128,1024]{1,0:T(8,128)(2,1)S(1)}, bf16[128,1024]{1,0:T(8,128)(2,1)S(1)}, u32[]{:S(2)}, u32[]{:S(2)}) %collective-permute-start.7) | collective-permute-done | bytes 262176 | tf_op jit(solution)/shard_map/ppermute | solution.py:24
  86.3 3.6 %all-to-all-done.1 = bf16[8,128,256]{2,1,0:T(8,128)(2,1)S(1)} async-done(((bf16[8,128,256]{2,1,0:T(8,128)(2,1)}), bf16[8,128,256]{2,1,0:T(8,128)(2,1)S(1)}, u32[]{:S(2)}, u32[]{:S(2)}) %all-to-all-start.1) | async-done | bytes 524320 | tf_op jit(solution)/shard_map/all_to_all | solution.py:30
  (19 shorter events, 8.1 us)
Async XLA Ops:
  2.3 26.7 %all-to-all-start = ((bf16[8,272,128]{2,1,0:T(8,128)(2,1)}), bf16[8,272,128]{2,1,0:T(8,128)(2,1)S(1)}, u32[]{:S(2)}, u32[]{:S(2)}) async-start(bf16[8,272,128]{2,1,0:T(8,128)(2,1)} %pack.1), calls=%async_computation | async-start | bytes 1114112 | tf_op jit(solution)/shard_map/all_to_all | solution.py:30
  10.8 13.7 %collective-permute-start.1 = (bf16[128,1024]{1,0:T(8,128)(2,1)}, bf16[128,1024]{1,0:T(8,128)(2,1)S(1)}, u32[]{:S(2)}, u32[]{:S(2)}) collective-permute-start(bf16[128,1024]{1,0:T(8,128)(2,1)} %q_ref.1), channel_id=1, source_target_pairs={{0,1},{1,0},{2,3},{3,2},{4,5},{5,4},{6,7},{7,6},{8,9},{9,8},{10,11... | collective-permute-start | bytes 786440 | tf_op jit(solution)/shard_map/ppermute | solution.py:24
  12.1 12.4 %collective-permute-start.2 = (bf16[128,1024]{1,0:T(8,128)(2,1)}, bf16[128,1024]{1,0:T(8,128)(2,1)S(1)}, u32[]{:S(2)}, u32[]{:S(2)}) collective-permute-start(bf16[128,1024]{1,0:T(8,128)(2,1)} %do_ref.1), channel_id=1, source_target_pairs={{0,1},{1,0},{2,3},{3,2},{4,5},{5,4},{6,7},{7,6},{8,9},{9,8},{10,11... | collective-permute-start | bytes 786440 | tf_op jit(solution)/shard_map/ppermute | solution.py:24
  12.8 11.6 %collective-permute-start = (s32[128]{0:T(128)}, s32[128]{0:T(128)S(1)}, u32[]{:S(2)}, u32[]{:S(2)}) collective-permute-start(s32[128]{0:T(128)} %position_ref.3), channel_id=1, source_target_pairs={{0,1},{1,0},{2,3},{3,2},{4,5},{5,4},{6,7},{7,6},{8,9},{9,8},{10,11... | collective-permute-start | bytes 1544 | tf_op jit(solution)/shard_map/ppermute | solution.py:24
  24.5 0.7 copy-start
  25.1 0.9 %copy-start.1 = (bf16[128,1024]{1,0:T(8,128)(2,1)S(1)}, bf16[128,1024]{1,0:T(8,128)(2,1)}, u32[]{:S(2)}) copy-start(bf16[128,1024]{1,0:T(8,128)(2,1)} %q_ref.1) | copy-start | bytes 786436
  26.1 0.9 %copy-start.2 = (bf16[128,1024]{1,0:T(8,128)(2,1)S(1)}, bf16[128,1024]{1,0:T(8,128)(2,1)}, u32[]{:S(2)}) copy-start(bf16[128,1024]{1,0:T(8,128)(2,1)} %do_ref.1) | copy-start | bytes 786436
  29.0 14.6 %collective-permute-start.3 = (bf16[8,272,128]{2,1,0:T(8,128)(2,1)S(1)}, bf16[8,272,128]{2,1,0:T(8,128)(2,1)S(1)}, u32[]{:S(2)}, u32[]{:S(2)}) collective-permute-start(bf16[8,272,128]{2,1,0:T(8,128)(2,1)S(1)} %all-to-all-done.kv_ref), channel_id=1, source_target_pairs={{0,16},{16,32},{32,48},{48,64},{64,80},{80,96},{96,112},{112,128},... | collective-permute-start | bytes 1671176 | tf_op jit(solution)/shard_map/ppermute | solution.py:20
  45.6 4.4 %collective-permute-start.5 = (f32[3,2,1,512]{3,2,1,0:T(1,128)S(1)}, f32[3,2,1,512]{3,2,1,0:T(1,128)S(1)}, u32[]{:S(2)}, u32[]{:S(2)}) collective-permute-start(f32[3,2,1,512]{3,2,1,0:T(1,128)S(1)} %get-tuple-element.60.stats_ref), channel_id=1, source_target_pairs={{0,1},{1,0},{2,3},{3,2},{4,5},{5,4},{6,7},{7,6},{8,9},{9,8},{10,11... | collective-permute-start | bytes 36872 | tf_op jit(solution)/shard_map/ppermute | solution.py:24
  49.0 4.0 %collective-permute-start.6 = (f32[3,2,1,512]{3,2,1,0:T(1,128)S(1)}, f32[3,2,1,512]{3,2,1,0:T(1,128)S(1)}, u32[]{:S(2)}, u32[]{:S(2)}) collective-permute-start(f32[3,2,1,512]{3,2,1,0:T(1,128)S(1)} %get-tuple-element.59.stats_ref), channel_id=1, source_target_pairs={{0,1},{1,0},{2,3},{3,2},{4,5},{5,4},{6,7},{7,6},{8,9},{9,8},{10,11... | collective-permute-start | bytes 36872 | tf_op jit(solution)/shard_map/ppermute | solution.py:24
  55.2 8.6 %collective-permute-start.9 = (bf16[8,128,128]{2,1,0:T(8,128)(2,1)S(1)}, bf16[8,128,128]{2,1,0:T(8,128)(2,1)S(1)}, u32[]{:S(2)}, u32[]{:S(2)}) collective-permute-start(bf16[8,128,128]{2,1,0:T(8,128)(2,1)S(1)} %get-tuple-element.81), channel_id=1, source_target_pairs={{16,0},{32,16},{48,32},{64,48},{80,64},{96,80},{112,96},{128,112},... | collective-permute-start | bytes 786440 | tf_op jit(solution)/shard_map/ppermute | solution.py:20
  57.1 6.7 %collective-permute-start.8 = (bf16[8,128,128]{2,1,0:T(8,128)(2,1)S(1)}, bf16[8,128,128]{2,1,0:T(8,128)(2,1)S(1)}, u32[]{:S(2)}, u32[]{:S(2)}) collective-permute-start(bf16[8,128,128]{2,1,0:T(8,128)(2,1)S(1)} %get-tuple-element.80), channel_id=1, source_target_pairs={{16,0},{32,16},{48,32},{64,48},{80,64},{96,80},{112,96},{128,112},... | collective-permute-start | bytes 786440 | tf_op jit(solution)/shard_map/ppermute | solution.py:20
  64.8 25.1 %all-to-all-start.1 = ((bf16[8,128,256]{2,1,0:T(8,128)(2,1)}), bf16[8,128,256]{2,1,0:T(8,128)(2,1)S(1)}, u32[]{:S(2)}, u32[]{:S(2)}) async-start(bf16[8,128,256]{2,1,0:T(8,128)(2,1)} %add_convert_fusion), calls=%async_computation.1 | async-start | bytes 1048576 | tf_op jit(solution)/shard_map/all_to_all | solution.py:30
  71.0 9.0 %collective-permute-start.4 = (bf16[2,128,512]{2,1,0:T(8,128)(2,1)S(1)}, bf16[2,128,512]{2,1,0:T(8,128)(2,1)S(1)}, u32[]{:S(2)}, u32[]{:S(2)}) collective-permute-start(bf16[2,128,512]{2,1,0:T(8,128)(2,1)S(1)} %get-tuple-element.56), channel_id=1, source_target_pairs={{0,1},{1,0},{2,3},{3,2},{4,5},{5,4},{6,7},{7,6},{8,9},{9,8},{10,11... | collective-permute-start | bytes 786440 | tf_op jit(solution)/shard_map/ppermute | solution.py:24
  71.7 13.8 %collective-permute-start.7 = (bf16[128,1024]{1,0:T(8,128)(2,1)S(1)}, bf16[128,1024]{1,0:T(8,128)(2,1)S(1)}, u32[]{:S(2)}, u32[]{:S(2)}) collective-permute-start(bf16[128,1024]{1,0:T(8,128)(2,1)S(1)} %get-tuple-element.78), channel_id=1, source_target_pairs={{0,1},{1,0},{2,3},{3,2},{4,5},{5,4},{6,7},{7,6},{8,9},{9,8},{10,11... | collective-permute-start | bytes 786440 | tf_op jit(solution)/shard_map/ppermute | solution.py:24

commit v12 on v7

--- a/solution.py
+++ b/solution.py
@@ -14,10 +14,14 @@
 tag_rows = 16
 
 
-def from_behind(block, axis, distance):
-    devices = range(lax.axis_size(axis))
-    route = [(i - distance, i) for i in devices if i - distance in devices]
-    return lax.ppermute(block, axis, route)
+def to_segment(block, distance):
+    outer, inner = lax.axis_size("outer"), lax.axis_size("inner")
+    route = []
+    for o in range(outer):
+        if o + distance in range(outer):
+            crossed = 1 if max(o, o + distance) == outer // 2 else 0
+            route += [(o * inner + i, (o + distance) * inner + (i ^ crossed)) for i in range(inner)]
+    return lax.ppermute(block, ("outer", "inner"), route)
 
 
 def to_partner(block, axis):
@@ -394,7 +398,7 @@
         stream=(2, 4),
     )(positions, position_partner, queries, query_partner, grad_output, grad_partner)
     group_kv, qs, dot, both_blocks = lax.optimization_barrier((group_kv, qs, dot, both_blocks))
-    prev_kv = from_behind(group_kv, "outer", 1)
+    prev_kv = to_segment(group_kv, 1)
     ks, vs, slots, allowed, p_own, m_own, l_own, o_own = call(
         own_forward,
         "own_forward",
@@ -454,7 +458,7 @@
         [half_query_16, half_stat],
         flops=4 * 2 * tiles * unit,
     )(has_prev, qs, dot, prev_kv, p_theirs, m_own, m_theirs, stats_theirs, other_theirs, first_terms)
-    returned = from_behind(prev_terms, "outer", -1)
+    returned = to_segment(prev_terms, -1)
     dq, dq_partner, own_terms = call(
         own_backward,
         "own_backward",

time: 88.2 us -> 87.8 us (level)
  waiting for transfers between devices: 35.4 us -> 34.5 us
    ppermute x2, waiting for transfers between devices: 10.7 us -> 9.06 us  [to_segment(): return lax.ppermute(block, ('outer', 'inner'), route)]
where the time goes in v12:
time: 87.8 us; the launch traced here: 87.3 us
  waiting for transfers between devices  34.5 us (39%)
  starting transfers between devices  26.7 us (30%)
  Pallas kernels  20.4 us (23%)
  local copies, waits for them, and re-layouts  3.18 us (4%)
  other arithmetic  1.8 us (2%)
    ppermute x7, waiting for transfers between devices, to_partner(): lax.ppermute(block, axis, [(i, i ^ 1) for i in range(lax.axis_size(axis))])  21.4 us
    pallas_call x8, Pallas kernels, run(): pl.pallas_call(kernel, name=name, grid=(1,) if stream else (), out_shape=...  18.7 us
    all_to_all x2, starting transfers between devices, exchange(): lax.all_to_all(parts, axis, 0, 0, axis_index_groups=groups, tiled=True)  14.7 us
    ppermute x2, waiting for transfers between devices, to_segment(): return lax.ppermute(block, ('outer', 'inner'), route)  9.06 us
    ppermute x7, starting transfers between devices, to_partner(): lax.ppermute(block, axis, [(i, i ^ 1) for i in range(lax.axis_size(axis))])  8.2 us
    all_to_all x2, waiting for transfers between devices, exchange(): lax.all_to_all(parts, axis, 0, 0, axis_index_groups=groups, tiled=True)  4.1 us
    ppermute x2, starting transfers between devices, to_segment(): return lax.ppermute(block, ('outer', 'inner'), route)  3.83 us
    unnamed x6, local copies, waits for them, and re-layouts  2.55 us
  transfers between devices with their start and end apart: 11, of which 8 were waited for; matrix products, arithmetic and copies ran while one was open for 1% of the time, Pallas kernels for 17%

profile of v12, /device:TPU:16, one launch (start us, length us, event | category | flops | bytes accessed | tf_op | source)
XLA Modules:
  0.0 87.3 jit_solution(9519815795319219977)
XLA Ops:
  0.6 1.7 %pack.1 = bf16[8,272,128]{2,1,0:T(8,128)(2,1)} custom-call(s32[128]{0:T(128)} %position_ref.3, bf16[128,128]{1,0:T(8,128)(2,1)} %key_ref.1, bf16[128,128]{1,0:T(8,128)(2,1)} %value_ref.1), custom_call_target="tpu_custom_call" | custom-call | tf_op jit(solution)/shard_map/pack/pallas_call | solution.py:366
  2.3 8.5 %all-to-all-start = ((bf16[8,272,128]{2,1,0:T(8,128)(2,1)}), bf16[8,272,128]{2,1,0:T(8,128)(2,1)S(1)}, u32[]{:S(2)}, u32[]{:S(2)}) async-start(bf16[8,272,128]{2,1,0:T(8,128)(2,1)} %pack.1), calls=%async_computation | async-start | bytes 1114112 | tf_op jit(solution)/shard_map/all_to_all | solution.py:34
  10.8 1.3 %collective-permute-start.1 = (bf16[128,1024]{1,0:T(8,128)(2,1)}, bf16[128,1024]{1,0:T(8,128)(2,1)S(1)}, u32[]{:S(2)}, u32[]{:S(2)}) collective-permute-start(bf16[128,1024]{1,0:T(8,128)(2,1)} %q_ref.1), channel_id=1, source_target_pairs={{0,1},{1,0},{2,3},{3,2},{4,5},{5,4},{6,7},{7,6},{8,9},{9,8},{10,11... | collective-permute-start | bytes 786440 | tf_op jit(solution)/shard_map/ppermute | solution.py:28
  12.8 1.3 %collective-permute-start = (s32[128]{0:T(128)}, s32[128]{0:T(128)S(1)}, u32[]{:S(2)}, u32[]{:S(2)}) collective-permute-start(s32[128]{0:T(128)} %position_ref.3), channel_id=1, source_target_pairs={{0,1},{1,0},{2,3},{3,2},{4,5},{5,4},{6,7},{7,6},{8,9},{9,8},{10,11... | collective-permute-start | bytes 1544 | tf_op jit(solution)/shard_map/ppermute | solution.py:28
  14.1 10.4 %collective-permute-done.position_partner_ref = s32[128]{0:T(128)S(1)} collective-permute-done((s32[128]{0:T(128)}, s32[128]{0:T(128)S(1)}, u32[]{:S(2)}, u32[]{:S(2)}) %collective-permute-start) | collective-permute-done | bytes 544 | tf_op jit(solution)/shard_map/ppermute | solution.py:28
  25.1 0.9 %copy-done.1 = bf16[128,1024]{1,0:T(8,128)(2,1)S(1)} copy-done((bf16[128,1024]{1,0:T(8,128)(2,1)S(1)}, bf16[128,1024]{1,0:T(8,128)(2,1)}, u32[]{:S(2)}) %copy-start.1) | copy-done | bytes 262168
  27.0 1.2 %stack_pair.1 = (s32[2]{0:T(128)S(1)}, bf16[4,512,128]{2,1,0:T(8,128)(2,1)S(1)}, bf16[4,128,512]{2,1,0:T(8,128)(2,1)S(1)}) custom-call(s32[128]{0:T(128)S(1)} %copy-done, s32[128]{0:T(128)S(1)} %collective-permute-done.position_partner_ref, bf16[128,1024]{1,0:T(8,128)(2,1)S(1)} %copy-done.1, bf16[128,1024]{1,0:T(8,128)(2,1)S(1)} %collective-permute-done.1.q_partner_ref, ...), custom_call_target="tpu_custom_call" | custom-call | flops 4000000000 | bytes 4194304 | tf_op jit(solution)/shard_map/stack_pair/pallas_call | solution.py:337
  29.0 1.9 %collective-permute-start.3 = (bf16[8,272,128]{2,1,0:T(8,128)(2,1)S(1)}, bf16[8,272,128]{2,1,0:T(8,128)(2,1)S(1)}, u32[]{:S(2)}, u32[]{:S(2)}) collective-permute-start(bf16[8,272,128]{2,1,0:T(8,128)(2,1)S(1)} %all-to-all-done.kv_ref), channel_id=1, source_target_pairs={{0,16},{1,17},{2,18},{3,19},{4,20},{5,21},{6,22},{7,23},{8,24},{9,... | collective-permute-start | bytes 1671176 | tf_op jit(solution)/shard_map/ppermute | solution.py:24
  30.9 3.9 %own_forward.1 = (bf16[1024,128]{1,0:T(8,128)(2,1)S(1)}, bf16[1024,128]{1,0:T(8,128)(2,1)S(1)}, s32[8]{0:T(128)S(1)}, s32[4]{0:T(128)S(1)}, bf16[10,256,512]{2,1...) custom-call(s32[2]{0:T(128)S(1)} %get-tuple-element.45.block_ref, ...), custom_call_target="tpu_custom_call" | custom-call | flops 671088640 | bytes 4194304 | tf_op jit(solution)/shard_map/own_forward/pallas_call | solution.py:337
  34.8 7.2 %collective-permute-done.3.kv_ref = bf16[8,272,128]{2,1,0:T(8,128)(2,1)S(1)} collective-permute-done((bf16[8,272,128]{2,1,0:T(8,128)(2,1)S(1)}, bf16[8,272,128]{2,1,0:T(8,128)(2,1)S(1)}, u32[]{:S(2)}, u32[]{:S(2)}) %collective-permute-start.3) | collective-permute-done | bytes 557088 | tf_op jit(solution)/shard_map/ppermute | solution.py:24
  41.9 2.0 %prev_forward_theirs.1 = (bf16[2,4,256,512]{3,2,1,0:T(8,128)(2,1)S(1)}, f32[2,1,512]{2,1,0:T(1,128)S(1)}, f32[3,2,1,512]{3,2,1,0:T(1,128)S(1)}, bf16[2,128,512]{2,1,0:T(8,128)(2,1)S(1)}) custom-call(s32[1]{0:T(128)} %bitcast.has_ref, bf16[4,512,128]{2,1,0:T(8,128)(2,1)S(1)} %get-tuple-element.42.qs_ref, bf16[4,128,512]{2,1,0:T(8,128)(2,1)S(1)} %get-tuple-element.43.dot_ref, ...), custom_call_target="tpu_custom_call" | custom-call | flops 536870912 | bytes 4194304 | tf_op jit(solution)/shard_map/prev_forward_theirs/pallas_call | solution.py:337
  43.9 2.6 %collective-permute-start.5 = (f32[3,2,1,512]{3,2,1,0:T(1,128)S(1)}, f32[3,2,1,512]{3,2,1,0:T(1,128)S(1)}, u32[]{:S(2)}, u32[]{:S(2)}) collective-permute-start(f32[3,2,1,512]{3,2,1,0:T(1,128)S(1)} %get-tuple-element.54.stats_ref), channel_id=1, source_target_pairs={{0,1},{1,0},{2,3},{3,2},{4,5},{5,4},{6,7},{7,6},{8,9},{9,8},{10,11... | collective-permute-start | bytes 36872 | tf_op jit(solution)/shard_map/ppermute | solution.py:28
  46.5 1.9 %prev_forward_mine.1 = (bf16[2,4,256,512]{3,2,1,0:T(8,128)(2,1)S(1)}, f32[2,1,512]{2,1,0:T(1,128)S(1)}, f32[3,2,1,512]{3,2,1,0:T(1,128)S(1)}, f32[2,128,512]{2,1,0:T(8,128)S(1)}) custom-call(s32[1]{0:T(128)} %bitcast.has_ref, bf16[4,512,128]{2,1,0:T(8,128)(2,1)S(1)} %get-tuple-element.42.qs_ref, bf16[4,128,512]{2,1,0:T(8,128)(2,1)S(1)} %get-tuple-element.43.dot_ref, ...), custom_call_target="tpu_custom_call" | custom-call | flops 536870912 | bytes 4194304 | tf_op jit(solution)/shard_map/prev_forward_mine/pallas_call | solution.py:337
  48.7 1.9 %prev_backward_mine.1 = (f32[1024,256]{1,0:T(8,128)S(1)}, bf16[2,128,512]{2,1,0:T(8,128)(2,1)S(1)}, f32[2,1,512]{2,1,0:T(1,128)S(1)}, bf16[2,4,256,512]{3,2,1,0:T(8,128)(2,1)S(1)}, f32[2,2,1,512]{3,2,1,0:T(1,128)S(1)}) custom-call(s32[1]{0:T(128)} %bitcast.has_ref, bf16[4,512,128]{2,1,0:T(8,128)(2,1)S(1)} %get-tuple-element.42.qs_ref, ...), custom_call_target="tpu_custom_call" | custom-call | flops 1073741824 | bytes 4194304 | tf_op jit(solution)/shard_map/prev_backward_mine/pallas_call | solution.py:337
  50.6 1.8 %collective-permute-done.6.other_ref = f32[3,2,1,512]{3,2,1,0:T(1,128)S(1)} collective-permute-done((f32[3,2,1,512]{3,2,1,0:T(1,128)S(1)}, f32[3,2,1,512]{3,2,1,0:T(1,128)S(1)}, u32[]{:S(2)}, u32[]{:S(2)}) %collective-permute-start.6) | collective-permute-done | bytes 12320 | tf_op jit(solution)/shard_map/ppermute | solution.py:28
  52.4 2.2 %prev_backward_theirs.1 = (bf16[8,128,256]{2,1,0:T(8,128)(2,1)S(1)}, bf16[2,128,512]{2,1,0:T(8,128)(2,1)S(1)}, f32[2,1,512]{2,1,0:T(1,128)S(1)}, bf16[2,4,256,512]{3,2,1,0:T(8,128)(2,1)S(1)}) custom-call(s32[1]{0:T(128)} %bitcast.has_ref, bf16[4,512,128]{2,1,0:T(8,128)(2,1)S(1)} %get-tuple-element.42.qs_ref, ...), custom_call_target="tpu_custom_call" | custom-call | flops 1073741824 | bytes 4194304 | tf_op jit(solution)/shard_map/prev_backward_theirs/pallas_call | solution.py:337
  54.6 1.9 %collective-permute-start.8 = (bf16[8,128,256]{2,1,0:T(8,128)(2,1)S(1)}, bf16[8,128,256]{2,1,0:T(8,128)(2,1)S(1)}, u32[]{:S(2)}, u32[]{:S(2)}) collective-permute-start(bf16[8,128,256]{2,1,0:T(8,128)(2,1)S(1)} %get-tuple-element.73), channel_id=1, source_target_pairs={{16,0},{17,1},{18,2},{19,3},{20,4},{21,5},{22,6},{23,7},{24,8},{25... | collective-permute-start | bytes 1572872 | tf_op jit(solution)/shard_map/ppermute | solution.py:24
  56.6 4.8 %own_backward.1 = (f32[128,1024]{1,0:T(8,128)S(1)}, bf16[128,1024]{1,0:T(8,128)(2,1)S(1)}, bf16[8,128,256]{2,1,0:T(8,128)(2,1)S(1)}) custom-call(s32[4]{0:T(128)S(1)} %get-tuple-element.56.allowed_ref, s32[8]{0:T(128)S(1)} %get-tuple-element.57.slots_ref, bf16[4,512,128]{2,1,0:T(8,128)(2,1)S(1)} %get-tuple-element.42.qs_ref, ...), custom_call_target="tpu_custom_call" | custom-call | flops 1342177280 | bytes 4194304 | tf_op jit(solution)/shard_map/own_backward/pallas_call | solution.py:337
  61.3 1.9 %collective-permute-done.8 = bf16[8,128,256]{2,1,0:T(8,128)(2,1)S(1)} collective-permute-done((bf16[8,128,256]{2,1,0:T(8,128)(2,1)S(1)}, bf16[8,128,256]{2,1,0:T(8,128)(2,1)S(1)}, u32[]{:S(2)}, u32[]{:S(2)}) %collective-permute-start.8) | collective-permute-done | bytes 524320 | tf_op jit(solution)/shard_map/ppermute | solution.py:24
  64.2 6.2 %all-to-all-start.1 = ((bf16[8,128,256]{2,1,0:T(8,128)(2,1)}), bf16[8,128,256]{2,1,0:T(8,128)(2,1)S(1)}, u32[]{:S(2)}, u32[]{:S(2)}) async-start(bf16[8,128,256]{2,1,0:T(8,128)(2,1)} %add_convert_fusion), calls=%async_computation.1 | async-start | bytes 1048576 | tf_op jit(solution)/shard_map/all_to_all | solution.py:34
  70.7 1.8 %collective-permute-start.7 = (bf16[128,1024]{1,0:T(8,128)(2,1)S(1)}, bf16[128,1024]{1,0:T(8,128)(2,1)S(1)}, u32[]{:S(2)}, u32[]{:S(2)}) collective-permute-start(bf16[128,1024]{1,0:T(8,128)(2,1)S(1)} %get-tuple-element.71), channel_id=1, source_target_pairs={{0,1},{1,0},{2,3},{3,2},{4,5},{5,4},{6,7},{7,6},{8,9},{9,8},{10,11... | collective-permute-start | bytes 786440 | tf_op jit(solution)/shard_map/ppermute | solution.py:28
  72.4 7.2 %collective-permute-done.4.got_ref = bf16[2,128,512]{2,1,0:T(8,128)(2,1)S(1)} collective-permute-done((bf16[2,128,512]{2,1,0:T(8,128)(2,1)S(1)}, bf16[2,128,512]{2,1,0:T(8,128)(2,1)S(1)}, u32[]{:S(2)}, u32[]{:S(2)}) %collective-permute-start.4) | collective-permute-done | bytes 262176 | tf_op jit(solution)/shard_map/ppermute | solution.py:28
  80.5 2.0 %collective-permute-done.7 = bf16[128,1024]{1,0:T(8,128)(2,1)S(1)} collective-permute-done((bf16[128,1024]{1,0:T(8,128)(2,1)S(1)}, bf16[128,1024]{1,0:T(8,128)(2,1)S(1)}, u32[]{:S(2)}, u32[]{:S(2)}) %collective-permute-start.7) | collective-permute-done | bytes 262176 | tf_op jit(solution)/shard_map/ppermute | solution.py:28
  83.3 3.3 %all-to-all-done.1 = bf16[8,128,256]{2,1,0:T(8,128)(2,1)S(1)} async-done(((bf16[8,128,256]{2,1,0:T(8,128)(2,1)}), bf16[8,128,256]{2,1,0:T(8,128)(2,1)S(1)}, u32[]{:S(2)}, u32[]{:S(2)}) %all-to-all-start.1) | async-done | bytes 524320 | tf_op jit(solution)/shard_map/all_to_all | solution.py:34
  (17 shorter events, 7.0 us)
Async XLA Ops:
  2.3 26.7 %all-to-all-start = ((bf16[8,272,128]{2,1,0:T(8,128)(2,1)}), bf16[8,272,128]{2,1,0:T(8,128)(2,1)S(1)}, u32[]{:S(2)}, u32[]{:S(2)}) async-start(bf16[8,272,128]{2,1,0:T(8,128)(2,1)} %pack.1), calls=%async_computation | async-start | bytes 1114112 | tf_op jit(solution)/shard_map/all_to_all | solution.py:34
  10.8 13.7 %collective-permute-start.1 = (bf16[128,1024]{1,0:T(8,128)(2,1)}, bf16[128,1024]{1,0:T(8,128)(2,1)S(1)}, u32[]{:S(2)}, u32[]{:S(2)}) collective-permute-start(bf16[128,1024]{1,0:T(8,128)(2,1)} %q_ref.1), channel_id=1, source_target_pairs={{0,1},{1,0},{2,3},{3,2},{4,5},{5,4},{6,7},{7,6},{8,9},{9,8},{10,11... | collective-permute-start | bytes 786440 | tf_op jit(solution)/shard_map/ppermute | solution.py:28
  12.1 12.4 %collective-permute-start.2 = (bf16[128,1024]{1,0:T(8,128)(2,1)}, bf16[128,1024]{1,0:T(8,128)(2,1)S(1)}, u32[]{:S(2)}, u32[]{:S(2)}) collective-permute-start(bf16[128,1024]{1,0:T(8,128)(2,1)} %do_ref.1), channel_id=1, source_target_pairs={{0,1},{1,0},{2,3},{3,2},{4,5},{5,4},{6,7},{7,6},{8,9},{9,8},{10,11... | collective-permute-start | bytes 786440 | tf_op jit(solution)/shard_map/ppermute | solution.py:28
  12.8 11.6 %collective-permute-start = (s32[128]{0:T(128)}, s32[128]{0:T(128)S(1)}, u32[]{:S(2)}, u32[]{:S(2)}) collective-permute-start(s32[128]{0:T(128)} %position_ref.3), channel_id=1, source_target_pairs={{0,1},{1,0},{2,3},{3,2},{4,5},{5,4},{6,7},{7,6},{8,9},{9,8},{10,11... | collective-permute-start | bytes 1544 | tf_op jit(solution)/shard_map/ppermute | solution.py:28
  24.5 0.7 copy-start
  25.1 0.9 %copy-start.1 = (bf16[128,1024]{1,0:T(8,128)(2,1)S(1)}, bf16[128,1024]{1,0:T(8,128)(2,1)}, u32[]{:S(2)}) copy-start(bf16[128,1024]{1,0:T(8,128)(2,1)} %q_ref.1) | copy-start | bytes 786436
  26.1 0.9 %copy-start.2 = (bf16[128,1024]{1,0:T(8,128)(2,1)S(1)}, bf16[128,1024]{1,0:T(8,128)(2,1)}, u32[]{:S(2)}) copy-start(bf16[128,1024]{1,0:T(8,128)(2,1)} %do_ref.1) | copy-start | bytes 786436
  29.0 12.9 %collective-permute-start.3 = (bf16[8,272,128]{2,1,0:T(8,128)(2,1)S(1)}, bf16[8,272,128]{2,1,0:T(8,128)(2,1)S(1)}, u32[]{:S(2)}, u32[]{:S(2)}) collective-permute-start(bf16[8,272,128]{2,1,0:T(8,128)(2,1)S(1)} %all-to-all-done.kv_ref), channel_id=1, source_target_pairs={{0,16},{1,17},{2,18},{3,19},{4,20},{5,21},{6,22},{7,23},{8,24},{9,... | collective-permute-start | bytes 1671176 | tf_op jit(solution)/shard_map/ppermute | solution.py:24
  43.9 4.8 %collective-permute-start.5 = (f32[3,2,1,512]{3,2,1,0:T(1,128)S(1)}, f32[3,2,1,512]{3,2,1,0:T(1,128)S(1)}, u32[]{:S(2)}, u32[]{:S(2)}) collective-permute-start(f32[3,2,1,512]{3,2,1,0:T(1,128)S(1)} %get-tuple-element.54.stats_ref), channel_id=1, source_target_pairs={{0,1},{1,0},{2,3},{3,2},{4,5},{5,4},{6,7},{7,6},{8,9},{9,8},{10,11... | collective-permute-start | bytes 36872 | tf_op jit(solution)/shard_map/ppermute | solution.py:28
  48.4 4.0 %collective-permute-start.6 = (f32[3,2,1,512]{3,2,1,0:T(1,128)S(1)}, f32[3,2,1,512]{3,2,1,0:T(1,128)S(1)}, u32[]{:S(2)}, u32[]{:S(2)}) collective-permute-start(f32[3,2,1,512]{3,2,1,0:T(1,128)S(1)} %get-tuple-element.53.stats_ref), channel_id=1, source_target_pairs={{0,1},{1,0},{2,3},{3,2},{4,5},{5,4},{6,7},{7,6},{8,9},{9,8},{10,11... | collective-permute-start | bytes 36872 | tf_op jit(solution)/shard_map/ppermute | solution.py:28
  54.6 8.6 %collective-permute-start.8 = (bf16[8,128,256]{2,1,0:T(8,128)(2,1)S(1)}, bf16[8,128,256]{2,1,0:T(8,128)(2,1)S(1)}, u32[]{:S(2)}, u32[]{:S(2)}) collective-permute-start(bf16[8,128,256]{2,1,0:T(8,128)(2,1)S(1)} %get-tuple-element.73), channel_id=1, source_target_pairs={{16,0},{17,1},{18,2},{19,3},{20,4},{21,5},{22,6},{23,7},{24,8},{25... | collective-permute-start | bytes 1572872 | tf_op jit(solution)/shard_map/ppermute | solution.py:24
  64.2 22.4 %all-to-all-start.1 = ((bf16[8,128,256]{2,1,0:T(8,128)(2,1)}), bf16[8,128,256]{2,1,0:T(8,128)(2,1)S(1)}, u32[]{:S(2)}, u32[]{:S(2)}) async-start(bf16[8,128,256]{2,1,0:T(8,128)(2,1)} %add_convert_fusion), calls=%async_computation.1 | async-start | bytes 1048576 | tf_op jit(solution)/shard_map/all_to_all | solution.py:34
  70.4 9.2 %collective-permute-start.4 = (bf16[2,128,512]{2,1,0:T(8,128)(2,1)S(1)}, bf16[2,128,512]{2,1,0:T(8,128)(2,1)S(1)}, u32[]{:S(2)}, u32[]{:S(2)}) collective-permute-start(bf16[2,128,512]{2,1,0:T(8,128)(2,1)S(1)} %get-tuple-element.50), channel_id=1, source_target_pairs={{0,1},{1,0},{2,3},{3,2},{4,5},{5,4},{6,7},{7,6},{8,9},{9,8},{10,11... | collective-permute-start | bytes 786440 | tf_op jit(solution)/shard_map/ppermute | solution.py:28
  70.7 11.9 %collective-permute-start.7 = (bf16[128,1024]{1,0:T(8,128)(2,1)S(1)}, bf16[128,1024]{1,0:T(8,128)(2,1)S(1)}, u32[]{:S(2)}, u32[]{:S(2)}) collective-permute-start(bf16[128,1024]{1,0:T(8,128)(2,1)S(1)} %get-tuple-element.71), channel_id=1, source_target_pairs={{0,1},{1,0},{2,3},{3,2},{4,5},{5,4},{6,7},{7,6},{8,9},{9,8},{10,11... | collective-permute-start | bytes 786440 | tf_op jit(solution)/shard_map/ppermute | solution.py:28

commit v13 on v12

--- a/solution.py
+++ b/solution.py
@@ -100,6 +100,13 @@
             qs_ref[2 * j + half] = stack_heads(query, half, heads, head_dim)
             stacked = stack_heads(grad, half, heads, head_dim).astype(jnp.float32)
             dot_ref[2 * j + half] = stacked.T.astype(jnp.bfloat16)
+
+
+def sum_parts(parts_ref, key_ref, value_ref):
+    head_dim = key_ref.shape[1]
+    total = sum(parts_ref[g].astype(jnp.float32) for g in range(parts_ref.shape[0]))
+    key_ref[...] = total[:, :head_dim].astype(key_ref.dtype)
+    value_ref[...] = total[:, head_dim:].astype(value_ref.dtype)
 
 
 def merge_attended(out_ref, got_ref, factor_ref, att_ref):
@@ -470,10 +477,11 @@
     (attended,) = call(merge_attended, "merge_attended", [tokens], (), [])(out, got, factor)
     dq_other = to_partner(dq_partner, "inner")
     terms = (own_terms.astype(f32) + returned.astype(f32)).astype(bf16)
-    key_grads = jnp.sum(exchange(terms, "inner").astype(f32), axis=0)
+    parts = exchange(terms, "inner")
+    grad_keys, grad_values = call(
+        sum_parts, "sum_parts", [((tok_rows, head_dim), bf16)] * 2, (), []
+    )(parts)
     grad_queries = (dq + dq_other.astype(f32)).astype(bf16)
-    grad_keys = key_grads[:, :head_dim].astype(bf16)
-    grad_values = key_grads[:, head_dim:].astype(bf16)
     return (attended, grad_queries, grad_keys, grad_values)
 
 

time: 87.8 us -> 87.7 us (level)
    pallas_call x8 -> x9, Pallas kernels: 18.7 us -> 19.3 us  [run(): pl.pallas_call(kernel, name=name, grid=(1,) if stream else (), out_shape=...]
where the time goes in v13:
time: 87.7 us; the launch traced here: 87.3 us
  waiting for transfers between devices  34.6 us (39%)
  starting transfers between devices  26.7 us (30%)
  Pallas kernels  21 us (24%)
  local copies, waits for them, and re-layouts  2.55 us (3%)
  other arithmetic  1.69 us (2%)
    ppermute x7, waiting for transfers between devices, to_partner(): lax.ppermute(block, axis, [(i, i ^ 1) for i in range(lax.axis_size(axis))])  21.4 us
    pallas_call x9, Pallas kernels, run(): pl.pallas_call(kernel, name=name, grid=(1,) if stream else (), out_shape=...  19.3 us
    all_to_all x2, starting transfers between devices, exchange(): lax.all_to_all(parts, axis, 0, 0, axis_index_groups=groups, tiled=True)  14.7 us
    ppermute x2, waiting for transfers between devices, to_segment(): return lax.ppermute(block, ('outer', 'inner'), route)  9.08 us
    ppermute x7, starting transfers between devices, to_partner(): lax.ppermute(block, axis, [(i, i ^ 1) for i in range(lax.axis_size(axis))])  8.2 us
    all_to_all x2, waiting for transfers between devices, exchange(): lax.all_to_all(parts, axis, 0, 0, axis_index_groups=groups, tiled=True)  4.11 us
    ppermute x2, starting transfers between devices, to_segment(): return lax.ppermute(block, ('outer', 'inner'), route)  3.83 us
    unnamed x6, local copies, waits for them, and re-layouts  2.55 us
  transfers between devices with their start and end apart: 11, of which 8 were waited for; matrix products, arithmetic and copies ran while one was open for 1% of the time, Pallas kernels for 17%

profile of v13, /device:TPU:16, one launch (start us, length us, event | category | flops | bytes accessed | tf_op | source)
XLA Modules:
  0.0 87.3 jit_solution(9492463988267819014)
XLA Ops:
  0.6 1.7 %pack.1 = bf16[8,272,128]{2,1,0:T(8,128)(2,1)} custom-call(s32[128]{0:T(128)} %position_ref.3, bf16[128,128]{1,0:T(8,128)(2,1)} %key_ref.1, bf16[128,128]{1,0:T(8,128)(2,1)} %value_ref.1), custom_call_target="tpu_custom_call" | custom-call | tf_op jit(solution)/shard_map/pack/pallas_call | solution.py:373
  2.3 8.5 %all-to-all-start = ((bf16[8,272,128]{2,1,0:T(8,128)(2,1)}), bf16[8,272,128]{2,1,0:T(8,128)(2,1)S(1)}, u32[]{:S(2)}, u32[]{:S(2)}) async-start(bf16[8,272,128]{2,1,0:T(8,128)(2,1)} %pack.1), calls=%async_computation | async-start | bytes 1114112 | tf_op jit(solution)/shard_map/all_to_all | solution.py:34
  10.8 1.3 %collective-permute-start.1 = (bf16[128,1024]{1,0:T(8,128)(2,1)}, bf16[128,1024]{1,0:T(8,128)(2,1)S(1)}, u32[]{:S(2)}, u32[]{:S(2)}) collective-permute-start(bf16[128,1024]{1,0:T(8,128)(2,1)} %q_ref.1), channel_id=1, source_target_pairs={{0,1},{1,0},{2,3},{3,2},{4,5},{5,4},{6,7},{7,6},{8,9},{9,8},{10,11... | collective-permute-start | bytes 786440 | tf_op jit(solution)/shard_map/ppermute | solution.py:28
  12.8 1.3 %collective-permute-start = (s32[128]{0:T(128)}, s32[128]{0:T(128)S(1)}, u32[]{:S(2)}, u32[]{:S(2)}) collective-permute-start(s32[128]{0:T(128)} %position_ref.3), channel_id=1, source_target_pairs={{0,1},{1,0},{2,3},{3,2},{4,5},{5,4},{6,7},{7,6},{8,9},{9,8},{10,11... | collective-permute-start | bytes 1544 | tf_op jit(solution)/shard_map/ppermute | solution.py:28
  14.1 10.4 %collective-permute-done.position_partner_ref = s32[128]{0:T(128)S(1)} collective-permute-done((s32[128]{0:T(128)}, s32[128]{0:T(128)S(1)}, u32[]{:S(2)}, u32[]{:S(2)}) %collective-permute-start) | collective-permute-done | bytes 544 | tf_op jit(solution)/shard_map/ppermute | solution.py:28
  26.1 0.9 %copy-done.2 = bf16[128,1024]{1,0:T(8,128)(2,1)S(1)} copy-done((bf16[128,1024]{1,0:T(8,128)(2,1)S(1)}, bf16[128,1024]{1,0:T(8,128)(2,1)}, u32[]{:S(2)}) %copy-start.2) | copy-done | bytes 262168
  27.0 1.2 %stack_pair.1 = (s32[2]{0:T(128)S(1)}, bf16[4,512,128]{2,1,0:T(8,128)(2,1)S(1)}, bf16[4,128,512]{2,1,0:T(8,128)(2,1)S(1)}) custom-call(s32[128]{0:T(128)S(1)} %copy-done, s32[128]{0:T(128)S(1)} %collective-permute-done.position_partner_ref, bf16[128,1024]{1,0:T(8,128)(2,1)S(1)} %copy-done.1, bf16[128,1024]{1,0:T(8,128)(2,1)S(1)} %collective-permute-done.1.q_partner_ref, ...), custom_call_target="tpu_custom_call" | custom-call | flops 4000000000 | bytes 4194304 | tf_op jit(solution)/shard_map/stack_pair/pallas_call | solution.py:344
  29.0 1.9 %collective-permute-start.3 = (bf16[8,272,128]{2,1,0:T(8,128)(2,1)S(1)}, bf16[8,272,128]{2,1,0:T(8,128)(2,1)S(1)}, u32[]{:S(2)}, u32[]{:S(2)}) collective-permute-start(bf16[8,272,128]{2,1,0:T(8,128)(2,1)S(1)} %all-to-all-done.kv_ref), channel_id=1, source_target_pairs={{0,16},{1,17},{2,18},{3,19},{4,20},{5,21},{6,22},{7,23},{8,24},{9,... | collective-permute-start | bytes 1671176 | tf_op jit(solution)/shard_map/ppermute | solution.py:24
  30.9 3.8 %own_forward.1 = (bf16[1024,128]{1,0:T(8,128)(2,1)S(1)}, bf16[1024,128]{1,0:T(8,128)(2,1)S(1)}, s32[8]{0:T(128)S(1)}, s32[4]{0:T(128)S(1)}, bf16[10,256,512]{2,1...) custom-call(s32[2]{0:T(128)S(1)} %get-tuple-element.47.block_ref, ...), custom_call_target="tpu_custom_call" | custom-call | flops 671088640 | bytes 4194304 | tf_op jit(solution)/shard_map/own_forward/pallas_call | solution.py:344
  34.8 7.2 %collective-permute-done.3.kv_ref = bf16[8,272,128]{2,1,0:T(8,128)(2,1)S(1)} collective-permute-done((bf16[8,272,128]{2,1,0:T(8,128)(2,1)S(1)}, bf16[8,272,128]{2,1,0:T(8,128)(2,1)S(1)}, u32[]{:S(2)}, u32[]{:S(2)}) %collective-permute-start.3) | collective-permute-done | bytes 557088 | tf_op jit(solution)/shard_map/ppermute | solution.py:24
  42.0 1.9 %prev_forward_theirs.1 = (bf16[2,4,256,512]{3,2,1,0:T(8,128)(2,1)S(1)}, f32[2,1,512]{2,1,0:T(1,128)S(1)}, f32[3,2,1,512]{3,2,1,0:T(1,128)S(1)}, bf16[2,128,512]{2,1,0:T(8,128)(2,1)S(1)}) custom-call(s32[1]{0:T(128)} %bitcast.has_ref, bf16[4,512,128]{2,1,0:T(8,128)(2,1)S(1)} %get-tuple-element.44.qs_ref, bf16[4,128,512]{2,1,0:T(8,128)(2,1)S(1)} %get-tuple-element.45.dot_ref, ...), custom_call_target="tpu_custom_call" | custom-call | flops 536870912 | bytes 4194304 | tf_op jit(solution)/shard_map/prev_forward_theirs/pallas_call | solution.py:344
  43.9 2.6 %collective-permute-start.5 = (f32[3,2,1,512]{3,2,1,0:T(1,128)S(1)}, f32[3,2,1,512]{3,2,1,0:T(1,128)S(1)}, u32[]{:S(2)}, u32[]{:S(2)}) collective-permute-start(f32[3,2,1,512]{3,2,1,0:T(1,128)S(1)} %get-tuple-element.56.stats_ref), channel_id=1, source_target_pairs={{0,1},{1,0},{2,3},{3,2},{4,5},{5,4},{6,7},{7,6},{8,9},{9,8},{10,11... | collective-permute-start | bytes 36872 | tf_op jit(solution)/shard_map/ppermute | solution.py:28
  46.5 1.9 %prev_forward_mine.1 = (bf16[2,4,256,512]{3,2,1,0:T(8,128)(2,1)S(1)}, f32[2,1,512]{2,1,0:T(1,128)S(1)}, f32[3,2,1,512]{3,2,1,0:T(1,128)S(1)}, f32[2,128,512]{2,1,0:T(8,128)S(1)}) custom-call(s32[1]{0:T(128)} %bitcast.has_ref, bf16[4,512,128]{2,1,0:T(8,128)(2,1)S(1)} %get-tuple-element.44.qs_ref, bf16[4,128,512]{2,1,0:T(8,128)(2,1)S(1)} %get-tuple-element.45.dot_ref, ...), custom_call_target="tpu_custom_call" | custom-call | flops 536870912 | bytes 4194304 | tf_op jit(solution)/shard_map/prev_forward_mine/pallas_call | solution.py:344
  48.7 1.9 %prev_backward_mine.1 = (f32[1024,256]{1,0:T(8,128)S(1)}, bf16[2,128,512]{2,1,0:T(8,128)(2,1)S(1)}, f32[2,1,512]{2,1,0:T(1,128)S(1)}, bf16[2,4,256,512]{3,2,1,0:T(8,128)(2,1)S(1)}, f32[2,2,1,512]{3,2,1,0:T(1,128)S(1)}) custom-call(s32[1]{0:T(128)} %bitcast.has_ref, bf16[4,512,128]{2,1,0:T(8,128)(2,1)S(1)} %get-tuple-element.44.qs_ref, ...), custom_call_target="tpu_custom_call" | custom-call | flops 1073741824 | bytes 4194304 | tf_op jit(solution)/shard_map/prev_backward_mine/pallas_call | solution.py:344
  50.6 1.8 %collective-permute-done.6.other_ref = f32[3,2,1,512]{3,2,1,0:T(1,128)S(1)} collective-permute-done((f32[3,2,1,512]{3,2,1,0:T(1,128)S(1)}, f32[3,2,1,512]{3,2,1,0:T(1,128)S(1)}, u32[]{:S(2)}, u32[]{:S(2)}) %collective-permute-start.6) | collective-permute-done | bytes 12320 | tf_op jit(solution)/shard_map/ppermute | solution.py:28
  52.4 2.2 %prev_backward_theirs.1 = (bf16[8,128,256]{2,1,0:T(8,128)(2,1)S(1)}, bf16[2,128,512]{2,1,0:T(8,128)(2,1)S(1)}, f32[2,1,512]{2,1,0:T(1,128)S(1)}, bf16[2,4,256,512]{3,2,1,0:T(8,128)(2,1)S(1)}) custom-call(s32[1]{0:T(128)} %bitcast.has_ref, bf16[4,512,128]{2,1,0:T(8,128)(2,1)S(1)} %get-tuple-element.44.qs_ref, ...), custom_call_target="tpu_custom_call" | custom-call | flops 1073741824 | bytes 4194304 | tf_op jit(solution)/shard_map/prev_backward_theirs/pallas_call | solution.py:344
  54.6 1.9 %collective-permute-start.8 = (bf16[8,128,256]{2,1,0:T(8,128)(2,1)S(1)}, bf16[8,128,256]{2,1,0:T(8,128)(2,1)S(1)}, u32[]{:S(2)}, u32[]{:S(2)}) collective-permute-start(bf16[8,128,256]{2,1,0:T(8,128)(2,1)S(1)} %get-tuple-element.75), channel_id=1, source_target_pairs={{16,0},{17,1},{18,2},{19,3},{20,4},{21,5},{22,6},{23,7},{24,8},{25... | collective-permute-start | bytes 1572872 | tf_op jit(solution)/shard_map/ppermute | solution.py:24
  56.6 4.8 %own_backward.1 = (f32[128,1024]{1,0:T(8,128)S(1)}, bf16[128,1024]{1,0:T(8,128)(2,1)S(1)}, bf16[8,128,256]{2,1,0:T(8,128)(2,1)S(1)}) custom-call(s32[4]{0:T(128)S(1)} %get-tuple-element.58.allowed_ref, s32[8]{0:T(128)S(1)} %get-tuple-element.59.slots_ref, bf16[4,512,128]{2,1,0:T(8,128)(2,1)S(1)} %get-tuple-element.44.qs_ref, ...), custom_call_target="tpu_custom_call" | custom-call | flops 1342177280 | bytes 4194304 | tf_op jit(solution)/shard_map/own_backward/pallas_call | solution.py:344
  61.3 1.9 %collective-permute-done.8 = bf16[8,128,256]{2,1,0:T(8,128)(2,1)S(1)} collective-permute-done((bf16[8,128,256]{2,1,0:T(8,128)(2,1)S(1)}, bf16[8,128,256]{2,1,0:T(8,128)(2,1)S(1)}, u32[]{:S(2)}, u32[]{:S(2)}) %collective-permute-start.8) | collective-permute-done | bytes 524320 | tf_op jit(solution)/shard_map/ppermute | solution.py:24
  64.2 6.2 %all-to-all-start.1 = ((bf16[8,128,256]{2,1,0:T(8,128)(2,1)}), bf16[8,128,256]{2,1,0:T(8,128)(2,1)S(1)}, u32[]{:S(2)}, u32[]{:S(2)}) async-start(bf16[8,128,256]{2,1,0:T(8,128)(2,1)} %add_convert_fusion), calls=%async_computation.1 | async-start | bytes 1048576 | tf_op jit(solution)/shard_map/all_to_all | solution.py:34
  70.6 1.8 %collective-permute-start.7 = (bf16[128,1024]{1,0:T(8,128)(2,1)S(1)}, bf16[128,1024]{1,0:T(8,128)(2,1)S(1)}, u32[]{:S(2)}, u32[]{:S(2)}) collective-permute-start(bf16[128,1024]{1,0:T(8,128)(2,1)S(1)} %get-tuple-element.73), channel_id=1, source_target_pairs={{0,1},{1,0},{2,3},{3,2},{4,5},{5,4},{6,7},{7,6},{8,9},{9,8},{10,11... | collective-permute-start | bytes 786440 | tf_op jit(solution)/shard_map/ppermute | solution.py:28
  72.4 7.2 %collective-permute-done.4.got_ref = bf16[2,128,512]{2,1,0:T(8,128)(2,1)S(1)} collective-permute-done((bf16[2,128,512]{2,1,0:T(8,128)(2,1)S(1)}, bf16[2,128,512]{2,1,0:T(8,128)(2,1)S(1)}, u32[]{:S(2)}, u32[]{:S(2)}) %collective-permute-start.4) | collective-permute-done | bytes 262176 | tf_op jit(solution)/shard_map/ppermute | solution.py:28
  80.4 2.1 %collective-permute-done.7 = bf16[128,1024]{1,0:T(8,128)(2,1)S(1)} collective-permute-done((bf16[128,1024]{1,0:T(8,128)(2,1)S(1)}, bf16[128,1024]{1,0:T(8,128)(2,1)S(1)}, u32[]{:S(2)}, u32[]{:S(2)}) %collective-permute-start.7) | collective-permute-done | bytes 262176 | tf_op jit(solution)/shard_map/ppermute | solution.py:28
  83.3 3.4 %all-to-all-done.1.parts_ref = bf16[8,128,256]{2,1,0:T(8,128)(2,1)S(1)} async-done(((bf16[8,128,256]{2,1,0:T(8,128)(2,1)}), bf16[8,128,256]{2,1,0:T(8,128)(2,1)S(1)}, u32[]{:S(2)}, u32[]{:S(2)}) %all-to-all-start.1) | async-done | bytes 524320 | tf_op jit(solution)/shard_map/all_to_all | solution.py:34
  (16 shorter events, 6.9 us)
Async XLA Ops:
  2.3 26.7 %all-to-all-start = ((bf16[8,272,128]{2,1,0:T(8,128)(2,1)}), bf16[8,272,128]{2,1,0:T(8,128)(2,1)S(1)}, u32[]{:S(2)}, u32[]{:S(2)}) async-start(bf16[8,272,128]{2,1,0:T(8,128)(2,1)} %pack.1), calls=%async_computation | async-start | bytes 1114112 | tf_op jit(solution)/shard_map/all_to_all | solution.py:34
  10.8 13.7 %collective-permute-start.1 = (bf16[128,1024]{1,0:T(8,128)(2,1)}, bf16[128,1024]{1,0:T(8,128)(2,1)S(1)}, u32[]{:S(2)}, u32[]{:S(2)}) collective-permute-start(bf16[128,1024]{1,0:T(8,128)(2,1)} %q_ref.1), channel_id=1, source_target_pairs={{0,1},{1,0},{2,3},{3,2},{4,5},{5,4},{6,7},{7,6},{8,9},{9,8},{10,11... | collective-permute-start | bytes 786440 | tf_op jit(solution)/shard_map/ppermute | solution.py:28
  12.1 12.4 %collective-permute-start.2 = (bf16[128,1024]{1,0:T(8,128)(2,1)}, bf16[128,1024]{1,0:T(8,128)(2,1)S(1)}, u32[]{:S(2)}, u32[]{:S(2)}) collective-permute-start(bf16[128,1024]{1,0:T(8,128)(2,1)} %do_ref.1), channel_id=1, source_target_pairs={{0,1},{1,0},{2,3},{3,2},{4,5},{5,4},{6,7},{7,6},{8,9},{9,8},{10,11... | collective-permute-start | bytes 786440 | tf_op jit(solution)/shard_map/ppermute | solution.py:28
  12.8 11.6 %collective-permute-start = (s32[128]{0:T(128)}, s32[128]{0:T(128)S(1)}, u32[]{:S(2)}, u32[]{:S(2)}) collective-permute-start(s32[128]{0:T(128)} %position_ref.3), channel_id=1, source_target_pairs={{0,1},{1,0},{2,3},{3,2},{4,5},{5,4},{6,7},{7,6},{8,9},{9,8},{10,11... | collective-permute-start | bytes 1544 | tf_op jit(solution)/shard_map/ppermute | solution.py:28
  24.5 0.7 copy-start
  25.1 0.9 %copy-start.1 = (bf16[128,1024]{1,0:T(8,128)(2,1)S(1)}, bf16[128,1024]{1,0:T(8,128)(2,1)}, u32[]{:S(2)}) copy-start(bf16[128,1024]{1,0:T(8,128)(2,1)} %q_ref.1) | copy-start | bytes 786436
  26.1 0.9 %copy-start.2 = (bf16[128,1024]{1,0:T(8,128)(2,1)S(1)}, bf16[128,1024]{1,0:T(8,128)(2,1)}, u32[]{:S(2)}) copy-start(bf16[128,1024]{1,0:T(8,128)(2,1)} %do_ref.1) | copy-start | bytes 786436
  29.0 12.9 %collective-permute-start.3 = (bf16[8,272,128]{2,1,0:T(8,128)(2,1)S(1)}, bf16[8,272,128]{2,1,0:T(8,128)(2,1)S(1)}, u32[]{:S(2)}, u32[]{:S(2)}) collective-permute-start(bf16[8,272,128]{2,1,0:T(8,128)(2,1)S(1)} %all-to-all-done.kv_ref), channel_id=1, source_target_pairs={{0,16},{1,17},{2,18},{3,19},{4,20},{5,21},{6,22},{7,23},{8,24},{9,... | collective-permute-start | bytes 1671176 | tf_op jit(solution)/shard_map/ppermute | solution.py:24
  43.9 4.8 %collective-permute-start.5 = (f32[3,2,1,512]{3,2,1,0:T(1,128)S(1)}, f32[3,2,1,512]{3,2,1,0:T(1,128)S(1)}, u32[]{:S(2)}, u32[]{:S(2)}) collective-permute-start(f32[3,2,1,512]{3,2,1,0:T(1,128)S(1)} %get-tuple-element.56.stats_ref), channel_id=1, source_target_pairs={{0,1},{1,0},{2,3},{3,2},{4,5},{5,4},{6,7},{7,6},{8,9},{9,8},{10,11... | collective-permute-start | bytes 36872 | tf_op jit(solution)/shard_map/ppermute | solution.py:28
  48.4 4.0 %collective-permute-start.6 = (f32[3,2,1,512]{3,2,1,0:T(1,128)S(1)}, f32[3,2,1,512]{3,2,1,0:T(1,128)S(1)}, u32[]{:S(2)}, u32[]{:S(2)}) collective-permute-start(f32[3,2,1,512]{3,2,1,0:T(1,128)S(1)} %get-tuple-element.55.stats_ref), channel_id=1, source_target_pairs={{0,1},{1,0},{2,3},{3,2},{4,5},{5,4},{6,7},{7,6},{8,9},{9,8},{10,11... | collective-permute-start | bytes 36872 | tf_op jit(solution)/shard_map/ppermute | solution.py:28
  54.6 8.6 %collective-permute-start.8 = (bf16[8,128,256]{2,1,0:T(8,128)(2,1)S(1)}, bf16[8,128,256]{2,1,0:T(8,128)(2,1)S(1)}, u32[]{:S(2)}, u32[]{:S(2)}) collective-permute-start(bf16[8,128,256]{2,1,0:T(8,128)(2,1)S(1)} %get-tuple-element.75), channel_id=1, source_target_pairs={{16,0},{17,1},{18,2},{19,3},{20,4},{21,5},{22,6},{23,7},{24,8},{25... | collective-permute-start | bytes 1572872 | tf_op jit(solution)/shard_map/ppermute | solution.py:24
  64.2 22.5 %all-to-all-start.1 = ((bf16[8,128,256]{2,1,0:T(8,128)(2,1)}), bf16[8,128,256]{2,1,0:T(8,128)(2,1)S(1)}, u32[]{:S(2)}, u32[]{:S(2)}) async-start(bf16[8,128,256]{2,1,0:T(8,128)(2,1)} %add_convert_fusion), calls=%async_computation.1 | async-start | bytes 1048576 | tf_op jit(solution)/shard_map/all_to_all | solution.py:34
  70.3 9.2 %collective-permute-start.4 = (bf16[2,128,512]{2,1,0:T(8,128)(2,1)S(1)}, bf16[2,128,512]{2,1,0:T(8,128)(2,1)S(1)}, u32[]{:S(2)}, u32[]{:S(2)}) collective-permute-start(bf16[2,128,512]{2,1,0:T(8,128)(2,1)S(1)} %get-tuple-element.52), channel_id=1, source_target_pairs={{0,1},{1,0},{2,3},{3,2},{4,5},{5,4},{6,7},{7,6},{8,9},{9,8},{10,11... | collective-permute-start | bytes 786440 | tf_op jit(solution)/shard_map/ppermute | solution.py:28
  70.6 11.9 %collective-permute-start.7 = (bf16[128,1024]{1,0:T(8,128)(2,1)S(1)}, bf16[128,1024]{1,0:T(8,128)(2,1)S(1)}, u32[]{:S(2)}, u32[]{:S(2)}) collective-permute-start(bf16[128,1024]{1,0:T(8,128)(2,1)S(1)} %get-tuple-element.73), channel_id=1, source_target_pairs={{0,1},{1,0},{2,3},{3,2},{4,5},{5,4},{6,7},{7,6},{8,9},{9,8},{10,11... | collective-permute-start | bytes 786440 | tf_op jit(solution)/shard_map/ppermute | solution.py:28

commit v14 on v13

--- a/solution.py
+++ b/solution.py
@@ -195,23 +195,27 @@
     sets, tiles = p_ref.shape[:2]
     exponent_scale = log2_e * float(head_dim) ** (-0.5)
     has_prev = has_ref[0] > 0
+    def score(at, tile):
+        scores = dot_nt(key_tile(kv_ref, tile, 0), qs_ref[first + at])
+        s_ref[at, tile] = scores
+        return jnp.max(scores, axis=0, keepdims=True)
+
+    peaks = [functools.reduce(jnp.maximum, [score(0, tile) for tile in range(tiles)])]
     for at in range(sets):
-        peak = jnp.full((1, width), masked_score, jnp.float32)
-        for tile in range(tiles):
-            scores = dot_nt(key_tile(kv_ref, tile, 0), qs_ref[first + at])
-            s_ref[at, tile] = scores
-            peak = jnp.maximum(peak, jnp.max(scores, axis=0, keepdims=True))
-        m_prev_ref[at] = peak
-    for at in range(sets):
-        peak = m_prev_ref[at]
+        peak = peaks[at]
         total = jnp.zeros((1, width), jnp.float32)
         out = jnp.zeros((head_dim, width), jnp.float32)
+        later = []
         for tile in range(tiles):
+            if at + 1 < sets:
+                later.append(score(at + 1, tile))
             raised = jnp.exp2((s_ref[at, tile] - peak) * exponent_scale)
             total += jnp.sum(raised, axis=0, keepdims=True)
             raised = raised.astype(jnp.bfloat16)
             p_ref[at, tile] = raised
             out += dot_tn(key_tile(kv_ref, tile, 1), raised)
+        if later:
+            peaks.append(functools.reduce(jnp.maximum, later))
         peak = jnp.where(has_prev, peak, masked_score)
         m_prev_ref[at] = peak
         top = jnp.maximum(peak, m_own_ref[first + at])

time: 87.7 us -> 88.1 us (level)
  no operation moved by 1% of the time
where the time goes in v14:
time: 88.1 us; the launch traced here: 87.7 us
  waiting for transfers between devices  34.6 us (39%)
  starting transfers between devices  26.7 us (30%)
  Pallas kernels  21.4 us (24%)
  local copies, waits for them, and re-layouts  2.55 us (3%)
  other arithmetic  1.69 us (2%)
    ppermute x7, waiting for transfers between devices, to_partner(): lax.ppermute(block, axis, [(i, i ^ 1) for i in range(lax.axis_size(axis))])  21.4 us
    pallas_call x9, Pallas kernels, run(): pl.pallas_call(kernel, name=name, grid=(1,) if stream else (), out_shape=...  19.7 us
    all_to_all x2, starting transfers between devices, exchange(): lax.all_to_all(parts, axis, 0, 0, axis_index_groups=groups, tiled=True)  14.7 us
    ppermute x2, waiting for transfers between devices, to_segment(): return lax.ppermute(block, ('outer', 'inner'), route)  9.09 us
    ppermute x7, starting transfers between devices, to_partner(): lax.ppermute(block, axis, [(i, i ^ 1) for i in range(lax.axis_size(axis))])  8.19 us
    all_to_all x2, waiting for transfers between devices, exchange(): lax.all_to_all(parts, axis, 0, 0, axis_index_groups=groups, tiled=True)  4.11 us
    ppermute x2, starting transfers between devices, to_segment(): return lax.ppermute(block, ('outer', 'inner'), route)  3.83 us
    unnamed x6, local copies, waits for them, and re-layouts  2.55 us
  transfers between devices with their start and end apart: 11, of which 8 were waited for; matrix products, arithmetic and copies ran while one was open for 1% of the time, Pallas kernels for 17%

profile of v14, /device:TPU:16, one launch (start us, length us, event | category | flops | bytes accessed | tf_op | source)
XLA Modules:
  0.0 87.7 jit_solution(18332290683975218891)
XLA Ops:
  0.6 1.7 %pack.1 = bf16[8,272,128]{2,1,0:T(8,128)(2,1)} custom-call(s32[128]{0:T(128)} %position_ref.3, bf16[128,128]{1,0:T(8,128)(2,1)} %key_ref.1, bf16[128,128]{1,0:T(8,128)(2,1)} %value_ref.1), custom_call_target="tpu_custom_call" | custom-call | tf_op jit(solution)/shard_map/pack/pallas_call | solution.py:377
  2.3 8.5 %all-to-all-start = ((bf16[8,272,128]{2,1,0:T(8,128)(2,1)}), bf16[8,272,128]{2,1,0:T(8,128)(2,1)S(1)}, u32[]{:S(2)}, u32[]{:S(2)}) async-start(bf16[8,272,128]{2,1,0:T(8,128)(2,1)} %pack.1), calls=%async_computation | async-start | bytes 1114112 | tf_op jit(solution)/shard_map/all_to_all | solution.py:34
  10.8 1.3 %collective-permute-start.1 = (bf16[128,1024]{1,0:T(8,128)(2,1)}, bf16[128,1024]{1,0:T(8,128)(2,1)S(1)}, u32[]{:S(2)}, u32[]{:S(2)}) collective-permute-start(bf16[128,1024]{1,0:T(8,128)(2,1)} %q_ref.1), channel_id=1, source_target_pairs={{0,1},{1,0},{2,3},{3,2},{4,5},{5,4},{6,7},{7,6},{8,9},{9,8},{10,11... | collective-permute-start | bytes 786440 | tf_op jit(solution)/shard_map/ppermute | solution.py:28
  12.8 1.3 %collective-permute-start = (s32[128]{0:T(128)}, s32[128]{0:T(128)S(1)}, u32[]{:S(2)}, u32[]{:S(2)}) collective-permute-start(s32[128]{0:T(128)} %position_ref.3), channel_id=1, source_target_pairs={{0,1},{1,0},{2,3},{3,2},{4,5},{5,4},{6,7},{7,6},{8,9},{9,8},{10,11... | collective-permute-start | bytes 1544 | tf_op jit(solution)/shard_map/ppermute | solution.py:28
  14.1 10.4 %collective-permute-done.position_partner_ref = s32[128]{0:T(128)S(1)} collective-permute-done((s32[128]{0:T(128)}, s32[128]{0:T(128)S(1)}, u32[]{:S(2)}, u32[]{:S(2)}) %collective-permute-start) | collective-permute-done | bytes 544 | tf_op jit(solution)/shard_map/ppermute | solution.py:28
  25.1 0.9 %copy-done.1 = bf16[128,1024]{1,0:T(8,128)(2,1)S(1)} copy-done((bf16[128,1024]{1,0:T(8,128)(2,1)S(1)}, bf16[128,1024]{1,0:T(8,128)(2,1)}, u32[]{:S(2)}) %copy-start.1) | copy-done | bytes 262168
  27.0 1.2 %stack_pair.1 = (s32[2]{0:T(128)S(1)}, bf16[4,512,128]{2,1,0:T(8,128)(2,1)S(1)}, bf16[4,128,512]{2,1,0:T(8,128)(2,1)S(1)}) custom-call(s32[128]{0:T(128)S(1)} %copy-done, s32[128]{0:T(128)S(1)} %collective-permute-done.position_partner_ref, bf16[128,1024]{1,0:T(8,128)(2,1)S(1)} %copy-done.1, bf16[128,1024]{1,0:T(8,128)(2,1)S(1)} %collective-permute-done.1.q_partner_ref, ...), custom_call_target="tpu_custom_call" | custom-call | flops 4000000000 | bytes 4194304 | tf_op jit(solution)/shard_map/stack_pair/pallas_call | solution.py:348
  29.0 1.9 %collective-permute-start.3 = (bf16[8,272,128]{2,1,0:T(8,128)(2,1)S(1)}, bf16[8,272,128]{2,1,0:T(8,128)(2,1)S(1)}, u32[]{:S(2)}, u32[]{:S(2)}) collective-permute-start(bf16[8,272,128]{2,1,0:T(8,128)(2,1)S(1)} %all-to-all-done.kv_ref), channel_id=1, source_target_pairs={{0,16},{1,17},{2,18},{3,19},{4,20},{5,21},{6,22},{7,23},{8,24},{9,... | collective-permute-start | bytes 1671176 | tf_op jit(solution)/shard_map/ppermute | solution.py:24
  30.9 3.8 %own_forward.1 = (bf16[1024,128]{1,0:T(8,128)(2,1)S(1)}, bf16[1024,128]{1,0:T(8,128)(2,1)S(1)}, s32[8]{0:T(128)S(1)}, s32[4]{0:T(128)S(1)}, bf16[10,256,512]{2,1...) custom-call(s32[2]{0:T(128)S(1)} %get-tuple-element.47.block_ref, ...), custom_call_target="tpu_custom_call" | custom-call | flops 671088640 | bytes 4194304 | tf_op jit(solution)/shard_map/own_forward/pallas_call | solution.py:348
  34.8 7.2 %collective-permute-done.3.kv_ref = bf16[8,272,128]{2,1,0:T(8,128)(2,1)S(1)} collective-permute-done((bf16[8,272,128]{2,1,0:T(8,128)(2,1)S(1)}, bf16[8,272,128]{2,1,0:T(8,128)(2,1)S(1)}, u32[]{:S(2)}, u32[]{:S(2)}) %collective-permute-start.3) | collective-permute-done | bytes 557088 | tf_op jit(solution)/shard_map/ppermute | solution.py:24
  42.0 2.1 %prev_forward_theirs.1 = (bf16[2,4,256,512]{3,2,1,0:T(8,128)(2,1)S(1)}, f32[2,1,512]{2,1,0:T(1,128)S(1)}, f32[3,2,1,512]{3,2,1,0:T(1,128)S(1)}, bf16[2,128,512]{2,1,0:T(8,128)(2,1)S(1)}) custom-call(s32[1]{0:T(128)} %bitcast.has_ref, bf16[4,512,128]{2,1,0:T(8,128)(2,1)S(1)} %get-tuple-element.44.qs_ref, bf16[4,128,512]{2,1,0:T(8,128)(2,1)S(1)} %get-tuple-element.45.dot_ref, ...), custom_call_target="tpu_custom_call" | custom-call | flops 536870912 | bytes 4194304 | tf_op jit(solution)/shard_map/prev_forward_theirs/pallas_call | solution.py:348
  44.1 2.6 %collective-permute-start.5 = (f32[3,2,1,512]{3,2,1,0:T(1,128)S(1)}, f32[3,2,1,512]{3,2,1,0:T(1,128)S(1)}, u32[]{:S(2)}, u32[]{:S(2)}) collective-permute-start(f32[3,2,1,512]{3,2,1,0:T(1,128)S(1)} %get-tuple-element.56.stats_ref), channel_id=1, source_target_pairs={{0,1},{1,0},{2,3},{3,2},{4,5},{5,4},{6,7},{7,6},{8,9},{9,8},{10,11... | collective-permute-start | bytes 36872 | tf_op jit(solution)/shard_map/ppermute | solution.py:28
  46.7 2.1 %prev_forward_mine.1 = (bf16[2,4,256,512]{3,2,1,0:T(8,128)(2,1)S(1)}, f32[2,1,512]{2,1,0:T(1,128)S(1)}, f32[3,2,1,512]{3,2,1,0:T(1,128)S(1)}, f32[2,128,512]{2,1,0:T(8,128)S(1)}) custom-call(s32[1]{0:T(128)} %bitcast.has_ref, bf16[4,512,128]{2,1,0:T(8,128)(2,1)S(1)} %get-tuple-element.44.qs_ref, bf16[4,128,512]{2,1,0:T(8,128)(2,1)S(1)} %get-tuple-element.45.dot_ref, ...), custom_call_target="tpu_custom_call" | custom-call | flops 536870912 | bytes 4194304 | tf_op jit(solution)/shard_map/prev_forward_mine/pallas_call | solution.py:348
  49.0 1.9 %prev_backward_mine.1 = (f32[1024,256]{1,0:T(8,128)S(1)}, bf16[2,128,512]{2,1,0:T(8,128)(2,1)S(1)}, f32[2,1,512]{2,1,0:T(1,128)S(1)}, bf16[2,4,256,512]{3,2,1,0:T(8,128)(2,1)S(1)}, f32[2,2,1,512]{3,2,1,0:T(1,128)S(1)}) custom-call(s32[1]{0:T(128)} %bitcast.has_ref, bf16[4,512,128]{2,1,0:T(8,128)(2,1)S(1)} %get-tuple-element.44.qs_ref, ...), custom_call_target="tpu_custom_call" | custom-call | flops 1073741824 | bytes 4194304 | tf_op jit(solution)/shard_map/prev_backward_mine/pallas_call | solution.py:348
  50.9 1.8 %collective-permute-done.6.other_ref = f32[3,2,1,512]{3,2,1,0:T(1,128)S(1)} collective-permute-done((f32[3,2,1,512]{3,2,1,0:T(1,128)S(1)}, f32[3,2,1,512]{3,2,1,0:T(1,128)S(1)}, u32[]{:S(2)}, u32[]{:S(2)}) %collective-permute-start.6) | collective-permute-done | bytes 12320 | tf_op jit(solution)/shard_map/ppermute | solution.py:28
  52.7 2.2 %prev_backward_theirs.1 = (bf16[8,128,256]{2,1,0:T(8,128)(2,1)S(1)}, bf16[2,128,512]{2,1,0:T(8,128)(2,1)S(1)}, f32[2,1,512]{2,1,0:T(1,128)S(1)}, bf16[2,4,256,512]{3,2,1,0:T(8,128)(2,1)S(1)}) custom-call(s32[1]{0:T(128)} %bitcast.has_ref, bf16[4,512,128]{2,1,0:T(8,128)(2,1)S(1)} %get-tuple-element.44.qs_ref, ...), custom_call_target="tpu_custom_call" | custom-call | flops 1073741824 | bytes 4194304 | tf_op jit(solution)/shard_map/prev_backward_theirs/pallas_call | solution.py:348
  55.0 1.9 %collective-permute-start.8 = (bf16[8,128,256]{2,1,0:T(8,128)(2,1)S(1)}, bf16[8,128,256]{2,1,0:T(8,128)(2,1)S(1)}, u32[]{:S(2)}, u32[]{:S(2)}) collective-permute-start(bf16[8,128,256]{2,1,0:T(8,128)(2,1)S(1)} %get-tuple-element.75), channel_id=1, source_target_pairs={{16,0},{17,1},{18,2},{19,3},{20,4},{21,5},{22,6},{23,7},{24,8},{25... | collective-permute-start | bytes 1572872 | tf_op jit(solution)/shard_map/ppermute | solution.py:24
  56.9 4.8 %own_backward.1 = (f32[128,1024]{1,0:T(8,128)S(1)}, bf16[128,1024]{1,0:T(8,128)(2,1)S(1)}, bf16[8,128,256]{2,1,0:T(8,128)(2,1)S(1)}) custom-call(s32[4]{0:T(128)S(1)} %get-tuple-element.58.allowed_ref, s32[8]{0:T(128)S(1)} %get-tuple-element.59.slots_ref, bf16[4,512,128]{2,1,0:T(8,128)(2,1)S(1)} %get-tuple-element.44.qs_ref, ...), custom_call_target="tpu_custom_call" | custom-call | flops 1342177280 | bytes 4194304 | tf_op jit(solution)/shard_map/own_backward/pallas_call | solution.py:348
  61.7 1.9 %collective-permute-done.8 = bf16[8,128,256]{2,1,0:T(8,128)(2,1)S(1)} collective-permute-done((bf16[8,128,256]{2,1,0:T(8,128)(2,1)S(1)}, bf16[8,128,256]{2,1,0:T(8,128)(2,1)S(1)}, u32[]{:S(2)}, u32[]{:S(2)}) %collective-permute-start.8) | collective-permute-done | bytes 524320 | tf_op jit(solution)/shard_map/ppermute | solution.py:24
  64.5 6.2 %all-to-all-start.1 = ((bf16[8,128,256]{2,1,0:T(8,128)(2,1)}), bf16[8,128,256]{2,1,0:T(8,128)(2,1)S(1)}, u32[]{:S(2)}, u32[]{:S(2)}) async-start(bf16[8,128,256]{2,1,0:T(8,128)(2,1)} %add_convert_fusion), calls=%async_computation.1 | async-start | bytes 1048576 | tf_op jit(solution)/shard_map/all_to_all | solution.py:34
  70.9 1.8 %collective-permute-start.7 = (bf16[128,1024]{1,0:T(8,128)(2,1)S(1)}, bf16[128,1024]{1,0:T(8,128)(2,1)S(1)}, u32[]{:S(2)}, u32[]{:S(2)}) collective-permute-start(bf16[128,1024]{1,0:T(8,128)(2,1)S(1)} %get-tuple-element.73), channel_id=1, source_target_pairs={{0,1},{1,0},{2,3},{3,2},{4,5},{5,4},{6,7},{7,6},{8,9},{9,8},{10,11... | collective-permute-start | bytes 786440 | tf_op jit(solution)/shard_map/ppermute | solution.py:28
  72.7 7.2 %collective-permute-done.4.got_ref = bf16[2,128,512]{2,1,0:T(8,128)(2,1)S(1)} collective-permute-done((bf16[2,128,512]{2,1,0:T(8,128)(2,1)S(1)}, bf16[2,128,512]{2,1,0:T(8,128)(2,1)S(1)}, u32[]{:S(2)}, u32[]{:S(2)}) %collective-permute-start.4) | collective-permute-done | bytes 262176 | tf_op jit(solution)/shard_map/ppermute | solution.py:28
  80.8 2.1 %collective-permute-done.7 = bf16[128,1024]{1,0:T(8,128)(2,1)S(1)} collective-permute-done((bf16[128,1024]{1,0:T(8,128)(2,1)S(1)}, bf16[128,1024]{1,0:T(8,128)(2,1)S(1)}, u32[]{:S(2)}, u32[]{:S(2)}) %collective-permute-start.7) | collective-permute-done | bytes 262176 | tf_op jit(solution)/shard_map/ppermute | solution.py:28
  83.6 3.4 %all-to-all-done.1.parts_ref = bf16[8,128,256]{2,1,0:T(8,128)(2,1)S(1)} async-done(((bf16[8,128,256]{2,1,0:T(8,128)(2,1)}), bf16[8,128,256]{2,1,0:T(8,128)(2,1)S(1)}, u32[]{:S(2)}, u32[]{:S(2)}) %all-to-all-start.1) | async-done | bytes 524320 | tf_op jit(solution)/shard_map/all_to_all | solution.py:34
  (16 shorter events, 6.9 us)
Async XLA Ops:
  2.3 26.7 %all-to-all-start = ((bf16[8,272,128]{2,1,0:T(8,128)(2,1)}), bf16[8,272,128]{2,1,0:T(8,128)(2,1)S(1)}, u32[]{:S(2)}, u32[]{:S(2)}) async-start(bf16[8,272,128]{2,1,0:T(8,128)(2,1)} %pack.1), calls=%async_computation | async-start | bytes 1114112 | tf_op jit(solution)/shard_map/all_to_all | solution.py:34
  10.8 13.7 %collective-permute-start.1 = (bf16[128,1024]{1,0:T(8,128)(2,1)}, bf16[128,1024]{1,0:T(8,128)(2,1)S(1)}, u32[]{:S(2)}, u32[]{:S(2)}) collective-permute-start(bf16[128,1024]{1,0:T(8,128)(2,1)} %q_ref.1), channel_id=1, source_target_pairs={{0,1},{1,0},{2,3},{3,2},{4,5},{5,4},{6,7},{7,6},{8,9},{9,8},{10,11... | collective-permute-start | bytes 786440 | tf_op jit(solution)/shard_map/ppermute | solution.py:28
  12.1 12.4 %collective-permute-start.2 = (bf16[128,1024]{1,0:T(8,128)(2,1)}, bf16[128,1024]{1,0:T(8,128)(2,1)S(1)}, u32[]{:S(2)}, u32[]{:S(2)}) collective-permute-start(bf16[128,1024]{1,0:T(8,128)(2,1)} %do_ref.1), channel_id=1, source_target_pairs={{0,1},{1,0},{2,3},{3,2},{4,5},{5,4},{6,7},{7,6},{8,9},{9,8},{10,11... | collective-permute-start | bytes 786440 | tf_op jit(solution)/shard_map/ppermute | solution.py:28
  12.8 11.6 %collective-permute-start = (s32[128]{0:T(128)}, s32[128]{0:T(128)S(1)}, u32[]{:S(2)}, u32[]{:S(2)}) collective-permute-start(s32[128]{0:T(128)} %position_ref.3), channel_id=1, source_target_pairs={{0,1},{1,0},{2,3},{3,2},{4,5},{5,4},{6,7},{7,6},{8,9},{9,8},{10,11... | collective-permute-start | bytes 1544 | tf_op jit(solution)/shard_map/ppermute | solution.py:28
  24.5 0.7 copy-start
  25.1 0.9 %copy-start.1 = (bf16[128,1024]{1,0:T(8,128)(2,1)S(1)}, bf16[128,1024]{1,0:T(8,128)(2,1)}, u32[]{:S(2)}) copy-start(bf16[128,1024]{1,0:T(8,128)(2,1)} %q_ref.1) | copy-start | bytes 786436
  26.1 0.9 %copy-start.2 = (bf16[128,1024]{1,0:T(8,128)(2,1)S(1)}, bf16[128,1024]{1,0:T(8,128)(2,1)}, u32[]{:S(2)}) copy-start(bf16[128,1024]{1,0:T(8,128)(2,1)} %do_ref.1) | copy-start | bytes 786436
  29.0 12.9 %collective-permute-start.3 = (bf16[8,272,128]{2,1,0:T(8,128)(2,1)S(1)}, bf16[8,272,128]{2,1,0:T(8,128)(2,1)S(1)}, u32[]{:S(2)}, u32[]{:S(2)}) collective-permute-start(bf16[8,272,128]{2,1,0:T(8,128)(2,1)S(1)} %all-to-all-done.kv_ref), channel_id=1, source_target_pairs={{0,16},{1,17},{2,18},{3,19},{4,20},{5,21},{6,22},{7,23},{8,24},{9,... | collective-permute-start | bytes 1671176 | tf_op jit(solution)/shard_map/ppermute | solution.py:24
  44.1 5.0 %collective-permute-start.5 = (f32[3,2,1,512]{3,2,1,0:T(1,128)S(1)}, f32[3,2,1,512]{3,2,1,0:T(1,128)S(1)}, u32[]{:S(2)}, u32[]{:S(2)}) collective-permute-start(f32[3,2,1,512]{3,2,1,0:T(1,128)S(1)} %get-tuple-element.56.stats_ref), channel_id=1, source_target_pairs={{0,1},{1,0},{2,3},{3,2},{4,5},{5,4},{6,7},{7,6},{8,9},{9,8},{10,11... | collective-permute-start | bytes 36872 | tf_op jit(solution)/shard_map/ppermute | solution.py:28
  48.8 4.0 %collective-permute-start.6 = (f32[3,2,1,512]{3,2,1,0:T(1,128)S(1)}, f32[3,2,1,512]{3,2,1,0:T(1,128)S(1)}, u32[]{:S(2)}, u32[]{:S(2)}) collective-permute-start(f32[3,2,1,512]{3,2,1,0:T(1,128)S(1)} %get-tuple-element.55.stats_ref), channel_id=1, source_target_pairs={{0,1},{1,0},{2,3},{3,2},{4,5},{5,4},{6,7},{7,6},{8,9},{9,8},{10,11... | collective-permute-start | bytes 36872 | tf_op jit(solution)/shard_map/ppermute | solution.py:28
  55.0 8.6 %collective-permute-start.8 = (bf16[8,128,256]{2,1,0:T(8,128)(2,1)S(1)}, bf16[8,128,256]{2,1,0:T(8,128)(2,1)S(1)}, u32[]{:S(2)}, u32[]{:S(2)}) collective-permute-start(bf16[8,128,256]{2,1,0:T(8,128)(2,1)S(1)} %get-tuple-element.75), channel_id=1, source_target_pairs={{16,0},{17,1},{18,2},{19,3},{20,4},{21,5},{22,6},{23,7},{24,8},{25... | collective-permute-start | bytes 1572872 | tf_op jit(solution)/shard_map/ppermute | solution.py:24
  64.5 22.5 %all-to-all-start.1 = ((bf16[8,128,256]{2,1,0:T(8,128)(2,1)}), bf16[8,128,256]{2,1,0:T(8,128)(2,1)S(1)}, u32[]{:S(2)}, u32[]{:S(2)}) async-start(bf16[8,128,256]{2,1,0:T(8,128)(2,1)} %add_convert_fusion), calls=%async_computation.1 | async-start | bytes 1048576 | tf_op jit(solution)/shard_map/all_to_all | solution.py:34
  70.7 9.2 %collective-permute-start.4 = (bf16[2,128,512]{2,1,0:T(8,128)(2,1)S(1)}, bf16[2,128,512]{2,1,0:T(8,128)(2,1)S(1)}, u32[]{:S(2)}, u32[]{:S(2)}) collective-permute-start(bf16[2,128,512]{2,1,0:T(8,128)(2,1)S(1)} %get-tuple-element.52), channel_id=1, source_target_pairs={{0,1},{1,0},{2,3},{3,2},{4,5},{5,4},{6,7},{7,6},{8,9},{9,8},{10,11... | collective-permute-start | bytes 786440 | tf_op jit(solution)/shard_map/ppermute | solution.py:28
  70.9 11.9 %collective-permute-start.7 = (bf16[128,1024]{1,0:T(8,128)(2,1)S(1)}, bf16[128,1024]{1,0:T(8,128)(2,1)S(1)}, u32[]{:S(2)}, u32[]{:S(2)}) collective-permute-start(bf16[128,1024]{1,0:T(8,128)(2,1)S(1)} %get-tuple-element.73), channel_id=1, source_target_pairs={{0,1},{1,0},{2,3},{3,2},{4,5},{5,4},{6,7},{7,6},{8,9},{9,8},{10,11... | collective-permute-start | bytes 786440 | tf_op jit(solution)/shard_map/ppermute | solution.py:28

commit v15 on v12

--- a/solution.py
+++ b/solution.py
@@ -467,9 +467,10 @@
         [((span_rows, 2 * head_dim), f32), by_query],
         flops=4 * steps * unit,
     )(allowed, slots, qs, ks, vs, p_own, dos_mine, shift_mine, ds_mine, dos_theirs, shift_theirs, ds_theirs, prev_kv)
+    own_terms, got, dq_partner = lax.optimization_barrier((own_terms, got, dq_partner))
+    terms = (own_terms.astype(f32) + returned.astype(f32)).astype(bf16)
     (attended,) = call(merge_attended, "merge_attended", [tokens], (), [])(out, got, factor)
     dq_other = to_partner(dq_partner, "inner")
-    terms = (own_terms.astype(f32) + returned.astype(f32)).astype(bf16)
     key_grads = jnp.sum(exchange(terms, "inner").astype(f32), axis=0)
     grad_queries = (dq + dq_other.astype(f32)).astype(bf16)
     grad_keys = key_grads[:, :head_dim].astype(bf16)

time: 87.8 us -> 91.1 us (1.038)
  waiting for transfers between devices: 34.5 us -> 39.3 us
  starting transfers between devices: 26.7 us -> 25.3 us
    all_to_all x2, waiting for transfers between devices: 4.1 us -> 9.73 us  [exchange(): lax.all_to_all(parts, axis, 0, 0, axis_index_groups=groups, tiled=True)]
    ppermute x2, waiting for transfers between devices: 9.06 us -> 7.18 us  [to_segment(): return lax.ppermute(block, ('outer', 'inner'), route)]
    ppermute x7, starting transfers between devices: 8.2 us -> 6.78 us  [to_partner(): lax.ppermute(block, axis, [(i, i ^ 1) for i in range(lax.axis_size(axis))])]
    ppermute x7, waiting for transfers between devices: 21.4 us -> 22.4 us  [to_partner(): lax.ppermute(block, axis, [(i, i ^ 1) for i in range(lax.axis_size(axis))])]
  transfers between devices with their start and end apart: 11 -> 11, of which waited for: 8 -> 7; matrix products, arithmetic and copies ran while one was open for 1% -> 1% of each run, Pallas kernels for 17% -> 16%
where the time goes in v15:
time: 91.1 us; the launch traced here: 90.6 us
  waiting for transfers between devices  39.3 us (43%)
  starting transfers between devices  25.3 us (28%)
  Pallas kernels  20.3 us (22%)
  local copies, waits for them, and re-layouts  3.18 us (3%)
  other arithmetic  1.77 us (2%)
    ppermute x7, waiting for transfers between devices, to_partner(): lax.ppermute(block, axis, [(i, i ^ 1) for i in range(lax.axis_size(axis))])  22.4 us
    pallas_call x8, Pallas kernels, run(): pl.pallas_call(kernel, name=name, grid=(1,) if stream else (), out_shape=...  18.6 us
    all_to_all x2, starting transfers between devices, exchange(): lax.all_to_all(parts, axis, 0, 0, axis_index_groups=groups, tiled=True)  14.7 us
    all_to_all x2, waiting for transfers between devices, exchange(): lax.all_to_all(parts, axis, 0, 0, axis_index_groups=groups, tiled=True)  9.73 us
    ppermute x2, waiting for transfers between devices, to_segment(): return lax.ppermute(block, ('outer', 'inner'), route)  7.18 us
    ppermute x7, starting transfers between devices, to_partner(): lax.ppermute(block, axis, [(i, i ^ 1) for i in range(lax.axis_size(axis))])  6.78 us
    ppermute x2, starting transfers between devices, to_segment(): return lax.ppermute(block, ('outer', 'inner'), route)  3.83 us
    unnamed x6, local copies, waits for them, and re-layouts  2.55 us
  transfers between devices with their start and end apart: 11, of which 7 were waited for; matrix products, arithmetic and copies ran while one was open for 1% of the time, Pallas kernels for 16%

profile of v15, /device:TPU:16, one launch (start us, length us, event | category | flops | bytes accessed | tf_op | source)
XLA Modules:
  0.0 90.6 jit_solution(14149444375247768656)
XLA Ops:
  0.6 1.7 %pack.1 = bf16[8,272,128]{2,1,0:T(8,128)(2,1)} custom-call(s32[128]{0:T(128)} %position_ref.3, bf16[128,128]{1,0:T(8,128)(2,1)} %key_ref.1, bf16[128,128]{1,0:T(8,128)(2,1)} %value_ref.1), custom_call_target="tpu_custom_call" | custom-call | tf_op jit(solution)/shard_map/pack/pallas_call | solution.py:366
  2.3 8.5 %all-to-all-start = ((bf16[8,272,128]{2,1,0:T(8,128)(2,1)}), bf16[8,272,128]{2,1,0:T(8,128)(2,1)S(1)}, u32[]{:S(2)}, u32[]{:S(2)}) async-start(bf16[8,272,128]{2,1,0:T(8,128)(2,1)} %pack.1), calls=%async_computation | async-start | bytes 1114112 | tf_op jit(solution)/shard_map/all_to_all | solution.py:34
  10.8 1.3 %collective-permute-start.1 = (bf16[128,1024]{1,0:T(8,128)(2,1)}, bf16[128,1024]{1,0:T(8,128)(2,1)S(1)}, u32[]{:S(2)}, u32[]{:S(2)}) collective-permute-start(bf16[128,1024]{1,0:T(8,128)(2,1)} %q_ref.1), channel_id=1, source_target_pairs={{0,1},{1,0},{2,3},{3,2},{4,5},{5,4},{6,7},{7,6},{8,9},{9,8},{10,11... | collective-permute-start | bytes 786440 | tf_op jit(solution)/shard_map/ppermute | solution.py:28
  12.8 1.3 %collective-permute-start = (s32[128]{0:T(128)}, s32[128]{0:T(128)S(1)}, u32[]{:S(2)}, u32[]{:S(2)}) collective-permute-start(s32[128]{0:T(128)} %position_ref.3), channel_id=1, source_target_pairs={{0,1},{1,0},{2,3},{3,2},{4,5},{5,4},{6,7},{7,6},{8,9},{9,8},{10,11... | collective-permute-start | bytes 1544 | tf_op jit(solution)/shard_map/ppermute | solution.py:28
  14.1 10.4 %collective-permute-done.position_partner_ref = s32[128]{0:T(128)S(1)} collective-permute-done((s32[128]{0:T(128)}, s32[128]{0:T(128)S(1)}, u32[]{:S(2)}, u32[]{:S(2)}) %collective-permute-start) | collective-permute-done | bytes 544 | tf_op jit(solution)/shard_map/ppermute | solution.py:28
  25.1 0.9 %copy-done.1 = bf16[128,1024]{1,0:T(8,128)(2,1)S(1)} copy-done((bf16[128,1024]{1,0:T(8,128)(2,1)S(1)}, bf16[128,1024]{1,0:T(8,128)(2,1)}, u32[]{:S(2)}) %copy-start.1) | copy-done | bytes 262168
  26.1 0.9 %copy-done.2 = bf16[128,1024]{1,0:T(8,128)(2,1)S(1)} copy-done((bf16[128,1024]{1,0:T(8,128)(2,1)S(1)}, bf16[128,1024]{1,0:T(8,128)(2,1)}, u32[]{:S(2)}) %copy-start.2) | copy-done | bytes 262168
  27.0 1.2 %stack_pair.1 = (s32[2]{0:T(128)S(1)}, bf16[4,512,128]{2,1,0:T(8,128)(2,1)S(1)}, bf16[4,128,512]{2,1,0:T(8,128)(2,1)S(1)}) custom-call(s32[128]{0:T(128)S(1)} %copy-done, s32[128]{0:T(128)S(1)} %collective-permute-done.position_partner_ref, bf16[128,1024]{1,0:T(8,128)(2,1)S(1)} %copy-done.1, bf16[128,1024]{1,0:T(8,128)(2,1)S(1)} %collective-permute-done.1.q_partner_ref, ...), custom_call_target="tpu_custom_call" | custom-call | flops 4000000000 | bytes 4194304 | tf_op jit(solution)/shard_map/stack_pair/pallas_call | solution.py:337
  29.0 1.9 %collective-permute-start.3 = (bf16[8,272,128]{2,1,0:T(8,128)(2,1)S(1)}, bf16[8,272,128]{2,1,0:T(8,128)(2,1)S(1)}, u32[]{:S(2)}, u32[]{:S(2)}) collective-permute-start(bf16[8,272,128]{2,1,0:T(8,128)(2,1)S(1)} %all-to-all-done.kv_ref), channel_id=1, source_target_pairs={{0,16},{1,17},{2,18},{3,19},{4,20},{5,21},{6,22},{7,23},{8,24},{9,... | collective-permute-start | bytes 1671176 | tf_op jit(solution)/shard_map/ppermute | solution.py:24
  30.9 3.8 %own_forward.1 = (bf16[1024,128]{1,0:T(8,128)(2,1)S(1)}, bf16[1024,128]{1,0:T(8,128)(2,1)S(1)}, s32[8]{0:T(128)S(1)}, s32[4]{0:T(128)S(1)}, bf16[10,256,512]{2,1...) custom-call(s32[2]{0:T(128)S(1)} %get-tuple-element.48.block_ref, ...), custom_call_target="tpu_custom_call" | custom-call | flops 671088640 | bytes 4194304 | tf_op jit(solution)/shard_map/own_forward/pallas_call | solution.py:337
  34.8 7.2 %collective-permute-done.3.kv_ref = bf16[8,272,128]{2,1,0:T(8,128)(2,1)S(1)} collective-permute-done((bf16[8,272,128]{2,1,0:T(8,128)(2,1)S(1)}, bf16[8,272,128]{2,1,0:T(8,128)(2,1)S(1)}, u32[]{:S(2)}, u32[]{:S(2)}) %collective-permute-start.3) | collective-permute-done | bytes 557088 | tf_op jit(solution)/shard_map/ppermute | solution.py:24
  41.9 1.9 %prev_forward_theirs.1 = (bf16[2,4,256,512]{3,2,1,0:T(8,128)(2,1)S(1)}, f32[2,1,512]{2,1,0:T(1,128)S(1)}, f32[3,2,1,512]{3,2,1,0:T(1,128)S(1)}, bf16[2,128,512]{2,1,0:T(8,128)(2,1)S(1)}) custom-call(s32[1]{0:T(128)} %bitcast.has_ref, bf16[4,512,128]{2,1,0:T(8,128)(2,1)S(1)} %get-tuple-element.45.qs_ref, bf16[4,128,512]{2,1,0:T(8,128)(2,1)S(1)} %get-tuple-element.46.dot_ref, ...), custom_call_target="tpu_custom_call" | custom-call | flops 536870912 | bytes 4194304 | tf_op jit(solution)/shard_map/prev_forward_theirs/pallas_call | solution.py:337
  43.9 2.6 %collective-permute-start.4 = (f32[3,2,1,512]{3,2,1,0:T(1,128)S(1)}, f32[3,2,1,512]{3,2,1,0:T(1,128)S(1)}, u32[]{:S(2)}, u32[]{:S(2)}) collective-permute-start(f32[3,2,1,512]{3,2,1,0:T(1,128)S(1)} %get-tuple-element.61.stats_ref), channel_id=1, source_target_pairs={{0,1},{1,0},{2,3},{3,2},{4,5},{5,4},{6,7},{7,6},{8,9},{9,8},{10,11... | collective-permute-start | bytes 36872 | tf_op jit(solution)/shard_map/ppermute | solution.py:28
  46.5 1.9 %prev_forward_mine.1 = (bf16[2,4,256,512]{3,2,1,0:T(8,128)(2,1)S(1)}, f32[2,1,512]{2,1,0:T(1,128)S(1)}, f32[3,2,1,512]{3,2,1,0:T(1,128)S(1)}, f32[2,128,512]{2,1,0:T(8,128)S(1)}) custom-call(s32[1]{0:T(128)} %bitcast.has_ref, bf16[4,512,128]{2,1,0:T(8,128)(2,1)S(1)} %get-tuple-element.45.qs_ref, bf16[4,128,512]{2,1,0:T(8,128)(2,1)S(1)} %get-tuple-element.46.dot_ref, ...), custom_call_target="tpu_custom_call" | custom-call | flops 536870912 | bytes 4194304 | tf_op jit(solution)/shard_map/prev_forward_mine/pallas_call | solution.py:337
  48.7 1.9 %prev_backward_mine.1 = (f32[1024,256]{1,0:T(8,128)S(1)}, bf16[2,128,512]{2,1,0:T(8,128)(2,1)S(1)}, f32[2,1,512]{2,1,0:T(1,128)S(1)}, bf16[2,4,256,512]{3,2,1,0:T(8,128)(2,1)S(1)}, f32[2,2,1,512]{3,2,1,0:T(1,128)S(1)}) custom-call(s32[1]{0:T(128)} %bitcast.has_ref, bf16[4,512,128]{2,1,0:T(8,128)(2,1)S(1)} %get-tuple-element.45.qs_ref, ...), custom_call_target="tpu_custom_call" | custom-call | flops 1073741824 | bytes 4194304 | tf_op jit(solution)/shard_map/prev_backward_mine/pallas_call | solution.py:337
  50.6 1.8 %collective-permute-done.5.other_ref = f32[3,2,1,512]{3,2,1,0:T(1,128)S(1)} collective-permute-done((f32[3,2,1,512]{3,2,1,0:T(1,128)S(1)}, f32[3,2,1,512]{3,2,1,0:T(1,128)S(1)}, u32[]{:S(2)}, u32[]{:S(2)}) %collective-permute-start.5) | collective-permute-done | bytes 12320 | tf_op jit(solution)/shard_map/ppermute | solution.py:28
  52.4 2.2 %prev_backward_theirs.1 = (bf16[8,128,256]{2,1,0:T(8,128)(2,1)S(1)}, bf16[2,128,512]{2,1,0:T(8,128)(2,1)S(1)}, f32[2,1,512]{2,1,0:T(1,128)S(1)}, bf16[2,4,256,512]{3,2,1,0:T(8,128)(2,1)S(1)}) custom-call(s32[1]{0:T(128)} %bitcast.has_ref, bf16[4,512,128]{2,1,0:T(8,128)(2,1)S(1)} %get-tuple-element.45.qs_ref, ...), custom_call_target="tpu_custom_call" | custom-call | flops 1073741824 | bytes 4194304 | tf_op jit(solution)/shard_map/prev_backward_theirs/pallas_call | solution.py:337
  54.6 1.9 %collective-permute-start.8 = (bf16[8,128,256]{2,1,0:T(8,128)(2,1)S(1)}, bf16[8,128,256]{2,1,0:T(8,128)(2,1)S(1)}, u32[]{:S(2)}, u32[]{:S(2)}) collective-permute-start(bf16[8,128,256]{2,1,0:T(8,128)(2,1)S(1)} %get-tuple-element.79), channel_id=1, source_target_pairs={{16,0},{17,1},{18,2},{19,3},{20,4},{21,5},{22,6},{23,7},{24,8},{25... | collective-permute-start | bytes 1572872 | tf_op jit(solution)/shard_map/ppermute | solution.py:24
  56.9 4.7 %own_backward.1 = (f32[128,1024]{1,0:T(8,128)S(1)}, bf16[128,1024]{1,0:T(8,128)(2,1)S(1)}, bf16[8,128,256]{2,1,0:T(8,128)(2,1)S(1)}) custom-call(s32[4]{0:T(128)S(1)} %get-tuple-element.53.allowed_ref, s32[8]{0:T(128)S(1)} %get-tuple-element.54.slots_ref, bf16[4,512,128]{2,1,0:T(8,128)(2,1)S(1)} %get-tuple-element.45.qs_ref, ...), custom_call_target="tpu_custom_call" | custom-call | flops 1342177280 | bytes 4194304 | tf_op jit(solution)/shard_map/own_backward/pallas_call | solution.py:337
  61.6 3.7 %collective-permute-done.6.got_ref = bf16[2,128,512]{2,1,0:T(8,128)(2,1)S(1)} collective-permute-done((bf16[2,128,512]{2,1,0:T(8,128)(2,1)S(1)}, bf16[2,128,512]{2,1,0:T(8,128)(2,1)S(1)}, u32[]{:S(2)}, u32[]{:S(2)}) %collective-permute-start.6) | collective-permute-done | bytes 262176 | tf_op jit(solution)/shard_map/ppermute | solution.py:28
  65.4 0.9 %add_convert_fusion = bf16[8,128,256]{2,1,0:T(8,128)(2,1)} fusion(bf16[8,128,256]{2,1,0:T(8,128)(2,1)S(1)} %collective-permute-done.8, bf16[8,128,256]{2,1,0:T(8,128)(2,1)S(1)} %get-tuple-element.78), kind=kLoop, calls=%fused_computation | loop fusion | flops 1048576 | bytes 1572864 | tf_op jit(solution)/shard_map/convert_element_type | solution.py:471
  66.3 6.2 %all-to-all-start.1 = ((bf16[8,128,256]{2,1,0:T(8,128)(2,1)}), bf16[8,128,256]{2,1,0:T(8,128)(2,1)S(1)}, u32[]{:S(2)}, u32[]{:S(2)}) async-start(bf16[8,128,256]{2,1,0:T(8,128)(2,1)} %add_convert_fusion), calls=%async_computation.1 | async-start | bytes 1048576 | tf_op jit(solution)/shard_map/all_to_all | solution.py:34
  73.6 6.5 %collective-permute-done.7 = bf16[128,1024]{1,0:T(8,128)(2,1)S(1)} collective-permute-done((bf16[128,1024]{1,0:T(8,128)(2,1)S(1)}, bf16[128,1024]{1,0:T(8,128)(2,1)S(1)}, u32[]{:S(2)}, u32[]{:S(2)}) %collective-permute-start.7) | collective-permute-done | bytes 262176 | tf_op jit(solution)/shard_map/ppermute | solution.py:28
  80.9 9.0 %all-to-all-done.1 = bf16[8,128,256]{2,1,0:T(8,128)(2,1)S(1)} async-done(((bf16[8,128,256]{2,1,0:T(8,128)(2,1)}), bf16[8,128,256]{2,1,0:T(8,128)(2,1)S(1)}, u32[]{:S(2)}, u32[]{:S(2)}) %all-to-all-start.1) | async-done | bytes 524320 | tf_op jit(solution)/shard_map/all_to_all | solution.py:34
  (17 shorter events, 5.4 us)
Async XLA Ops:
  2.3 26.7 %all-to-all-start = ((bf16[8,272,128]{2,1,0:T(8,128)(2,1)}), bf16[8,272,128]{2,1,0:T(8,128)(2,1)S(1)}, u32[]{:S(2)}, u32[]{:S(2)}) async-start(bf16[8,272,128]{2,1,0:T(8,128)(2,1)} %pack.1), calls=%async_computation | async-start | bytes 1114112 | tf_op jit(solution)/shard_map/all_to_all | solution.py:34
  10.8 13.7 %collective-permute-start.1 = (bf16[128,1024]{1,0:T(8,128)(2,1)}, bf16[128,1024]{1,0:T(8,128)(2,1)S(1)}, u32[]{:S(2)}, u32[]{:S(2)}) collective-permute-start(bf16[128,1024]{1,0:T(8,128)(2,1)} %q_ref.1), channel_id=1, source_target_pairs={{0,1},{1,0},{2,3},{3,2},{4,5},{5,4},{6,7},{7,6},{8,9},{9,8},{10,11... | collective-permute-start | bytes 786440 | tf_op jit(solution)/shard_map/ppermute | solution.py:28
  12.1 12.4 %collective-permute-start.2 = (bf16[128,1024]{1,0:T(8,128)(2,1)}, bf16[128,1024]{1,0:T(8,128)(2,1)S(1)}, u32[]{:S(2)}, u32[]{:S(2)}) collective-permute-start(bf16[128,1024]{1,0:T(8,128)(2,1)} %do_ref.1), channel_id=1, source_target_pairs={{0,1},{1,0},{2,3},{3,2},{4,5},{5,4},{6,7},{7,6},{8,9},{9,8},{10,11... | collective-permute-start | bytes 786440 | tf_op jit(solution)/shard_map/ppermute | solution.py:28
  12.8 11.6 %collective-permute-start = (s32[128]{0:T(128)}, s32[128]{0:T(128)S(1)}, u32[]{:S(2)}, u32[]{:S(2)}) collective-permute-start(s32[128]{0:T(128)} %position_ref.3), channel_id=1, source_target_pairs={{0,1},{1,0},{2,3},{3,2},{4,5},{5,4},{6,7},{7,6},{8,9},{9,8},{10,11... | collective-permute-start | bytes 1544 | tf_op jit(solution)/shard_map/ppermute | solution.py:28
  24.5 0.7 copy-start
  25.1 0.9 %copy-start.1 = (bf16[128,1024]{1,0:T(8,128)(2,1)S(1)}, bf16[128,1024]{1,0:T(8,128)(2,1)}, u32[]{:S(2)}) copy-start(bf16[128,1024]{1,0:T(8,128)(2,1)} %q_ref.1) | copy-start | bytes 786436
  26.1 0.9 %copy-start.2 = (bf16[128,1024]{1,0:T(8,128)(2,1)S(1)}, bf16[128,1024]{1,0:T(8,128)(2,1)}, u32[]{:S(2)}) copy-start(bf16[128,1024]{1,0:T(8,128)(2,1)} %do_ref.1) | copy-start | bytes 786436
  29.0 12.9 %collective-permute-start.3 = (bf16[8,272,128]{2,1,0:T(8,128)(2,1)S(1)}, bf16[8,272,128]{2,1,0:T(8,128)(2,1)S(1)}, u32[]{:S(2)}, u32[]{:S(2)}) collective-permute-start(bf16[8,272,128]{2,1,0:T(8,128)(2,1)S(1)} %all-to-all-done.kv_ref), channel_id=1, source_target_pairs={{0,16},{1,17},{2,18},{3,19},{4,20},{5,21},{6,22},{7,23},{8,24},{9,... | collective-permute-start | bytes 1671176 | tf_op jit(solution)/shard_map/ppermute | solution.py:24
  43.9 4.8 %collective-permute-start.4 = (f32[3,2,1,512]{3,2,1,0:T(1,128)S(1)}, f32[3,2,1,512]{3,2,1,0:T(1,128)S(1)}, u32[]{:S(2)}, u32[]{:S(2)}) collective-permute-start(f32[3,2,1,512]{3,2,1,0:T(1,128)S(1)} %get-tuple-element.61.stats_ref), channel_id=1, source_target_pairs={{0,1},{1,0},{2,3},{3,2},{4,5},{5,4},{6,7},{7,6},{8,9},{9,8},{10,11... | collective-permute-start | bytes 36872 | tf_op jit(solution)/shard_map/ppermute | solution.py:28
  48.4 4.0 %collective-permute-start.5 = (f32[3,2,1,512]{3,2,1,0:T(1,128)S(1)}, f32[3,2,1,512]{3,2,1,0:T(1,128)S(1)}, u32[]{:S(2)}, u32[]{:S(2)}) collective-permute-start(f32[3,2,1,512]{3,2,1,0:T(1,128)S(1)} %get-tuple-element.60.stats_ref), channel_id=1, source_target_pairs={{0,1},{1,0},{2,3},{3,2},{4,5},{5,4},{6,7},{7,6},{8,9},{9,8},{10,11... | collective-permute-start | bytes 36872 | tf_op jit(solution)/shard_map/ppermute | solution.py:28
  54.6 10.7 %collective-permute-start.8 = (bf16[8,128,256]{2,1,0:T(8,128)(2,1)S(1)}, bf16[8,128,256]{2,1,0:T(8,128)(2,1)S(1)}, u32[]{:S(2)}, u32[]{:S(2)}) collective-permute-start(bf16[8,128,256]{2,1,0:T(8,128)(2,1)S(1)} %get-tuple-element.79), channel_id=1, source_target_pairs={{16,0},{17,1},{18,2},{19,3},{20,4},{21,5},{22,6},{23,7},{24,8},{25... | collective-permute-start | bytes 1572872 | tf_op jit(solution)/shard_map/ppermute | solution.py:24
  56.6 8.8 %collective-permute-start.6 = (bf16[2,128,512]{2,1,0:T(8,128)(2,1)S(1)}, bf16[2,128,512]{2,1,0:T(8,128)(2,1)S(1)}, u32[]{:S(2)}, u32[]{:S(2)}) collective-permute-start(bf16[2,128,512]{2,1,0:T(8,128)(2,1)S(1)} %get-tuple-element.72), channel_id=1, source_target_pairs={{0,1},{1,0},{2,3},{3,2},{4,5},{5,4},{6,7},{7,6},{8,9},{9,8},{10,11... | collective-permute-start | bytes 786440 | tf_op jit(solution)/shard_map/ppermute | solution.py:28
  66.3 23.6 %all-to-all-start.1 = ((bf16[8,128,256]{2,1,0:T(8,128)(2,1)}), bf16[8,128,256]{2,1,0:T(8,128)(2,1)S(1)}, u32[]{:S(2)}, u32[]{:S(2)}) async-start(bf16[8,128,256]{2,1,0:T(8,128)(2,1)} %add_convert_fusion), calls=%async_computation.1 | async-start | bytes 1048576 | tf_op jit(solution)/shard_map/all_to_all | solution.py:34
  72.5 7.6 %collective-permute-start.7 = (bf16[128,1024]{1,0:T(8,128)(2,1)S(1)}, bf16[128,1024]{1,0:T(8,128)(2,1)S(1)}, u32[]{:S(2)}, u32[]{:S(2)}) collective-permute-start(bf16[128,1024]{1,0:T(8,128)(2,1)S(1)} %get-tuple-element.77), channel_id=1, source_target_pairs={{0,1},{1,0},{2,3},{3,2},{4,5},{5,4},{6,7},{7,6},{8,9},{9,8},{10,11... | collective-permute-start | bytes 786440 | tf_op jit(solution)/shard_map/ppermute | solution.py:28
